TPU v7x, 32 devices: a whole 2x2x4 slice. The times are simulated.
32 devices in a mesh: dp: 16 (over z, x, core), mem: 2 (over y).
Axes of the slice: x: 2, y: 2, z: 4, core: 2. Of those that a mesh axis runs over, the one named last changes fastest.
Arguments:
- target_in: bfloat16 [16384, 1024], P(('dp', 'mem')), may hold values from -6 to 6
- memory_in: bfloat16 [16, 2, 2, 2, 384, 1024], P('dp', None, 'mem'), may hold values from -6 to 6
- bucket_ids: int32 [16, 2], P('dp'), may hold values from 0 to 1, as said below
- target_lengths: int32 [16, 2, 2], P('dp', 'mem'), may hold values from 0 to 512, as said below
- memory_mask: int32 [16, 2, 2, 2, 384], P('dp', None, 'mem'), may hold values from 0 to 1, as said below
- self_qkv: float32 [1024, 3072], P(('dp', 'mem')), may hold values from -0.1875 to 0.1875
- self_out: float32 [1024, 1024], P(('dp', 'mem')), may hold values from -4 to 4
- cross_q: float32 [1024, 1024], P(('dp', 'mem')), may hold values from -0.1875 to 0.1875
- cross_kv: float32 [1024, 2048], P(('dp', 'mem')), may hold values from -0.1875 to 0.1875
- cross_out: float32 [1024, 1024], P(('dp', 'mem')), may hold values from -4 to 4
- ffn_in: float32 [1024, 4096], P(('dp', 'mem')), may hold values from -0.1875 to 0.1875
- ffn_out: float32 [4096, 1024], P(('dp', 'mem')), may hold values from -0.5 to 0.5
- norm_gains: float32 [1024, 3], P(('dp', 'mem')), may hold values from 0.5 to 1.5
- norm_biases: float32 [1024, 3], P(('dp', 'mem')), may hold values from -1.8 to 1.8
- grad_out: bfloat16 [16384, 1024], P(('dp', 'mem')), may hold values from -6 to 6
Outputs:
- layer_out: bfloat16 [16384, 1024], P(('dp', 'mem'))
- target_grad: bfloat16 [16384, 1024], P(('dp', 'mem'))
- memory_grad: bfloat16 [16, 2, 2, 2, 384, 1024], P('dp', None, 'mem')
- self_qkv_grad: float32 [1024, 3072], P(('dp', 'mem'))
- self_out_grad: float32 [1024, 1024], P(('dp', 'mem'))
- cross_q_grad: float32 [1024, 1024], P(('dp', 'mem'))
- cross_kv_grad: float32 [1024, 2048], P(('dp', 'mem'))
- cross_out_grad: float32 [1024, 1024], P(('dp', 'mem'))
- ffn_in_grad: float32 [1024, 4096], P(('dp', 'mem'))
- ffn_out_grad: float32 [4096, 1024], P(('dp', 'mem'))
- norm_gains_grad: float32 [1024, 3], P(('dp', 'mem'))
- norm_biases_grad: float32 [1024, 3], P(('dp', 'mem'))
Inputs may be any that keep to these rules, and one draw needn't show every extreme that they name: `bucket_ids`: slots of a device hold 512 / 2^bucket rows each, and 2^bucket slots are used; the first device has bucket 0. `target_lengths`: A used slot's length lies above half its slot length and at most at it; slot 0 of every device is full; entries past the device's used slots are 0. `memory_mask`: for a used slot, 1 on a prefix of the sequence's 768 memory positions (position = piece * 384 + row) that reaches into its last piece, 0 after it; 0 everywhere in unused slots.
All inputs are finite; a program needn't handle non-finite values.
Results may differ from a plain program's by a relative error of at most 0.03.
Values may be sent and summed in bfloat16 or wider, within the bound.
No kernel may reach another device: no remote copies, remote signals or barrier semaphores. Data moves between devices by JAX's collectives and lax.ppermute only.
A program may use at most 320 MiB of HBM per device.

v0:
```python
import jax
import jax.numpy as jnp
from jax import lax
from jax.sharding import PartitionSpec as P

HD = 64


ALPHA = 300.0**0.25
NEG_LARGE = -1e30
EPSILON = 1e-05


def merged(shard, axis, join):
    gathered = jax.tree.map(
        lambda a, kind: lax.all_gather(a.astype(kind), axis), shard, (jnp.bfloat16, jnp.bfloat16)
    )

    def take(source):
        return jax.tree.map(
            lambda a, own: lax.dynamic_index_in_dim(a, source, 0, False).astype(own.dtype),
            gathered,
            shard,
        )

    return lax.fori_loop(
        1, lax.axis_size(axis), lambda source, state: join(state, take(source)), take(0)
    )


def layer_norm(values, gain_row, shift_row):
    centred = values - jnp.mean(values, axis=-1, keepdims=True)
    spread = jnp.mean(centred * centred, axis=-1, keepdims=True)
    return centred * lax.rsqrt(spread + EPSILON) * gain_row + shift_row


def norm_backward(values, gain_row, shift_row, cotangent):
    normed, pullback = jax.vjp(layer_norm, values, gain_row, shift_row)
    return pullback(cotangent)


def exact_gelu(values):
    return jax.nn.gelu(values, approximate=False)


def gelu_backward(hidden, cotangent):
    gelu_value, pullback = jax.vjp(exact_gelu, hidden)
    return pullback(cotangent)[0]


def plain_dot(first_op, second_op):
    return jnp.dot(first_op, second_op, preferred_element_type=jnp.float32)


def lead_dot(first_op, second_op):
    return lax.dot_general(
        first_op, second_op, (((0,), (0,)), ((), ())), preferred_element_type=jnp.float32
    )


def back_dot(first_op, second_op):
    return lax.dot_general(
        first_op, second_op, (((1,), (1,)), ((), ())), preferred_element_type=jnp.float32
    )


def pick_entry(values, wanted):
    return jnp.sum(jnp.where(jnp.arange(values.shape[0]) == wanted, values, 0))


def head_dots(first_op, second_op):
    first_heads = first_op.reshape(first_op.shape[0], -1, HD)
    second_heads = second_op.reshape(second_op.shape[0], -1, HD)
    return jnp.einsum("qhd,khd->hqk", first_heads, second_heads, preferred_element_type=jnp.float32)


def head_mix(weights_low, values):
    value_heads = values.reshape(values.shape[0], -1, HD)
    mixed = jnp.einsum("hqk,khd->qhd", weights_low, value_heads, preferred_element_type=jnp.float32)
    return mixed.reshape(mixed.shape[0], -1)


def head_back(grad_scores, operand):
    operand_heads = operand.reshape(operand.shape[0], -1, HD)
    result = jnp.einsum(
        "hqk,qhd->khd", grad_scores, operand_heads, preferred_element_type=jnp.float32
    )
    return result.reshape(result.shape[0], -1)


def self_mask(slot_len, lengths, row_count):
    row_ids = jnp.arange(row_count, dtype=jnp.int32)
    slot_ids = row_ids // slot_len
    slot_table = slot_ids[:, None] == jnp.arange(lengths.shape[0], dtype=jnp.int32)[None, :]
    key_limit = jnp.sum(jnp.where(slot_table, lengths[None, :], 0), axis=1)
    visible = row_ids % slot_len < key_limit
    return (
        (slot_ids[:, None] == slot_ids[None, :])
        & (row_ids[None, :] <= row_ids[:, None])
        & visible[None, :]
    )


def cross_mask(slot_len, key_live, row_count, mem_piece, slot_count):
    query_slot = jnp.arange(row_count, dtype=jnp.int32) // slot_len
    key_ids = jnp.arange(key_live.shape[0], dtype=jnp.int32)
    key_slot = key_ids // mem_piece % slot_count
    return (query_slot[:, None] == key_slot[None, :]) & key_live[None, :]


def merge_stats(earlier, later):
    peak_a, total_a = earlier
    peak_b, total_b = later
    joined = jnp.maximum(peak_a, peak_b)
    return (joined, total_a * jnp.exp(peak_a - joined) + total_b * jnp.exp(peak_b - joined))


def attend_forward(queries, keys_all, values_all, allowed):
    model_width = queries.shape[1]
    block_width = min(4 * HD, model_width)
    score_scale = HD ** (-0.5)
    mixed_parts, lse_parts = ([], [])
    for column in range(0, model_width, block_width):
        scores = jnp.where(
            allowed[None],
            head_dots(
                queries[:, column : column + block_width],
                keys_all[:, column : column + block_width],
            )
            * score_scale,
            NEG_LARGE,
        )
        row_peak = jnp.max(scores, axis=2, keepdims=True)
        raised = jnp.exp(scores - row_peak)
        row_total = jnp.sum(raised, axis=2, keepdims=True)
        mixed_parts.append(
            head_mix(
                (raised / row_total).astype(jnp.bfloat16),
                values_all[:, column : column + block_width],
            )
        )
        lse_parts.append(row_peak + jnp.log(row_total))
    return (jnp.concatenate(mixed_parts, axis=1), jnp.concatenate(lse_parts, axis=0))


def attend_backward(queries, keys_all, values_all, allowed, log_totals, upstream):
    model_width = queries.shape[1]
    block_width = min(4 * HD, model_width)
    heads_block = block_width // HD
    score_scale = HD ** (-0.5)
    grads_q, grads_k, grads_v = ([], [], [])
    for column in range(0, model_width, block_width):
        head_first = column // HD
        query_cols = queries[:, column : column + block_width]
        key_cols = keys_all[:, column : column + block_width]
        upstream_cols = upstream[:, column : column + block_width]
        scores = jnp.where(allowed[None], head_dots(query_cols, key_cols) * score_scale, NEG_LARGE)
        attn_probs = jnp.exp(scores - log_totals[head_first : head_first + heads_block])
        grad_probs = head_dots(upstream_cols, values_all[:, column : column + block_width])
        row_dot = jnp.sum(attn_probs * grad_probs, axis=2, keepdims=True)
        grad_scores = (attn_probs * (grad_probs - row_dot)).astype(jnp.bfloat16)
        grads_q.append(head_mix(grad_scores, key_cols) * score_scale)
        grads_k.append(head_back(grad_scores, query_cols) * score_scale)
        grads_v.append(head_back(attn_probs.astype(jnp.bfloat16), upstream_cols))
    return (
        jnp.concatenate(grads_q, axis=1),
        jnp.concatenate(grads_k, axis=1),
        jnp.concatenate(grads_v, axis=1),
    )


def piece_scores(query_rows, key_rows, allowed, column, block_width):
    dots = head_dots(
        query_rows[:, column : column + block_width], key_rows[:, column : column + block_width]
    ) * HD ** (-0.5)
    return jnp.where(allowed[None], dots, NEG_LARGE)


def split_forward(query_all, key_value, allowed_list, row_count, source_rows):
    model_width = query_all.shape[1]
    block_width = min(4 * HD, model_width)
    heads_block = block_width // HD
    groups = model_width // block_width
    peak_parts, total_parts = ([], [])
    for source in range(len(allowed_list)):
        query_rows = query_all[source * row_count : (source + 1) * row_count]
        key_rows = key_value[source * source_rows : (source + 1) * source_rows]
        for column in range(0, model_width, block_width):
            scores = piece_scores(query_rows, key_rows, allowed_list[source], column, block_width)
            row_peak = jnp.max(scores, axis=2)
            peak_parts.append(row_peak)
            total_parts.append(jnp.sum(jnp.exp(scores - row_peak[:, :, None]), axis=2))
    joint_peak, totals = merged(
        (jnp.concatenate(peak_parts, 0), jnp.concatenate(total_parts, 0)), "mem", merge_stats
    )
    log_totals = joint_peak + jnp.log(totals)
    mixed_rows = []
    for source in range(len(allowed_list)):
        query_rows = query_all[source * row_count : (source + 1) * row_count]
        key_rows = key_value[source * source_rows : (source + 1) * source_rows]
        column_parts = []
        for group_index in range(groups):
            set_index = source * groups + group_index
            column = group_index * block_width
            scores = piece_scores(query_rows, key_rows, allowed_list[source], column, block_width)
            lse_rows = log_totals[set_index * heads_block : (set_index + 1) * heads_block]
            attn_probs = jnp.exp(scores - lse_rows[:, :, None]).astype(jnp.bfloat16)
            column_parts.append(
                head_mix(
                    attn_probs,
                    key_rows[:, model_width + column : model_width + column + block_width],
                )
            )
        mixed_rows.append(jnp.concatenate(column_parts, axis=1))
    summed = lax.psum_scatter(
        jnp.concatenate(mixed_rows, axis=0).astype(jnp.bfloat16),
        "mem",
        scatter_dimension=0,
        tiled=True,
    ).astype(jnp.float32)
    return (summed, log_totals)


def split_backward(
    query_all, key_value, allowed_list, log_totals, grad_all, row_count, source_rows
):
    model_width = query_all.shape[1]
    block_width = min(4 * HD, model_width)
    heads_block = block_width // HD
    groups = model_width // block_width
    score_scale = HD ** (-0.5)

    def probs_pair(source, group_index):
        set_index = source * groups + group_index
        column = group_index * block_width
        query_rows = query_all[source * row_count : (source + 1) * row_count]
        key_rows = key_value[source * source_rows : (source + 1) * source_rows]
        upstream_rows = grad_all[source * row_count : (source + 1) * row_count]
        scores = piece_scores(query_rows, key_rows, allowed_list[source], column, block_width)
        lse_rows = log_totals[set_index * heads_block : (set_index + 1) * heads_block]
        attn_probs = jnp.exp(scores - lse_rows[:, :, None])
        grad_probs = head_dots(
            upstream_rows[:, column : column + block_width],
            key_rows[:, model_width + column : model_width + column + block_width],
        )
        return (attn_probs, grad_probs)

    dot_parts = []
    for source in range(len(allowed_list)):
        for group_index in range(groups):
            attn_probs, grad_probs = probs_pair(source, group_index)
            dot_parts.append(jnp.sum(attn_probs * grad_probs, axis=2))
    row_dots = lax.psum(jnp.concatenate(dot_parts, 0).astype(jnp.bfloat16), "mem").astype(
        jnp.float32
    )
    query_blocks, kv_blocks = ([], [])
    for source in range(len(allowed_list)):
        query_rows = query_all[source * row_count : (source + 1) * row_count]
        key_rows = key_value[source * source_rows : (source + 1) * source_rows]
        upstream_rows = grad_all[source * row_count : (source + 1) * row_count]
        query_parts, key_parts, value_parts = ([], [], [])
        for group_index in range(groups):
            set_index = source * groups + group_index
            column = group_index * block_width
            attn_probs, grad_probs = probs_pair(source, group_index)
            dot_rows = row_dots[set_index * heads_block : (set_index + 1) * heads_block]
            grad_scores = (attn_probs * (grad_probs - dot_rows[:, :, None])).astype(jnp.bfloat16)
            query_parts.append(
                head_mix(grad_scores, key_rows[:, column : column + block_width]) * score_scale
            )
            key_parts.append(
                head_back(grad_scores, query_rows[:, column : column + block_width]) * score_scale
            )
            value_parts.append(
                head_back(
                    attn_probs.astype(jnp.bfloat16), upstream_rows[:, column : column + block_width]
                )
            )
        query_blocks.append(jnp.concatenate(query_parts, axis=1))
        kv_blocks.append(jnp.concatenate(key_parts + value_parts, axis=1))
    grad_query = lax.psum_scatter(
        jnp.concatenate(query_blocks, axis=0).astype(jnp.bfloat16),
        "mem",
        scatter_dimension=0,
        tiled=True,
    ).astype(jnp.float32)
    return (grad_query, jnp.concatenate(kv_blocks, axis=0).astype(jnp.bfloat16))


def per_device(
    target_in,
    memory_in,
    bucket_ids,
    target_lengths,
    memory_mask,
    self_qkv,
    self_out,
    cross_q,
    cross_kv,
    cross_out,
    ffn_in,
    ffn_out,
    norm_gains,
    norm_biases,
    grad_out,
):
    gathered = (
        lax.all_gather(self_qkv.astype(jnp.bfloat16), ("dp", "mem"), axis=0, tiled=True),
        lax.all_gather(self_out.astype(jnp.bfloat16), ("dp", "mem"), axis=0, tiled=True),
        lax.all_gather(cross_q.astype(jnp.bfloat16), ("dp", "mem"), axis=0, tiled=True),
        lax.all_gather(cross_kv.astype(jnp.bfloat16), ("dp", "mem"), axis=0, tiled=True),
        lax.all_gather(cross_out.astype(jnp.bfloat16), ("dp", "mem"), axis=0, tiled=True),
        lax.all_gather(ffn_in.astype(jnp.bfloat16), ("dp", "mem"), axis=0, tiled=True),
        lax.all_gather(ffn_out.astype(jnp.bfloat16), ("dp", "mem"), axis=0, tiled=True),
        lax.all_gather(norm_gains.astype(jnp.bfloat16), ("dp", "mem"), axis=0, tiled=True),
        lax.all_gather(norm_biases.astype(jnp.bfloat16), ("dp", "mem"), axis=0, tiled=True),
    )
    w_qkv, w_so, w_cq, w_ckv, w_co, w_in, w_out, gains_low, biases_low = gathered
    gain_cols = gains_low.astype(jnp.float32)
    bias_cols = biases_low.astype(jnp.float32)
    row_count, model_width = target_in.shape
    pieces = lax.axis_size("mem")
    slot_count = memory_in.shape[3]
    mem_piece = memory_in.shape[4]
    source_rows = slot_count * mem_piece
    own_index = lax.axis_index("mem")
    slot_lens = jnp.right_shift(jnp.int32(row_count), bucket_ids[0])
    own_slot = pick_entry(slot_lens, own_index)
    inputs = target_in.astype(jnp.float32)
    self_allowed = self_mask(own_slot, target_lengths[0, 0], row_count)
    united_qkv = plain_dot(target_in, w_qkv).astype(jnp.bfloat16)
    self_mixed_sum, self_lse = attend_forward(
        united_qkv[:, :model_width],
        united_qkv[:, model_width : 2 * model_width],
        united_qkv[:, 2 * model_width :],
        self_allowed,
    )
    self_mixed = self_mixed_sum.astype(jnp.bfloat16)
    sum_one = ALPHA * inputs + plain_dot(self_mixed, w_so)
    first_out = layer_norm(sum_one, gain_cols[:, 0], bias_cols[:, 0])
    first_low = first_out.astype(jnp.bfloat16)
    cross_query = plain_dot(first_low, w_cq).astype(jnp.bfloat16)
    memory_rows = memory_in.reshape(-1, model_width)
    key_value = plain_dot(memory_rows, w_ckv).astype(jnp.bfloat16)
    piece_masks = memory_mask.reshape(pieces, source_rows) == 1
    cross_allowed = [
        cross_mask(slot_lens[source], piece_masks[source], row_count, mem_piece, slot_count)
        for source in range(pieces)
    ]
    query_all = lax.all_gather(cross_query, "mem", axis=0, tiled=True)
    cross_sum, cross_lse = split_forward(
        query_all, key_value, cross_allowed, row_count, source_rows
    )
    cross_mixed = cross_sum.astype(jnp.bfloat16)
    sum_two = ALPHA * first_out + plain_dot(cross_mixed, w_co)
    second_out = layer_norm(sum_two, gain_cols[:, 1], bias_cols[:, 1])
    second_low = second_out.astype(jnp.bfloat16)
    hidden = plain_dot(second_low, w_in)
    activated = exact_gelu(hidden).astype(jnp.bfloat16)
    sum_three = ALPHA * second_out + plain_dot(activated, w_out)
    layer_out = layer_norm(sum_three, gain_cols[:, 2], bias_cols[:, 2]).astype(jnp.bfloat16)
    grad_three, grad_gain_three, grad_bias_three = norm_backward(
        sum_three, gain_cols[:, 2], bias_cols[:, 2], grad_out.astype(jnp.float32)
    )
    grad_ffn = grad_three.astype(jnp.bfloat16)
    w_out_grad = lead_dot(activated, grad_ffn)
    grad_hidden = gelu_backward(hidden, back_dot(grad_ffn, w_out)).astype(jnp.bfloat16)
    w_in_grad = lead_dot(second_low, grad_hidden)
    grad_second = ALPHA * grad_three + back_dot(grad_hidden, w_in)
    grad_two, grad_gain_two, grad_bias_two = norm_backward(
        sum_two, gain_cols[:, 1], bias_cols[:, 1], grad_second
    )
    grad_cross_out = grad_two.astype(jnp.bfloat16)
    w_co_grad = lead_dot(cross_mixed, grad_cross_out)
    grad_cross_mixed = back_dot(grad_cross_out, w_co).astype(jnp.bfloat16)
    grad_all = lax.all_gather(grad_cross_mixed, "mem", axis=0, tiled=True)
    grad_query, grad_kv = split_backward(
        query_all, key_value, cross_allowed, cross_lse, grad_all, row_count, source_rows
    )
    grad_query_low = grad_query.astype(jnp.bfloat16)
    w_ckv_grad = lead_dot(memory_rows, grad_kv)
    memory_grad = back_dot(grad_kv, w_ckv).astype(jnp.bfloat16).reshape(memory_in.shape)
    w_cq_grad = lead_dot(first_low, grad_query_low)
    grad_first = ALPHA * grad_two + back_dot(grad_query_low, w_cq)
    grad_one, grad_gain_one, grad_bias_one = norm_backward(
        sum_one, gain_cols[:, 0], bias_cols[:, 0], grad_first
    )
    grad_self_out = grad_one.astype(jnp.bfloat16)
    w_so_grad = lead_dot(self_mixed, grad_self_out)
    grad_self_mixed = back_dot(grad_self_out, w_so).astype(jnp.bfloat16)
    grad_q, grad_k, grad_v = attend_backward(
        united_qkv[:, :model_width],
        united_qkv[:, model_width : 2 * model_width],
        united_qkv[:, 2 * model_width :],
        self_allowed,
        self_lse,
        grad_self_mixed,
    )
    grad_united = jnp.concatenate((grad_q, grad_k, grad_v), axis=1).astype(jnp.bfloat16)
    w_qkv_grad = lead_dot(target_in, grad_united)
    target_grad = (ALPHA * grad_one + back_dot(grad_united, w_qkv)).astype(jnp.bfloat16)
    gains_grad = jnp.stack((grad_gain_one, grad_gain_two, grad_gain_three), axis=1)
    biases_grad = jnp.stack((grad_bias_one, grad_bias_two, grad_bias_three), axis=1)
    shards = (
        lax.psum_scatter(w_qkv_grad, ("dp", "mem"), scatter_dimension=0, tiled=True),
        lax.psum_scatter(w_so_grad, ("dp", "mem"), scatter_dimension=0, tiled=True),
        lax.psum_scatter(w_cq_grad, ("dp", "mem"), scatter_dimension=0, tiled=True),
        lax.psum_scatter(w_ckv_grad, ("dp", "mem"), scatter_dimension=0, tiled=True),
        lax.psum_scatter(w_co_grad, ("dp", "mem"), scatter_dimension=0, tiled=True),
        lax.psum_scatter(w_in_grad, ("dp", "mem"), scatter_dimension=0, tiled=True),
        lax.psum_scatter(w_out_grad, ("dp", "mem"), scatter_dimension=0, tiled=True),
        lax.psum_scatter(gains_grad, ("dp", "mem"), scatter_dimension=0, tiled=True),
        lax.psum_scatter(biases_grad, ("dp", "mem"), scatter_dimension=0, tiled=True),
    )
    return (
        layer_out,
        target_grad,
        memory_grad,
        shards[0],
        shards[1],
        shards[2],
        shards[3],
        shards[4],
        shards[5],
        shards[6],
        shards[7],
        shards[8],
    )


def solution(mesh):
    return jax.shard_map(
        per_device,
        mesh=mesh,
        in_specs=(
            P(("dp", "mem"), None),
            P("dp", None, "mem", None, None, None),
            P("dp", None),
            P("dp", "mem", None),
            P("dp", None, "mem", None, None),
            P(("dp", "mem"), None),
            P(("dp", "mem"), None),
            P(("dp", "mem"), None),
            P(("dp", "mem"), None),
            P(("dp", "mem"), None),
            P(("dp", "mem"), None),
            P(("dp", "mem"), None),
            P(("dp", "mem"), None),
            P(("dp", "mem"), None),
            P(("dp", "mem"), None),
        ),
        out_specs=(
            P(("dp", "mem"), None),
            P(("dp", "mem"), None),
            P("dp", None, "mem", None, None, None),
            P(("dp", "mem"), None),
            P(("dp", "mem"), None),
            P(("dp", "mem"), None),
            P(("dp", "mem"), None),
            P(("dp", "mem"), None),
            P(("dp", "mem"), None),
            P(("dp", "mem"), None),
            P(("dp", "mem"), None),
            P(("dp", "mem"), None),
        ),
        check_vma=False,
    )
```

profile of v0, /device:TPU:0, one launch (start us, length us, event | category | flops | bytes accessed | tf_op | source)
XLA Modules:
  0.0 2674.5 jit_solution(13932832631121639818)
XLA Ops:
  18.8 70.2 %all-gather.1 = bf16[32,32,3]{1,2,0:T(4,128)(2,1)S(1)} all-gather(bf16[1,32,3]{1,2,0:T(4,128)(2,1)S(1)} %convert_bitcast_fusion.16), channel_id=1, replica_groups=mesh['dp'=16,'mem'=2] {'dp','mem'}, dimensions={0}, use_global_device_ids=true | all-gather | bytes 6336 | tf_op jit(solution)/shard_map/all_gather | solution.py:316
  90.4 63.4 %all-gather = bf16[32,32,3]{1,2,0:T(4,128)(2,1)S(1)} all-gather(bf16[1,32,3]{1,2,0:T(4,128)(2,1)S(1)} %convert_bitcast_fusion.17), channel_id=1, replica_groups=mesh['dp'=16,'mem'=2] {'dp','mem'}, dimensions={0}, use_global_device_ids=true | all-gather | bytes 6336 | tf_op jit(solution)/shard_map/all_gather | solution.py:315
  155.6 6.5 convolution_convert_fusion.1
  215.1 50.9 %all-gather.16.cloned.1.call-done = bf16[1024,2048]{1,0:T(8,128)(2,1)} async-done(((bf16[32,2048]{1,0:T(8,128)(2,1)}), bf16[1024,2048]{1,0:T(8,128)(2,1)}) %all-gather.16.cloned.1.call-update) | async-done | bytes 4194320 | tf_op jit(solution)/shard_map/all_gather | solution.py:311
  265.9 9.2 convolution_convert_fusion
  334.6 5.5 fusion.9
  340.1 9.7 exponential_reduce_fusion.4
  349.8 7.7 fusion.13
  358.1 10.3 exponential_reduce_fusion
  369.1 8.1 exponential_reduce_fusion.1
  377.2 5.3 concatenate.120
  382.5 5.8 all_gather.49
  397.9 4.9 convolution_convert_fusion.13
  418.8 13.6 maximum_maximum_fusion
  436.2 26.5 reduce-scatter.20.cloned.1.call-done
  469.5 74.7 %all-gather.24.cloned.1.call-done = bf16[1024,4096]{1,0:T(8,128)(2,1)} async-done(((bf16[32,4096]{1,0:T(8,128)(2,1)}), bf16[1024,4096]{1,0:T(8,128)(2,1)}) %all-gather.24.cloned.1.call-update) | async-done | bytes 8388624 | tf_op jit(solution)/shard_map/all_gather | solution.py:313
  544.3 27.0 %multiply_convert_fusion = (bf16[512,4096]{1,0:T(8,128)(2,1)}, f32[512,4096]{1,0:T(8,128)}, f32[512,4096]{1,0:T(8,128)}) fusion(bf16[1024,4096]{1,0:T(8,128)(2,1)} %all-gather.24.cloned.1.call-done, f32[512,1024]{1,0:T(8,128)} %copy-done.34, f32[1024]{0:T(1024)} %bitcast.642, f32[1024]{0:T(1024)} %bitcast.620, f32[512]{0:T(512)} %fusion.121, f32[512]{0:T(512)} %copy-done.155), kind=kOutput, calls=%fused_computation.3 | convolution fusion | flops 4433903616 | bytes 31469568 | tf_op jit(solution)/shard_map/dot_general | solution.py:52
  571.3 53.0 %all-gather.26.cloned.1.call-done = bf16[4096,1024]{1,0:T(8,128)(2,1)} async-done(((bf16[128,1024]{1,0:T(8,128)(2,1)}), bf16[4096,1024]{1,0:T(8,128)(2,1)}) %all-gather.26.cloned.1.call-update) | async-done | bytes 8388624 | tf_op jit(solution)/shard_map/all_gather | solution.py:314
  624.3 10.0 fusion.175
  638.0 15.6 add_convert_fusion
  653.7 9.6 multiply_reduce_fusion.12
  668.2 31.3 %all-gather.28.cloned.1.call-done = bf16[1024,1024]{1,0:T(8,128)(2,1)} async-done(((bf16[512,1024]{1,0:T(8,128)(2,1)}), bf16[1024,1024]{1,0:T(8,128)(2,1)}) %all-gather.28.cloned.1.call-update) | async-done | bytes 2097168 | tf_op jit(solution)/shard_map/all_gather | solution.py:376
  745.2 21.0 multiply_reduce_fusion.4
  766.2 21.0 multiply_reduce_fusion
  787.2 5.2 concatenate.124
  792.4 8.6 psum.7
  802.5 19.5 multiply_convert_fusion.4
  832.8 17.2 multiply_convert_fusion.8
  856.3 13.8 maximum_maximum_fusion.1
  870.2 33.1 %reduce-scatter.22.cloned.1.call-done = bf16[512,1024]{0,1:T(8,128)(2,1)} async-done(((bf16[1024,1024]{0,1:T(8,128)(2,1)}), bf16[512,1024]{0,1:T(8,128)(2,1)}) %reduce-scatter.22.cloned.1.call-update) | async-done | bytes 1048592 | tf_op jit(solution)/shard_map/reduce_scatter | solution.py:281
  903.3 7.1 multiply_reduce_fusion.13
  916.0 5.3 fusion.130
  982.8 8.9 convolution_bitcast_fusion.1
  991.7 9.2 copy.436
  1044.3 6.4 convolution_bitcast_fusion
  1050.7 12.7 copy.434
  1064.1 13.4 fusion.147
  1078.1 13.3 fusion.128
  1091.4 11.8 fusion.15
  1103.2 7.4 add_convert_fusion.1
  1111.9 67.4 %reduce-scatter.40.cloned.1.call-done = f32[32,3]{1,0:T(8,128)} async-done(((f32[1024,3]{1,0:T(8,128)}), f32[32,3]{1,0:T(8,128)}) %reduce-scatter.40.cloned.1.call-update) | async-done | bytes 400
  1180.7 138.7 %reduce-scatter.28.cloned.1.call-done = f32[32,1024]{1,0:T(8,128)} async-done(((f32[1024,1024]{1,0:T(8,128)}), f32[32,1024]{1,0:T(8,128)}) %reduce-scatter.28.cloned.1.call-update) | async-done | bytes 131088 | tf_op jit(solution)/shard_map/reduce_scatter | solution.py:409
  1319.4 141.2 %reduce-scatter.24.cloned.1.call-done = f32[32,1024]{1,0:T(8,128)} async-done(((f32[1024,1024]{1,0:T(8,128)}), f32[32,1024]{1,0:T(8,128)}) %reduce-scatter.24.cloned.1.call-update) | async-done | bytes 131088 | tf_op jit(solution)/shard_map/reduce_scatter | solution.py:406
  1460.5 141.0 %reduce-scatter.26.cloned.1.call-done = f32[32,1024]{1,0:T(8,128)} async-done(((f32[1024,1024]{1,0:T(8,128)}), f32[32,1024]{1,0:T(8,128)}) %reduce-scatter.26.cloned.1.call-update) | async-done | bytes 131088 | tf_op jit(solution)/shard_map/reduce_scatter | solution.py:407
  1601.5 182.9 %reduce-scatter.36.cloned.1.call-done = f32[32,2048]{1,0:T(8,128)} async-done(((f32[1024,2048]{1,0:T(8,128)}), f32[32,2048]{1,0:T(8,128)}) %reduce-scatter.36.cloned.1.call-update) | async-done | bytes 262160
  1784.4 162.3 %reduce-scatter.34.cloned.1.call-done = f32[32,3072]{1,0:T(8,128)} async-done(((f32[1024,3072]{1,0:T(8,128)}), f32[32,3072]{1,0:T(8,128)}) %reduce-scatter.34.cloned.1.call-update) | async-done | bytes 393232
  1946.7 359.4 %reduce-scatter.30.cloned.1.call-done = f32[32,4096]{1,0:T(8,128)} async-done(((f32[1024,4096]{1,0:T(8,128)}), f32[32,4096]{1,0:T(8,128)}) %reduce-scatter.30.cloned.1.call-update) | async-done | bytes 524304 | tf_op jit(solution)/shard_map/reduce_scatter | solution.py:410
  2306.1 361.3 %reduce-scatter.32.cloned.1.call-done = f32[128,1024]{1,0:T(8,128)} async-done(((f32[4096,1024]{1,0:T(8,128)}), f32[128,1024]{1,0:T(8,128)}) %reduce-scatter.32.cloned.1.call-update) | async-done | bytes 524304 | tf_op jit(solution)/shard_map/reduce_scatter | solution.py:411
  (715 shorter events, 346.1 us)
Async XLA Ops:
  7.2 258.8 %copy-start = (bf16[1,2,1,2,384,1024]{5,4,3,2,1,0:T(8,128)(2,1)S(1)}, bf16[1,2,1,2,384,1024]{5,4,3,2,1,0:T(8,128)(2,1)}, u32[]{:S(2)}) copy-start(bf16[1,2,1,2,384,1024]{5,4,3,2,1,0:T(8,128)(2,1)} %param.16) | copy-start | bytes 9437188
  7.2 148.4 %all-gather.12.cloned.1.call-start = ((), (), s32[]{:S(2)}) async-start(), calls=%async_computation.11 | async-start | bytes 6488064 | tf_op jit(solution)/shard_map/all_gather | solution.py:308
  9.1 190.0 %all-gather.14.cloned.1.call-start = ((), (), s32[]{:S(2)}) async-start(), calls=%async_computation.12 | async-start | bytes 2162688 | tf_op jit(solution)/shard_map/all_gather | solution.py:309
  10.7 194.1 %all-gather.18.cloned.1.call-start = ((), (), s32[]{:S(2)}) async-start(), calls=%async_computation.14 | async-start | bytes 2162688 | tf_op jit(solution)/shard_map/all_gather | solution.py:310
  12.3 253.6 %all-gather.16.cloned.1.call-start = ((), (), s32[]{:S(2)}) async-start(), calls=%async_computation.13 | async-start | bytes 4325376 | tf_op jit(solution)/shard_map/all_gather | solution.py:311
  14.0 294.7 %all-gather.20.cloned.1.call-start = ((), (), s32[]{:S(2)}) async-start(), calls=%async_computation.15 | async-start | bytes 3145728 | tf_op jit(solution)/shard_map/all_gather | solution.py:350
  89.7 115.1 %copy-start.177 = (f32[1024,1]{0,1:T(1,128)}, f32[1024,1]{0,1:T(1,128)S(1)}, u32[]{:S(2)}) copy-start(f32[1024,1]{0,1:T(1,128)S(1)} %get-tuple-element.209) | copy-start | bytes 12292
  154.5 50.3 %copy-start.165 = (f32[1024,1]{0,1:T(1,128)}, f32[1024,1]{0,1:T(1,128)S(1)}, u32[]{:S(2)}) copy-start(f32[1024,1]{0,1:T(1,128)S(1)} %get-tuple-element.206) | copy-start | bytes 12292
  209.5 226.8 %all-gather.22.cloned.1.call-start = ((), (), s32[]{:S(2)}) async-start(), calls=%async_computation.17 | async-start | bytes 2162688 | tf_op jit(solution)/shard_map/all_gather | solution.py:312
  210.2 252.5 %reduce-scatter.20.cloned.1.call-start = ((), (), s32[]{:S(2)}) async-start(), calls=%async_computation.16 | async-start | bytes 3145728 | tf_op jit(solution)/shard_map/reduce_scatter | solution.py:215
  333.0 36.1 %copy-start.9 = (f32[4,512,768]{2,1,0:T(8,128)}, f32[4,512,768]{2,1,0:T(8,128)S(1)}, u32[]{:S(2)}) copy-start(f32[4,512,768]{2,1,0:T(8,128)S(1)} %fusion.177) | copy-start | bytes 18874372
  334.5 34.6 %copy-start.11 = (f32[4,512,768]{2,1,0:T(8,128)}, f32[4,512,768]{2,1,0:T(8,128)S(1)}, u32[]{:S(2)}) copy-start(f32[4,512,768]{2,1,0:T(8,128)S(1)} %fusion.179) | copy-start | bytes 18874372
  340.1 9.7 copy-start.28
  340.1 9.7 copy-start.47
  358.1 11.0 slice-start.20
  358.1 10.9 slice-start.21
  397.9 16.7 copy-start.124
  397.9 18.8 copy-start.127
  432.5 111.8 %all-gather.24.cloned.1.call-start = ((), (), s32[]{:S(2)}) async-start(), calls=%async_computation.18 | async-start | bytes 8650752 | tf_op jit(solution)/shard_map/all_gather | solution.py:313
  434.3 190.0 %all-gather.26.cloned.1.call-start = ((), (), s32[]{:S(2)}) async-start(), calls=%async_computation.19 | async-start | bytes 8650752 | tf_op jit(solution)/shard_map/all_gather | solution.py:314
  436.2 263.4 %all-gather.28.cloned.1.call-start = ((), (), s32[]{:S(2)}) async-start(), calls=%async_computation.20 | async-start | bytes 3145728 | tf_op jit(solution)/shard_map/all_gather | solution.py:376
  624.3 10.4 copy-start.39
  624.3 10.4 copy-start.141
  638.0 15.7 copy-start.77
  638.0 15.7 copy-start.179
  638.0 15.7 copy-start.35
  638.0 15.7 copy-start.156
  638.0 15.7 copy-start.163
  638.0 15.7 copy-start.169
  667.7 235.6 %reduce-scatter.22.cloned.1.call-start = ((), (), s32[]{:S(2)}) async-start(), calls=%async_computation.21 | async-start | bytes 3145728 | tf_op jit(solution)/shard_map/reduce_scatter | solution.py:281
  802.5 30.2 %slice-start.8 = ((s8[6291456]{0:T(1024)(128)(4,1)}), s8[4194304]{0:T(1024)(128)(4,1)S(1)}, s32[]{:S(2)}) async-start(s8[6291456]{0:T(1024)(128)(4,1)} %bitcast.447), calls=%async_computation.39 | async-start | bytes 8388608
  802.5 19.5 copy-start.48
  802.5 30.2 %slice-start.9 = ((s8[6291456]{0:T(1024)(128)(4,1)}), s8[2097152]{0:T(1024)(128)(4,1)S(1)}, s32[]{:S(2)}) async-start(s8[6291456]{0:T(1024)(128)(4,1)} %bitcast.447), calls=%async_computation.40 | async-start | bytes 4194304
  832.7 17.2 copy-start.43
  832.8 18.3 copy-start.45
  870.1 240.4 %reduce-scatter.38.cloned.1.call-start = ((), (), s32[]{:S(2)}) async-start(), calls=%async_computation.29 | async-start | bytes 540672
  912.8 266.5 %reduce-scatter.40.cloned.1.call-start = ((), (), s32[]{:S(2)}) async-start(), calls=%async_computation.30 | async-start | bytes 540672
  915.9 403.4 %reduce-scatter.28.cloned.1.call-start = ((), (), s32[]{:S(2)}) async-start(), calls=%async_computation.24 | async-start | bytes 4325376 | tf_op jit(solution)/shard_map/reduce_scatter | solution.py:409
  921.3 539.2 %reduce-scatter.24.cloned.1.call-start = ((), (), s32[]{:S(2)}) async-start(), calls=%async_computation.22 | async-start | bytes 4325376 | tf_op jit(solution)/shard_map/reduce_scatter | solution.py:406
  929.8 671.7 %reduce-scatter.26.cloned.1.call-start = ((), (), s32[]{:S(2)}) async-start(), calls=%async_computation.23 | async-start | bytes 4325376 | tf_op jit(solution)/shard_map/reduce_scatter | solution.py:407
  947.6 836.8 %reduce-scatter.36.cloned.1.call-start = ((), (), s32[]{:S(2)}) async-start(), calls=%async_computation.28 | async-start | bytes 8650752
  964.5 10.3 slice-start.24
  966.4 14.7 copy-start.140
  1001.0 945.7 %reduce-scatter.34.cloned.1.call-start = ((), (), s32[]{:S(2)}) async-start(), calls=%async_computation.27 | async-start | bytes 12976128
  1063.4 1242.7 %reduce-scatter.30.cloned.1.call-start = ((), (), s32[]{:S(2)}) async-start(), calls=%async_computation.25 | async-start | bytes 17301504 | tf_op jit(solution)/shard_map/reduce_scatter | solution.py:410
  1077.5 1589.9 %reduce-scatter.32.cloned.1.call-start = ((), (), s32[]{:S(2)}) async-start(), calls=%async_computation.26 | async-start | bytes 17301504 | tf_op jit(solution)/shard_map/reduce_scatter | solution.py:411
  1091.4 11.8 copy-start.37
  1091.4 11.8 copy-start.152
  (185 other events, 679.5 us)
Sparse Core Ops, SparseCore 0:
  11.5 72.3 all-gather.11
  87.5 55.0 all-gather.13
  146.3 55.3 all-gather.17
  205.0 60.9 all-gather.15
  267.9 31.6 all-gather.19
  303.1 56.4 all-gather.21
  432.6 30.0 reduce-scatter.19
  466.8 77.3 all-gather.23
  548.4 75.8 all-gather.25
  667.8 31.6 all-gather.27
  870.3 32.9 reduce-scatter.21
  912.9 133.9 reduce-scatter.37
  1049.3 129.9 reduce-scatter.39
  1182.0 137.3 reduce-scatter.27
  1322.0 138.4 reduce-scatter.23
  1463.2 138.2 reduce-scatter.25
  1604.2 180.1 reduce-scatter.35
  1790.9 155.7 reduce-scatter.33
  1949.6 356.3 reduce-scatter.29
  2308.9 358.4 reduce-scatter.31
where the time goes:
time: 2690 us; the launch traced here: 2670 us
  waiting for transfers between devices  1820 us (68%)
  matrix products  380 us (14%)
  local copies, waits for them, and re-layouts  182 us (7%)
  blocking collectives  153 us (6%)
  other arithmetic  113 us (4%)
    unnamed x24, waiting for transfers between devices  413 us
    reduce_scatter x1, waiting for transfers between devices, per_device(): lax.psum_scatter(w_out_grad, ('dp', 'mem'), scatter_dimension=0, tiled=True)  361 us
    reduce_scatter x1, waiting for transfers between devices, per_device(): lax.psum_scatter(w_in_grad, ('dp', 'mem'), scatter_dimension=0, tiled=True)  359 us
    reduce_scatter x1, waiting for transfers between devices, per_device(): lax.psum_scatter(w_so_grad, ('dp', 'mem'), scatter_dimension=0, tiled=True)  141 us
    reduce_scatter x1, waiting for transfers between devices, per_device(): lax.psum_scatter(w_cq_grad, ('dp', 'mem'), scatter_dimension=0, tiled=True)  141 us
    reduce_scatter x1, waiting for transfers between devices, per_device(): lax.psum_scatter(w_co_grad, ('dp', 'mem'), scatter_dimension=0, tiled=True)  139 us
    dot_general x24, matrix products, head_dots(): jnp.einsum('qhd,khd->hqk', first_heads, second_heads, preferred_element_t...  125 us
    all_gather x1, waiting for transfers between devices, per_device(): lax.all_gather(ffn_in.astype(jnp.bfloat16), ('dp', 'mem'), axis=0, tiled=...  74.7 us
  transfers between devices with their start and end apart: 20, of which 14 were waited for; matrix products, arithmetic and copies ran while one was open for 16% of the time, Pallas kernels for 0%

commit v1 on v0

v1 whole, which is shorter than its diff:
```python
import functools

import jax
import jax.numpy as jnp
from jax import lax
from jax.experimental import pallas as pl
from jax.experimental.pallas import tpu as pltpu
from jax.sharding import PartitionSpec as P

HD = 64
LANES = 128
ALPHA = 300.0**0.25
NEG_LARGE = -1e30
EPSILON = 1e-05
VMEM_BYTES = 52 * 1024 * 1024
SCALE = HD**-0.5

BF16 = jnp.bfloat16
F32 = jnp.float32


def plain_dot(first_op, second_op):
    return jnp.dot(first_op, second_op, preferred_element_type=F32)


def lead_dot(first_op, second_op):
    return lax.dot_general(
        first_op, second_op, (((0,), (0,)), ((), ())), preferred_element_type=F32
    )


def back_dot(first_op, second_op):
    return lax.dot_general(
        first_op, second_op, (((1,), (1,)), ((), ())), preferred_element_type=F32
    )


def pick_entry(values, wanted):
    return jnp.sum(jnp.where(jnp.arange(values.shape[0]) == wanted, values, 0))


def kernel_params():
    return pltpu.CompilerParams(vmem_limit_bytes=VMEM_BYTES)


def whole_spec(shape):
    return pl.BlockSpec(shape, lambda *_: (0,) * len(shape))


def head_lanes(rows, head):
    lane = lax.broadcasted_iota(jnp.int32, (rows, LANES), 1)
    return (lane < HD) if head == 0 else (lane >= HD)


def visible(query_ids, key_ids, slot_len, first_len, second_len):
    query_slot = (query_ids >= slot_len).astype(jnp.int32)
    key_slot = (key_ids >= slot_len).astype(jnp.int32)
    place = key_ids - key_slot * slot_len
    limit = jnp.where(key_slot == 0, first_len, second_len)
    return (query_slot == key_slot) & (key_ids <= query_ids) & (place < limit)


def pair_forward(query, keys, values, bias):
    rows, key_rows = query.shape[0], keys.shape[0]
    mixed, peaks = [], []
    for head in range(2):
        mine = head_lanes(rows, head)
        masked = jnp.where(mine, query * BF16(SCALE), BF16(0))
        scores = back_dot(masked, keys) + bias
        peak = jnp.max(scores, axis=1, keepdims=True)
        raised = jnp.exp(scores - peak).astype(BF16)
        widened = jnp.where(head_lanes(key_rows, head), values, BF16(1))
        mixed.append(plain_dot(raised, widened))
        peaks.append(peak)
    first = head_lanes(rows, 0)
    totals = pltpu.roll(jnp.where(first, mixed[1], mixed[0]), HD, 1)
    joined = jnp.where(first, mixed[0], mixed[1])
    log_totals = jnp.where(first, peaks[0], peaks[1]) + jnp.log(totals)
    return joined / totals, log_totals


def pair_backward(query, keys, values, upstream, bias, log_rows, delta_rows):
    rows, key_rows = query.shape[0], keys.shape[0]
    grad_q, grad_k, grad_v = None, None, None
    for head in range(2):
        mine = head_lanes(rows, head)
        masked = jnp.where(mine, query * BF16(SCALE), BF16(0))
        masked_up = jnp.where(mine, upstream, BF16(0))
        scores = back_dot(keys, masked) + bias
        probs = jnp.exp(scores - log_rows[head])
        grad_probs = back_dot(values, masked_up)
        grad_scores = (probs * (grad_probs - delta_rows[head])).astype(BF16)
        part_v = plain_dot(probs.astype(BF16), masked_up)
        part_k = plain_dot(grad_scores, masked)
        masked_keys = jnp.where(head_lanes(key_rows, head), keys, BF16(0))
        part_q = lead_dot(grad_scores, masked_keys)
        grad_q = part_q if grad_q is None else grad_q + part_q
        grad_k = part_k if grad_k is None else grad_k + part_k
        grad_v = part_v if grad_v is None else grad_v + part_v
    return grad_q * SCALE, grad_k, grad_v


def stat_rows(log_block, mixed, upstream):
    log_turned = log_block.T
    products = (mixed.astype(F32) * upstream.astype(F32)).T
    log_rows = [log_turned[:1], log_turned[HD : HD + 1]]
    delta_rows = [jnp.sum(products[h * HD : (h + 1) * HD], axis=0, keepdims=True) for h in range(2)]
    return log_rows, delta_rows


def self_forward_kernel(meta, q_ref, k_ref, v_ref, mixed_ref, log_ref, bias):
    rows = q_ref.shape[0]

    @pl.when(pl.program_id(0) == 0)
    def _():
        query_ids = lax.broadcasted_iota(jnp.int32, (rows, rows), 0)
        key_ids = lax.broadcasted_iota(jnp.int32, (rows, rows), 1)
        seen = visible(query_ids, key_ids, meta[0], meta[1], meta[2])
        bias[...] = jnp.where(seen, 0.0, NEG_LARGE)

    half = rows // 2
    for start, stop in ((0, half), (half, rows)):
        mixed, log_totals = pair_forward(
            q_ref[start:stop, :], k_ref[:stop, :], v_ref[:stop, :], bias[start:stop, :stop]
        )
        mixed_ref[start:stop, :] = mixed.astype(BF16)
        log_ref[start:stop, :] = log_totals


def self_forward(meta, united):
    rows, width = united.shape[0], united.shape[1] // 3
    pairs = width // LANES
    spec = lambda third: pl.BlockSpec((rows, LANES), lambda i, _: (0, third * pairs + i))
    out_spec = pl.BlockSpec((rows, LANES), lambda i, _: (0, i))
    return pl.pallas_call(
        self_forward_kernel,
        grid_spec=pltpu.PrefetchScalarGridSpec(
            num_scalar_prefetch=1,
            grid=(pairs,),
            in_specs=[spec(0), spec(1), spec(2)],
            out_specs=[out_spec, out_spec],
            scratch_shapes=[pltpu.VMEM((rows, rows), F32)],
        ),
        out_shape=[
            jax.ShapeDtypeStruct((rows, width), BF16),
            jax.ShapeDtypeStruct((rows, width), F32),
        ],
        compiler_params=kernel_params(),
        cost_estimate=pl.CostEstimate(
            flops=12 * rows * rows * width, bytes_accessed=12 * rows * width, transcendentals=0
        ),
        name="self_forward",
    )(meta, united, united, united)


def self_backward_kernel(
    meta, q_ref, k_ref, v_ref, mixed_ref, up_ref, log_ref, grad_ref, bias
):
    rows = q_ref.shape[0]
    width = grad_ref.shape[1] // 3
    pair = pl.program_id(0)

    @pl.when(pair == 0)
    def _():
        key_ids = lax.broadcasted_iota(jnp.int32, (rows, rows), 0)
        query_ids = lax.broadcasted_iota(jnp.int32, (rows, rows), 1)
        seen = visible(query_ids, key_ids, meta[0], meta[1], meta[2])
        bias[...] = jnp.where(seen, 0.0, NEG_LARGE)

    log_rows, delta_rows = stat_rows(log_ref[...], mixed_ref[...], up_ref[...])
    half = rows // 2
    parts = []
    for start, stop in ((0, half), (half, rows)):
        parts.append(
            pair_backward(
                q_ref[start:stop, :],
                k_ref[:stop, :],
                v_ref[:stop, :],
                up_ref[start:stop, :],
                bias[:stop, start:stop],
                [row[:, start:stop] for row in log_rows],
                [row[:, start:stop] for row in delta_rows],
            )
        )
    low, high = parts
    columns = lambda third: pl.ds(pl.multiple_of(third * width + pair * LANES, LANES), LANES)
    grad_ref[:half, columns(0)] = low[0].astype(BF16)
    grad_ref[half:, columns(0)] = high[0].astype(BF16)
    for third in (1, 2):
        grad_ref[:half, columns(third)] = (low[third] + high[third][:half]).astype(BF16)
        grad_ref[half:, columns(third)] = high[third][half:].astype(BF16)


def self_backward(meta, united, mixed, upstream, log_totals):
    rows, width = united.shape[0], united.shape[1] // 3
    pairs = width // LANES
    spec = lambda third: pl.BlockSpec((rows, LANES), lambda i, _: (0, third * pairs + i))
    return pl.pallas_call(
        self_backward_kernel,
        grid_spec=pltpu.PrefetchScalarGridSpec(
            num_scalar_prefetch=1,
            grid=(pairs,),
            in_specs=[spec(0), spec(1), spec(2), spec(0), spec(0), spec(0)],
            out_specs=whole_spec((rows, 3 * width)),
            scratch_shapes=[pltpu.VMEM((rows, rows), F32)],
        ),
        out_shape=jax.ShapeDtypeStruct((rows, 3 * width), BF16),
        compiler_params=kernel_params(),
        cost_estimate=pl.CostEstimate(
            flops=30 * rows * rows * width, bytes_accessed=20 * rows * width, transcendentals=0
        ),
        name="self_backward",
    )(meta, united, united, united, mixed, upstream, log_totals)


def join_keys(near_ref, far_ref, joined):
    slots, piece = near_ref.shape[0], near_ref.shape[1]
    for slot in range(slots):
        joined[slot, :piece, :] = near_ref[slot]
        joined[slot, piece:, :] = far_ref[slot]


def cross_forward_kernel(
    meta, q_ref, kn_ref, vn_ref, kf_ref, vf_ref, bias_ref, mixed_ref, log_ref, keys, values
):
    half = q_ref.shape[0] // 2
    join_keys(kn_ref, kf_ref, keys)
    join_keys(vn_ref, vf_ref, values)
    for part in range(2):
        slot = part * meta[0]
        rows = slice(part * half, (part + 1) * half)
        mixed, log_totals = pair_forward(q_ref[rows, :], keys[slot], values[slot], bias_ref[slot])
        mixed_ref[rows, :] = mixed.astype(BF16)
        log_ref[rows, :] = log_totals


def cross_forward(meta, query, near, far, bias):
    rows, width = query.shape
    slots, piece = near.shape[0], near.shape[1]
    pairs = width // LANES
    row_spec = pl.BlockSpec((rows, LANES), lambda i, _: (0, i))
    spec = lambda half: pl.BlockSpec((slots, piece, LANES), lambda i, _: (0, 0, half * pairs + i))
    return pl.pallas_call(
        cross_forward_kernel,
        grid_spec=pltpu.PrefetchScalarGridSpec(
            num_scalar_prefetch=1,
            grid=(pairs,),
            in_specs=[row_spec, spec(0), spec(1), spec(0), spec(1), whole_spec(bias.shape)],
            out_specs=[row_spec, row_spec],
            scratch_shapes=[pltpu.VMEM((slots, 2 * piece, LANES), BF16)] * 2,
        ),
        out_shape=[
            jax.ShapeDtypeStruct((rows, width), BF16),
            jax.ShapeDtypeStruct((rows, width), F32),
        ],
        compiler_params=kernel_params(),
        cost_estimate=pl.CostEstimate(
            flops=32 * rows * piece * width, bytes_accessed=24 * rows * width, transcendentals=0
        ),
        name="cross_forward",
    )(meta, query, near, near, far, far, bias)


def cross_backward_kernel(
    meta,
    q_ref,
    kn_ref,
    vn_ref,
    kf_ref,
    vf_ref,
    bias_ref,
    mixed_ref,
    up_ref,
    log_ref,
    grad_q_ref,
    grad_kv_ref,
    keys,
    values,
):
    half = q_ref.shape[0] // 2
    slots, piece = kn_ref.shape[0], kn_ref.shape[1]
    width = grad_kv_ref.shape[1] // 2
    join_keys(kn_ref, kf_ref, keys)
    join_keys(vn_ref, vf_ref, values)
    log_rows, delta_rows = stat_rows(log_ref[...], mixed_ref[...], up_ref[...])
    parts = []
    for part in range(2):
        slot = part * meta[0]
        rows = slice(part * half, (part + 1) * half)
        bias_column = bias_ref[slot]
        grads = pair_backward(
            q_ref[rows, :],
            keys[slot],
            values[slot],
            up_ref[rows, :],
            jnp.concatenate([bias_column] * (half // LANES), axis=1),
            [row[:, rows] for row in log_rows],
            [row[:, rows] for row in delta_rows],
        )
        grad_q_ref[rows, :] = grads[0].astype(BF16)
        parts.append(grads)
    split = meta[0].astype(F32)
    start = pl.program_id(0) * LANES
    for which in range(2):
        early, late = parts[0][1 + which], parts[1][1 + which]
        columns = pl.ds(pl.multiple_of(which * width + start, LANES), LANES)
        by_slot = (early + late * (1.0 - split), late * split)
        for slot in range(slots):
            for source in range(2):
                first = (source * slots + slot) * piece
                grad_kv_ref[first : first + piece, columns] = by_slot[slot][
                    source * piece : (source + 1) * piece
                ].astype(BF16)


def cross_backward(meta, query, near, far, bias, mixed, upstream, log_totals):
    rows, width = query.shape
    slots, piece = near.shape[0], near.shape[1]
    pairs = width // LANES
    memory_rows = 2 * slots * piece
    row_spec = pl.BlockSpec((rows, LANES), lambda i, _: (0, i))
    spec = lambda half: pl.BlockSpec((slots, piece, LANES), lambda i, _: (0, 0, half * pairs + i))
    return pl.pallas_call(
        cross_backward_kernel,
        grid_spec=pltpu.PrefetchScalarGridSpec(
            num_scalar_prefetch=1,
            grid=(pairs,),
            in_specs=[row_spec, spec(0), spec(1), spec(0), spec(1), whole_spec(bias.shape)]
            + [row_spec] * 3,
            out_specs=[row_spec, whole_spec((memory_rows, 2 * width))],
            scratch_shapes=[pltpu.VMEM((slots, 2 * piece, LANES), BF16)] * 2,
        ),
        out_shape=[
            jax.ShapeDtypeStruct((rows, width), BF16),
            jax.ShapeDtypeStruct((memory_rows, 2 * width), BF16),
        ],
        compiler_params=kernel_params(),
        cost_estimate=pl.CostEstimate(
            flops=80 * rows * piece * width, bytes_accessed=40 * rows * width, transcendentals=0
        ),
        name="cross_backward",
    )(meta, query, near, near, far, far, bias, mixed, upstream, log_totals)


def swap_core(values):
    size = lax.axis_size("dp")
    return lax.ppermute(values, "dp", [(i, i ^ 1) for i in range(size)])


def swap_next(values):
    size = lax.axis_size("dp")
    return lax.ppermute(values, "dp", [(i, i ^ 2) for i in range(size)])


def swap_mem(values):
    return lax.ppermute(values, "mem", [(0, 1), (1, 0)])


def swap_outer(values, far):
    size = lax.axis_size("dp")
    return lax.ppermute(values, "dp", [(i, i ^ (4 * far)) for i in range(size)])


def outer_groups():
    size = lax.axis_size("dp")
    return [list(range(base, size, 4)) for base in range(4)]


def place_bits():
    dp, mem = lax.axis_index("dp"), lax.axis_index("mem")
    return jnp.stack([(dp >> 1) & 1, dp & 1, mem]).astype(jnp.int32)


def outer_gather(shard, direct):
    outer, rows = lax.axis_size("dp") // 4, shard.shape[0]
    if not direct:
        stacked = lax.all_gather(shard, "dp", axis_index_groups=outer_groups(), axis=0, tiled=True)
        return stacked.reshape(outer, rows, -1)
    place = lax.axis_index("dp") >> 2
    blocks = jnp.stack([shard] + [swap_outer(shard, far) for far in range(1, outer)])
    bit = 1
    while bit < outer:
        turned = jnp.stack([blocks[i ^ bit] for i in range(outer)])
        blocks = jnp.where((place & bit) != 0, turned, blocks)
        bit *= 2
    return blocks


FIRST = (swap_next, swap_mem)
SECOND = (swap_mem, swap_next)


class Wave:
    def __init__(self, shard, cut, direct):
        self.rows, self.columns, self.cut = shard.shape[0], shard.shape[1], cut
        stacked = outer_gather(shard, direct)
        self.outer = stacked.shape[0]
        self.halves = []
        for half, part in enumerate((stacked[:, :, :cut], stacked[:, :, cut:])):
            near = jnp.stack((part, FIRST[half](part)))
            far = SECOND[half](near)
            self.halves.append((near, far, swap_core(near), swap_core(far)))


class Weight:
    def __init__(self, wave, start, width, whole=None):
        self.wave, self.start, self.width, self.whole = wave, start, width, whole
        if whole is not None:
            self.arrays, self.rows, self.outer = [whole], whole.shape[4], whole.shape[0]
        else:
            self.rows, self.outer = wave.rows, wave.outer
            used = [start < wave.cut, start + width > wave.cut]
            self.arrays = [a for half in range(2) if used[half] for a in wave.halves[half]]

    def copies(self, kind, start, size, bits, find, target):
        if self.whole is not None:
            source = find(self.whole)
            if kind == "columns":
                return [(source.at[:, :, :, :, :, pl.ds(start, size)], target)]
            return [(source.at[start], target)]
        wave, pairs = self.wave, []
        for half in range(2):
            if kind == "columns" and (self.start + start >= wave.cut) != (half == 1):
                continue
            for number, array in enumerate(wave.halves[half]):
                for first in range(2):
                    second, core = number & 1, number >> 1
                    near, mem = (first, second) if half == 0 else (second, first)
                    place = (bits[0] ^ near, bits[1] ^ core, bits[2] ^ mem)
                    if kind == "columns":
                        local = self.start + start - half * wave.cut
                        source = find(array).at[first, :, :, pl.ds(local, size)]
                        pairs.append((source, target.at[:, place[0], place[1], place[2]]))
                    else:
                        source = find(array).at[first, start]
                        columns = pl.ds(half * wave.cut, array.shape[-1])
                        pairs.append((source, target.at[place[0], place[1], place[2], :, columns]))
        return pairs


def weight_call(name, bits, weights, plan, inputs, outs, scratch, body, flops):
    arrays = []
    for weight in weights:
        arrays += [a for a in weight.arrays if not any(a is b for b in arrays)]
    kind, size = plan[0][1], plan[0][3]
    lead = weights[plan[0][0]]
    if kind == "columns":
        chunk = (lead.outer, 2, 2, 2, lead.rows, size)
    else:
        chunk = (2, 2, 2, lead.rows, lead.width)
    n_in, n_arrays, n_out = len(inputs), len(arrays), len(outs)

    def kernel(bits_ref, *refs):
        ins, refs = refs[:n_in], refs[n_in:]
        pieces, refs = refs[:n_arrays], refs[n_arrays:]
        out_refs, refs = refs[:n_out], refs[n_out:]
        held, sems = refs[-2:]
        bits_now = [bits_ref[i] for i in range(3)]

        def find(array):
            return next(ref for ref, known in zip(pieces, arrays) if known is array)

        def issue(number):
            which, kind, start, size = plan[number]
            slot = number % 2
            for source, target in weights[which].copies(
                kind, start, size, bits_now, find, held.at[slot]
            ):
                pltpu.make_async_copy(source, target, sems.at[slot]).start()

        taken = [0]

        def fetch():
            number = taken[0]
            taken[0] += 1
            if number + 1 < len(plan):
                issue(number + 1)
            slot = number % 2
            pltpu.make_async_copy(held.at[slot], held.at[slot], sems.at[slot]).wait()
            return held[slot].reshape(-1, chunk[-1])

        issue(0)
        body(fetch, ins, out_refs, refs[:-2])

    moved = sum(a.size * a.dtype.itemsize for a in inputs) + 2 * len(plan) * lead.outer * size
    return pl.pallas_call(
        kernel,
        in_specs=[pl.BlockSpec(memory_space=pltpu.SMEM)]
        + [pl.BlockSpec(memory_space=pltpu.VMEM)] * n_in
        + [pl.BlockSpec(memory_space=pl.ANY)] * n_arrays,
        out_specs=[pl.BlockSpec(memory_space=pltpu.VMEM)] * n_out,
        out_shape=[jax.ShapeDtypeStruct(shape, kind) for shape, kind in outs],
        scratch_shapes=[pltpu.VMEM(shape, kind) for shape, kind in scratch]
        + [pltpu.VMEM((2, *chunk), BF16), pltpu.SemaphoreType.DMA((2,))],
        compiler_params=kernel_params(),
        cost_estimate=pl.CostEstimate(flops=flops, bytes_accessed=moved, transcendentals=0),
        name=name,
    )(bits, *inputs, *arrays)


def columns_plan(which, width, size):
    return [(which, "columns", start, size) for start in range(0, width, size)]


def row_blocks(rows, size, step):
    def run(i, carry):
        step(pl.ds(pl.multiple_of(i * size, size), size))
        return carry

    lax.fori_loop(0, rows // size, run, 0)


def normed_parts(values):
    centred = values - jnp.mean(values, axis=-1, keepdims=True)
    spread = jnp.mean(centred * centred, axis=-1, keepdims=True)
    rate = lax.rsqrt(spread + EPSILON)
    return centred * rate, rate


def norm_gradient(normed, rate, gain, cotangent):
    inner = cotangent * gain
    mean_inner = jnp.mean(inner, axis=-1, keepdims=True)
    mean_both = jnp.mean(inner * normed, axis=-1, keepdims=True)
    return rate * (inner - mean_inner - normed * mean_both)


def add_stats(stats, normed, cotangent):
    fold = lambda values: jnp.sum(values.reshape(-1, 8, values.shape[-1]), axis=0)
    stats[:8, :] += fold(cotangent * normed)
    stats[8:, :] += fold(cotangent)


def norm_table(bits, weight):
    features = weight.outer * 8 * weight.rows

    def body(fetch, ins, outs, scratch):
        outs[0][...] = fetch().astype(F32).T[:8]

    return weight_call(
        "norm_table", bits, [weight], [(0, "columns", 0, LANES)], [],
        [((8, features), F32)], [], body, 0,
    )[0]


def project(name, bits, weight, sources, size):
    def body(fetch, ins, outs, scratch):
        for start in range(0, weight.width, size):
            chunk = fetch()
            for source, target in zip(ins, outs):
                target[:, start : start + size] = plain_dot(source[...], chunk).astype(BF16)

    flops = sum(2 * source.size * weight.width for source in sources)
    return weight_call(
        name, bits, [weight], columns_plan(0, weight.width, size), sources,
        [((source.shape[0], weight.width), BF16) for source in sources], [], body, flops,
    )


def mix_norm(name, bits, weight, mixed, residual, table, index, query_weight=None):
    rows, width = mixed.shape
    size = 512 if width % 512 == 0 else width

    def body(fetch, ins, outs, scratch):
        mixed_ref, residual_ref, table_ref = ins
        summed, out, out_low = outs[:3]
        for start in range(0, width, size):
            part = plain_dot(mixed_ref[...], fetch())
            columns = slice(start, start + size)
            summed[:, columns] = ALPHA * residual_ref[:, columns].astype(F32) + part
        gain, shift = table_ref[index : index + 1, :], table_ref[3 + index : 4 + index, :]

        def step(block):
            normed, _ = normed_parts(summed[block, :])
            values = normed * gain + shift
            out[block, :] = values
            out_low[block, :] = values.astype(BF16)

        row_blocks(rows, 32, step)
        if query_weight is not None:
            for start in range(0, width, size):
                part = plain_dot(out_low[...], fetch())
                outs[3][:, start : start + size] = part.astype(BF16)

    weights = [weight] + ([query_weight] if query_weight is not None else [])
    plan = [entry for i in range(len(weights)) for entry in columns_plan(i, width, size)]
    outs = [((rows, width), F32), ((rows, width), F32), ((rows, width), BF16)]
    if query_weight is not None:
        outs.append(((rows, width), BF16))
    flops = 2 * rows * width * width * len(weights)
    return weight_call(
        name, bits, weights, plan, [mixed, residual, table], outs, [], body, flops
    )


def feed_in(bits, weight, source):
    rows, size = source.shape[0], 512

    def body(fetch, ins, outs, scratch):
        held = scratch[0]
        for start in range(0, weight.width, size):
            held[...] = plain_dot(ins[0][...], fetch())

            def step(block):
                hidden = held[block, :]
                below = 0.5 + 0.5 * lax.erf(hidden * (0.5**0.5))
                density = jnp.exp(-0.5 * hidden * hidden) * (2.0 * jnp.pi) ** -0.5
                outs[0][block, start : start + size] = (hidden * below).astype(BF16)
                outs[1][block, start : start + size] = (below + hidden * density).astype(BF16)

            row_blocks(rows, 64, step)

    out = ((rows, weight.width), BF16)
    return weight_call(
        "feed_in", bits, [weight], columns_plan(0, weight.width, size), [source], [out, out],
        [((rows, size), F32)], body, 2 * source.size * weight.width,
    )


def feed_out(bits, weight, activated, residual, table, cotangent):
    rows, width = residual.shape
    size = 512 if width % 512 == 0 else width

    def body(fetch, ins, outs, scratch):
        act_ref, residual_ref, table_ref, up_ref = ins
        layer_out, grad, grad_low, stats = outs
        summed = scratch[0]
        for start in range(0, width, size):
            columns = slice(start, start + size)
            part = plain_dot(act_ref[...], fetch())
            summed[:, columns] = ALPHA * residual_ref[:, columns] + part
        gain, shift = table_ref[2:3, :], table_ref[5:6, :]
        stats[...] = jnp.zeros_like(stats)

        def step(block):
            normed, rate = normed_parts(summed[block, :])
            layer_out[block, :] = (normed * gain + shift).astype(BF16)
            upstream = up_ref[block, :].astype(F32)
            values = norm_gradient(normed, rate, gain, upstream)
            grad[block, :] = values
            grad_low[block, :] = values.astype(BF16)
            add_stats(stats, normed, upstream)

        row_blocks(rows, 32, step)

    outs = [((rows, width), BF16), ((rows, width), F32), ((rows, width), BF16), ((16, width), F32)]
    return weight_call(
        "feed_out", bits, [weight], columns_plan(0, width, size),
        [activated, residual, table, cotangent], outs, [((rows, width), F32)], body,
        2 * activated.size * width,
    )


def feed_back(bits, weight, cotangent, slope):
    rows, features = slope.shape
    size = features // weight.outer

    def body(fetch, ins, outs, scratch):
        for block in range(weight.outer):
            part = back_dot(ins[0][...], fetch())
            columns = slice(block * size, (block + 1) * size)
            outs[0][:, columns] = (part * ins[1][:, columns].astype(F32)).astype(BF16)

    return weight_call(
        "feed_back", bits, [weight], [(0, "outer", i, 1) for i in range(weight.outer)],
        [cotangent, slope], [((rows, features), BF16)], [], body, 2 * cotangent.size * features,
    )[0]


def norm_back(name, bits, weight, cotangent, carried, summed, table, index, mix_weight):
    rows, width = summed.shape
    size = min(1024, weight.width)

    def body(fetch, ins, outs, scratch):
        up_ref, carried_ref, summed_ref, table_ref = ins
        grad, grad_low, grad_mixed, stats = outs
        total = scratch[0]
        for start in range(0, weight.width, size):
            part = back_dot(up_ref[:, start : start + size], fetch())
            total[...] = part + (ALPHA * carried_ref[...] if start == 0 else total[...])
        gain = table_ref[index : index + 1, :]
        stats[...] = jnp.zeros_like(stats)

        def step(block):
            normed, rate = normed_parts(summed_ref[block, :])
            upstream = total[block, :]
            values = norm_gradient(normed, rate, gain, upstream)
            grad[block, :] = values
            grad_low[block, :] = values.astype(BF16)
            add_stats(stats, normed, upstream)

        row_blocks(rows, 32, step)
        grad_mixed[...] = back_dot(grad_low[...], fetch()).astype(BF16)

    outs = [((rows, width), F32), ((rows, width), BF16), ((rows, width), BF16), ((16, width), F32)]
    return weight_call(
        name, bits, [weight, mix_weight],
        columns_plan(0, weight.width, size) + columns_plan(1, width, size),
        [cotangent, carried, summed, table], outs, [((rows, width), F32)], body,
        2 * cotangent.size * width + 2 * rows * width * width,
    )


def input_back(name, bits, weight, cotangent, carried, size):
    rows, features = cotangent.shape[0], weight.outer * 8 * weight.rows
    step = min(rows, 512)
    starts = list(range(0, weight.width, size))

    def body(fetch, ins, outs, scratch):
        for start in starts:
            chunk = fetch()
            for row in range(0, rows, step):
                block = slice(row, row + step)
                part = back_dot(ins[0][block, start : start + size], chunk)
                if start == 0 and carried is not None:
                    part += ALPHA * ins[1][block, :]
                elif start > 0:
                    part += scratch[0][block, :]
                if start == starts[-1]:
                    outs[0][block, :] = part.astype(BF16)
                else:
                    scratch[0][block, :] = part

    return weight_call(
        name, bits, [weight], columns_plan(0, weight.width, size),
        [cotangent] + ([carried] if carried is not None else []), [((rows, features), BF16)],
        [((rows, features), F32)], body, 2 * cotangent.size * features,
    )[0]


def weight_grad(bits, sources, cotangent, outer):
    features = sources[0].shape[1]
    total_rows, width = cotangent.shape
    shard_rows = features // (8 * outer)
    chunk = min(512, width)

    def kernel(bits_ref, *refs):
        source_refs = refs[: len(sources)]
        grads, own_ref, other_ref, turned = refs[len(sources) :]

        @pl.when(pl.program_id(0) == 0)
        def _():
            filled = 0
            for ref in source_refs:
                stop = filled + ref.shape[0]
                for block in range(features // LANES):
                    turned_block = ref[:, block * LANES : (block + 1) * LANES].T
                    for part in range(LANES // shard_rows):
                        device = block * (LANES // shard_rows) + part
                        mem, core, near = device & 1, (device >> 1) & 1, (device >> 2) & 1
                        place = (core ^ bits_ref[1]) * 2 + (mem ^ bits_ref[2])
                        place = (place * 2 + (near ^ bits_ref[0])) * outer + (device >> 3)
                        target = pl.ds(pl.multiple_of(place * shard_rows, shard_rows), shard_rows)
                        turned[target, filled:stop] = turned_block[
                            part * shard_rows : (part + 1) * shard_rows
                        ]
                filled = stop

        half = features // 2
        for number, ref in enumerate((own_ref, other_ref)):
            product = plain_dot(turned[number * half : (number + 1) * half, :], grads[...])
            ref[...] = product.astype(BF16).reshape(ref.shape)

    shape = (2, 2, outer, shard_rows)
    out_spec = pl.BlockSpec((*shape, chunk), lambda i, _: (0, 0, 0, 0, i))
    return pl.pallas_call(
        kernel,
        grid_spec=pltpu.PrefetchScalarGridSpec(
            num_scalar_prefetch=1,
            grid=(width // chunk,),
            in_specs=[whole_spec(source.shape) for source in sources]
            + [pl.BlockSpec((total_rows, chunk), lambda i, _: (0, i))],
            out_specs=[out_spec, out_spec],
            scratch_shapes=[pltpu.VMEM((features, total_rows), BF16)],
        ),
        out_shape=[jax.ShapeDtypeStruct((*shape, width), BF16)] * 2,
        compiler_params=kernel_params(),
        cost_estimate=pl.CostEstimate(
            flops=2 * total_rows * features * width,
            bytes_accessed=2 * (total_rows + features) * width,
            transcendentals=0,
        ),
        name="weight_grad",
    )(bits, *sources, cotangent)


def relative_rows(bits, values, outer):
    rows = values.shape[0] // (8 * outer)
    blocks = values.reshape(outer, 2, 2, 2, rows, -1)
    for axis, bit in ((1, bits[0]), (2, bits[1]), (3, bits[2])):
        blocks = jnp.where(bit == 1, jnp.flip(blocks, axis), blocks)
    blocks = blocks.transpose(2, 3, 1, 0, 4, 5)
    return blocks[0], blocks[1]


def add_up(*terms):
    return sum(term.astype(F32) for term in terms).astype(BF16)


def scatter_pieces(own, other, cut, direct):
    far = swap_core(other)
    halves = []
    for half in range(2):
        columns = slice(0, cut) if half == 0 else slice(cut, None)
        near, far_part = own[..., columns], far[..., columns]
        if half == 0:
            first = swap_mem(add_up(near[1], far_part[1]))
            second = swap_next(add_up(near[0, 1], far_part[0, 1], first[1]))
        else:
            first = swap_next(add_up(near[:, 1], far_part[:, 1]))
            second = swap_mem(add_up(near[1, 0], far_part[1, 0], first[1]))
        halves.append(add_up(near[0, 0], far_part[0, 0], first[0], second))
    joined = jnp.concatenate(halves, axis=-1)
    if not direct:
        joined = joined.reshape(-1, joined.shape[-1])
        return lax.psum_scatter(
            joined, "dp", axis_index_groups=outer_groups(), scatter_dimension=0, tiled=True
        ).astype(F32)
    place = lax.axis_index("dp") >> 2
    block = lambda far: lax.dynamic_index_in_dim(joined, place ^ far, 0, False)
    parts = [block(0)] + [swap_outer(block(far), far) for far in range(1, joined.shape[0])]
    return sum(part.astype(F32) for part in parts)


def per_device(
    target_in,
    memory_in,
    bucket_ids,
    target_lengths,
    memory_mask,
    self_qkv,
    self_out,
    cross_q,
    cross_kv,
    cross_out,
    ffn_in,
    ffn_out,
    norm_gains,
    norm_biases,
    grad_out,
):
    both = ("dp", "mem")
    row_count, model_width = target_in.shape
    shard_rows = self_qkv.shape[0]
    outer = lax.axis_size("dp") // 4
    staged = shard_rows % 16 == 0 and shard_rows <= LANES and model_width % LANES == 0
    bits = place_bits()
    own_index = lax.axis_index("mem")
    slot_count, mem_piece = memory_in.shape[3], memory_in.shape[4]

    norm_shard = jnp.concatenate((norm_gains, norm_biases), axis=1)
    norm_columns = norm_shard.shape[1]
    norm_shard = jnp.pad(norm_shard, ((0, 0), (0, LANES - norm_columns)))

    def gather(parts, cut, direct=False):
        shard = jnp.concatenate([part.astype(BF16) for part in parts], axis=1)
        widths = [part.shape[1] for part in parts]
        starts = [sum(widths[:i]) for i in range(len(widths))]
        if staged:
            wave = Wave(shard, sum(widths[:cut]) if cut else widths[0] // 2, direct)
            return [Weight(wave, at, size) for at, size in zip(starts, widths)]
        full = lax.all_gather(shard, both, axis=0, tiled=True)
        rows = full.shape[0] // 32
        return [
            Weight(None, 0, size, full[:, at : at + size].reshape(4, 2, 2, 2, rows, size))
            for at, size in zip(starts, widths)
        ]

    def give(source, cotangent):
        if staged:
            return weight_grad(bits, source, cotangent, outer)
        return lead_dot(jnp.concatenate(source, axis=0), cotangent).astype(BF16)

    def spread(parts, direct=False):
        if not staged:
            return lax.psum_scatter(
                parts[0] if len(parts) == 1 else jnp.concatenate(parts, axis=-1),
                both,
                scatter_dimension=0,
                tiled=True,
            ).astype(F32)
        own, other = (
            parts[0]
            if len(parts) == 1
            else [jnp.concatenate([part[side] for part in parts], axis=-1) for side in range(2)]
        )
        return scatter_pieces(own, other, own.shape[-1] // 2 // LANES * LANES, direct)

    def at_mem(values, index):
        return lax.dynamic_index_in_dim(values, index, 0, False)

    mem_rows = memory_in[0, :, 0]
    mem_live = memory_mask[0, :, 0]
    near_rows = at_mem(mem_rows, own_index)
    near_live = at_mem(mem_live, own_index)
    far_rows = swap_mem(at_mem(mem_rows, 1 - own_index))
    far_live = swap_mem(at_mem(mem_live, 1 - own_index))

    (w_qkv,) = gather((self_qkv,), 0, True)
    w_cq, w_co, w_norm, w_ckv, w_so = gather((cross_q, cross_out, norm_shard, cross_kv, self_out), 3)
    (w_in,) = gather((ffn_in,), 0)
    (w_out,) = gather((ffn_out,), 0)

    bucket = pick_entry(bucket_ids[0], own_index)
    lengths = target_lengths[0, 0]
    self_meta = jnp.stack([jnp.right_shift(jnp.int32(row_count), bucket), lengths[0], lengths[1]])
    cross_meta = bucket[None]
    live = jnp.concatenate((near_live, far_live), axis=1)
    key_bias = jnp.where(live == 1, 0.0, NEG_LARGE).astype(F32)
    key_columns = jnp.broadcast_to(key_bias[:, :, None], (*key_bias.shape, LANES))
    near_flat = near_rows.reshape(-1, model_width)
    far_flat = far_rows.reshape(-1, model_width)
    slotted = (slot_count, mem_piece, 2 * model_width)

    (united,) = project("self_project", bits, w_qkv, [target_in], 512)
    self_mixed, self_log = self_forward(self_meta, united)
    table = norm_table(bits, w_norm)
    near_kv, far_kv = project("cross_project", bits, w_ckv, [near_flat, far_flat], 512)
    near_kv, far_kv = near_kv.reshape(slotted), far_kv.reshape(slotted)
    sum_one, first_out, first_low, cross_query = mix_norm(
        "self_mix", bits, w_so, self_mixed, target_in, table, 0, w_cq
    )
    cross_mixed, cross_log = cross_forward(
        cross_meta, cross_query, near_kv, far_kv, key_bias[:, None, :]
    )
    sum_two, second_out, second_low = mix_norm(
        "cross_mix", bits, w_co, cross_mixed, first_out, table, 1
    )
    activated, slope = feed_in(bits, w_in, second_low)
    layer_out, grad_three, grad_ffn, stats_three = feed_out(
        bits, w_out, activated, second_out, table, grad_out
    )

    out_shard = spread([give([activated], grad_ffn)])
    grad_hidden = feed_back(bits, w_out, grad_ffn, slope)
    in_shard = spread([give([second_low], grad_hidden)])
    grad_two, grad_cross_out, grad_cross_mixed, stats_two = norm_back(
        "cross_back", bits, w_in, grad_hidden, grad_three, sum_two, table, 1, w_co
    )
    co_grad = give([cross_mixed], grad_cross_out)
    grad_query_low, grad_kv = cross_backward(
        cross_meta,
        cross_query,
        near_kv,
        far_kv,
        key_columns,
        cross_mixed,
        grad_cross_mixed,
        cross_log,
    )
    cq_grad = give([first_low], grad_query_low)
    ckv_grad = give([near_flat, far_flat], grad_kv)
    first_shards = spread([co_grad, cq_grad, ckv_grad])
    grad_memory = input_back("memory_back", bits, w_ckv, grad_kv, None, model_width)
    half_rows = near_flat.shape[0]
    grad_near = grad_memory[:half_rows].reshape(near_rows.shape)
    grad_far = swap_mem(grad_memory[half_rows:].reshape(near_rows.shape))
    grad_pair = jnp.stack((grad_near, grad_far))
    memory_grad = jnp.where(own_index == 0, grad_pair, grad_pair[::-1])[None, :, None]

    grad_one, grad_self_out, grad_self_mixed, stats_one = norm_back(
        "self_back", bits, w_cq, grad_query_low, grad_two, sum_one, table, 0, w_so
    )
    stats = [jnp.sum(s.reshape(2, 8, model_width), axis=1) for s in (stats_one, stats_two, stats_three)]
    norm_grads = jnp.stack([s[0] for s in stats] + [s[1] for s in stats], axis=1).astype(BF16)
    norm_grads = jnp.pad(norm_grads, ((0, 0), (0, LANES - norm_columns)))
    if staged:
        norm_grads = relative_rows(bits, norm_grads, outer)
    so_shard = spread([give([self_mixed], grad_self_out), norm_grads])
    grad_united = self_backward(self_meta, united, self_mixed, grad_self_mixed, self_log)
    qkv_shard = spread([give([target_in], grad_united)], True)
    target_grad = input_back(
        "target_back", bits, w_qkv, grad_united, grad_one, w_qkv.width // 2
    )

    return (
        layer_out,
        target_grad,
        memory_grad,
        qkv_shard,
        so_shard[:, :model_width],
        first_shards[:, model_width : 2 * model_width],
        first_shards[:, 2 * model_width :],
        first_shards[:, :model_width],
        in_shard,
        out_shard,
        so_shard[:, model_width : model_width + 3],
        so_shard[:, model_width + 3 : model_width + norm_columns],
    )


def solution(mesh):
    rows = P(("dp", "mem"), None)
    memory = P("dp", None, "mem", None, None, None)
    return jax.shard_map(
        per_device,
        mesh=mesh,
        in_specs=(
            rows,
            memory,
            P("dp", None),
            P("dp", "mem", None),
            P("dp", None, "mem", None, None),
        )
        + (rows,) * 10,
        out_specs=(rows, rows, memory) + (rows,) * 9,
        check_vma=False,
    )
```

time: 2690 us -> 782 us (0.29)
  waiting for transfers between devices: 1820 us -> 309 us
  matrix products: 380 us -> 0 us
  Pallas kernels: 0 us -> 266 us
  blocking collectives: 153 us -> 0 us
  local copies, waits for them, and re-layouts: 182 us -> 31.6 us
  starting transfers between devices: 1.69 us -> 68.7 us
  other arithmetic: 113 us -> 83.5 us
    reduce_scatter x7 -> x3, waiting for transfers between devices: 1200 us -> 0.01 us  [scatter_pieces(): lax.psum_scatter(joined, 'dp', axis_index_groups=outer_groups(), scatter_...]
    unnamed x24 -> x8, waiting for transfers between devices: 413 us -> 0.12 us
    dot_general x93 -> x0, matrix products: 380 us -> none  [the longest x24 125 us: head_dots(): jnp.einsum('qhd,khd->hqk', first_heads, second_heads, preferred_element_t...]
    ppermute x0 -> x66, waiting for transfers between devices: none -> 275 us  [the longest x21 150 us: swap_mem(): return lax.ppermute(values, 'mem', [(0, 1), (1, 0)])]
    pallas_call x0 -> x23, Pallas kernels: none -> 266 us  [the longest x12 139 us: weight_call(): pl.pallas_call(kernel, in_specs=[pl.BlockSpec(memory_space=pltpu.SMEM)] +...]
    all_gather x9 -> x3, waiting for transfers between devices: 210 us -> 33.9 us  [outer_gather(): lax.all_gather(shard, 'dp', axis_index_groups=outer_groups(), axis=0, til...]
    all_gather x4 -> x0, blocking collectives: 144 us -> none  [the longest x1 70.2 us: per_device(): lax.all_gather(norm_biases.astype(jnp.bfloat16), ('dp', 'mem'), axis=0, t...]
    slice x61 -> x7, local copies, waits for them, and re-layouts: 101 us -> 6.41 us  [the longest x1 1.93 us: per_device(): grad_near = grad_memory[:half_rows].reshape(near_rows.shape)]
  transfers between devices with their start and end apart: 20 -> 73, of which waited for: 14 -> 25; matrix products, arithmetic and copies ran while one was open for 16% -> 13% of each run, Pallas kernels for 0% -> 19%
where the time goes in v1:
time: 782 us; the launch traced here: 775 us
  waiting for transfers between devices  309 us (40%)
  Pallas kernels  266 us (34%)
  other arithmetic  83.5 us (11%)
  starting transfers between devices  68.7 us (9%)
  local copies, waits for them, and re-layouts  31.6 us (4%)
  between operations  16 us (2%)
    ppermute x21, waiting for transfers between devices, swap_mem(): return lax.ppermute(values, 'mem', [(0, 1), (1, 0)])  150 us
    pallas_call x12, Pallas kernels, weight_call(): pl.pallas_call(kernel, in_specs=[pl.BlockSpec(memory_space=pltpu.SMEM)] +...  139 us
    ppermute x18, waiting for transfers between devices, swap_next(): return lax.ppermute(values, 'dp', [(i, i ^ 2) for i in range(size)])  86 us
    pallas_call x7, Pallas kernels, weight_grad(): pl.pallas_call(kernel, grid_spec=pltpu.PrefetchScalarGridSpec(num_scalar_...  54 us
    convert_element_type x26, other arithmetic, add_up(): return sum((term.astype(F32) for term in terms)).astype(BF16)  44 us
    ppermute x6, waiting for transfers between devices, swap_outer(): return lax.ppermute(values, 'dp', [(i, i ^ 4 * far) for i in range(size)])  39.6 us
    all_gather x3, waiting for transfers between devices, outer_gather(): lax.all_gather(shard, 'dp', axis_index_groups=outer_groups(), axis=0, til...  33.9 us
    ppermute x6, starting transfers between devices, swap_outer(): return lax.ppermute(values, 'dp', [(i, i ^ 4 * far) for i in range(size)])  25.4 us
  transfers between devices with their start and end apart: 73, of which 25 were waited for; matrix products, arithmetic and copies ran while one was open for 13% of the time, Pallas kernels for 19%

profile of v1, /device:TPU:0, one launch (start us, length us, event | category | flops | bytes accessed | tf_op | source)
XLA Modules:
  0.0 774.7 jit_solution(1517006872144451589)
XLA Ops:
  10.2 4.1 collective-permute-start.2
  20.1 15.5 %collective-permute-done.2 = bf16[32,3072]{1,0:T(8,128)(2,1)S(1)} collective-permute-done((bf16[32,3072]{1,0:T(8,128)(2,1)S(1)}, bf16[32,3072]{1,0:T(8,128)(2,1)S(1)}, u32[]{:S(2)}, u32[]{:S(2)}) %collective-permute-start.2) | collective-permute-done | bytes 196640 | tf_op jit(solution)/shard_map/ppermute | solution.py:361
  58.4 27.3 %all-gather.4.cloned.1.call-done = bf16[128,5248]{1,0:T(8,128)(2,1)} async-done(((bf16[32,5248]{1,0:T(8,128)(2,1)}), bf16[128,5248]{1,0:T(8,128)(2,1)}) %all-gather.4.cloned.1.call-update) | async-done | bytes 1343504 | tf_op jit(solution)/shard_map/all_gather | solution.py:377
  88.2 13.7 %collective-permute-done.4.refs_2_.refs_3_ = bf16[2,4,32,1536]{3,2,1,0:T(8,128)(2,1)} collective-permute-done((bf16[2,4,32,1536]{3,2,1,0:T(8,128)(2,1)S(1)}, bf16[2,4,32,1536]{3,2,1,0:T(8,128)(2,1)}, u32[]{:S(2)}, u32[]{:S(2)}) %collective-permute-start.4) | collective-permute-done | bytes 786464 | tf_op jit(solution)/shard_map/ppermute | solution.py:356
  107.6 6.6 all-gather.8.cloned.1.call-done
  123.6 9.5 %collective-permute-done.25 = bf16[4,32,2048]{2,1,0:T(8,128)(2,1)S(1)} collective-permute-done((bf16[4,32,2048]{2,1,0:T(8,128)(2,1)S(1)}, bf16[4,32,2048]{2,1,0:T(8,128)(2,1)S(1)}, u32[]{:S(2)}, u32[]{:S(2)}) %collective-permute-start.25) | collective-permute-done | bytes 524320 | tf_op jit(solution)/shard_map/ppermute | solution.py:356
  137.3 7.0 collective-permute-done.33
  148.2 19.4 %collective-permute-done.16.refs_4_.refs_3_.refs_9_.refs_2_ = bf16[2,4,32,3072]{3,2,1,0:T(8,128)(2,1)} collective-permute-done((bf16[2,4,32,3072]{3,2,1,0:T(8,128)(2,1)S(1)}, bf16[2,4,32,3072]{3,2,1,0:T(8,128)(2,1)}, u32[]{:S(2)}, u32[]{:S(2)}) %collective-permute-start.16) | collective-permute-done | bytes 1572896 | tf_op jit(solution)/shard_map/ppermute | solution.py:352
  169.9 20.4 %collective-permute-done.22.refs_2_.refs_5_ = bf16[2,4,32,2048]{3,2,1,0:T(8,128)(2,1)} collective-permute-done((bf16[2,4,32,2048]{3,2,1,0:T(8,128)(2,1)}, bf16[2,4,32,2048]{3,2,1,0:T(8,128)(2,1)}, u32[]{:S(2)}, u32[]{:S(2)}) %collective-permute-start.22) | collective-permute-done | bytes 1048608 | tf_op jit(solution)/shard_map/ppermute | solution.py:356
  196.5 10.4 %self_project.1.q_ref.k_ref.v_ref = bf16[512,3072]{1,0:T(8,128)(2,1)} custom-call(s32[3]{0:T(128)S(1)} %pad_add_fusion.bits_ref, bf16[512,1024]{1,0:T(8,128)(2,1)} %refs_0_.3, bf16[2,4,32,1536]{3,2,1,0:T(8,128)(2,1)S(1)} %pad_maximum_fusion.12.refs_1_.refs_2_, bf16[2,4,32,1536]{3,2,1,0:T(8,128)(2,1)} %collective-permute-done.4.refs_2_.refs_3_, ...), custom_call_target="tpu_custom_call" | custom-call | flops 3221225472 | bytes 1073152 | tf_op jit(solution)/shard_map/self_project/pallas_call | solution.py:486
  206.9 8.4 %collective-permute-done.26.refs_6_.refs_9_ = bf16[2,4,32,2048]{3,2,1,0:T(8,128)(2,1)} collective-permute-done((bf16[2,4,32,2048]{3,2,1,0:T(8,128)(2,1)}, bf16[2,4,32,2048]{3,2,1,0:T(8,128)(2,1)}, u32[]{:S(2)}, u32[]{:S(2)}) %collective-permute-start.26) | collective-permute-done | bytes 1048608 | tf_op jit(solution)/shard_map/ppermute | solution.py:352
  218.3 14.0 %self_forward.1 = (bf16[512,1024]{1,0:T(8,128)(2,1)S(1)}, f32[512,1024]{1,0:T(8,128)}) custom-call(s32[3]{0:T(128)S(1)} %pad_add_fusion.1.meta, bf16[512,3072]{1,0:T(8,128)(2,1)} %self_project.1.q_ref.k_ref.v_ref, bf16[512,3072]{1,0:T(8,128)(2,1)} %self_project.1.q_ref.k_ref.v_ref, bf16[512,3072]{1,0:T(8,128)(2,1)} %self_project.1.q_ref.k_ref.v_ref), custom_call_target="tpu_custom_call" | custom-call | flops 3221225472 | bytes 6291456 | tf_op jit(solution)/shard_map/self_forward/pallas_call | solution.py:135
  235.4 11.7 %cross_project.1 = (bf16[768,2048]{1,0:T(8,128)(2,1)}, bf16[768,2048]{1,0:T(8,128)(2,1)}) custom-call(s32[3]{0:T(128)S(1)} %pad_add_fusion.bits_ref, bf16[768,1024]{1,0:T(8,128)(2,1)S(1)} %bitcast.287, bf16[768,1024]{1,0:T(8,128)(2,1)} %bitcast.24.refs_1_, bf16[2,4,32,3072]{3,2,1,0:T(8,128)(2,1)} %copy-done.1, ...), custom_call_target="tpu_custom_call" | custom-call | flops 6442450944 | bytes 3162112 | tf_op jit(solution)/shard_map/cross_project/pallas_call | solution.py:486
  247.1 11.2 %self_mix.1 = (f32[512,1024]{1,0:T(8,128)}, f32[512,1024]{1,0:T(8,128)}, bf16[512,1024]{1,0:T(8,128)(2,1)S(1)}, bf16[512,1024]{1,0:T(8,128)(2,1)}) custom-call(s32[3]{0:T(128)S(1)} %pad_add_fusion.bits_ref, bf16[512,1024]{1,0:T(8,128)(2,1)} %copy-done.7, bf16[512,1024]{1,0:T(8,128)(2,1)} %refs_0_.3, f32[8,1024]{1,0:T(8,128)S(1)} %norm_table.1.refs_2_.refs_3_, ...), custom_call_target="tpu_custom_call" | custom-call | flops 2147483648 | bytes 2146304 | tf_op jit(solution)/shard_map/self_mix/pallas_call | solution.py:486
  259.5 18.2 %cross_forward.1 = (bf16[512,1024]{1,0:T(8,128)(2,1)S(1)}, f32[512,1024]{1,0:T(8,128)}) custom-call(s32[1]{0:T(128)} %bitcast.5.meta, bf16[512,1024]{1,0:T(8,128)(2,1)} %get-tuple-element.56.q_ref, bf16[2,384,2048]{2,1,0:T(8,128)(2,1)} %bitcast.309, bf16[2,384,2048]{2,1,0:T(8,128)(2,1)} %bitcast.310, bf16[2,384,2048]{2,1,0:T(8,128)(2,1)} %bitcast.313, ...), custom_call_target="tpu_custom_call" | custom-call | flops 6442450944 | bytes 12582912 | tf_op jit(solution)/shard_map/cross_forward/pallas_call | solution.py:243
  278.7 9.7 %cross_mix.1 = (f32[512,1024]{1,0:T(8,128)}, f32[512,1024]{1,0:T(8,128)}, bf16[512,1024]{1,0:T(8,128)(2,1)S(1)}) custom-call(s32[3]{0:T(128)S(1)} %pad_add_fusion.bits_ref, bf16[512,1024]{1,0:T(8,128)(2,1)} %copy-done.10, f32[512,1024]{1,0:T(8,128)} %get-tuple-element.60.refs_1_, f32[8,1024]{1,0:T(8,128)S(1)} %norm_table.1.refs_2_.refs_3_, ...), custom_call_target="tpu_custom_call" | custom-call | flops 1073741824 | bytes 3186688 | tf_op jit(solution)/shard_map/cross_mix/pallas_call | solution.py:486
  289.4 15.8 %feed_in.1 = (bf16[512,4096]{1,0:T(8,128)(2,1)}, bf16[512,4096]{1,0:T(8,128)(2,1)}) custom-call(s32[3]{0:T(128)S(1)} %pad_add_fusion.bits_ref, bf16[512,1024]{1,0:T(8,128)(2,1)S(1)} %get-tuple-element.61.refs_0_, bf16[2,4,32,2048]{3,2,1,0:T(8,128)(2,1)} %pad_maximum_fusion.5.refs_1_.refs_4_, ...), custom_call_target="tpu_custom_call" | custom-call | flops 4294967296 | bytes 1081344 | tf_op jit(solution)/shard_map/feed_in/pallas_call | solution.py:486
  305.2 16.7 %feed_out.1 = (bf16[512,1024]{1,0:T(8,128)(2,1)}, f32[512,1024]{1,0:T(8,128)}, bf16[512,1024]{1,0:T(8,128)(2,1)S(1)}, f32[16,1024]{1,0:T(8,128)S(1)}) custom-call(s32[3]{0:T(128)S(1)} %pad_add_fusion.bits_ref, bf16[512,4096]{1,0:T(8,128)(2,1)} %get-tuple-element.62.refs_0_, f32[512,1024]{1,0:T(8,128)} %get-tuple-element.63.refs_1_, ...), custom_call_target="tpu_custom_call" | custom-call | flops 4294967296 | bytes 7380992 | tf_op jit(solution)/shard_map/feed_out/pallas_call | solution.py:486
  321.9 11.3 %feed_back.1.refs_0_.refs_1_ = bf16[512,4096]{1,0:T(8,128)(2,1)} custom-call(s32[3]{0:T(128)S(1)} %pad_add_fusion.bits_ref, bf16[512,1024]{1,0:T(8,128)(2,1)S(1)} %get-tuple-element.65.refs_0_.refs_1_, bf16[512,4096]{1,0:T(8,128)(2,1)} %get-tuple-element.66.refs_1_, bf16[2,4,128,512]{3,2,1,0:T(8,128)(2,1)} %copy-done.17, ...), custom_call_target="tpu_custom_call" | custom-call | flops 4294967296 | bytes 5242912 | tf_op jit(solution)/shard_map/feed_back/pallas_call | solution.py:486
  334.1 10.2 %weight_grad.12 = (bf16[2,2,4,32,4096]{4,3,2,1,0:T(8,128)(2,1)}, bf16[2,2,4,32,4096]{4,3,2,1,0:T(8,128)(2,1)}) custom-call(s32[3]{0:T(128)S(1)} %pad_add_fusion.bits_ref, bf16[512,1024]{1,0:T(8,128)(2,1)S(1)} %get-tuple-element.61.refs_0_, bf16[512,4096]{1,0:T(8,128)(2,1)} %feed_back.1.refs_0_.refs_1_), custom_call_target="tpu_custom_call" | custom-call | flops 4294967296 | bytes 12582912 | tf_op jit(solution)/shard_map/weight_grad/pallas_call | solution.py:765
  344.3 17.1 %cross_back.1 = (f32[512,1024]{1,0:T(8,128)}, bf16[512,1024]{1,0:T(8,128)(2,1)S(1)}, bf16[512,1024]{1,0:T(8,128)(2,1)}, f32[16,1024]{1,0:T(8,128)S(1)}) custom-call(s32[3]{0:T(128)S(1)} %pad_add_fusion.bits_ref, bf16[512,4096]{1,0:T(8,128)(2,1)} %feed_back.1.refs_0_.refs_1_, f32[512,1024]{1,0:T(8,128)} %get-tuple-element.67.refs_1_, ...), custom_call_target="tpu_custom_call" | custom-call | flops 5368709120 | bytes 8462336 | tf_op jit(solution)/shard_map/cross_back/pallas_call | solution.py:486
  361.7 24.6 %cross_backward.1 = (bf16[512,1024]{1,0:T(8,128)(2,1)S(1)}, bf16[1536,2048]{1,0:T(8,128)(2,1)}) custom-call(s32[1]{0:T(128)} %bitcast.5.meta, bf16[512,1024]{1,0:T(8,128)(2,1)} %get-tuple-element.56.q_ref, bf16[2,384,2048]{2,1,0:T(8,128)(2,1)} %bitcast.311, bf16[2,384,2048]{2,1,0:T(8,128)(2,1)} %bitcast.312, bf16[2,384,2048]{2,1,0:T(8,128)(2,1)} %bitcast.315, ...), custom_call_target="tpu_custom_call" | custom-call | flops 16106127360 | bytes 20971520 | tf_op jit(solution)/shard_map/cross_backward/pallas_call | solution.py:323
  387.2 12.4 %self_back.1 = (f32[512,1024]{1,0:T(8,128)}, bf16[512,1024]{1,0:T(8,128)(2,1)S(1)}, bf16[512,1024]{1,0:T(8,128)(2,1)}, f32[16,1024]{1,0:T(8,128)S(1)}) custom-call(s32[3]{0:T(128)S(1)} %pad_add_fusion.bits_ref, bf16[512,1024]{1,0:T(8,128)(2,1)} %copy-done.9, f32[512,1024]{1,0:T(8,128)} %get-tuple-element.72.refs_1_, f32[512,1024]{1,0:T(8,128)} %get-tuple-element.73.refs_2_, ...), custom_call_target="tpu_custom_call" | custom-call | flops 2147483648 | bytes 5292032 | tf_op jit(solution)/shard_map/self_back/pallas_call | solution.py:486
  399.6 15.5 %self_backward.1.refs_0_.refs_1_ = bf16[512,3072]{1,0:T(8,128)(2,1)} custom-call(s32[3]{0:T(128)S(1)} %pad_add_fusion.1.meta, bf16[512,3072]{1,0:T(8,128)(2,1)} %self_project.1.q_ref.k_ref.v_ref, bf16[512,3072]{1,0:T(8,128)(2,1)} %self_project.1.q_ref.k_ref.v_ref, bf16[512,3072]{1,0:T(8,128)(2,1)} %self_project.1.q_ref.k_ref.v_ref, ...), custom_call_target="tpu_custom_call" | custom-call | flops 8053063680 | bytes 10485760 | tf_op jit(solution)/shard_map/self_backward/pallas_call | solution.py:198
  415.2 8.2 %weight_grad.7 = (bf16[2,2,4,32,3072]{4,3,2,1,0:T(8,128)(2,1)}, bf16[2,2,4,32,3072]{4,3,2,1,0:T(8,128)(2,1)}) custom-call(s32[3]{0:T(128)S(1)} %pad_add_fusion.bits_ref, bf16[512,1024]{1,0:T(8,128)(2,1)S(1)} %copy-done.4, bf16[512,3072]{1,0:T(8,128)(2,1)} %self_backward.1.refs_0_.refs_1_), custom_call_target="tpu_custom_call" | custom-call | flops 3221225472 | bytes 9437184 | tf_op jit(solution)/shard_map/weight_grad/pallas_call | solution.py:765
  423.5 4.6 weight_grad.8
  430.4 11.4 %weight_grad.11 = (bf16[2,2,4,32,2048]{4,3,2,1,0:T(8,128)(2,1)}, bf16[2,2,4,32,2048]{4,3,2,1,0:T(8,128)(2,1)}) custom-call(s32[3]{0:T(128)S(1)} %pad_add_fusion.bits_ref, bf16[768,1024]{1,0:T(8,128)(2,1)S(1)} %bitcast.288, bf16[768,1024]{1,0:T(8,128)(2,1)} %bitcast.24.refs_1_, bf16[1536,2048]{1,0:T(8,128)(2,1)} %get-tuple-element.77.refs_0_.refs_2_), custom_call_target="tpu_custom_call" | custom-call | flops 6442450944 | bytes 10485760 | tf_op jit(solution)/shard_map/weight_grad/pallas_call | solution.py:765
  441.8 4.6 weight_grad.10
  446.3 4.8 weight_grad.9
  451.2 3.5 pad_maximum_fusion
  456.8 12.7 %memory_back.1 = bf16[1536,1024]{1,0:T(8,128)(2,1)} custom-call(s32[3]{0:T(128)S(1)} %pad_add_fusion.bits_ref, bf16[1536,2048]{1,0:T(8,128)(2,1)} %get-tuple-element.77.refs_0_.refs_2_, bf16[2,4,32,3072]{3,2,1,0:T(8,128)(2,1)S(1)} %copy-done.2, bf16[2,4,32,3072]{3,2,1,0:T(8,128)(2,1)} %collective-permute-done.16.refs_4_.refs_3_.refs_9_.refs_2_, ...), custom_call_target="tpu_custom_call" | custom-call | flops 6442450944 | bytes 6307840 | tf_op jit(solution)/shard_map/memory_back/pallas_call | solution.py:486
  469.6 9.1 %target_back.1 = bf16[512,1024]{1,0:T(8,128)(2,1)} custom-call(s32[3]{0:T(128)S(1)} %pad_add_fusion.bits_ref, bf16[512,3072]{1,0:T(8,128)(2,1)} %self_backward.1.refs_0_.refs_1_, f32[512,1024]{1,0:T(8,128)} %get-tuple-element.76.refs_1_, bf16[2,4,32,1536]{3,2,1,0:T(8,128)(2,1)S(1)} %pad_maximum_fusion.12.refs_1_.refs_2_, ...), custom_call_target="tpu_custom_call" | custom-call | flops 3221225472 | bytes 5267456 | tf_op jit(solution)/shard_map/target_back/pallas_call | solution.py:486
  480.6 10.3 %weight_grad.13 = (bf16[2,2,4,128,1024]{4,3,2,1,0:T(8,128)(2,1)}, bf16[2,2,4,128,1024]{4,3,2,1,0:T(8,128)(2,1)}) custom-call(s32[3]{0:T(128)S(1)} %pad_add_fusion.bits_ref, bf16[512,4096]{1,0:T(8,128)(2,1)} %get-tuple-element.62.refs_0_, bf16[512,1024]{1,0:T(8,128)(2,1)S(1)} %copy-done.6), custom_call_target="tpu_custom_call" | custom-call | flops 4294967296 | bytes 9437184 | tf_op jit(solution)/shard_map/weight_grad/pallas_call | solution.py:765
  494.3 6.0 collective-permute-done.47
  504.7 3.4 collective-permute-done.48
  510.6 29.1 %collective-permute-done.50 = bf16[4,32,640]{2,1,0:T(8,128)(2,1)S(1)} collective-permute-done((bf16[4,32,640]{2,1,0:T(8,128)(2,1)S(1)}, bf16[4,32,640]{2,1,0:T(8,128)(2,1)S(1)}, u32[]{:S(2)}, u32[]{:S(2)}) %collective-permute-start.50) | collective-permute-done | bytes 163872 | tf_op jit(solution)/shard_map/ppermute | solution.py:356
  551.6 20.0 %collective-permute-done.52 = bf16[2,4,32,2048]{3,2,1,0:T(8,128)(2,1)S(1)} collective-permute-done((bf16[2,4,32,2048]{3,2,1,0:T(8,128)(2,1)S(1)}, bf16[2,4,32,2048]{3,2,1,0:T(8,128)(2,1)S(1)}, u32[]{:S(2)}, u32[]{:S(2)}) %collective-permute-start.52) | collective-permute-done | bytes 1048608 | tf_op jit(solution)/shard_map/ppermute | solution.py:356
  577.2 25.0 %collective-permute-done.53 = bf16[4,32,2048]{2,1,0:T(8,128)(2,1)S(1)} collective-permute-done((bf16[4,32,2048]{2,1,0:T(8,128)(2,1)S(1)}, bf16[4,32,2048]{2,1,0:T(8,128)(2,1)S(1)}, u32[]{:S(2)}, u32[]{:S(2)}) %collective-permute-start.53) | collective-permute-done | bytes 524320 | tf_op jit(solution)/shard_map/ppermute | solution.py:352
  609.3 7.4 collective-permute-done.55
  620.0 12.7 %collective-permute-done.59 = bf16[2,4,32,2048]{3,2,1,0:T(8,128)(2,1)S(1)} collective-permute-done((bf16[2,4,32,2048]{3,2,1,0:T(8,128)(2,1)S(1)}, bf16[2,4,32,2048]{3,2,1,0:T(8,128)(2,1)S(1)}, u32[]{:S(2)}, u32[]{:S(2)}) %collective-permute-start.59) | collective-permute-done | bytes 1048608 | tf_op jit(solution)/shard_map/ppermute | solution.py:352
  633.9 8.1 %collective-permute-done.58 = bf16[4,32,2048]{2,1,0:T(8,128)(2,1)} collective-permute-done((bf16[4,32,2048]{2,1,0:T(8,128)(2,1)}, bf16[4,32,2048]{2,1,0:T(8,128)(2,1)}, u32[]{:S(2)}, u32[]{:S(2)}) %collective-permute-start.58) | collective-permute-done | bytes 524320 | tf_op jit(solution)/shard_map/ppermute | solution.py:352
  650.8 12.1 %collective-permute-done.60 = bf16[4,32,2048]{2,1,0:T(8,128)(2,1)S(1)} collective-permute-done((bf16[4,32,2048]{2,1,0:T(8,128)(2,1)S(1)}, bf16[4,32,2048]{2,1,0:T(8,128)(2,1)S(1)}, u32[]{:S(2)}, u32[]{:S(2)}) %collective-permute-start.60) | collective-permute-done | bytes 524320 | tf_op jit(solution)/shard_map/ppermute | solution.py:356
  666.6 15.4 %collective-permute-done.62 = bf16[2,4,128,512]{3,2,1,0:T(8,128)(2,1)S(1)} collective-permute-done((bf16[2,4,128,512]{3,2,1,0:T(8,128)(2,1)S(1)}, bf16[2,4,128,512]{3,2,1,0:T(8,128)(2,1)S(1)}, u32[]{:S(2)}, u32[]{:S(2)}) %collective-permute-start.62) | collective-permute-done | bytes 1048608 | tf_op jit(solution)/shard_map/ppermute | solution.py:356
  688.5 6.1 collective-permute-done.63
  700.9 5.8 collective-permute-done.65
  715.7 7.4 collective-permute-start.45
  723.1 11.8 %collective-permute-start.44 = (bf16[32,3072]{1,0:T(8,128)(2,1)S(1)}, bf16[32,3072]{1,0:T(8,128)(2,1)S(1)}, u32[]{:S(2)}, u32[]{:S(2)}) collective-permute-start(bf16[32,3072]{1,0:T(8,128)(2,1)S(1)} %get-tuple-element.159), channel_id=1, source_target_pairs={{0,16},{2,18},{4,20},{6,22},{8,24},{10,26},{12,28},{14,30},{16,0},... | collective-permute-start | bytes 589832 | tf_op jit(solution)/shard_map/ppermute | solution.py:361
  736.0 24.1 %collective-permute-done.44 = bf16[32,3072]{1,0:T(8,128)(2,1)S(1)} collective-permute-done((bf16[32,3072]{1,0:T(8,128)(2,1)S(1)}, bf16[32,3072]{1,0:T(8,128)(2,1)S(1)}, u32[]{:S(2)}, u32[]{:S(2)}) %collective-permute-start.44) | collective-permute-done | bytes 196640 | tf_op jit(solution)/shard_map/ppermute | solution.py:361
  (340 shorter events, 164.6 us)
Async XLA Ops:
  7.2 48.4 %all-gather.6.cloned.1.call-start = ((), (), s32[]{:S(2)}) async-start(), calls=%async_computation.5 | async-start | bytes 1310720 | tf_op jit(solution)/shard_map/all_gather | solution.py:377
  9.1 76.6 %all-gather.4.cloned.1.call-start = ((), (), s32[]{:S(2)}) async-start(), calls=%async_computation.4 | async-start | bytes 1679360 | tf_op jit(solution)/shard_map/all_gather | solution.py:377
  10.2 25.4 %collective-permute-start.2 = (bf16[32,3072]{1,0:T(8,128)(2,1)S(1)}, bf16[32,3072]{1,0:T(8,128)(2,1)S(1)}, u32[]{:S(2)}, u32[]{:S(2)}) collective-permute-start(bf16[32,3072]{1,0:T(8,128)(2,1)S(1)} %convert_element_type.564), channel_id=1, source_target_pairs={{0,16},{2,18},{4,20},{6,22},{8,24},{10,26},{12,28},{14,30},{16,0},... | collective-permute-start | bytes 589832 | tf_op jit(solution)/shard_map/ppermute | solution.py:361
  20.0 94.2 %all-gather.8.cloned.1.call-start = ((), (), s32[]{:S(2)}) async-start(), calls=%async_computation.6 | async-start | bytes 1310720 | tf_op jit(solution)/shard_map/all_gather | solution.py:377
  45.6 74.3 %collective-permute-start.19 = (bf16[2,384,1024]{2,1,0:T(8,128)(2,1)}, bf16[2,384,1024]{2,1,0:T(8,128)(2,1)}, u32[]{:S(2)}, u32[]{:S(2)}) collective-permute-start(bf16[2,384,1024]{2,1,0:T(8,128)(2,1)} %get-tuple-element.144), channel_id=1, source_target_pairs={{0,1},{1,0},{2,3},{3,2},{4,5},{5,4},{6,7},{7,6},{8,9},{9,8},{10,11... | collective-permute-start | bytes 4718600 | tf_op jit(solution)/shard_map/ppermute | solution.py:356
  46.1 42.1 %collective-permute-start.20 = (s32[2,384]{1,0:T(2,128)S(1)}, s32[2,384]{1,0:T(2,128)S(1)}, u32[]{:S(2)}, u32[]{:S(2)}) collective-permute-start(s32[2,384]{1,0:T(2,128)S(1)} %get-tuple-element.174), channel_id=1, source_target_pairs={{0,1},{1,0},{2,3},{3,2},{4,5},{5,4},{6,7},{7,6},{8,9},{9,8},{10,11... | collective-permute-start | bytes 9224 | tf_op jit(solution)/shard_map/ppermute | solution.py:356
  48.4 663.7 %reduce-scatter.13.cloned.1.call-start = ((), (), s32[]{:S(2)}) async-start(), calls=%async_computation.10 | async-start | bytes 368640
  49.6 52.3 %collective-permute-start.4 = (bf16[2,4,32,1536]{3,2,1,0:T(8,128)(2,1)S(1)}, bf16[2,4,32,1536]{3,2,1,0:T(8,128)(2,1)}, u32[]{:S(2)}, u32[]{:S(2)}) collective-permute-start(bf16[2,4,32,1536]{3,2,1,0:T(8,128)(2,1)S(1)} %pad_maximum_fusion.12.refs_1_.refs_2_), channel_id=1, source_target_pairs={{0,1},{1,0},{2,3},{3,2},{4,5},{5,4},{6,7},{7,6},{8,9},{9,8},{10,11... | collective-permute-start | bytes 2359304 | tf_op jit(solution)/shard_map/ppermute | solution.py:356
  51.2 54.4 %collective-permute-start.5 = (bf16[2,4,32,1536]{3,2,1,0:T(8,128)(2,1)S(1)}, bf16[2,4,32,1536]{3,2,1,0:T(8,128)(2,1)S(1)}, u32[]{:S(2)}, u32[]{:S(2)}) collective-permute-start(bf16[2,4,32,1536]{3,2,1,0:T(8,128)(2,1)S(1)} %pad_maximum_fusion.12.refs_1_.refs_2_), channel_id=1, source_target_pairs={{0,2},{2,0},{4,6},{6,4},{8,10},{10,8},{12,14},{14,12},{16,18},{18,... | collective-permute-start | bytes 2359304 | tf_op jit(solution)/shard_map/ppermute | solution.py:347
  55.5 50.1 %collective-permute-start.8 = (bf16[2,4,32,1536]{3,2,1,0:T(8,128)(2,1)S(1)}, bf16[2,4,32,1536]{3,2,1,0:T(8,128)(2,1)}, u32[]{:S(2)}, u32[]{:S(2)}) collective-permute-start(bf16[2,4,32,1536]{3,2,1,0:T(8,128)(2,1)S(1)} %pad_maximum_fusion.13.refs_5_.refs_6_), channel_id=1, source_target_pairs={{0,4},{2,6},{4,0},{6,2},{8,12},{10,14},{12,8},{14,10},{16,20},{18,... | collective-permute-start | bytes 2359304 | tf_op jit(solution)/shard_map/ppermute | solution.py:352
  88.2 30.1 %collective-permute-start.9 = (bf16[2,4,32,1536]{3,2,1,0:T(8,128)(2,1)S(1)}, bf16[2,4,32,1536]{3,2,1,0:T(8,128)(2,1)}, u32[]{:S(2)}, u32[]{:S(2)}) collective-permute-start(bf16[2,4,32,1536]{3,2,1,0:T(8,128)(2,1)S(1)} %pad_maximum_fusion.13.refs_5_.refs_6_), channel_id=1, source_target_pairs={{0,2},{2,0},{4,6},{6,4},{8,10},{10,8},{12,14},{14,12},{16,18},{18,... | collective-permute-start | bytes 2359304 | tf_op jit(solution)/shard_map/ppermute | solution.py:347
  116.5 29.3 %collective-permute-start.6 = (bf16[2,4,32,1536]{3,2,1,0:T(8,128)(2,1)}, bf16[2,4,32,1536]{3,2,1,0:T(8,128)(2,1)S(1)}, u32[]{:S(2)}, u32[]{:S(2)}) collective-permute-start(bf16[2,4,32,1536]{3,2,1,0:T(8,128)(2,1)} %collective-permute-done.4.refs_2_.refs_3_), channel_id=1, source_target_pairs={{0,2},{2,0},{4,6},{6,4},{8,10},{10,8},{12,14},{14,12},{16,18},{18,... | collective-permute-start | bytes 2359304 | tf_op jit(solution)/shard_map/ppermute | solution.py:347
  121.3 46.3 %collective-permute-start.16 = (bf16[2,4,32,3072]{3,2,1,0:T(8,128)(2,1)S(1)}, bf16[2,4,32,3072]{3,2,1,0:T(8,128)(2,1)}, u32[]{:S(2)}, u32[]{:S(2)}) collective-permute-start(bf16[2,4,32,3072]{3,2,1,0:T(8,128)(2,1)S(1)} %pad_maximum_fusion.2.refs_3_.refs_2_.refs_8_.refs_1_), channel_id=1, source_target_pairs={{0,4},{2,6},{4,0},{6,2},{8,12},{10,14},{12,8},{14,10},{16,20},{18,... | collective-permute-start | bytes 4718600 | tf_op jit(solution)/shard_map/ppermute | solution.py:352
  134.6 57.2 %collective-permute-start.12 = (bf16[2,4,32,2176]{3,2,1,0:T(8,128)(2,1)S(1)}, bf16[2,4,32,2176]{3,2,1,0:T(8,128)(2,1)}, u32[]{:S(2)}, u32[]{:S(2)}) collective-permute-start(bf16[2,4,32,2176]{3,2,1,0:T(8,128)(2,1)S(1)} %pad_maximum_fusion.4.refs_0_.refs_7_.refs_3_.refs_12_.refs_4_), channel_id=1, source_target_pairs={{0,1},{1,0},{2,3},{3,2},{4,5},{5,4},{6,7},{7,6},{8,9},{9,8},{10,11... | collective-permute-start | bytes 3342344 | tf_op jit(solution)/shard_map/ppermute | solution.py:356
  144.3 46.0 %collective-permute-start.22 = (bf16[2,4,32,2048]{3,2,1,0:T(8,128)(2,1)}, bf16[2,4,32,2048]{3,2,1,0:T(8,128)(2,1)}, u32[]{:S(2)}, u32[]{:S(2)}) collective-permute-start(bf16[2,4,32,2048]{3,2,1,0:T(8,128)(2,1)} %pad_maximum_fusion.5.refs_1_.refs_4_), channel_id=1, source_target_pairs={{0,1},{1,0},{2,3},{3,2},{4,5},{5,4},{6,7},{7,6},{8,9},{9,8},{10,11... | collective-permute-start | bytes 3145736 | tf_op jit(solution)/shard_map/ppermute | solution.py:356
  145.8 46.0 %collective-permute-start.23 = (bf16[2,4,32,2048]{3,2,1,0:T(8,128)(2,1)}, bf16[2,4,32,2048]{3,2,1,0:T(8,128)(2,1)}, u32[]{:S(2)}, u32[]{:S(2)}) collective-permute-start(bf16[2,4,32,2048]{3,2,1,0:T(8,128)(2,1)} %pad_maximum_fusion.5.refs_1_.refs_4_), channel_id=1, source_target_pairs={{0,2},{2,0},{4,6},{6,4},{8,10},{10,8},{12,14},{14,12},{16,18},{18,... | collective-permute-start | bytes 3145736 | tf_op jit(solution)/shard_map/ppermute | solution.py:347
  147.6 69.2 %collective-permute-start.17 = (bf16[2,4,32,3072]{3,2,1,0:T(8,128)(2,1)S(1)}, bf16[2,4,32,3072]{3,2,1,0:T(8,128)(2,1)}, u32[]{:S(2)}, u32[]{:S(2)}) collective-permute-start(bf16[2,4,32,3072]{3,2,1,0:T(8,128)(2,1)S(1)} %pad_maximum_fusion.2.refs_3_.refs_2_.refs_8_.refs_1_), channel_id=1, source_target_pairs={{0,2},{2,0},{4,6},{6,4},{8,10},{10,8},{12,14},{14,12},{16,18},{18,... | collective-permute-start | bytes 4718600 | tf_op jit(solution)/shard_map/ppermute | solution.py:347
  167.6 67.2 %collective-permute-start.18 = (bf16[2,4,32,3072]{3,2,1,0:T(8,128)(2,1)}, bf16[2,4,32,3072]{3,2,1,0:T(8,128)(2,1)}, u32[]{:S(2)}, u32[]{:S(2)}) collective-permute-start(bf16[2,4,32,3072]{3,2,1,0:T(8,128)(2,1)} %collective-permute-done.16.refs_4_.refs_3_.refs_9_.refs_2_), channel_id=1, source_target_pairs={{0,2},{2,0},{4,6},{6,4},{8,10},{10,8},{12,14},{14,12},{16,18},{18,... | collective-permute-start | bytes 4718600 | tf_op jit(solution)/shard_map/ppermute | solution.py:347
  191.8 26.5 %collective-permute-start.14 = (bf16[2,4,32,2176]{3,2,1,0:T(8,128)(2,1)}, bf16[2,4,32,2176]{3,2,1,0:T(8,128)(2,1)}, u32[]{:S(2)}, u32[]{:S(2)}) collective-permute-start(bf16[2,4,32,2176]{3,2,1,0:T(8,128)(2,1)} %collective-permute-done.12.refs_1_.refs_8_.refs_4_.refs_13_.refs_5_), channel_id=1, source_target_pairs={{0,2},{2,0},{4,6},{6,4},{8,10},{10,8},{12,14},{14,12},{16,18},{18,... | collective-permute-start | bytes 3342344 | tf_op jit(solution)/shard_map/ppermute | solution.py:347
  215.3 43.0 %collective-permute-start.27 = (bf16[2,4,32,2048]{3,2,1,0:T(8,128)(2,1)}, bf16[2,4,32,2048]{3,2,1,0:T(8,128)(2,1)S(1)}, u32[]{:S(2)}, u32[]{:S(2)}) collective-permute-start(bf16[2,4,32,2048]{3,2,1,0:T(8,128)(2,1)} %pad_maximum_fusion.6.refs_5_.refs_8_), channel_id=1, source_target_pairs={{0,2},{2,0},{4,6},{6,4},{8,10},{10,8},{12,14},{14,12},{16,18},{18,... | collective-permute-start | bytes 3145736 | tf_op jit(solution)/shard_map/ppermute | solution.py:347
  215.3 43.1 %collective-permute-start.30 = (bf16[2,4,128,512]{3,2,1,0:T(8,128)(2,1)S(1)}, bf16[2,4,128,512]{3,2,1,0:T(8,128)(2,1)S(1)}, u32[]{:S(2)}, u32[]{:S(2)}) collective-permute-start(bf16[2,4,128,512]{3,2,1,0:T(8,128)(2,1)S(1)} %pad_maximum_fusion.7.refs_4_.refs_2_), channel_id=1, source_target_pairs={{0,1},{1,0},{2,3},{3,2},{4,5},{5,4},{6,7},{7,6},{8,9},{9,8},{10,11... | collective-permute-start | bytes 3145736 | tf_op jit(solution)/shard_map/ppermute | solution.py:356
  216.8 42.2 %collective-permute-start.34 = (bf16[2,4,128,512]{3,2,1,0:T(8,128)(2,1)S(1)}, bf16[2,4,128,512]{3,2,1,0:T(8,128)(2,1)}, u32[]{:S(2)}, u32[]{:S(2)}) collective-permute-start(bf16[2,4,128,512]{3,2,1,0:T(8,128)(2,1)S(1)} %pad_maximum_fusion.8.refs_8_.refs_6_), channel_id=1, source_target_pairs={{0,4},{2,6},{4,0},{6,2},{8,12},{10,14},{12,8},{14,10},{16,20},{18,... | collective-permute-start | bytes 3145736 | tf_op jit(solution)/shard_map/ppermute | solution.py:352
  218.3 40.8 %collective-permute-start.24 = (bf16[2,4,32,2048]{3,2,1,0:T(8,128)(2,1)}, bf16[2,4,32,2048]{3,2,1,0:T(8,128)(2,1)S(1)}, u32[]{:S(2)}, u32[]{:S(2)}) collective-permute-start(bf16[2,4,32,2048]{3,2,1,0:T(8,128)(2,1)} %collective-permute-done.22.refs_2_.refs_5_), channel_id=1, source_target_pairs={{0,2},{2,0},{4,6},{6,4},{8,10},{10,8},{12,14},{14,12},{16,18},{18,... | collective-permute-start | bytes 3145736 | tf_op jit(solution)/shard_map/ppermute | solution.py:347
  234.8 53.5 %collective-permute-start.28 = (bf16[2,4,32,2048]{3,2,1,0:T(8,128)(2,1)}, bf16[2,4,32,2048]{3,2,1,0:T(8,128)(2,1)S(1)}, u32[]{:S(2)}, u32[]{:S(2)}) collective-permute-start(bf16[2,4,32,2048]{3,2,1,0:T(8,128)(2,1)} %collective-permute-done.26.refs_6_.refs_9_), channel_id=1, source_target_pairs={{0,2},{2,0},{4,6},{6,4},{8,10},{10,8},{12,14},{14,12},{16,18},{18,... | collective-permute-start | bytes 3145736 | tf_op jit(solution)/shard_map/ppermute | solution.py:347
  258.4 46.8 %collective-permute-start.31 = (bf16[2,4,128,512]{3,2,1,0:T(8,128)(2,1)S(1)}, bf16[2,4,128,512]{3,2,1,0:T(8,128)(2,1)}, u32[]{:S(2)}, u32[]{:S(2)}) collective-permute-start(bf16[2,4,128,512]{3,2,1,0:T(8,128)(2,1)S(1)} %pad_maximum_fusion.7.refs_4_.refs_2_), channel_id=1, source_target_pairs={{0,2},{2,0},{4,6},{6,4},{8,10},{10,8},{12,14},{14,12},{16,18},{18,... | collective-permute-start | bytes 3145736 | tf_op jit(solution)/shard_map/ppermute | solution.py:347
  258.5 46.7 %collective-permute-start.35 = (bf16[2,4,128,512]{3,2,1,0:T(8,128)(2,1)S(1)}, bf16[2,4,128,512]{3,2,1,0:T(8,128)(2,1)}, u32[]{:S(2)}, u32[]{:S(2)}) collective-permute-start(bf16[2,4,128,512]{3,2,1,0:T(8,128)(2,1)S(1)} %pad_maximum_fusion.8.refs_8_.refs_6_), channel_id=1, source_target_pairs={{0,2},{2,0},{4,6},{6,4},{8,10},{10,8},{12,14},{14,12},{16,18},{18,... | collective-permute-start | bytes 3145736 | tf_op jit(solution)/shard_map/ppermute | solution.py:347
  259.0 46.1 %collective-permute-start.32 = (bf16[2,4,128,512]{3,2,1,0:T(8,128)(2,1)S(1)}, bf16[2,4,128,512]{3,2,1,0:T(8,128)(2,1)}, u32[]{:S(2)}, u32[]{:S(2)}) collective-permute-start(bf16[2,4,128,512]{3,2,1,0:T(8,128)(2,1)S(1)} %collective-permute-done.30.refs_5_.refs_3_), channel_id=1, source_target_pairs={{0,2},{2,0},{4,6},{6,4},{8,10},{10,8},{12,14},{14,12},{16,18},{18,... | collective-permute-start | bytes 3145736 | tf_op jit(solution)/shard_map/ppermute | solution.py:347
  259.1 46.1 %collective-permute-start.36 = (bf16[2,4,128,512]{3,2,1,0:T(8,128)(2,1)}, bf16[2,4,128,512]{3,2,1,0:T(8,128)(2,1)}, u32[]{:S(2)}, u32[]{:S(2)}) collective-permute-start(bf16[2,4,128,512]{3,2,1,0:T(8,128)(2,1)} %collective-permute-done.34.refs_9_.refs_7_), channel_id=1, source_target_pairs={{0,2},{2,0},{4,6},{6,4},{8,10},{10,8},{12,14},{14,12},{16,18},{18,... | collective-permute-start | bytes 3145736 | tf_op jit(solution)/shard_map/ppermute | solution.py:347
  423.4 118.1 %collective-permute-start.38 = (bf16[2,2,4,32,3072]{4,3,2,1,0:T(8,128)(2,1)}, bf16[2,2,4,32,3072]{4,3,2,1,0:T(8,128)(2,1)}, u32[]{:S(2)}, u32[]{:S(2)}) collective-permute-start(bf16[2,2,4,32,3072]{4,3,2,1,0:T(8,128)(2,1)} %get-tuple-element.79), channel_id=1, source_target_pairs={{0,2},{2,0},{4,6},{6,4},{8,10},{10,8},{12,14},{14,12},{16,18},{18,... | collective-permute-start | bytes 9437192 | tf_op jit(solution)/shard_map/ppermute | solution.py:347
  454.7 89.5 %collective-permute-start.51 = (bf16[2,2,4,32,4096]{4,3,2,1,0:T(8,128)(2,1)}, bf16[2,2,4,32,4096]{4,3,2,1,0:T(8,128)(2,1)}, u32[]{:S(2)}, u32[]{:S(2)}) collective-permute-start(bf16[2,2,4,32,4096]{4,3,2,1,0:T(8,128)(2,1)} %pad_maximum_fusion), channel_id=1, source_target_pairs={{0,2},{2,0},{4,6},{6,4},{8,10},{10,8},{12,14},{14,12},{16,18},{18,... | collective-permute-start | bytes 12582920 | tf_op jit(solution)/shard_map/ppermute | solution.py:347
  456.2 34.6 %collective-permute-start.46 = (bf16[2,2,4,32,1152]{4,3,2,1,0:T(8,128)(2,1)}, bf16[2,2,4,32,1152]{4,3,2,1,0:T(8,128)(2,1)}, u32[]{:S(2)}, u32[]{:S(2)}) collective-permute-start(bf16[2,2,4,32,1152]{4,3,2,1,0:T(8,128)(2,1)} %pad_maximum_fusion.3), channel_id=1, source_target_pairs={{0,2},{2,0},{4,6},{6,4},{8,10},{10,8},{12,14},{14,12},{16,18},{18,... | collective-permute-start | bytes 3538952 | tf_op jit(solution)/shard_map/ppermute | solution.py:347
  456.3 117.1 %collective-permute-start.56 = (bf16[2,2,4,32,4096]{4,3,2,1,0:T(8,128)(2,1)}, bf16[2,2,4,32,4096]{4,3,2,1,0:T(8,128)(2,1)}, u32[]{:S(2)}, u32[]{:S(2)}) collective-permute-start(bf16[2,2,4,32,4096]{4,3,2,1,0:T(8,128)(2,1)} %get-tuple-element.95), channel_id=1, source_target_pairs={{0,2},{2,0},{4,6},{6,4},{8,10},{10,8},{12,14},{14,12},{16,18},{18,... | collective-permute-start | bytes 12582920 | tf_op jit(solution)/shard_map/ppermute | solution.py:347
  500.3 186.3 %collective-permute-start.37 = (bf16[2,384,1024]{2,1,0:T(8,128)(2,1)}, bf16[2,384,1024]{2,1,0:T(8,128)(2,1)}, u32[]{:S(2)}, u32[]{:S(2)}) collective-permute-start(bf16[2,384,1024]{2,1,0:T(8,128)(2,1)} %bitcast.40), channel_id=1, source_target_pairs={{0,1},{1,0},{2,3},{3,2},{4,5},{5,4},{6,7},{7,6},{8,9},{9,8},{10,11... | collective-permute-start | bytes 4718600 | tf_op jit(solution)/shard_map/ppermute | solution.py:356
  508.1 31.6 %collective-permute-start.50 = (bf16[4,32,640]{2,1,0:T(8,128)(2,1)S(1)}, bf16[4,32,640]{2,1,0:T(8,128)(2,1)S(1)}, u32[]{:S(2)}, u32[]{:S(2)}) collective-permute-start(bf16[4,32,640]{2,1,0:T(8,128)(2,1)S(1)} %fusion.36), channel_id=1, source_target_pairs={{0,1},{1,0},{2,3},{3,2},{4,5},{5,4},{6,7},{7,6},{8,9},{9,8},{10,11... | collective-permute-start | bytes 491528 | tf_op jit(solution)/shard_map/ppermute | solution.py:356
  539.7 105.5 %collective-permute-start.61 = (bf16[2,2,4,128,1024]{4,3,2,1,0:T(8,128)(2,1)}, bf16[2,2,4,128,1024]{4,3,2,1,0:T(8,128)(2,1)}, u32[]{:S(2)}, u32[]{:S(2)}) collective-permute-start(bf16[2,2,4,128,1024]{4,3,2,1,0:T(8,128)(2,1)} %get-tuple-element.97), channel_id=1, source_target_pairs={{0,2},{2,0},{4,6},{6,4},{8,10},{10,8},{12,14},{14,12},{16,18},{18,... | collective-permute-start | bytes 12582920 | tf_op jit(solution)/shard_map/ppermute | solution.py:347
  541.5 219.5 %reduce-scatter.7.cloned.1.call-start = ((), (), s32[]{:S(2)}) async-start(), calls=%async_computation.7 | async-start | bytes 1310720 | tf_op jit(solution)/shard_map/reduce_scatter | solution.py:815
  545.9 25.6 %collective-permute-start.52 = (bf16[2,4,32,2048]{3,2,1,0:T(8,128)(2,1)S(1)}, bf16[2,4,32,2048]{3,2,1,0:T(8,128)(2,1)S(1)}, u32[]{:S(2)}, u32[]{:S(2)}) collective-permute-start(bf16[2,4,32,2048]{3,2,1,0:T(8,128)(2,1)S(1)} %fusion.1), channel_id=1, source_target_pairs={{0,1},{1,0},{2,3},{3,2},{4,5},{5,4},{6,7},{7,6},{8,9},{9,8},{10,11... | collective-permute-start | bytes 3145736 | tf_op jit(solution)/shard_map/ppermute | solution.py:356
  548.2 28.4 %collective-permute-start.54 = (bf16[2,4,32,2048]{3,2,1,0:T(8,128)(2,1)S(1)}, bf16[2,4,32,2048]{3,2,1,0:T(8,128)(2,1)S(1)}, u32[]{:S(2)}, u32[]{:S(2)}) collective-permute-start(bf16[2,4,32,2048]{3,2,1,0:T(8,128)(2,1)S(1)} %fusion.2), channel_id=1, source_target_pairs={{0,4},{2,6},{4,0},{6,2},{8,12},{10,14},{12,8},{14,10},{16,20},{18,... | collective-permute-start | bytes 3145736 | tf_op jit(solution)/shard_map/ppermute | solution.py:352
  571.6 112.9 %collective-permute-start.41 = (bf16[2,4,32,1536]{3,2,1,0:T(8,128)(2,1)}, bf16[2,4,32,1536]{3,2,1,0:T(8,128)(2,1)}, u32[]{:S(2)}, u32[]{:S(2)}) collective-permute-start(bf16[2,4,32,1536]{3,2,1,0:T(8,128)(2,1)} %fusion.26), channel_id=1, source_target_pairs={{0,4},{2,6},{4,0},{6,2},{8,12},{10,14},{12,8},{14,10},{16,20},{18,... | collective-permute-start | bytes 2359304 | tf_op jit(solution)/shard_map/ppermute | solution.py:352
  573.4 28.7 %collective-permute-start.53 = (bf16[4,32,2048]{2,1,0:T(8,128)(2,1)S(1)}, bf16[4,32,2048]{2,1,0:T(8,128)(2,1)S(1)}, u32[]{:S(2)}, u32[]{:S(2)}) collective-permute-start(bf16[4,32,2048]{2,1,0:T(8,128)(2,1)S(1)} %fusion.22), channel_id=1, source_target_pairs={{0,4},{2,6},{4,0},{6,2},{8,12},{10,14},{12,8},{14,10},{16,20},{18,... | collective-permute-start | bytes 1572872 | tf_op jit(solution)/shard_map/ppermute | solution.py:352
  576.6 30.0 %collective-permute-start.57 = (bf16[2,4,32,2048]{3,2,1,0:T(8,128)(2,1)S(1)}, bf16[2,4,32,2048]{3,2,1,0:T(8,128)(2,1)S(1)}, u32[]{:S(2)}, u32[]{:S(2)}) collective-permute-start(bf16[2,4,32,2048]{3,2,1,0:T(8,128)(2,1)S(1)} %fusion.3), channel_id=1, source_target_pairs={{0,1},{1,0},{2,3},{3,2},{4,5},{5,4},{6,7},{7,6},{8,9},{9,8},{10,11... | collective-permute-start | bytes 3145736 | tf_op jit(solution)/shard_map/ppermute | solution.py:356
  606.6 26.2 %collective-permute-start.59 = (bf16[2,4,32,2048]{3,2,1,0:T(8,128)(2,1)S(1)}, bf16[2,4,32,2048]{3,2,1,0:T(8,128)(2,1)S(1)}, u32[]{:S(2)}, u32[]{:S(2)}) collective-permute-start(bf16[2,4,32,2048]{3,2,1,0:T(8,128)(2,1)S(1)} %fusion.4), channel_id=1, source_target_pairs={{0,4},{2,6},{4,0},{6,2},{8,12},{10,14},{12,8},{14,10},{16,20},{18,... | collective-permute-start | bytes 3145736 | tf_op jit(solution)/shard_map/ppermute | solution.py:352
  620.0 142.6 %reduce-scatter.9.cloned.1.call-start = ((), (), s32[]{:S(2)}) async-start(), calls=%async_computation.8 | async-start | bytes 1310720 | tf_op jit(solution)/shard_map/reduce_scatter | solution.py:815
  632.8 64.5 %collective-permute-start.39 = (bf16[2,4,32,1536]{3,2,1,0:T(8,128)(2,1)}, bf16[2,4,32,1536]{3,2,1,0:T(8,128)(2,1)}, u32[]{:S(2)}, u32[]{:S(2)}) collective-permute-start(bf16[2,4,32,1536]{3,2,1,0:T(8,128)(2,1)} %fusion.25), channel_id=1, source_target_pairs={{0,1},{1,0},{2,3},{3,2},{4,5},{5,4},{6,7},{7,6},{8,9},{9,8},{10,11... | collective-permute-start | bytes 2359304 | tf_op jit(solution)/shard_map/ppermute | solution.py:356
  646.9 35.2 %collective-permute-start.62 = (bf16[2,4,128,512]{3,2,1,0:T(8,128)(2,1)S(1)}, bf16[2,4,128,512]{3,2,1,0:T(8,128)(2,1)S(1)}, u32[]{:S(2)}, u32[]{:S(2)}) collective-permute-start(bf16[2,4,128,512]{3,2,1,0:T(8,128)(2,1)S(1)} %fusion.5), channel_id=1, source_target_pairs={{0,1},{1,0},{2,3},{3,2},{4,5},{5,4},{6,7},{7,6},{8,9},{9,8},{10,11... | collective-permute-start | bytes 3145736 | tf_op jit(solution)/shard_map/ppermute | solution.py:356
  662.9 25.6 %collective-permute-start.64 = (bf16[2,4,128,512]{3,2,1,0:T(8,128)(2,1)}, bf16[2,4,128,512]{3,2,1,0:T(8,128)(2,1)}, u32[]{:S(2)}, u32[]{:S(2)}) collective-permute-start(bf16[2,4,128,512]{3,2,1,0:T(8,128)(2,1)} %fusion.6), channel_id=1, source_target_pairs={{0,4},{2,6},{4,0},{6,2},{8,12},{10,14},{12,8},{14,10},{16,20},{18,... | collective-permute-start | bytes 3145736 | tf_op jit(solution)/shard_map/ppermute | solution.py:352
  666.1 99.8 %reduce-scatter.11.cloned.1.call-start = ((), (), s32[]{:S(2)}) async-start(), calls=%async_computation.9 | async-start | bytes 1310720 | tf_op jit(solution)/shard_map/reduce_scatter | solution.py:815
  723.1 37.0 %collective-permute-start.44 = (bf16[32,3072]{1,0:T(8,128)(2,1)S(1)}, bf16[32,3072]{1,0:T(8,128)(2,1)S(1)}, u32[]{:S(2)}, u32[]{:S(2)}) collective-permute-start(bf16[32,3072]{1,0:T(8,128)(2,1)S(1)} %get-tuple-element.159), channel_id=1, source_target_pairs={{0,16},{2,18},{4,20},{6,22},{8,24},{10,26},{12,28},{14,30},{16,0},... | collective-permute-start | bytes 589832 | tf_op jit(solution)/shard_map/ppermute | solution.py:361
  (81 other events, 1225.0 us)
Sparse Core Ops, SparseCore 0:
  10.2 38.8 all-gather.5
  51.2 34.4 all-gather.3
  87.3 26.8 all-gather.7
  541.6 35.5 reduce-scatter.12
  620.1 43.1 reduce-scatter.6
  666.2 42.9 reduce-scatter.8
  711.5 47.2 reduce-scatter.10

commit v2 on v1

v2 whole, which is shorter than its diff:
```python
import math

import jax
import jax.numpy as jnp
from jax import lax
from jax.experimental import pallas as pl
from jax.experimental.pallas import tpu as pltpu
from jax.sharding import PartitionSpec as P

HD = 64
LANES = 128
ALPHA = 300.0**0.25
NEG_LARGE = -1e30
EPSILON = 1e-05
VMEM_BYTES = 62 * 1024 * 1024
SCALE = HD**-0.5
BF16 = jnp.bfloat16
F32 = jnp.float32


def plain_dot(first_op, second_op):
    return jnp.dot(first_op, second_op, preferred_element_type=F32)


def lead_dot(first_op, second_op):
    return lax.dot_general(
        first_op, second_op, (((0,), (0,)), ((), ())), preferred_element_type=F32
    )


def back_dot(first_op, second_op):
    return lax.dot_general(
        first_op, second_op, (((1,), (1,)), ((), ())), preferred_element_type=F32
    )


def pick_entry(values, wanted):
    return jnp.sum(jnp.where(jnp.arange(values.shape[0]) == wanted, values, 0))


def kernel_params():
    return pltpu.CompilerParams(vmem_limit_bytes=VMEM_BYTES)


class Order:
    def __init__(self):
        self.last, self.due, self.parted = None, [], False

    def before(self, *arrays):
        self.due += arrays

    def part(self):
        self.parted = True

    def launch(self, kernel, name, operands, in_specs, out_specs, out_shape, scratch, grid, aliases):
        ties = self.due + ([self.last] if self.last is not None else [])
        ties = [tie for tie in ties if not any(tie is operand for operand in operands)]
        self.due = []
        count, n_ties = len(operands), len(ties)

        def tied(*refs):
            kernel(*refs[:count], *refs[count + n_ties :])

        specs = list(in_specs) + [pl.BlockSpec(memory_space=pltpu.HBM)] * n_ties
        cost = pl.CostEstimate(
            flops=10**12 if self.parted else 10**6, bytes_accessed=1, transcendentals=0
        )
        self.parted = False
        if grid is None:
            run = pl.pallas_call(
                tied,
                in_specs=[pl.BlockSpec(memory_space=pltpu.SMEM)] + specs,
                out_specs=out_specs,
                out_shape=out_shape,
                scratch_shapes=scratch,
                input_output_aliases=aliases,
                compiler_params=kernel_params(),
                cost_estimate=cost,
                name=name,
            )
        else:
            run = pl.pallas_call(
                tied,
                grid_spec=pltpu.PrefetchScalarGridSpec(
                    num_scalar_prefetch=1,
                    grid=grid,
                    in_specs=specs,
                    out_specs=out_specs,
                    scratch_shapes=scratch,
                ),
                out_shape=out_shape,
                input_output_aliases=aliases,
                compiler_params=kernel_params(),
                cost_estimate=cost,
                name=name,
            )
        results = run(*operands, *ties)
        self.last = results[0]
        return results


def whole_spec(shape):
    return pl.BlockSpec(shape, lambda *_: (0,) * len(shape))


def head_lanes(rows, head):
    lane = lax.broadcasted_iota(jnp.int32, (rows, LANES), 1)
    return (lane < HD) if head == 0 else (lane >= HD)


def visible(query_ids, key_ids, slot_len, first_len, second_len):
    query_slot = (query_ids >= slot_len).astype(jnp.int32)
    key_slot = (key_ids >= slot_len).astype(jnp.int32)
    place = key_ids - key_slot * slot_len
    limit = jnp.where(key_slot == 0, first_len, second_len)
    return (query_slot == key_slot) & (key_ids <= query_ids) & (place < limit)


def pair_forward(query, keys, values, bias):
    rows, key_rows = query.shape[0], keys.shape[0]
    mixed, peaks = [], []
    for head in range(2):
        mine = head_lanes(rows, head)
        masked = jnp.where(mine, query * BF16(SCALE), BF16(0))
        scores = back_dot(masked, keys) + bias
        peak = jnp.max(scores, axis=1, keepdims=True)
        raised = jnp.exp(scores - peak).astype(BF16)
        widened = jnp.where(head_lanes(key_rows, head), values, BF16(1))
        mixed.append(plain_dot(raised, widened))
        peaks.append(peak)
    first = head_lanes(rows, 0)
    totals = pltpu.roll(jnp.where(first, mixed[1], mixed[0]), HD, 1)
    joined = jnp.where(first, mixed[0], mixed[1])
    log_totals = jnp.where(first, peaks[0], peaks[1]) + jnp.log(totals)
    return joined / totals, log_totals


def pair_backward(query, keys, values, upstream, bias, log_rows, delta_rows):
    rows, key_rows = query.shape[0], keys.shape[0]
    grad_q, grad_k, grad_v = None, None, None
    for head in range(2):
        mine = head_lanes(rows, head)
        masked = jnp.where(mine, query * BF16(SCALE), BF16(0))
        masked_up = jnp.where(mine, upstream, BF16(0))
        scores = back_dot(keys, masked) + bias
        probs = jnp.exp(scores - log_rows[head])
        grad_probs = back_dot(values, masked_up)
        grad_scores = (probs * (grad_probs - delta_rows[head])).astype(BF16)
        part_v = plain_dot(probs.astype(BF16), masked_up)
        part_k = plain_dot(grad_scores, masked)
        masked_keys = jnp.where(head_lanes(key_rows, head), keys, BF16(0))
        part_q = lead_dot(grad_scores, masked_keys)
        grad_q = part_q if grad_q is None else grad_q + part_q
        grad_k = part_k if grad_k is None else grad_k + part_k
        grad_v = part_v if grad_v is None else grad_v + part_v
    return grad_q * SCALE, grad_k, grad_v


def stat_rows(log_block, mixed, upstream):
    log_turned = log_block.T
    products = (mixed.astype(F32) * upstream.astype(F32)).T
    log_rows = [log_turned[:1], log_turned[HD : HD + 1]]
    delta_rows = [jnp.sum(products[h * HD : (h + 1) * HD], axis=0, keepdims=True) for h in range(2)]
    return log_rows, delta_rows


def self_forward_kernel(meta, q_ref, k_ref, v_ref, mixed_ref, log_ref, bias):
    rows = q_ref.shape[0]

    @pl.when(pl.program_id(0) == 0)
    def _():
        query_ids = lax.broadcasted_iota(jnp.int32, (rows, rows), 0)
        key_ids = lax.broadcasted_iota(jnp.int32, (rows, rows), 1)
        seen = visible(query_ids, key_ids, meta[0], meta[1], meta[2])
        bias[...] = jnp.where(seen, 0.0, NEG_LARGE)

    half = rows // 2
    for start, stop in ((0, half), (half, rows)):
        mixed, log_totals = pair_forward(
            q_ref[start:stop, :], k_ref[:stop, :], v_ref[:stop, :], bias[start:stop, :stop]
        )
        mixed_ref[start:stop, :] = mixed.astype(BF16)
        log_ref[start:stop, :] = log_totals


def self_forward(order, meta, united):
    rows, width = united.shape[0], united.shape[1] // 3
    pairs = width // LANES
    spec = lambda third: pl.BlockSpec((rows, LANES), lambda i, _: (0, third * pairs + i))
    return order.launch(
        self_forward_kernel,
        "self_forward",
        [meta, united, united, united],
        [spec(0), spec(1), spec(2)],
        [spec(0), spec(0)],
        [jax.ShapeDtypeStruct((rows, width), kind) for kind in (BF16, F32)],
        [pltpu.VMEM((rows, rows), F32)],
        (pairs,),
        {},
    )


def self_backward_kernel(
    meta, q_ref, k_ref, v_ref, mixed_ref, up_ref, log_ref, grad_ref, bias
):
    rows = q_ref.shape[0]
    width = grad_ref.shape[1] // 3
    pair = pl.program_id(0)

    @pl.when(pair == 0)
    def _():
        key_ids = lax.broadcasted_iota(jnp.int32, (rows, rows), 0)
        query_ids = lax.broadcasted_iota(jnp.int32, (rows, rows), 1)
        seen = visible(query_ids, key_ids, meta[0], meta[1], meta[2])
        bias[...] = jnp.where(seen, 0.0, NEG_LARGE)

    log_rows, delta_rows = stat_rows(log_ref[...], mixed_ref[...], up_ref[...])
    half = rows // 2
    parts = []
    for start, stop in ((0, half), (half, rows)):
        parts.append(
            pair_backward(
                q_ref[start:stop, :],
                k_ref[:stop, :],
                v_ref[:stop, :],
                up_ref[start:stop, :],
                bias[:stop, start:stop],
                [row[:, start:stop] for row in log_rows],
                [row[:, start:stop] for row in delta_rows],
            )
        )
    low, high = parts
    columns = lambda third: pl.ds(pl.multiple_of(third * width + pair * LANES, LANES), LANES)
    grad_ref[:half, columns(0)] = low[0].astype(BF16)
    grad_ref[half:, columns(0)] = high[0].astype(BF16)
    for third in (1, 2):
        grad_ref[:half, columns(third)] = (low[third] + high[third][:half]).astype(BF16)
        grad_ref[half:, columns(third)] = high[third][half:].astype(BF16)


def self_backward(order, meta, united, mixed, upstream, log_totals, first, pairs):
    rows, width = mixed.shape
    third = width // LANES
    spec = lambda at: pl.BlockSpec((rows, LANES), lambda i, _: (0, at * third + first + i))
    shape = (rows, 3 * pairs * LANES)
    return order.launch(
        self_backward_kernel,
        "self_backward",
        [meta, united, united, united, mixed, upstream, log_totals],
        [spec(0), spec(1), spec(2), spec(0), spec(0), spec(0)],
        [whole_spec(shape)],
        [jax.ShapeDtypeStruct(shape, BF16)],
        [pltpu.VMEM((rows, rows), F32)],
        (pairs,),
        {},
    )[0]


def join_keys(near_ref, far_ref, joined):
    slots, piece = near_ref.shape[0], near_ref.shape[1]
    for slot in range(slots):
        joined[slot, :piece, :] = near_ref[slot]
        joined[slot, piece:, :] = far_ref[slot]


def cross_forward_kernel(
    meta, q_ref, kn_ref, vn_ref, kf_ref, vf_ref, bias_ref, mixed_ref, log_ref, keys, values
):
    half = q_ref.shape[0] // 2
    join_keys(kn_ref, kf_ref, keys)
    join_keys(vn_ref, vf_ref, values)
    for part in range(2):
        slot = part * meta[0]
        rows = slice(part * half, (part + 1) * half)
        mixed, log_totals = pair_forward(q_ref[rows, :], keys[slot], values[slot], bias_ref[slot])
        mixed_ref[rows, :] = mixed.astype(BF16)
        log_ref[rows, :] = log_totals


def cross_specs(rows, slots, piece, pairs):
    row_spec = pl.BlockSpec((rows, LANES), lambda i, _: (0, i))
    half = lambda at: pl.BlockSpec((slots, piece, LANES), lambda i, _: (0, 0, at * pairs + i))
    return row_spec, [row_spec, half(0), half(1), half(0), half(1)]


def cross_forward(order, meta, query, near, far, bias):
    rows, width = query.shape
    slots, piece = near.shape[0], near.shape[1]
    pairs = width // LANES
    row_spec, specs = cross_specs(rows, slots, piece, pairs)
    return order.launch(
        cross_forward_kernel,
        "cross_forward",
        [meta, query, near, near, far, far, bias],
        specs + [whole_spec(bias.shape)],
        [row_spec, row_spec],
        [jax.ShapeDtypeStruct((rows, width), kind) for kind in (BF16, F32)],
        [pltpu.VMEM((slots, 2 * piece, LANES), BF16)] * 2,
        (pairs,),
        {},
    )


def cross_backward_kernel(
    meta,
    q_ref,
    kn_ref,
    vn_ref,
    kf_ref,
    vf_ref,
    bias_ref,
    mixed_ref,
    up_ref,
    log_ref,
    grad_q_ref,
    grad_near_ref,
    grad_far_ref,
    keys,
    values,
):
    half = q_ref.shape[0] // 2
    slots, piece = kn_ref.shape[0], kn_ref.shape[1]
    width = grad_near_ref.shape[1] // 2
    join_keys(kn_ref, kf_ref, keys)
    join_keys(vn_ref, vf_ref, values)
    log_rows, delta_rows = stat_rows(log_ref[...], mixed_ref[...], up_ref[...])
    parts = []
    for part in range(2):
        slot = part * meta[0]
        rows = slice(part * half, (part + 1) * half)
        bias_column = bias_ref[slot]
        grads = pair_backward(
            q_ref[rows, :],
            keys[slot],
            values[slot],
            up_ref[rows, :],
            jnp.concatenate([bias_column] * (half // LANES), axis=1),
            [row[:, rows] for row in log_rows],
            [row[:, rows] for row in delta_rows],
        )
        grad_q_ref[rows, :] = grads[0].astype(BF16)
        parts.append(grads)
    split = meta[0].astype(F32)
    start = pl.program_id(0) * LANES
    for which in range(2):
        early, late = parts[0][1 + which], parts[1][1 + which]
        columns = pl.ds(pl.multiple_of(which * width + start, LANES), LANES)
        by_slot = (early + late * (1.0 - split), late * split)
        for slot in range(slots):
            for source, target in enumerate((grad_near_ref, grad_far_ref)):
                target[slot * piece : (slot + 1) * piece, columns] = by_slot[slot][
                    source * piece : (source + 1) * piece
                ].astype(BF16)


def cross_backward(order, meta, query, near, far, bias, mixed, upstream, log_totals):
    rows, width = query.shape
    slots, piece = near.shape[0], near.shape[1]
    pairs = width // LANES
    memory = (slots * piece, 2 * width)
    row_spec, specs = cross_specs(rows, slots, piece, pairs)
    return order.launch(
        cross_backward_kernel,
        "cross_backward",
        [meta, query, near, near, far, far, bias, mixed, upstream, log_totals],
        specs + [whole_spec(bias.shape)] + [row_spec] * 3,
        [row_spec, whole_spec(memory), whole_spec(memory)],
        [jax.ShapeDtypeStruct(shape, BF16) for shape in ((rows, width), memory, memory)],
        [pltpu.VMEM((slots, 2 * piece, LANES), BF16)] * 2,
        (pairs,),
        {},
    )


def swap_core(values):
    size = lax.axis_size("dp")
    return lax.ppermute(values, "dp", [(i, i ^ 1) for i in range(size)])


def swap_next(values):
    size = lax.axis_size("dp")
    return lax.ppermute(values, "dp", [(i, i ^ 2) for i in range(size)])


def swap_mem(values):
    return lax.ppermute(values, "mem", [(0, 1), (1, 0)])


def swap_outer(values, far):
    size = lax.axis_size("dp")
    return lax.ppermute(values, "dp", [(i, i ^ (4 * far)) for i in range(size)])


def outer_groups():
    size = lax.axis_size("dp")
    return [list(range(base, size, 4)) for base in range(4)]


def place_bits():
    dp, mem = lax.axis_index("dp"), lax.axis_index("mem")
    return jnp.stack([(dp >> 1) & 1, dp & 1, mem]).astype(jnp.int32)


def outer_gather(shard, direct):
    outer, rows = lax.axis_size("dp") // 4, shard.shape[0]
    if not direct:
        stacked = lax.all_gather(shard, "dp", axis_index_groups=outer_groups(), axis=0, tiled=True)
        return stacked.reshape(outer, rows, -1)
    place = lax.axis_index("dp") >> 2
    blocks = jnp.stack([shard] + [swap_outer(shard, far) for far in range(1, outer)])
    bit = 1
    while bit < outer:
        turned = jnp.stack([blocks[i ^ bit] for i in range(outer)])
        blocks = jnp.where((place & bit) != 0, turned, blocks)
        bit *= 2
    return blocks


FIRST = (swap_next, swap_mem)
SECOND = (swap_mem, swap_next)


def gate(order, bits, arrays):
    def kernel(*refs):
        pass

    return order.launch(
        kernel,
        "gate",
        [bits, *arrays],
        [pl.BlockSpec(memory_space=pltpu.HBM)] * len(arrays),
        [pl.BlockSpec(memory_space=pltpu.HBM)] * len(arrays),
        [jax.ShapeDtypeStruct(array.shape, array.dtype) for array in arrays],
        [],
        None,
        {1 + i: i for i in range(len(arrays))},
    )


class Moves:
    def __init__(self, order, bits):
        self.order, self.bits = order, bits
        self.sources, self.shapes, self.moves, self.aliases, self.then = [], [], [], {}, []

    def source(self, array):
        self.sources.append(array)
        return len(self.sources) - 1

    def target(self, shape, held=None):
        self.shapes.append(shape)
        if held is not None:
            self.aliases[1 + self.source(held)] = len(self.shapes) - 1
        return len(self.shapes) - 1

    def move(self, source, source_at, shape, *goals):
        self.moves.append((source, source_at, shape, goals))

    def run(self):
        moves, n_in, n_out = self.moves, len(self.sources), len(self.shapes)
        most = max(len(move[3]) for move in moves)

        def kernel(bits_ref, *refs):
            bits = [bits_ref[i] for i in range(3)]
            taken, given = refs[:n_in], refs[n_in : n_in + n_out]
            slots, sems = refs[n_in + n_out : -1], refs[-1]
            loads, stores = [], []
            for number, (source, source_at, _, goals) in enumerate(moves):
                slot = slots[number]
                loads.append(
                    pltpu.make_async_copy(taken[source].at[source_at], slot, sems.at[0, number])
                )
                stores.append(
                    [
                        pltpu.make_async_copy(
                            slot, given[which].at[at(bits) if callable(at) else at], sems.at[1 + i, number]
                        )
                        for i, (which, at) in enumerate(goals)
                    ]
                )
            for load in loads:
                load.start()
            for load, group in zip(loads, stores):
                load.wait()
                for store in group:
                    store.start()
            for group in stores:
                for store in group:
                    store.wait()

        filled = self.order.launch(
            kernel,
            "move_blocks",
            [self.bits, *self.sources],
            [pl.BlockSpec(memory_space=pltpu.HBM)] * n_in,
            [pl.BlockSpec(memory_space=pltpu.HBM)] * n_out,
            [jax.ShapeDtypeStruct(shape, BF16) for shape in self.shapes],
            [pltpu.VMEM(shape, BF16) for _, _, shape, _ in moves]
            + [pltpu.SemaphoreType.DMA((1 + most, len(moves)))],
            None,
            self.aliases,
        )
        for step in self.then:
            step(filled)


def cast_shards(order, bits, groups):
    shapes = [(group[0].shape[0], sum(part.shape[1] for part in group)) for group in groups]
    parts = [part for group in groups for part in group]

    def kernel(bits_ref, *refs):
        number = 0
        for group, target in zip(groups, refs[len(parts) :]):
            start = 0
            for part in group:
                stop = start + part.shape[1]
                target[:, start:stop] = refs[number][...].astype(BF16)
                start, number = stop, number + 1

    return order.launch(
        kernel,
        "cast_shards",
        [bits, *parts],
        [pl.BlockSpec(memory_space=pltpu.VMEM)] * len(parts),
        [pl.BlockSpec(memory_space=pltpu.VMEM)] * len(shapes),
        [jax.ShapeDtypeStruct(shape, BF16) for shape in shapes],
        [],
        None,
        {},
    )


class Wave:
    def __init__(self, order, bits, shard, cut, direct):
        self.order, self.bits, self.cut, self.direct = order, bits, cut, direct
        self.rows, self.columns = shard.shape
        self.stacked = outer_gather(shard, direct)
        self.outer = self.stacked.shape[0]
        self.windows = (pl.ds(0, cut), pl.ds(cut, self.columns - cut))

    def first(self, moves):
        def send(parts):
            self.pairs = [(part, FIRST[half](part)) for half, part in enumerate(parts)]

        if self.direct:
            send((self.stacked[:, :, : self.cut], self.stacked[:, :, self.cut :]))
            return
        source = moves.source(self.stacked)
        targets = [moves.target((self.outer, self.rows, w.size)) for w in self.windows]
        for place in range(self.outer):
            for target, window in zip(targets, self.windows):
                shape = (self.rows, window.size)
                moves.move(source, (place, slice(None), window), shape, (target, (place,)))
        moves.then.append(lambda filled: send([filled[target] for target in targets]))

    def place(self, half, second, first, block, window):
        near, mem = (first, second) if half == 0 else (second, first)
        return lambda bits: (block, bits[0] ^ near, bits[2] ^ mem, slice(None), window)

    def second(self, moves):
        sources = [[moves.source(part) for part in pair] for pair in self.pairs]
        targets = [moves.target((2, *pair[0].shape)) for pair in self.pairs]
        own = moves.target((self.outer, 2, 2, self.rows, self.columns))
        for block in range(self.outer):
            for half, window in enumerate(self.windows):
                for side in range(2):
                    goal = (targets[half], (side, block))
                    again = (own, self.place(half, 0, side, block, window))
                    shape = (self.rows, window.size)
                    moves.move(sources[half][side], (block,), shape, goal, again)

        def send(filled):
            self.own = filled[own]
            self.far = [SECOND[half](filled[target]) for half, target in enumerate(targets)]

        moves.then.append(send)

    def third(self, moves):
        own = moves.target(self.own.shape, self.own)
        for half, window in enumerate(self.windows):
            source = moves.source(self.far[half])
            for block in range(self.outer):
                for side in range(2):
                    goal = (own, self.place(half, 1, side, block, window))
                    moves.move(source, (side, block), (self.rows, window.size), goal)

        def send(filled):
            shape = (2 * self.outer, 2 * self.rows, self.columns)
            self.own = filled[own].reshape(shape)
            self.other = swap_core(self.own)

        moves.then.append(send)


class Weight:
    def __init__(self, wave, start, width, whole=None):
        self.wave, self.start, self.width, self.whole = wave, start, width, whole
        if whole is not None:
            self.blocks, self.rows = whole.shape[0], whole.shape[2]
        else:
            self.blocks, self.rows = 2 * wave.outer, 2 * wave.rows
        self.features = self.blocks * 2 * self.rows

    def pieces(self):
        return [self.whole] if self.whole is not None else [self.wave.own, self.wave.other]

    def copies(self, kind, start, size, bits, find, target):
        if kind == "columns":
            blocks, columns = slice(None), pl.ds(self.start + start, size)
        else:
            blocks, columns = pl.ds(start, size), pl.ds(self.start, self.width)
        if self.whole is not None:
            return [(find(self.whole).at[blocks, :, :, columns], target)]
        return [
            (find(array).at[blocks, :, columns], target.at[:, bits[1] ^ core])
            for core, array in enumerate((self.wave.own, self.wave.other))
        ]


def weight_call(order, name, bits, weights, plan, inputs, outs, scratch, body):
    arrays = []
    for weight in weights:
        arrays += [a for a in weight.pieces() if not any(a is b for b in arrays)]
    kind, size = plan[0][1], plan[0][3]
    lead = weights[plan[0][0]]
    if kind == "columns":
        chunk = (lead.blocks, 2, lead.rows, size)
    else:
        chunk = (size, 2, lead.rows, lead.width)
    n_in, n_arrays, n_out = len(inputs), len(arrays), len(outs)

    def kernel(bits_ref, *refs):
        ins, refs = refs[:n_in], refs[n_in:]
        pieces, refs = refs[:n_arrays], refs[n_arrays:]
        out_refs, refs = refs[:n_out], refs[n_out:]
        held, sems = refs[-2:]
        bits_now = [bits_ref[i] for i in range(3)]

        def find(array):
            return next(ref for ref, known in zip(pieces, arrays) if known is array)

        def issue(number):
            which, kind, start, size = plan[number]
            slot = number % 2
            for source, target in weights[which].copies(
                kind, start, size, bits_now, find, held.at[slot]
            ):
                pltpu.make_async_copy(source, target, sems.at[slot]).start()

        taken = [0]

        def fetch():
            number = taken[0]
            taken[0] += 1
            if number + 1 < len(plan):
                issue(number + 1)
            slot = number % 2
            pltpu.make_async_copy(held.at[slot], held.at[slot], sems.at[slot]).wait()
            return held[slot].reshape(-1, chunk[-1])

        issue(0)
        body(fetch, ins, out_refs, refs[:-2])

    return order.launch(
        kernel,
        name,
        [bits, *inputs, *arrays],
        [pl.BlockSpec(memory_space=pltpu.VMEM)] * n_in
        + [pl.BlockSpec(memory_space=pltpu.HBM)] * n_arrays,
        [pl.BlockSpec(memory_space=pltpu.VMEM)] * n_out,
        [jax.ShapeDtypeStruct(shape, kind) for shape, kind in outs],
        [pltpu.VMEM(shape, kind) for shape, kind in scratch]
        + [pltpu.VMEM((2, *chunk), BF16), pltpu.SemaphoreType.DMA((2,))],
        None,
        {},
    )


def columns_plan(which, width, size):
    return [(which, "columns", start, size) for start in range(0, width, size)]


def row_blocks(rows, size, step):
    def run(i, carry):
        step(pl.ds(pl.multiple_of(i * size, size), size))
        return carry

    lax.fori_loop(0, rows // size, run, 0)


def normed_parts(values):
    centred = values - jnp.mean(values, axis=-1, keepdims=True)
    spread = jnp.mean(centred * centred, axis=-1, keepdims=True)
    rate = lax.rsqrt(spread + EPSILON)
    return centred * rate, rate


def norm_gradient(normed, rate, gain, cotangent):
    inner = cotangent * gain
    mean_inner = jnp.mean(inner, axis=-1, keepdims=True)
    mean_both = jnp.mean(inner * normed, axis=-1, keepdims=True)
    return rate * (inner - mean_inner - normed * mean_both)


def add_stats(stats, normed, cotangent):
    fold = lambda values: jnp.sum(values.reshape(-1, 8, values.shape[-1]), axis=0)
    stats[:8, :] += fold(cotangent * normed)
    stats[8:, :] += fold(cotangent)


def norm_table(order, bits, weight):
    features = weight.features

    def body(fetch, ins, outs, scratch):
        outs[0][...] = fetch().astype(F32).T[:8]

    return weight_call(
        order, "norm_table", bits, [weight], [(0, "columns", 0, LANES)], [],
        [((8, features), F32)], [], body,
    )[0]


def project(order, name, bits, weight, sources, size):
    def body(fetch, ins, outs, scratch):
        for start in range(0, weight.width, size):
            chunk = fetch()
            for source, target in zip(ins, outs):
                target[:, start : start + size] = plain_dot(source[...], chunk).astype(BF16)

    return weight_call(
        order, name, bits, [weight], columns_plan(0, weight.width, size), sources,
        [((source.shape[0], weight.width), BF16) for source in sources], [], body,
    )


def mix_norm(order, name, bits, weight, mixed, residual, table, index, query_weight=None):
    rows, width = mixed.shape
    size = min(1024, width)

    def body(fetch, ins, outs, scratch):
        mixed_ref, residual_ref, table_ref = ins
        summed, out, out_low = outs[:3]
        for start in range(0, width, size):
            part = plain_dot(mixed_ref[...], fetch())
            columns = slice(start, start + size)
            summed[:, columns] = ALPHA * residual_ref[:, columns].astype(F32) + part
        gain, shift = table_ref[index : index + 1, :], table_ref[3 + index : 4 + index, :]

        def step(block):
            normed, _ = normed_parts(summed[block, :])
            values = normed * gain + shift
            out[block, :] = values
            out_low[block, :] = values.astype(BF16)

        row_blocks(rows, 128, step)
        if query_weight is not None:
            for start in range(0, width, size):
                part = plain_dot(out_low[...], fetch())
                outs[3][:, start : start + size] = part.astype(BF16)

    weights = [weight] + ([query_weight] if query_weight is not None else [])
    plan = [entry for i in range(len(weights)) for entry in columns_plan(i, width, size)]
    outs = [((rows, width), F32), ((rows, width), F32), ((rows, width), BF16)]
    if query_weight is not None:
        outs.append(((rows, width), BF16))
    return weight_call(
        order, name, bits, weights, plan, [mixed, residual, table], outs, [], body
    )


def feed_in(order, bits, weight, source):
    rows, size = source.shape[0], 1024

    def body(fetch, ins, outs, scratch):
        held = scratch[0]
        for start in range(0, weight.width, size):
            held[...] = plain_dot(ins[0][...], fetch())

            def step(block):
                hidden = held[block, :]
                below = 0.5 + 0.5 * lax.erf(hidden * (0.5**0.5))
                density = jnp.exp(-0.5 * hidden * hidden) * (2.0 * jnp.pi) ** -0.5
                outs[0][block, start : start + size] = (hidden * below).astype(BF16)
                outs[1][block, start : start + size] = (below + hidden * density).astype(BF16)

            row_blocks(rows, 256, step)

    out = ((rows, weight.width), BF16)
    return weight_call(
        order, "feed_in", bits, [weight], columns_plan(0, weight.width, size), [source], [out, out],
        [((rows, size), F32)], body,
    )


def feed_out(order, bits, weight, activated, residual, table, cotangent):
    rows, width = residual.shape
    size = 512 if width % 512 == 0 else width

    def body(fetch, ins, outs, scratch):
        act_ref, residual_ref, table_ref, up_ref = ins
        layer_out, grad, grad_low, stats = outs
        summed = scratch[0]
        for start in range(0, width, size):
            columns = slice(start, start + size)
            part = plain_dot(act_ref[...], fetch())
            summed[:, columns] = ALPHA * residual_ref[:, columns] + part
        gain, shift = table_ref[2:3, :], table_ref[5:6, :]
        stats[...] = jnp.zeros_like(stats)

        def step(block):
            normed, rate = normed_parts(summed[block, :])
            layer_out[block, :] = (normed * gain + shift).astype(BF16)
            upstream = up_ref[block, :].astype(F32)
            values = norm_gradient(normed, rate, gain, upstream)
            grad[block, :] = values
            grad_low[block, :] = values.astype(BF16)
            add_stats(stats, normed, upstream)

        row_blocks(rows, 128, step)

    outs = [((rows, width), BF16), ((rows, width), F32), ((rows, width), BF16), ((16, width), F32)]
    return weight_call(
        order, "feed_out", bits, [weight], columns_plan(0, width, size),
        [activated, residual, table, cotangent], outs, [((rows, width), F32)], body,
    )


def feed_back(order, bits, weight, cotangent, slope):
    rows, features = slope.shape
    size = 1024 if features % 1024 == 0 else features
    steps = features // size

    def body(fetch, ins, outs, scratch):
        for number in range(steps):
            part = back_dot(ins[0][...], fetch())
            columns = slice(number * size, (number + 1) * size)
            outs[0][:, columns] = (part * ins[1][:, columns].astype(F32)).astype(BF16)

    blocks = weight.blocks // steps
    return weight_call(
        order, "feed_back", bits, [weight], [(0, "rows", i * blocks, blocks) for i in range(steps)],
        [cotangent, slope], [((rows, features), BF16)], [], body,
    )[0]


def norm_back(order, name, bits, weight, cotangent, carried, summed, table, index, mix_weight):
    rows, width = summed.shape
    size = min(1024, weight.width)

    def body(fetch, ins, outs, scratch):
        up_ref, carried_ref, summed_ref, table_ref = ins
        grad, grad_low, grad_mixed, stats = outs
        total = scratch[0]
        for start in range(0, weight.width, size):
            part = back_dot(up_ref[:, start : start + size], fetch())
            total[...] = part + (ALPHA * carried_ref[...] if start == 0 else total[...])
        gain = table_ref[index : index + 1, :]
        stats[...] = jnp.zeros_like(stats)

        def step(block):
            normed, rate = normed_parts(summed_ref[block, :])
            upstream = total[block, :]
            values = norm_gradient(normed, rate, gain, upstream)
            grad[block, :] = values
            grad_low[block, :] = values.astype(BF16)
            add_stats(stats, normed, upstream)

        row_blocks(rows, 128, step)
        grad_mixed[...] = back_dot(grad_low[...], fetch()).astype(BF16)

    outs = [((rows, width), F32), ((rows, width), BF16), ((rows, width), BF16), ((16, width), F32)]
    return weight_call(
        order, name, bits, [weight, mix_weight],
        columns_plan(0, weight.width, size) + columns_plan(1, width, size),
        [cotangent, carried, summed, table], outs, [((rows, width), F32)], body,
    )


def input_back(order, name, bits, weight, cotangents, carried, spans):
    rows, features = cotangents[0].shape[0], weight.features
    step = 512 if rows % 512 == 0 else rows // 2
    count = len(cotangents)

    def body(fetch, ins, outs, scratch):
        for number, (which, first, _, size) in enumerate(spans):
            chunk = fetch()
            for row in range(0, rows, step):
                block = slice(row, row + step)
                part = back_dot(ins[which][block, first : first + size], chunk)
                if number == 0 and carried is not None:
                    part += ALPHA * ins[count][block, :]
                elif number > 0:
                    part += scratch[0][block, :]
                if number == len(spans) - 1:
                    outs[0][block, :] = part.astype(BF16)
                else:
                    scratch[0][block, :] = part

    return weight_call(
        order, name, bits, [weight], [(0, "columns", start, size) for _, _, start, size in spans],
        [*cotangents] + ([carried] if carried is not None else []),
        [((rows, features), BF16)], [((rows, features), F32)], body,
    )[0]


def turn_rows(order, bits, sources, outer):
    features = sources[0].shape[1]
    total_rows = sum(source.shape[0] for source in sources)
    shard_rows = features // (8 * outer)

    def kernel(bits_ref, *refs):
        targets, filled = refs[len(sources) :], 0
        for ref in refs[: len(sources)]:
            stop = filled + ref.shape[0]
            for block in range(features // LANES):
                turned_block = ref[:, block * LANES : (block + 1) * LANES].T
                for part in range(LANES // shard_rows):
                    device = block * (LANES // shard_rows) + part
                    mem, core, near = device & 1, (device >> 1) & 1, (device >> 2) & 1
                    place = (mem ^ bits_ref[2]) * 2 + (near ^ bits_ref[0])
                    place = place * outer + (device >> 3)
                    rows = pl.ds(pl.multiple_of(place * shard_rows, shard_rows), shard_rows)
                    values = turned_block[part * shard_rows : (part + 1) * shard_rows]
                    side = core ^ bits_ref[1]

                    @pl.when(side == 0)
                    def _():
                        targets[0][rows, filled:stop] = values

                    @pl.when(side == 1)
                    def _():
                        targets[1][rows, filled:stop] = values

            filled = stop

    return order.launch(
        kernel,
        "turn_rows",
        [bits, *sources],
        [pl.BlockSpec(memory_space=pltpu.VMEM)] * len(sources),
        [pl.BlockSpec(memory_space=pltpu.VMEM)] * 2,
        [jax.ShapeDtypeStruct((features // 2, total_rows), BF16)] * 2,
        [],
        None,
        {},
    )


def weight_grad(
    order, bits, turned, cotangents, outer, cut, extra=None, held=None, place=None
):
    half_features = turned[0][0].shape[0]
    each, width = cotangents[0].shape
    n_turned = len(turned)
    n_grads = len(cotangents)
    total_rows = n_grads // 2 * each
    shard_rows = half_features // (4 * outer)
    chunk = 512 if cut is None or cut % 512 == 0 else 256
    added = 0 if extra is None else LANES
    n_held = 2 if held is not None else 0
    if place is None:
        halves = [(0, 0, cut // chunk, cut), (1, 0, (width - cut) // chunk, width - cut)]
    else:
        halves = [(place[0], place[1] // chunk, width // chunk, place[2])]
    steps = [count for _, _, count, _ in halves]
    first_steps = [sum(steps[:i]) for i in range(len(steps))]

    def kernel(bits_ref, *refs):
        n_in = n_turned + n_grads
        targets = refs[n_in + n_held + (len(halves) if added else 0) :]
        step = pl.program_id(0)
        features = jnp.concatenate([ref[...] for ref in refs[:n_turned]], axis=1)
        grads = jnp.concatenate([ref[...] for ref in refs[n_turned:n_in]], axis=0)
        product = plain_dot(features, grads)
        blocks = product.astype(BF16).reshape(2, 2, outer, shard_rows, chunk)
        for number, (half, _, count, _) in enumerate(halves):

            @pl.when((step >= first_steps[number]) & (step < first_steps[number] + count))
            def _():
                for side in range(2):
                    target = targets[2 * number + side]
                    picked = blocks[1 - side] if half == 0 else blocks[:, 1 - side]
                    target[..., :chunk] = picked
                    if added:
                        beside = refs[n_in + number]
                        picked = beside[1 - side] if half == 0 else beside[:, 1 - side]
                        target[..., chunk:] = picked

    def out_spec(number):
        _, first, count, _ = halves[number]
        at = lambda i, _: (0, 0, 0, first + jnp.clip(i - first_steps[number], 0, count - 1))
        return pl.BlockSpec((2, outer, shard_rows, chunk + added), at)

    def turned_spec(start, size):
        return pl.BlockSpec((half_features, size), lambda i, _: (0, start // size))

    whole = (2, 2, outer, shard_rows, LANES)
    specs = [turned_spec(start, size) for _, start, size in turned]
    specs += [pl.BlockSpec((each, chunk), lambda i, _: (0, i))] * n_grads
    specs += [pl.BlockSpec(memory_space=pltpu.HBM)] * n_held
    specs += [whole_spec(whole)] * (len(halves) if added else 0)
    return order.launch(
        kernel,
        "weight_grad",
        [bits, *(part for part, _, _ in turned), *cotangents, *(held or ()), *(extra or ())],
        specs,
        [out_spec(number) for number in range(len(halves)) for _ in range(2)],
        [
            jax.ShapeDtypeStruct((2, outer, shard_rows, columns + added), BF16)
            for _, _, _, columns in halves
            for _ in range(2)
        ],
        [],
        (sum(steps),),
        {1 + n_turned + n_grads: 0, 2 + n_turned + n_grads: 1} if n_held else {},
    )


def relative_rows(bits, values, outer):
    rows = values.shape[0] // (8 * outer)
    blocks = values.reshape(outer, 2, 2, 2, rows, -1)
    for axis, bit in ((1, bits[0]), (2, bits[1]), (3, bits[2])):
        blocks = jnp.where(bit == 1, jnp.flip(blocks, axis), blocks)
    blocks = blocks.transpose(2, 3, 1, 0, 4, 5)
    return blocks[0], blocks[1]


def add_blocks(order, bits, sums, shapes):
    arrays = []
    for group, _, _ in sums:
        arrays += [a for a, _ in group if not any(a is b for b in arrays)]
    blocks = [group[0][0].shape[-3:] for group, _, _ in sums]
    find = lambda array: next(i for i, known in enumerate(arrays) if known is array)
    chunks = [(number, place) for place in range(blocks[0][0]) for number in range(len(sums))]

    def kernel(bits_ref, *refs):
        sources, refs = refs[: len(arrays)], refs[len(arrays) :]
        targets, refs = refs[: len(shapes)], refs[len(shapes) :]
        held, summed, (load_sems, store_sems) = refs[: len(sums)], refs[len(sums) : -2], refs[-2:]
        loads, stores = [], []
        for index, (number, place) in enumerate(chunks):
            loads.append([])
            for term, (array, at) in enumerate(sums[number][0]):
                load = pltpu.make_async_copy(
                    sources[find(array)].at[(*at, place)],
                    held[number].at[term, place],
                    load_sems.at[index, term],
                )
                load.start()
                loads[-1].append(load)
        for index, (number, place) in enumerate(chunks):
            group, which, column = sums[number]
            for load in loads[index]:
                load.wait()
            values = [held[number][term, place].astype(F32) for term in range(len(group))]
            summed[number][place] = sum(values[1:], values[0]).astype(BF16)
            store = pltpu.make_async_copy(
                summed[number].at[place],
                targets[which].at[place, :, pl.ds(column, blocks[number][2])],
                store_sems.at[index],
            )
            store.start()
            stores.append(store)
        for store in stores:
            store.wait()

    most = max(len(group) for group, _, _ in sums)
    return order.launch(
        kernel,
        "add_blocks",
        [bits, *arrays],
        [pl.BlockSpec(memory_space=pltpu.HBM)] * len(arrays),
        [pl.BlockSpec(memory_space=pltpu.HBM)] * len(shapes),
        [jax.ShapeDtypeStruct(shape, BF16) for shape in shapes],
        [pltpu.VMEM((len(group), *block), BF16) for (group, _, _), block in zip(sums, blocks)]
        + [pltpu.VMEM(block, BF16) for block in blocks]
        + [
            pltpu.SemaphoreType.DMA((len(chunks), most)),
            pltpu.SemaphoreType.DMA((len(chunks),)),
        ],
        None,
        {},
    )


class Spread:
    def __init__(self, parts):
        self.kept = (parts[1], parts[3])
        self.once = [FIRST_BACK[half](parts[2 * half]) for half in range(2)]

    def second(self):
        return [[(self.kept[half], (1,)), (self.once[half], (1,))] for half in range(2)]

    def send(self, sent):
        self.twice = [SECOND_BACK[half](part) for half, part in enumerate(sent)]

    def third(self):
        return [
            [(self.kept[half], (0,)), (self.once[half], (0,)), (self.twice[half], ())]
            for half in range(2)
        ]


def block_shape(group):
    return group[0][0].shape[-3:]


def spread_steps(order, bits, seconds, thirds, together=False):
    sums, shapes = [], []
    for wave in seconds:
        for group in wave.second():
            sums.append((group, len(shapes), 0))
            shapes.append(block_shape(group))
    joined = len(shapes)
    for number, wave in enumerate(thirds):
        if number == 0 or not together:
            shapes.append((*block_shape(wave.third()[0])[:2], 0))
        for group in wave.third():
            outer, rows, columns = shapes[-1]
            sums.append((group, len(shapes) - 1, columns))
            shapes[-1] = (outer, rows, columns + block_shape(group)[2])
    filled = add_blocks(order, bits, sums, shapes)
    for number, wave in enumerate(seconds):
        wave.send(filled[2 * number : 2 * number + 2])
    return filled[joined:]


def outer_sum(joined):
    joined = joined.reshape(-1, joined.shape[-1])
    return lax.psum_scatter(
        joined, "dp", axis_index_groups=outer_groups(), scatter_dimension=0, tiled=True
    )


def outer_sum_direct(joined):
    place = lax.axis_index("dp") >> 2
    block = lambda far: lax.dynamic_index_in_dim(joined, place ^ far, 0, False)
    parts = [block(0)] + [swap_outer(block(far), far) for far in range(1, joined.shape[0])]
    return sum(part.astype(F32) for part in parts)


FIRST_BACK = (swap_mem, swap_next)
SECOND_BACK = (swap_next, swap_mem)


def per_device(
    target_in,
    memory_in,
    bucket_ids,
    target_lengths,
    memory_mask,
    self_qkv,
    self_out,
    cross_q,
    cross_kv,
    cross_out,
    ffn_in,
    ffn_out,
    norm_gains,
    norm_biases,
    grad_out,
):
    both = ("dp", "mem")
    row_count, model_width = target_in.shape
    shard_rows = self_qkv.shape[0]
    outer = lax.axis_size("dp") // 4
    staged = shard_rows % 16 == 0 and shard_rows <= LANES and model_width % LANES == 0
    bits = place_bits()
    order = Order()
    own_index, pieces = lax.axis_index("mem"), lax.axis_size("mem")
    slot_count, mem_piece = memory_in.shape[3], memory_in.shape[4]

    norm_shard = jnp.concatenate((norm_gains, norm_biases), axis=1)
    norm_columns = norm_shard.shape[1]
    norm_shard = jnp.pad(norm_shard, ((0, 0), (0, LANES - norm_columns)))

    groups = [
        (self_qkv,),
        (cross_q, cross_out, norm_shard, cross_kv, self_out),
        (ffn_in,),
        (ffn_out,),
    ]
    if staged:
        shards = cast_shards(order, bits, groups[:1])
    else:
        shards = [jnp.concatenate([part.astype(BF16) for part in group], axis=1) for group in groups]

    def gather(index, cut, direct=False):
        shard = shards[index]
        widths = [part.shape[1] for part in groups[index]]
        starts = [sum(widths[:i]) for i in range(len(widths))]
        if staged:
            wave = Wave(order, bits, shard, cut, direct)
            return [Weight(wave, at, size) for at, size in zip(starts, widths)]
        full = lax.all_gather(shard, both, axis=0, tiled=True)
        rows = full.shape[0] // 16
        return [
            Weight(None, 0, size, full[:, at : at + size].reshape(8, 2, rows, size))
            for at, size in zip(starts, widths)
        ]

    def whole_sum(gradient):
        return lax.psum_scatter(gradient, both, scatter_dimension=0, tiled=True).astype(F32)

    class Turned:
        def __init__(self, *sources):
            self.sources = sources
            own, other = turn_rows(order, bits, sources, outer) if staged else (None, None)
            self.both = (own, swap_core(other)) if staged else ()

        def due(self):
            order.before(*self.both[1:])

    class Grad:
        def __init__(self, *places):
            self.sources = [source for _, source in places]
            self.turned = []
            for side in range(2 if staged else 0):
                for turned, source in places:
                    start = 0
                    for other in turned.sources:
                        if other is source:
                            break
                        start += other.shape[0]
                    stop = start + source.shape[0]
                    size = math.gcd(start, stop)
                    for at in range(start, stop, size):
                        self.turned.append((turned.both[side], at, size))

        def take(self, *cotangents):
            self.cotangents = cotangents
            if staged:
                self.cotangents += tuple(swap_core(part) for part in cotangents)

        def make(self, cut=None, **options):
            if staged:
                return weight_grad(
                    order, bits, self.turned, self.cotangents, outer, cut, **options
                )
            rows = [jnp.concatenate(part, axis=0) for part in (self.sources, self.cotangents)]
            return lead_dot(*rows).astype(BF16)

    def at_mem(values, index):
        return lax.dynamic_index_in_dim(values, index, 0, False)

    mem_rows = memory_in[0, :, 0]
    mem_live = memory_mask[0, :, 0]
    near_rows = at_mem(mem_rows, own_index)
    near_live = at_mem(mem_live, own_index)
    far_live = swap_mem(at_mem(mem_live, 1 - own_index))
    sent_rows = [at_mem(mem_rows[:, slot], 1 - own_index) for slot in range(slot_count)]

    (w_qkv,) = gather(0, model_width, True)
    far_parts = [swap_mem(sent_rows[0])]
    if staged:
        order.before(w_qkv.wave.stacked)
        shards += cast_shards(order, bits, groups[1:])
    w_cq, w_co, w_norm, w_ckv, w_so = gather(1, 2 * model_width + LANES)
    (w_in,) = gather(2, 3 * model_width // 2)
    (w_out,) = gather(3, 3 * model_width // 8)

    bucket = pick_entry(bucket_ids[0], own_index)
    lengths = target_lengths[0, 0]
    self_meta = jnp.stack([jnp.right_shift(jnp.int32(row_count), bucket), lengths[0], lengths[1]])
    cross_meta = bucket[None]
    live = jnp.concatenate((near_live, far_live), axis=1)
    key_bias = jnp.where(live == 1, 0.0, NEG_LARGE).astype(F32)
    key_columns = jnp.broadcast_to(key_bias[:, :, None], (*key_bias.shape, LANES))
    near_flat = near_rows.reshape(-1, model_width)
    slotted = (slot_count, mem_piece, 2 * model_width)

    def steps(*wanted):
        if staged:
            moves = Moves(order, bits)
            for weight, name in wanted:
                getattr(weight.wave, name)(moves)
            if moves.moves:
                moves.run()

    steps((w_qkv, "first"))
    order.before(far_parts[0], far_live)
    steps((w_qkv, "second"))
    order.part()
    first_turned = Turned(target_in, near_flat)
    steps((w_ckv, "first"))
    order.part()
    steps((w_qkv, "third"))
    first_turned.due()
    (united,) = project(order, "self_project", bits, w_qkv, [target_in], 1024)
    far_parts += [swap_mem(part) for part in gate(order, bits, sent_rows[1:])]
    order.part()
    steps((w_ckv, "second"))
    steps((w_in, "first"))
    self_mixed, self_log = self_forward(order, self_meta, united)
    far_flat = jnp.concatenate(far_parts, axis=0)
    order.part()
    steps((w_ckv, "third"))
    order.before(*far_parts[1:])
    order.part()
    steps((w_in, "second"))
    steps((w_out, "first"))
    table = norm_table(order, bits, w_norm)
    near_kv, far_kv = project(order, "cross_project", bits, w_ckv, [near_flat, far_flat], 1024)
    near_kv, far_kv = near_kv.reshape(slotted), far_kv.reshape(slotted)
    sum_one, first_out, first_low, cross_query = mix_norm(
        order, "self_mix", bits, w_so, self_mixed, target_in, table, 0, w_cq
    )
    order.part()
    steps((w_in, "third"))
    order.part()
    steps((w_out, "second"))
    cross_mixed, cross_log = cross_forward(
        order, cross_meta, cross_query, near_kv, far_kv, key_bias[:, None, :]
    )
    sum_two, second_out, second_low = mix_norm(
        order, "cross_mix", bits, w_co, cross_mixed, first_out, table, 1
    )
    steps((w_out, "third"))
    later = Turned(self_mixed, first_low, cross_mixed, second_low, far_flat)
    activated, slope = feed_in(order, bits, w_in, second_low)
    later.due()
    hidden = Turned(activated)
    layer_out, grad_three, grad_ffn, stats_three = feed_out(
        order, bits, w_out, activated, second_out, table, grad_out
    )
    qkv_grad = Grad((first_turned, target_in))
    so_grad = Grad((later, self_mixed))
    ckv_grad = Grad((first_turned, near_flat), (later, far_flat))
    cq_grad = Grad((later, first_low))
    co_grad = Grad((later, cross_mixed))
    in_grad = Grad((later, second_low))
    out_grad = Grad((hidden, activated))

    shards = {}

    def spread(name, parts):
        if staged:
            return Spread(parts)
        shards[name] = whole_sum(parts)
        return None

    def advance(seconds=(), thirds=()):
        if staged:
            waves = [wave for _, wave in thirds]
            joined = spread_steps(order, bits, seconds, waves)
            for (name, _), part in zip(thirds, joined):
                shards[name] = outer_sum(part)

    out_grad.take(grad_ffn)
    out_wave = spread("out", out_grad.make(model_width // 2))
    grad_hidden = feed_back(order, bits, w_out, grad_ffn, slope)
    in_grad.take(grad_hidden)
    grad_two, grad_cross_out, grad_cross_mixed, stats_two = norm_back(
        order, "cross_back", bits, w_in, grad_hidden, grad_three, sum_two, table, 1, w_co
    )
    co_grad.take(grad_cross_out)
    order.part()
    advance([out_wave])
    in_wave = spread("in", in_grad.make(2 * model_width))
    pair_width = 2 * model_width
    near_parts = co_grad.make(place=(0, 0, pair_width))
    grad_query_low, grad_near_kv, grad_far_kv = cross_backward(
        order,
        cross_meta,
        cross_query,
        near_kv,
        far_kv,
        key_columns,
        cross_mixed,
        grad_cross_mixed,
        cross_log,
    )
    cq_grad.take(grad_query_low)
    ckv_grad.take(grad_near_kv, grad_far_kv)
    order.part()
    advance([in_wave], [("out", out_wave)])

    def memory_back(cotangent):
        spans = [(0, start, start, model_width) for start in (0, model_width)]
        return input_back(order, "memory_back", bits, w_ckv, [cotangent], None, spans)

    grad_one, grad_self_out, grad_self_mixed, stats_one = norm_back(
        order, "self_back", bits, w_cq, grad_query_low, grad_two, sum_one, table, 0, w_so
    )
    so_grad.take(grad_self_out)
    stats = [jnp.sum(s.reshape(2, 8, model_width), axis=1) for s in (stats_one, stats_two, stats_three)]
    norm_grads = [
        jnp.pad(jnp.stack([s[i] for s in stats], axis=1), ((0, 0), (0, LANES - len(stats))))
        for i in range(2)
    ]
    norm_grads = jnp.concatenate(norm_grads, axis=1).astype(BF16)
    if staged:
        own, other = relative_rows(bits, norm_grads, outer)
        own = (own.astype(F32) + swap_core(other).astype(F32)).astype(BF16)
        norm_grads = (own[..., :LANES], own[..., LANES:])
        near_parts = cq_grad.make(place=(0, model_width, pair_width), held=near_parts)
        mid_wave = spread("mid", [*near_parts, *ckv_grad.make(place=(1, 0, pair_width))])
    else:
        parts = [near_parts, cq_grad.make(), ckv_grad.make()]
        mid_wave = spread("mid", jnp.concatenate(parts, axis=1))
    grad_far = swap_mem(memory_back(grad_far_kv))
    order.part()
    advance([], [("in", in_wave)])
    grad_united = self_backward(
        order,
        self_meta,
        united,
        self_mixed,
        grad_self_mixed,
        self_log,
        0,
        model_width // LANES,
    )
    qkv_grad.take(grad_united)
    order.part()
    advance([mid_wave])
    if staged:
        order.before(shards["out"])
    qkv_wave = spread("qkv", qkv_grad.make(w_qkv.width // 2))
    order.before(grad_far)
    grad_near = memory_back(grad_near_kv)
    half_width = model_width // 2
    if staged:
        so_wave = spread("so", so_grad.make(half_width, extra=norm_grads))
    else:
        part = so_grad.make()
        columns = [part[:, :half_width], norm_grads[:, :LANES], part[:, half_width:], norm_grads[:, LANES:]]
        so_wave = spread("so", jnp.concatenate(columns, axis=1))
    if staged:
        order.before(shards["in"])
        order.part()
        advance([qkv_wave], [("mid", mid_wave)])
    if staged:
        advance([so_wave])
        (joined,) = spread_steps(order, bits, [], [so_wave, qkv_wave], True)
        last = outer_sum_direct(joined)
        split = 2 * (half_width + LANES)
        shards["so"], shards["qkv"] = last[:, :split], last[:, split:]
    target_grad = input_back(
        order,
        "target_back",
        bits,
        w_qkv,
        [grad_united],
        grad_one,
        [(0, start, start, model_width) for start in range(0, w_qkv.width, model_width)],
    )
    if staged:
        moves = Moves(order, bits)
        target = moves.target((2, *near_flat.shape))
        for number, part in enumerate((grad_near, grad_far)):
            place = lambda bits, number=number: (bits[2] ^ number,)
            moves.move(moves.source(part), (slice(None),), near_flat.shape, (target, place))
        moves.then.append(lambda filled: shards.update(memory=filled[target]))
        moves.run()
        grad_pair = shards["memory"]
    else:
        grad_pair = jnp.stack((grad_near, grad_far))
        grad_pair = jnp.where(own_index == 0, grad_pair, grad_pair[::-1])
    qkv_shard = shards["qkv"]
    memory_grad = grad_pair.reshape(1, pieces, 1, *near_rows.shape)
    so_shard, mid_shard = shards["so"], shards["mid"].astype(F32)
    split = half_width + LANES

    return (
        layer_out,
        target_grad,
        memory_grad,
        qkv_shard,
        jnp.concatenate((so_shard[:, :half_width], so_shard[:, split : split + half_width]), axis=1),
        mid_shard[:, model_width : 2 * model_width],
        mid_shard[:, 2 * model_width :],
        mid_shard[:, :model_width],
        shards["in"].astype(F32),
        shards["out"].astype(F32),
        so_shard[:, half_width : half_width + 3],
        so_shard[:, split + half_width : split + half_width + 3],
    )


def solution(mesh):
    rows = P(("dp", "mem"), None)
    memory = P("dp", None, "mem", None, None, None)
    return jax.shard_map(
        per_device,
        mesh=mesh,
        in_specs=(
            rows,
            memory,
            P("dp", None),
            P("dp", "mem", None),
            P("dp", None, "mem", None, None),
        )
        + (rows,) * 10,
        out_specs=(rows, rows, memory) + (rows,) * 9,
        check_vma=False,
    )
```

time: 782 us -> 589 us (0.75)
  waiting for transfers between devices: 309 us -> 101 us
  Pallas kernels: 266 us -> 355 us
  other arithmetic: 83.5 us -> 10.7 us
  starting transfers between devices: 68.7 us -> 59.1 us
    ppermute x21 -> x22, waiting for transfers between devices: 150 us -> 24.1 us  [swap_mem(): return lax.ppermute(values, 'mem', [(0, 1), (1, 0)])]
    pallas_call x23 -> x49, Pallas kernels: 266 us -> 355 us  [launch(): results = run(*operands, *ties)]
    ppermute x18, waiting for transfers between devices: 86 us -> 35.4 us  [swap_next(): return lax.ppermute(values, 'dp', [(i, i ^ 2) for i in range(size)])]
    convert_element_type x31 -> x3, other arithmetic: 51.1 us -> 2.7 us  [the longest x1 1.03 us: per_device(): own = (own.astype(F32) + swap_core(other).astype(F32)).astype(BF16)]
    all_gather x3, waiting for transfers between devices: 33.9 us -> 15.2 us  [outer_gather(): lax.all_gather(shard, 'dp', axis_index_groups=outer_groups(), axis=0, til...]
    ppermute x6, waiting for transfers between devices: 39.6 us -> 21 us  [swap_outer(): return lax.ppermute(values, 'dp', [(i, i ^ 4 * far) for i in range(size)])]
    ppermute x6, starting transfers between devices: 25.4 us -> 10.1 us  [swap_outer(): return lax.ppermute(values, 'dp', [(i, i ^ 4 * far) for i in range(size)])]
    another operation x12 -> x1, other arithmetic: 14.1 us -> 0.04 us  [per_device(): jnp.stack([s[i] for s in stats], axis=1)]
  transfers between devices with their start and end apart: 73 -> 68, of which waited for: 25 -> 20; matrix products, arithmetic and copies ran while one was open for 13% -> 5% of each run, Pallas kernels for 19% -> 58%
where the time goes in v2:
time: 589 us; the launch traced here: 577 us
  Pallas kernels  355 us (60%)
  waiting for transfers between devices  101 us (17%)
  starting transfers between devices  59.1 us (10%)
  local copies, waits for them, and re-layouts  35.9 us (6%)
  between operations  15.9 us (3%)
  other arithmetic  10.7 us (2%)
    pallas_call x49, Pallas kernels, launch(): results = run(*operands, *ties)  355 us
    ppermute x18, waiting for transfers between devices, swap_next(): return lax.ppermute(values, 'dp', [(i, i ^ 2) for i in range(size)])  35.4 us
    ppermute x22, starting transfers between devices, swap_mem(): return lax.ppermute(values, 'mem', [(0, 1), (1, 0)])  24.3 us
    ppermute x22, waiting for transfers between devices, swap_mem(): return lax.ppermute(values, 'mem', [(0, 1), (1, 0)])  24.1 us
    ppermute x18, starting transfers between devices, swap_next(): return lax.ppermute(values, 'dp', [(i, i ^ 2) for i in range(size)])  21.1 us
    ppermute x6, waiting for transfers between devices, swap_outer(): return lax.ppermute(values, 'dp', [(i, i ^ 4 * far) for i in range(size)])  21 us
    all_gather x3, waiting for transfers between devices, outer_gather(): lax.all_gather(shard, 'dp', axis_index_groups=outer_groups(), axis=0, til...  15.2 us
    unnamed x93, local copies, waits for them, and re-layouts  13.9 us
  transfers between devices with their start and end apart: 68, of which 20 were waited for; matrix products, arithmetic and copies ran while one was open for 5% of the time, Pallas kernels for 58%

profile of v2, /device:TPU:0, one launch (start us, length us, event | category | flops | bytes accessed | tf_op | source)
XLA Modules:
  0.0 577.5 jit_solution(6773855885839857628)
XLA Ops:
  9.6 5.0 collective-permute-start.1
  15.2 3.5 fusion.5
  21.4 10.1 %collective-permute-done.2 = bf16[32,3072]{1,0:T(8,128)(2,1)S(1)} collective-permute-done((bf16[32,3072]{1,0:T(8,128)(2,1)}, bf16[32,3072]{1,0:T(8,128)(2,1)S(1)}, u32[]{:S(2)}, u32[]{:S(2)}) %collective-permute-start.2) | collective-permute-done | bytes 196640 | tf_op jit(solution)/shard_map/ppermute | solution.py:391
  45.4 4.6 collective-permute-done.6.refs_6_
  50.6 3.6 move_blocks.12
  57.3 5.5 turn_rows.3
  62.8 15.1 %all-gather.4.cloned.1.call-done = bf16[128,5248]{1,0:T(8,128)(2,1)} async-done(((bf16[32,5248]{1,0:T(8,128)(2,1)}), bf16[128,5248]{1,0:T(8,128)(2,1)}) %all-gather.4.cloned.1.call-update) | async-done | bytes 1343504 | tf_op jit(solution)/shard_map/all_gather | solution.py:407
  92.6 8.6 %self_project.1.refs_2_.refs_1_.refs_3_ = bf16[512,3072]{1,0:T(8,128)(2,1)} custom-call(s32[3]{0:T(128)} %pad_add_fusion.refs_0_, bf16[512,1024]{1,0:T(8,128)(2,1)} %refs_2_.3, bf16[8,64,3072]{2,1,0:T(8,128)(2,1)} %bitcast.96, bf16[8,64,3072]{2,1,0:T(8,128)(2,1)} %collective-permute-done.9.refs_3_.refs_4_, bf16[512,1280]{1,0:T(8,128)(2,1)} %copy-done, ...), custom_call_target="tpu_custom_call" | custom-call | flops 1000000 | bytes 1 | tf_op jit(solution)/shard_map/self_project/pallas_call | solution.py:97
  104.5 4.5 move_blocks.15
  121.2 14.2 %self_forward.1 = (bf16[512,1024]{1,0:T(8,128)(2,1)}, f32[512,1024]{1,0:T(8,128)}) custom-call(s32[3]{0:T(128)} %pad_add_fusion.1.refs_0_, bf16[512,3072]{1,0:T(8,128)(2,1)} %self_project.1.refs_2_.refs_1_.refs_3_, bf16[512,3072]{1,0:T(8,128)(2,1)} %self_project.1.refs_2_.refs_1_.refs_3_, bf16[512,3072]{1,0:T(8,128)(2,1)} %self_project.1.refs_2_.refs_1_.refs_3_, ...), custom_call_target="tpu_custom_call" | custom-call | flops 1000000 | bytes 1 | tf_op jit(solution)/shard_map/self_forward/pallas_call | solution.py:97
  138.3 8.3 %collective-permute-done.14.refs_3_ = bf16[2,4,32,3072]{3,2,1,0:T(8,128)(2,1)S(1)} collective-permute-done((bf16[2,4,32,3072]{3,2,1,0:T(8,128)(2,1)}, bf16[2,4,32,3072]{3,2,1,0:T(8,128)(2,1)S(1)}, u32[]{:S(2)}, u32[]{:S(2)}) %collective-permute-start.14) | collective-permute-done | bytes 1572896 | tf_op jit(solution)/shard_map/ppermute | solution.py:382
  147.7 3.5 move_blocks.17.refs_6_
  153.3 13.8 %collective-permute-done.17.refs_4_ = bf16[4,32,2560]{2,1,0:T(8,128)(2,1)} collective-permute-done((bf16[4,32,2560]{2,1,0:T(8,128)(2,1)}, bf16[4,32,2560]{2,1,0:T(8,128)(2,1)}, u32[]{:S(2)}, u32[]{:S(2)}) %collective-permute-start.17) | collective-permute-done | bytes 655392 | tf_op jit(solution)/shard_map/ppermute | solution.py:386
  167.1 3.9 move_blocks.18
  182.9 12.0 %cross_project.1 = (bf16[768,2048]{1,0:T(8,128)(2,1)}, bf16[768,2048]{1,0:T(8,128)(2,1)}) custom-call(s32[3]{0:T(128)} %pad_add_fusion.refs_0_, bf16[768,1024]{1,0:T(8,128)(2,1)} %bitcast.103, bf16[768,1024]{1,0:T(8,128)(2,1)} %copy-done.1, bf16[8,64,5248]{2,1,0:T(8,128)(2,1)} %bitcast.77, ...), custom_call_target="tpu_custom_call" | custom-call | flops 1000000 | bytes 1 | tf_op jit(solution)/shard_map/cross_project/pallas_call | solution.py:97
  194.8 8.2 %self_mix.1 = (f32[512,1024]{1,0:T(8,128)}, f32[512,1024]{1,0:T(8,128)}, bf16[512,1024]{1,0:T(8,128)(2,1)}, bf16[512,1024]{1,0:T(8,128)(2,1)}) custom-call(s32[3]{0:T(128)} %pad_add_fusion.refs_0_, bf16[512,1024]{1,0:T(8,128)(2,1)} %get-tuple-element.114.refs_4_.refs_1_, bf16[512,1024]{1,0:T(8,128)(2,1)} %refs_2_.3, ...), custom_call_target="tpu_custom_call" | custom-call | flops 1000000 | bytes 1 | tf_op jit(solution)/shard_map/self_mix/pallas_call | solution.py:97
  208.6 4.1 move_blocks.21
  215.5 17.8 %cross_forward.1 = (bf16[512,1024]{1,0:T(8,128)(2,1)}, f32[512,1024]{1,0:T(8,128)}) custom-call(s32[1]{0:T(128)} %bitcast.4.refs_0_, bf16[512,1024]{1,0:T(8,128)(2,1)} %get-tuple-element.122.refs_1_, bf16[2,384,2048]{2,1,0:T(8,128)(2,1)} %bitcast.84, bf16[2,384,2048]{2,1,0:T(8,128)(2,1)} %bitcast.85, bf16[2,384,2048]{2,1,0:T(8,128)(2,1)} %bitcast.91, ...), custom_call_target="tpu_custom_call" | custom-call | flops 1000000 | bytes 1 | tf_op jit(solution)/shard_map/cross_forward/pallas_call | solution.py:97
  233.3 8.3 %cross_mix.1 = (f32[512,1024]{1,0:T(8,128)}, f32[512,1024]{1,0:T(8,128)}, bf16[512,1024]{1,0:T(8,128)(2,1)}) custom-call(s32[3]{0:T(128)} %pad_add_fusion.refs_0_, bf16[512,1024]{1,0:T(8,128)(2,1)} %get-tuple-element.129.refs_1_.refs_3_.refs_7_, f32[512,1024]{1,0:T(8,128)} %get-tuple-element.130.refs_2_, f32[8,1024]{1,0:T(8,128)} %norm_table.1.refs_5_.refs_3_.refs_4_, ...), custom_call_target="tpu_custom_call" | custom-call | flops 1000000 | bytes 1 | tf_op jit(solution)/shard_map/cross_mix/pallas_call | solution.py:97
  242.7 3.3 move_blocks.22.refs_6_
  246.3 10.5 %turn_rows.4 = (bf16[512,2816]{1,0:T(8,128)(2,1)}, bf16[512,2816]{1,0:T(8,128)(2,1)}) custom-call(s32[3]{0:T(128)} %pad_add_fusion.refs_0_, bf16[512,1024]{1,0:T(8,128)(2,1)} %get-tuple-element.114.refs_4_.refs_1_, bf16[512,1024]{1,0:T(8,128)(2,1)} %get-tuple-element.132.refs_2_, bf16[512,1024]{1,0:T(8,128)(2,1)} %get-tuple-element.129.refs_1_.refs_3_.refs_7_, ...), custom_call_target="tpu_custom_call" | custom-call | flops 1000000 | bytes 1 | tf_op jit(solution)/shard_map/turn_rows/pallas_call | solution.py:97
  256.9 14.6 %feed_in.1 = (bf16[512,4096]{1,0:T(8,128)(2,1)}, bf16[512,4096]{1,0:T(8,128)(2,1)}) custom-call(s32[3]{0:T(128)} %pad_add_fusion.refs_0_, bf16[512,1024]{1,0:T(8,128)(2,1)} %get-tuple-element.131.refs_4_.refs_1_, bf16[8,64,4096]{2,1,0:T(8,128)(2,1)} %bitcast.99, bf16[8,64,4096]{2,1,0:T(8,128)(2,1)} %collective-permute-done.23.refs_3_.refs_6_, ...), custom_call_target="tpu_custom_call" | custom-call | flops 1000000 | bytes 1 | tf_op jit(solution)/shard_map/feed_in/pallas_call | solution.py:97
  271.6 7.4 %turn_rows.5 = (bf16[2048,512]{1,0:T(8,128)(2,1)}, bf16[2048,512]{1,0:T(8,128)(2,1)}) custom-call(s32[3]{0:T(128)} %pad_add_fusion.refs_0_, bf16[512,4096]{1,0:T(8,128)(2,1)} %get-tuple-element.137.refs_1_, bf16[512,2816]{1,0:T(8,128)(2,1)} %collective-permute-done.27.refs_2_.refs_10_.refs_11_.refs_12_), custom_call_target="tpu_custom_call" | custom-call | flops 1000000 | bytes 1 | tf_op jit(solution)/shard_map/turn_rows/pallas_call | solution.py:97
  279.4 14.1 %feed_out.1 = (bf16[512,1024]{1,0:T(8,128)(2,1)}, f32[512,1024]{1,0:T(8,128)}, bf16[512,1024]{1,0:T(8,128)(2,1)}, f32[16,1024]{1,0:T(8,128)}) custom-call(s32[3]{0:T(128)} %pad_add_fusion.refs_0_, bf16[512,4096]{1,0:T(8,128)(2,1)} %get-tuple-element.137.refs_1_, f32[512,1024]{1,0:T(8,128)} %get-tuple-element.138.refs_2_, ...), custom_call_target="tpu_custom_call" | custom-call | flops 1000000 | bytes 1 | tf_op jit(solution)/shard_map/feed_out/pallas_call | solution.py:97
  297.5 10.4 %weight_grad.7 = (bf16[2,4,128,512]{3,2,1,0:T(8,128)(2,1)}, bf16[2,4,128,512]{3,2,1,0:T(8,128)(2,1)}, bf16[2,4,128,512]{3,2,1,0:T(8,128)(2,1)}, bf16[2,4,128,512]{3,2,1,0:T(8,128)(2,1)}) custom-call(s32[3]{0:T(128)} %pad_add_fusion.refs_0_, bf16[2048,512]{1,0:T(8,128)(2,1)} %get-tuple-element.140.refs_7_.refs_1_, ...), custom_call_target="tpu_custom_call" | custom-call | flops 1000000 | bytes 1 | tf_op jit(solution)/shard_map/weight_grad/pallas_call | solution.py:97
  309.9 11.5 %feed_back.1.refs_1_.refs_3_ = bf16[512,4096]{1,0:T(8,128)(2,1)} custom-call(s32[3]{0:T(128)} %pad_add_fusion.refs_0_, bf16[512,1024]{1,0:T(8,128)(2,1)} %get-tuple-element.142.refs_3_.refs_1_, bf16[512,4096]{1,0:T(8,128)(2,1)} %get-tuple-element.143.refs_2_, bf16[8,256,1024]{2,1,0:T(8,128)(2,1)} %bitcast.90, ...), custom_call_target="tpu_custom_call" | custom-call | flops 1000000 | bytes 1 | tf_op jit(solution)/shard_map/feed_back/pallas_call | solution.py:97
  321.5 14.7 %cross_back.1 = (f32[512,1024]{1,0:T(8,128)}, bf16[512,1024]{1,0:T(8,128)(2,1)}, bf16[512,1024]{1,0:T(8,128)(2,1)}, f32[16,1024]{1,0:T(8,128)}) custom-call(s32[3]{0:T(128)} %pad_add_fusion.refs_0_, bf16[512,4096]{1,0:T(8,128)(2,1)} %feed_back.1.refs_1_.refs_3_, f32[512,1024]{1,0:T(8,128)} %get-tuple-element.146.refs_2_, ...), custom_call_target="tpu_custom_call" | custom-call | flops 1000000 | bytes 1 | tf_op jit(solution)/shard_map/cross_back/pallas_call | solution.py:97
  341.0 11.6 %weight_grad.8 = (bf16[2,4,32,2048]{3,2,1,0:T(8,128)(2,1)}, bf16[2,4,32,2048]{3,2,1,0:T(8,128)(2,1)}, bf16[2,4,32,2048]{3,2,1,0:T(8,128)(2,1)}, bf16[2,4,32,2048]{3,2,1,0:T(8,128)(2,1)}) custom-call(s32[3]{0:T(128)} %pad_add_fusion.refs_0_, bf16[512,2816]{1,0:T(8,128)(2,1)} %get-tuple-element.136.refs_4_.refs_1_.refs_5_.refs_6_, ...), custom_call_target="tpu_custom_call" | custom-call | flops 1000000 | bytes 1 | tf_op jit(solution)/shard_map/weight_grad/pallas_call | solution.py:97
  358.0 4.6 weight_grad.9
  363.7 24.1 %cross_backward.1 = (bf16[512,1024]{1,0:T(8,128)(2,1)}, bf16[768,2048]{1,0:T(8,128)(2,1)}, bf16[768,2048]{1,0:T(8,128)(2,1)}) custom-call(s32[1]{0:T(128)} %bitcast.4.refs_0_, bf16[512,1024]{1,0:T(8,128)(2,1)} %get-tuple-element.122.refs_1_, bf16[2,384,2048]{2,1,0:T(8,128)(2,1)} %bitcast.86, bf16[2,384,2048]{2,1,0:T(8,128)(2,1)} %bitcast.87, ...), custom_call_target="tpu_custom_call" | custom-call | flops 1000000 | bytes 1 | tf_op jit(solution)/shard_map/cross_backward/pallas_call | solution.py:97
  391.8 5.0 add_blocks.8
  398.2 9.4 %self_back.1 = (f32[512,1024]{1,0:T(8,128)}, bf16[512,1024]{1,0:T(8,128)(2,1)}, bf16[512,1024]{1,0:T(8,128)(2,1)}, f32[16,1024]{1,0:T(8,128)}) custom-call(s32[3]{0:T(128)} %pad_add_fusion.refs_0_, bf16[512,1024]{1,0:T(8,128)(2,1)} %get-tuple-element.157.refs_11_.refs_1_.refs_3_, f32[512,1024]{1,0:T(8,128)} %get-tuple-element.153.refs_5_.refs_2_, ...), custom_call_target="tpu_custom_call" | custom-call | flops 1000000 | bytes 1 | tf_op jit(solution)/shard_map/self_back/pallas_call | solution.py:97
  407.6 4.7 weight_grad.10
  417.0 12.5 %weight_grad.11 = (bf16[2,4,32,2048]{3,2,1,0:T(8,128)(2,1)}, bf16[2,4,32,2048]{3,2,1,0:T(8,128)(2,1)}) custom-call(s32[3]{0:T(128)} %pad_add_fusion.refs_0_, bf16[512,1280]{1,0:T(8,128)(2,1)} %get-tuple-element.107.refs_2_.refs_1_.refs_3_, bf16[512,1280]{1,0:T(8,128)(2,1)} %get-tuple-element.107.refs_2_.refs_1_.refs_3_, ...), custom_call_target="tpu_custom_call" | custom-call | flops 1000000 | bytes 1 | tf_op jit(solution)/shard_map/weight_grad/pallas_call | solution.py:97
  429.5 8.2 %memory_back.2.refs_7_ = bf16[768,1024]{1,0:T(8,128)(2,1)} custom-call(s32[3]{0:T(128)} %pad_add_fusion.refs_0_, bf16[768,2048]{1,0:T(8,128)(2,1)} %get-tuple-element.166.refs_14_.refs_1_, bf16[8,64,5248]{2,1,0:T(8,128)(2,1)} %bitcast.82, bf16[8,64,5248]{2,1,0:T(8,128)(2,1)} %collective-permute-done.15.refs_2_.refs_4_.refs_5_.refs_8_.refs_6_.refs_3_, ...), custom_call_target="tpu_custom_call" | custom-call | flops 1000000 | bytes 1 | tf_op jit(solution)/shard_map/memory_back/pallas_call | solution.py:97
  440.0 3.5 add_blocks.9.refs_7_
  443.6 15.4 %self_backward.1.refs_5_.refs_3_.refs_1_ = bf16[512,3072]{1,0:T(8,128)(2,1)} custom-call(s32[3]{0:T(128)} %pad_add_fusion.1.refs_0_, bf16[512,3072]{1,0:T(8,128)(2,1)} %self_project.1.refs_2_.refs_1_.refs_3_, bf16[512,3072]{1,0:T(8,128)(2,1)} %self_project.1.refs_2_.refs_1_.refs_3_, bf16[512,3072]{1,0:T(8,128)(2,1)} %self_project.1.refs_2_.refs_1_.refs_3_, ...), custom_call_target="tpu_custom_call" | custom-call | flops 1000000 | bytes 1 | tf_op jit(solution)/shard_map/self_backward/pallas_call | solution.py:97
  459.1 4.2 collective-permute-done.48.refs_4_.refs_9_
  466.5 9.4 %weight_grad.12 = (bf16[2,4,32,1536]{3,2,1,0:T(8,128)(2,1)}, bf16[2,4,32,1536]{3,2,1,0:T(8,128)(2,1)}, bf16[2,4,32,1536]{3,2,1,0:T(8,128)(2,1)}, bf16[2,4,32,1536]{3,2,1,0:T(8,128)(2,1)}) custom-call(s32[3]{0:T(128)} %pad_add_fusion.refs_0_, bf16[512,1280]{1,0:T(8,128)(2,1)} %get-tuple-element.107.refs_2_.refs_1_.refs_3_, bf16[512,1280]{1,0:T(8,128)(2,1)} %copy-done, ...), custom_call_target="tpu_custom_call" | custom-call | flops 1000000 | bytes 1 | tf_op jit(solution)/shard_map/weight_grad/pallas_call | solution.py:97
  481.8 8.2 %memory_back.3.refs_7_.refs_1_ = bf16[768,1024]{1,0:T(8,128)(2,1)} custom-call(s32[3]{0:T(128)} %pad_add_fusion.refs_0_, bf16[768,2048]{1,0:T(8,128)(2,1)} %get-tuple-element.167.refs_13_.refs_1_, bf16[8,64,5248]{2,1,0:T(8,128)(2,1)} %bitcast.83, bf16[8,64,5248]{2,1,0:T(8,128)(2,1)} %collective-permute-done.15.refs_2_.refs_4_.refs_5_.refs_8_.refs_6_.refs_3_, ...), custom_call_target="tpu_custom_call" | custom-call | flops 1000000 | bytes 1 | tf_op jit(solution)/shard_map/memory_back/pallas_call | solution.py:97
  490.0 5.1 weight_grad.13
  496.1 10.7 %collective-permute-done.53.refs_7_ = bf16[4,32,2048]{2,1,0:T(8,128)(2,1)} collective-permute-done((bf16[4,32,2048]{2,1,0:T(8,128)(2,1)S(1)}, bf16[4,32,2048]{2,1,0:T(8,128)(2,1)}, u32[]{:S(2)}, u32[]{:S(2)}) %collective-permute-start.53) | collective-permute-done | bytes 524320 | tf_op jit(solution)/shard_map/ppermute | solution.py:382
  509.0 4.7 add_blocks.11
  521.0 5.6 collective-permute-done.55.refs_3_
  528.2 3.9 add_blocks.13.refs_5_
  539.6 9.1 %target_back.1.refs_3_ = bf16[512,1024]{1,0:T(8,128)(2,1)} custom-call(s32[3]{0:T(128)} %pad_add_fusion.refs_0_, bf16[512,3072]{1,0:T(8,128)(2,1)} %self_backward.1.refs_5_.refs_3_.refs_1_, f32[512,1024]{1,0:T(8,128)} %get-tuple-element.169.refs_7_.refs_2_, bf16[8,64,3072]{2,1,0:T(8,128)(2,1)} %bitcast.97, ...), custom_call_target="tpu_custom_call" | custom-call | flops 1000000 | bytes 1 | tf_op jit(solution)/shard_map/target_back/pallas_call | solution.py:97
  548.7 3.8 move_blocks.23
  555.5 7.9 %collective-permute-done.60 = bf16[32,4352]{1,0:T(8,128)(2,1)S(1)} collective-permute-done((bf16[32,4352]{1,0:T(8,128)(2,1)S(1)}, bf16[32,4352]{1,0:T(8,128)(2,1)S(1)}, u32[]{:S(2)}, u32[]{:S(2)}) %collective-permute-start.60) | collective-permute-done | bytes 278560 | tf_op jit(solution)/shard_map/ppermute | solution.py:391
  (286 shorter events, 148.5 us)
Async XLA Ops:
  7.2 70.7 %all-gather.4.cloned.1.call-start = ((), (), s32[]{:S(2)}) async-start(), calls=%async_computation.3 | async-start | bytes 1679360 | tf_op jit(solution)/shard_map/all_gather | solution.py:407
  19.7 30.3 %collective-permute-start.5 = (bf16[384,1024]{1,0:T(8,128)(2,1)}, bf16[384,1024]{1,0:T(8,128)(2,1)}, u32[]{:S(2)}, u32[]{:S(2)}) collective-permute-start(bf16[384,1024]{1,0:T(8,128)(2,1)} %dynamic-slice_bitcast_fusion.1), channel_id=1, source_target_pairs={{0,1},{1,0},{2,3},{3,2},{4,5},{5,4},{6,7},{7,6},{8,9},{9,8},{10,11... | collective-permute-start | bytes 2359304 | tf_op jit(solution)/shard_map/ppermute | solution.py:386
  45.3 71.0 %all-gather.6.cloned.1.call-start = ((), (), s32[]{:S(2)}) async-start(), calls=%async_computation.4 | async-start | bytes 1310720 | tf_op jit(solution)/shard_map/all_gather | solution.py:407
  54.2 26.6 %collective-permute-start.8 = (bf16[2,4,32,2048]{3,2,1,0:T(8,128)(2,1)}, bf16[2,4,32,2048]{3,2,1,0:T(8,128)(2,1)}, u32[]{:S(2)}, u32[]{:S(2)}) collective-permute-start(bf16[2,4,32,2048]{3,2,1,0:T(8,128)(2,1)} %get-tuple-element.106), channel_id=1, source_target_pairs={{0,4},{2,6},{4,0},{6,2},{8,12},{10,14},{12,8},{14,10},{16,20},{18,... | collective-permute-start | bytes 3145736 | tf_op jit(solution)/shard_map/ppermute | solution.py:382
  55.8 25.1 %collective-permute-start.7 = (bf16[2,4,32,1024]{3,2,1,0:T(8,128)(2,1)}, bf16[2,4,32,1024]{3,2,1,0:T(8,128)(2,1)}, u32[]{:S(2)}, u32[]{:S(2)}) collective-permute-start(bf16[2,4,32,1024]{3,2,1,0:T(8,128)(2,1)} %get-tuple-element.105.refs_3_), channel_id=1, source_target_pairs={{0,1},{1,0},{2,3},{3,2},{4,5},{5,4},{6,7},{7,6},{8,9},{9,8},{10,11... | collective-permute-start | bytes 1572872 | tf_op jit(solution)/shard_map/ppermute | solution.py:386
  84.6 19.8 %collective-permute-start.12 = (bf16[4,32,3072]{2,1,0:T(8,128)(2,1)}, bf16[4,32,3072]{2,1,0:T(8,128)(2,1)}, u32[]{:S(2)}, u32[]{:S(2)}) collective-permute-start(bf16[4,32,3072]{2,1,0:T(8,128)(2,1)} %get-tuple-element.111.refs_3_), channel_id=1, source_target_pairs={{0,1},{1,0},{2,3},{3,2},{4,5},{5,4},{6,7},{7,6},{8,9},{9,8},{10,11... | collective-permute-start | bytes 2359304 | tf_op jit(solution)/shard_map/ppermute | solution.py:386
  89.7 85.9 %all-gather.8.cloned.1.call-start = ((), (), s32[]{:S(2)}) async-start(), calls=%async_computation.5 | async-start | bytes 1310720 | tf_op jit(solution)/shard_map/all_gather | solution.py:407
  109.0 37.6 %collective-permute-start.14 = (bf16[2,4,32,3072]{3,2,1,0:T(8,128)(2,1)}, bf16[2,4,32,3072]{3,2,1,0:T(8,128)(2,1)S(1)}, u32[]{:S(2)}, u32[]{:S(2)}) collective-permute-start(bf16[2,4,32,3072]{3,2,1,0:T(8,128)(2,1)} %get-tuple-element.116), channel_id=1, source_target_pairs={{0,4},{2,6},{4,0},{6,2},{8,12},{10,14},{12,8},{14,10},{16,20},{18,... | collective-permute-start | bytes 4718600 | tf_op jit(solution)/shard_map/ppermute | solution.py:382
  110.5 27.8 %collective-permute-start.13 = (bf16[2,4,32,2176]{3,2,1,0:T(8,128)(2,1)}, bf16[2,4,32,2176]{3,2,1,0:T(8,128)(2,1)}, u32[]{:S(2)}, u32[]{:S(2)}) collective-permute-start(bf16[2,4,32,2176]{3,2,1,0:T(8,128)(2,1)} %get-tuple-element.112.refs_2_), channel_id=1, source_target_pairs={{0,1},{1,0},{2,3},{3,2},{4,5},{5,4},{6,7},{7,6},{8,9},{9,8},{10,11... | collective-permute-start | bytes 3342344 | tf_op jit(solution)/shard_map/ppermute | solution.py:386
  115.6 350.8 %reduce-scatter.4.cloned.1.call-start = ((), (), s32[]{:S(2)}) async-start(), calls=%async_computation.6 | async-start | bytes 1310720 | tf_op jit(solution)/shard_map/reduce_scatter | solution.py:1129
  115.7 51.5 %collective-permute-start.18 = (bf16[384,1024]{1,0:T(8,128)(2,1)}, bf16[384,1024]{1,0:T(8,128)(2,1)}, u32[]{:S(2)}, u32[]{:S(2)}) collective-permute-start(bf16[384,1024]{1,0:T(8,128)(2,1)} %gate.1.refs_5_), channel_id=1, source_target_pairs={{0,1},{1,0},{2,3},{3,2},{4,5},{5,4},{6,7},{7,6},{8,9},{9,8},{10,11... | collective-permute-start | bytes 2359304 | tf_op jit(solution)/shard_map/ppermute | solution.py:386
  119.1 48.0 %collective-permute-start.17 = (bf16[4,32,2560]{2,1,0:T(8,128)(2,1)}, bf16[4,32,2560]{2,1,0:T(8,128)(2,1)}, u32[]{:S(2)}, u32[]{:S(2)}) collective-permute-start(bf16[4,32,2560]{2,1,0:T(8,128)(2,1)} %get-tuple-element.118.refs_3_), channel_id=1, source_target_pairs={{0,1},{1,0},{2,3},{3,2},{4,5},{5,4},{6,7},{7,6},{8,9},{9,8},{10,11... | collective-permute-start | bytes 1966088 | tf_op jit(solution)/shard_map/ppermute | solution.py:386
  120.6 32.7 %collective-permute-start.16 = (bf16[4,32,1536]{2,1,0:T(8,128)(2,1)}, bf16[4,32,1536]{2,1,0:T(8,128)(2,1)}, u32[]{:S(2)}, u32[]{:S(2)}) collective-permute-start(bf16[4,32,1536]{2,1,0:T(8,128)(2,1)} %get-tuple-element.113.refs_4_.refs_1_), channel_id=1, source_target_pairs={{0,4},{2,6},{4,0},{6,2},{8,12},{10,14},{12,8},{14,10},{16,20},{18,... | collective-permute-start | bytes 1179656 | tf_op jit(solution)/shard_map/ppermute | solution.py:382
  151.2 29.2 %collective-permute-start.15 = (bf16[8,64,5248]{2,1,0:T(8,128)(2,1)}, bf16[8,64,5248]{2,1,0:T(8,128)(2,1)}, u32[]{:S(2)}, u32[]{:S(2)}) collective-permute-start(bf16[8,64,5248]{2,1,0:T(8,128)(2,1)} %bitcast.75), channel_id=1, source_target_pairs={{0,2},{2,0},{4,6},{6,4},{8,10},{10,8},{12,14},{14,12},{16,18},{18,... | collective-permute-start | bytes 16121864 | tf_op jit(solution)/shard_map/ppermute | solution.py:377
  171.1 32.1 %collective-permute-start.22 = (bf16[2,4,32,2560]{3,2,1,0:T(8,128)(2,1)}, bf16[2,4,32,2560]{3,2,1,0:T(8,128)(2,1)}, u32[]{:S(2)}, u32[]{:S(2)}) collective-permute-start(bf16[2,4,32,2560]{3,2,1,0:T(8,128)(2,1)} %get-tuple-element.126), channel_id=1, source_target_pairs={{0,4},{2,6},{4,0},{6,2},{8,12},{10,14},{12,8},{14,10},{16,20},{18,... | collective-permute-start | bytes 3932168 | tf_op jit(solution)/shard_map/ppermute | solution.py:382
  171.7 31.3 %collective-permute-start.21 = (bf16[2,4,32,1536]{3,2,1,0:T(8,128)(2,1)}, bf16[2,4,32,1536]{3,2,1,0:T(8,128)(2,1)}, u32[]{:S(2)}, u32[]{:S(2)}) collective-permute-start(bf16[2,4,32,1536]{3,2,1,0:T(8,128)(2,1)} %get-tuple-element.119.refs_2_), channel_id=1, source_target_pairs={{0,1},{1,0},{2,3},{3,2},{4,5},{5,4},{6,7},{7,6},{8,9},{9,8},{10,11... | collective-permute-start | bytes 2359304 | tf_op jit(solution)/shard_map/ppermute | solution.py:386
  178.3 30.3 %collective-permute-start.20 = (bf16[4,128,640]{2,1,0:T(8,128)(2,1)}, bf16[4,128,640]{2,1,0:T(8,128)(2,1)}, u32[]{:S(2)}, u32[]{:S(2)}) collective-permute-start(bf16[4,128,640]{2,1,0:T(8,128)(2,1)} %get-tuple-element.124.refs_3_), channel_id=1, source_target_pairs={{0,1},{1,0},{2,3},{3,2},{4,5},{5,4},{6,7},{7,6},{8,9},{9,8},{10,11... | collective-permute-start | bytes 1966088 | tf_op jit(solution)/shard_map/ppermute | solution.py:386
  179.0 29.6 %collective-permute-start.19 = (bf16[4,128,384]{2,1,0:T(8,128)(2,1)}, bf16[4,128,384]{2,1,0:T(8,128)(2,1)}, u32[]{:S(2)}, u32[]{:S(2)}) collective-permute-start(bf16[4,128,384]{2,1,0:T(8,128)(2,1)} %get-tuple-element.120.refs_3_.refs_1_), channel_id=1, source_target_pairs={{0,4},{2,6},{4,0},{6,2},{8,12},{10,14},{12,8},{14,10},{16,20},{18,... | collective-permute-start | bytes 1179656 | tf_op jit(solution)/shard_map/ppermute | solution.py:382
  212.8 28.8 %collective-permute-start.25 = (bf16[2,4,128,640]{3,2,1,0:T(8,128)(2,1)}, bf16[2,4,128,640]{3,2,1,0:T(8,128)(2,1)S(1)}, u32[]{:S(2)}, u32[]{:S(2)}) collective-permute-start(bf16[2,4,128,640]{3,2,1,0:T(8,128)(2,1)} %get-tuple-element.134), channel_id=1, source_target_pairs={{0,4},{2,6},{4,0},{6,2},{8,12},{10,14},{12,8},{14,10},{16,20},{18,... | collective-permute-start | bytes 3932168 | tf_op jit(solution)/shard_map/ppermute | solution.py:382
  213.5 43.4 %collective-permute-start.23 = (bf16[8,64,4096]{2,1,0:T(8,128)(2,1)}, bf16[8,64,4096]{2,1,0:T(8,128)(2,1)}, u32[]{:S(2)}, u32[]{:S(2)}) collective-permute-start(bf16[8,64,4096]{2,1,0:T(8,128)(2,1)} %bitcast.98), channel_id=1, source_target_pairs={{0,2},{2,0},{4,6},{6,4},{8,10},{10,8},{12,14},{14,12},{16,18},{18,... | collective-permute-start | bytes 12582920 | tf_op jit(solution)/shard_map/ppermute | solution.py:377
  213.5 28.1 %collective-permute-start.24 = (bf16[2,4,128,384]{3,2,1,0:T(8,128)(2,1)}, bf16[2,4,128,384]{3,2,1,0:T(8,128)(2,1)}, u32[]{:S(2)}, u32[]{:S(2)}) collective-permute-start(bf16[2,4,128,384]{3,2,1,0:T(8,128)(2,1)} %get-tuple-element.128.refs_7_), channel_id=1, source_target_pairs={{0,1},{1,0},{2,3},{3,2},{4,5},{5,4},{6,7},{7,6},{8,9},{9,8},{10,11... | collective-permute-start | bytes 2359304 | tf_op jit(solution)/shard_map/ppermute | solution.py:386
  246.0 33.5 %collective-permute-start.26 = (bf16[8,256,1024]{2,1,0:T(8,128)(2,1)}, bf16[8,256,1024]{2,1,0:T(8,128)(2,1)}, u32[]{:S(2)}, u32[]{:S(2)}) collective-permute-start(bf16[8,256,1024]{2,1,0:T(8,128)(2,1)} %bitcast.88), channel_id=1, source_target_pairs={{0,2},{2,0},{4,6},{6,4},{8,10},{10,8},{12,14},{14,12},{16,18},{18,... | collective-permute-start | bytes 12582920 | tf_op jit(solution)/shard_map/ppermute | solution.py:377
  307.9 28.9 %collective-permute-start.32 = (bf16[2,4,128,512]{3,2,1,0:T(8,128)(2,1)}, bf16[2,4,128,512]{3,2,1,0:T(8,128)(2,1)S(1)}, u32[]{:S(2)}, u32[]{:S(2)}) collective-permute-start(bf16[2,4,128,512]{3,2,1,0:T(8,128)(2,1)} %get-tuple-element.145.refs_5_), channel_id=1, source_target_pairs={{0,1},{1,0},{2,3},{3,2},{4,5},{5,4},{6,7},{7,6},{8,9},{9,8},{10,11... | collective-permute-start | bytes 3145736 | tf_op jit(solution)/shard_map/ppermute | solution.py:386
  308.6 28.1 %collective-permute-start.33 = (bf16[2,4,128,512]{3,2,1,0:T(8,128)(2,1)}, bf16[2,4,128,512]{3,2,1,0:T(8,128)(2,1)}, u32[]{:S(2)}, u32[]{:S(2)}) collective-permute-start(bf16[2,4,128,512]{3,2,1,0:T(8,128)(2,1)} %get-tuple-element.152), channel_id=1, source_target_pairs={{0,4},{2,6},{4,0},{6,2},{8,12},{10,14},{12,8},{14,10},{16,20},{18,... | collective-permute-start | bytes 3145736 | tf_op jit(solution)/shard_map/ppermute | solution.py:382
  336.2 21.8 %collective-permute-start.30 = (bf16[512,1024]{1,0:T(8,128)(2,1)}, bf16[512,1024]{1,0:T(8,128)(2,1)}, u32[]{:S(2)}, u32[]{:S(2)}) collective-permute-start(bf16[512,1024]{1,0:T(8,128)(2,1)} %get-tuple-element.149.refs_3_), channel_id=1, source_target_pairs={{0,2},{2,0},{4,6},{6,4},{8,10},{10,8},{12,14},{14,12},{16,18},{18,... | collective-permute-start | bytes 3145736 | tf_op jit(solution)/shard_map/ppermute | solution.py:377
  352.5 38.3 %collective-permute-start.34 = (bf16[2,4,32,2048]{3,2,1,0:T(8,128)(2,1)}, bf16[2,4,32,2048]{3,2,1,0:T(8,128)(2,1)S(1)}, u32[]{:S(2)}, u32[]{:S(2)}) collective-permute-start(bf16[2,4,32,2048]{3,2,1,0:T(8,128)(2,1)} %get-tuple-element.155.refs_5_), channel_id=1, source_target_pairs={{0,1},{1,0},{2,3},{3,2},{4,5},{5,4},{6,7},{7,6},{8,9},{9,8},{10,11... | collective-permute-start | bytes 3145736 | tf_op jit(solution)/shard_map/ppermute | solution.py:386
  353.9 36.9 %collective-permute-start.35 = (bf16[2,4,32,2048]{3,2,1,0:T(8,128)(2,1)}, bf16[2,4,32,2048]{3,2,1,0:T(8,128)(2,1)}, u32[]{:S(2)}, u32[]{:S(2)}) collective-permute-start(bf16[2,4,32,2048]{3,2,1,0:T(8,128)(2,1)} %get-tuple-element.160), channel_id=1, source_target_pairs={{0,4},{2,6},{4,0},{6,2},{8,12},{10,14},{12,8},{14,10},{16,20},{18,... | collective-permute-start | bytes 3145736 | tf_op jit(solution)/shard_map/ppermute | solution.py:382
  354.7 35.6 %collective-permute-start.36 = (bf16[4,128,512]{2,1,0:T(8,128)(2,1)S(1)}, bf16[4,128,512]{2,1,0:T(8,128)(2,1)}, u32[]{:S(2)}, u32[]{:S(2)}) collective-permute-start(bf16[4,128,512]{2,1,0:T(8,128)(2,1)S(1)} %copy-done.14), channel_id=1, source_target_pairs={{0,4},{2,6},{4,0},{6,2},{8,12},{10,14},{12,8},{14,10},{16,20},{18,... | collective-permute-start | bytes 1572872 | tf_op jit(solution)/shard_map/ppermute | solution.py:382
  356.1 34.2 %collective-permute-start.37 = (bf16[4,128,512]{2,1,0:T(8,128)(2,1)}, bf16[4,128,512]{2,1,0:T(8,128)(2,1)}, u32[]{:S(2)}, u32[]{:S(2)}) collective-permute-start(bf16[4,128,512]{2,1,0:T(8,128)(2,1)} %get-tuple-element.161), channel_id=1, source_target_pairs={{0,1},{1,0},{2,3},{3,2},{4,5},{5,4},{6,7},{7,6},{8,9},{9,8},{10,11... | collective-permute-start | bytes 1572872 | tf_op jit(solution)/shard_map/ppermute | solution.py:386
  390.3 26.2 %collective-permute-start.40 = (bf16[768,2048]{1,0:T(8,128)(2,1)}, bf16[768,2048]{1,0:T(8,128)(2,1)}, u32[]{:S(2)}, u32[]{:S(2)}) collective-permute-start(bf16[768,2048]{1,0:T(8,128)(2,1)} %get-tuple-element.167.refs_13_.refs_1_), channel_id=1, source_target_pairs={{0,2},{2,0},{4,6},{6,4},{8,10},{10,8},{12,14},{14,12},{16,18},{18,... | collective-permute-start | bytes 9437192 | tf_op jit(solution)/shard_map/ppermute | solution.py:377
  390.3 26.2 %collective-permute-start.41 = (bf16[768,2048]{1,0:T(8,128)(2,1)}, bf16[768,2048]{1,0:T(8,128)(2,1)}, u32[]{:S(2)}, u32[]{:S(2)}) collective-permute-start(bf16[768,2048]{1,0:T(8,128)(2,1)} %get-tuple-element.166.refs_14_.refs_1_), channel_id=1, source_target_pairs={{0,2},{2,0},{4,6},{6,4},{8,10},{10,8},{12,14},{14,12},{16,18},{18,... | collective-permute-start | bytes 9437192 | tf_op jit(solution)/shard_map/ppermute | solution.py:377
  396.7 41.0 %collective-permute-start.38 = (bf16[4,32,2048]{2,1,0:T(8,128)(2,1)}, bf16[4,32,2048]{2,1,0:T(8,128)(2,1)S(1)}, u32[]{:S(2)}, u32[]{:S(2)}) collective-permute-start(bf16[4,32,2048]{2,1,0:T(8,128)(2,1)} %get-tuple-element.162.refs_7_), channel_id=1, source_target_pairs={{0,4},{2,6},{4,0},{6,2},{8,12},{10,14},{12,8},{14,10},{16,20},{18,... | collective-permute-start | bytes 1572872 | tf_op jit(solution)/shard_map/ppermute | solution.py:382
  397.5 41.8 %collective-permute-start.39 = (bf16[4,32,2048]{2,1,0:T(8,128)(2,1)}, bf16[4,32,2048]{2,1,0:T(8,128)(2,1)S(1)}, u32[]{:S(2)}, u32[]{:S(2)}) collective-permute-start(bf16[4,32,2048]{2,1,0:T(8,128)(2,1)} %get-tuple-element.165), channel_id=1, source_target_pairs={{0,1},{1,0},{2,3},{3,2},{4,5},{5,4},{6,7},{7,6},{8,9},{9,8},{10,11... | collective-permute-start | bytes 1572872 | tf_op jit(solution)/shard_map/ppermute | solution.py:386
  412.3 46.7 %collective-permute-start.47 = (bf16[2,4,32,2048]{3,2,1,0:T(8,128)(2,1)}, bf16[2,4,32,2048]{3,2,1,0:T(8,128)(2,1)}, u32[]{:S(2)}, u32[]{:S(2)}) collective-permute-start(bf16[2,4,32,2048]{3,2,1,0:T(8,128)(2,1)} %get-tuple-element.170.refs_17_), channel_id=1, source_target_pairs={{0,1},{1,0},{2,3},{3,2},{4,5},{5,4},{6,7},{7,6},{8,9},{9,8},{10,11... | collective-permute-start | bytes 3145736 | tf_op jit(solution)/shard_map/ppermute | solution.py:386
  413.7 94.4 %reduce-scatter.6.cloned.1.call-start = ((), (), s32[]{:S(2)}) async-start(), calls=%async_computation.7 | async-start | bytes 1310720 | tf_op jit(solution)/shard_map/reduce_scatter | solution.py:1129
  416.5 61.6 %collective-permute-start.44 = (bf16[2,2,4,32,256]{4,3,2,1,0:T(8,128)(2,1)}, bf16[2,2,4,32,256]{4,3,2,1,0:T(8,128)(2,1)}, u32[]{:S(2)}, u32[]{:S(2)}) collective-permute-start(bf16[2,2,4,32,256]{4,3,2,1,0:T(8,128)(2,1)} %slice_bitcast_fusion), channel_id=1, source_target_pairs={{0,2},{2,0},{4,6},{6,4},{8,10},{10,8},{12,14},{14,12},{16,18},{18,... | collective-permute-start | bytes 786440 | tf_op jit(solution)/shard_map/ppermute | solution.py:377
  416.5 73.5 %collective-permute-start.43 = (bf16[512,1024]{1,0:T(8,128)(2,1)}, bf16[512,1024]{1,0:T(8,128)(2,1)}, u32[]{:S(2)}, u32[]{:S(2)}) collective-permute-start(bf16[512,1024]{1,0:T(8,128)(2,1)} %get-tuple-element.172.refs_3_), channel_id=1, source_target_pairs={{0,2},{2,0},{4,6},{6,4},{8,10},{10,8},{12,14},{14,12},{16,18},{18,... | collective-permute-start | bytes 3145736 | tf_op jit(solution)/shard_map/ppermute | solution.py:377
  437.7 25.5 %collective-permute-start.48 = (bf16[2,4,32,2048]{3,2,1,0:T(8,128)(2,1)}, bf16[2,4,32,2048]{3,2,1,0:T(8,128)(2,1)}, u32[]{:S(2)}, u32[]{:S(2)}) collective-permute-start(bf16[2,4,32,2048]{3,2,1,0:T(8,128)(2,1)} %get-tuple-element.171.refs_4_), channel_id=1, source_target_pairs={{0,4},{2,6},{4,0},{6,2},{8,12},{10,14},{12,8},{14,10},{16,20},{18,... | collective-permute-start | bytes 3145736 | tf_op jit(solution)/shard_map/ppermute | solution.py:382
  439.2 39.7 %collective-permute-start.45 = (bf16[768,1024]{1,0:T(8,128)(2,1)}, bf16[768,1024]{1,0:T(8,128)(2,1)}, u32[]{:S(2)}, u32[]{:S(2)}) collective-permute-start(bf16[768,1024]{1,0:T(8,128)(2,1)} %memory_back.2.refs_7_), channel_id=1, source_target_pairs={{0,1},{1,0},{2,3},{3,2},{4,5},{5,4},{6,7},{7,6},{8,9},{9,8},{10,11... | collective-permute-start | bytes 4718600 | tf_op jit(solution)/shard_map/ppermute | solution.py:386
  443.6 123.6 %reduce-scatter.8.cloned.1.call-start = ((), (), s32[]{:S(2)}) async-start(), calls=%async_computation.8 | async-start | bytes 1310720 | tf_op jit(solution)/shard_map/reduce_scatter | solution.py:1129
  476.0 32.1 %collective-permute-start.51 = (bf16[2,4,32,1536]{3,2,1,0:T(8,128)(2,1)}, bf16[2,4,32,1536]{3,2,1,0:T(8,128)(2,1)S(1)}, u32[]{:S(2)}, u32[]{:S(2)}) collective-permute-start(bf16[2,4,32,1536]{3,2,1,0:T(8,128)(2,1)} %get-tuple-element.180.refs_5_), channel_id=1, source_target_pairs={{0,1},{1,0},{2,3},{3,2},{4,5},{5,4},{6,7},{7,6},{8,9},{9,8},{10,11... | collective-permute-start | bytes 2359304 | tf_op jit(solution)/shard_map/ppermute | solution.py:386
  476.9 31.2 %collective-permute-start.52 = (bf16[2,4,32,1536]{3,2,1,0:T(8,128)(2,1)}, bf16[2,4,32,1536]{3,2,1,0:T(8,128)(2,1)}, u32[]{:S(2)}, u32[]{:S(2)}) collective-permute-start(bf16[2,4,32,1536]{3,2,1,0:T(8,128)(2,1)} %get-tuple-element.187), channel_id=1, source_target_pairs={{0,4},{2,6},{4,0},{6,2},{8,12},{10,14},{12,8},{14,10},{16,20},{18,... | collective-permute-start | bytes 2359304 | tf_op jit(solution)/shard_map/ppermute | solution.py:382
  478.1 28.7 %collective-permute-start.53 = (bf16[4,32,2048]{2,1,0:T(8,128)(2,1)S(1)}, bf16[4,32,2048]{2,1,0:T(8,128)(2,1)}, u32[]{:S(2)}, u32[]{:S(2)}) collective-permute-start(bf16[4,32,2048]{2,1,0:T(8,128)(2,1)S(1)} %copy-done.15), channel_id=1, source_target_pairs={{0,4},{2,6},{4,0},{6,2},{8,12},{10,14},{12,8},{14,10},{16,20},{18,... | collective-permute-start | bytes 1572872 | tf_op jit(solution)/shard_map/ppermute | solution.py:382
  478.9 29.2 %collective-permute-start.54 = (bf16[4,32,2048]{2,1,0:T(8,128)(2,1)}, bf16[4,32,2048]{2,1,0:T(8,128)(2,1)}, u32[]{:S(2)}, u32[]{:S(2)}) collective-permute-start(bf16[4,32,2048]{2,1,0:T(8,128)(2,1)} %get-tuple-element.188), channel_id=1, source_target_pairs={{0,1},{1,0},{2,3},{3,2},{4,5},{5,4},{6,7},{7,6},{8,9},{9,8},{10,11... | collective-permute-start | bytes 1572872 | tf_op jit(solution)/shard_map/ppermute | solution.py:386
  495.1 20.7 %collective-permute-start.49 = (bf16[2,4,32,640]{3,2,1,0:T(8,128)(2,1)}, bf16[2,4,32,640]{3,2,1,0:T(8,128)(2,1)}, u32[]{:S(2)}, u32[]{:S(2)}) collective-permute-start(bf16[2,4,32,640]{3,2,1,0:T(8,128)(2,1)} %get-tuple-element.182.refs_12_), channel_id=1, source_target_pairs={{0,1},{1,0},{2,3},{3,2},{4,5},{5,4},{6,7},{7,6},{8,9},{9,8},{10,11... | collective-permute-start | bytes 983048 | tf_op jit(solution)/shard_map/ppermute | solution.py:386
  533.4 22.1 %collective-permute-start.59 = (bf16[32,4352]{1,0:T(8,128)(2,1)S(1)}, bf16[32,4352]{1,0:T(8,128)(2,1)S(1)}, u32[]{:S(2)}, u32[]{:S(2)}) collective-permute-start(bf16[32,4352]{1,0:T(8,128)(2,1)S(1)} %get-tuple-element.232), channel_id=1, source_target_pairs={{0,8},{2,10},{4,12},{6,14},{8,0},{10,2},{12,4},{14,6},{16,24},{18,... | collective-permute-start | bytes 835592 | tf_op jit(solution)/shard_map/ppermute | solution.py:391
  534.2 29.1 %collective-permute-start.60 = (bf16[32,4352]{1,0:T(8,128)(2,1)S(1)}, bf16[32,4352]{1,0:T(8,128)(2,1)S(1)}, u32[]{:S(2)}, u32[]{:S(2)}) collective-permute-start(bf16[32,4352]{1,0:T(8,128)(2,1)S(1)} %get-tuple-element.234), channel_id=1, source_target_pairs={{0,16},{2,18},{4,20},{6,22},{8,24},{10,26},{12,28},{14,30},{16,0},... | collective-permute-start | bytes 835592 | tf_op jit(solution)/shard_map/ppermute | solution.py:391
  535.6 27.7 %collective-permute-start.61 = (bf16[32,4352]{1,0:T(8,128)(2,1)S(1)}, bf16[32,4352]{1,0:T(8,128)(2,1)S(1)}, u32[]{:S(2)}, u32[]{:S(2)}) collective-permute-start(bf16[32,4352]{1,0:T(8,128)(2,1)S(1)} %get-tuple-element.233), channel_id=1, source_target_pairs={{0,24},{2,26},{4,28},{6,30},{8,16},{10,18},{12,20},{14,22},{16,8},... | collective-permute-start | bytes 835592 | tf_op jit(solution)/shard_map/ppermute | solution.py:391
  (64 other events, 498.7 us)
Sparse Core Ops, SparseCore 0:
  45.4 32.4 all-gather.3
  89.8 25.0 all-gather.5
  116.5 27.4 all-gather.7
  413.8 25.1 reduce-scatter.3
  443.7 25.1 reduce-scatter.5
  521.1 34.0 reduce-scatter.7

commit v3 on v2

--- a/solution.py
+++ b/solution.py
@@ -12,7 +12,7 @@
 ALPHA = 300.0**0.25
 NEG_LARGE = -1e30
 EPSILON = 1e-05
-VMEM_BYTES = 62 * 1024 * 1024
+VMEM_BYTES = 64 * 1024 * 1024 - 128 * 1024
 SCALE = HD**-0.5
 BF16 = jnp.bfloat16
 F32 = jnp.float32
@@ -398,26 +398,12 @@
 
 def place_bits():
     dp, mem = lax.axis_index("dp"), lax.axis_index("mem")
-    return jnp.stack([(dp >> 1) & 1, dp & 1, mem]).astype(jnp.int32)
-
-
-def outer_gather(shard, direct):
-    outer, rows = lax.axis_size("dp") // 4, shard.shape[0]
-    if not direct:
-        stacked = lax.all_gather(shard, "dp", axis_index_groups=outer_groups(), axis=0, tiled=True)
-        return stacked.reshape(outer, rows, -1)
-    place = lax.axis_index("dp") >> 2
-    blocks = jnp.stack([shard] + [swap_outer(shard, far) for far in range(1, outer)])
-    bit = 1
-    while bit < outer:
-        turned = jnp.stack([blocks[i ^ bit] for i in range(outer)])
-        blocks = jnp.where((place & bit) != 0, turned, blocks)
-        bit *= 2
-    return blocks
-
-
-FIRST = (swap_next, swap_mem)
-SECOND = (swap_mem, swap_next)
+    return jnp.stack([(dp >> 1) & 1, dp & 1, mem, dp >> 2]).astype(jnp.int32)
+
+
+def outer_gather(shard):
+    stacked = lax.all_gather(shard, "dp", axis_index_groups=outer_groups(), axis=0, tiled=True)
+    return stacked.reshape(-1, *shard.shape)
 
 
 def gate(order, bits, arrays):
@@ -452,22 +438,29 @@
             self.aliases[1 + self.source(held)] = len(self.shapes) - 1
         return len(self.shapes) - 1
 
+    def passed(self, array):
+        return self.target(array.shape, array)
+
     def move(self, source, source_at, shape, *goals):
         self.moves.append((source, source_at, shape, goals))
 
     def run(self):
         moves, n_in, n_out = self.moves, len(self.sources), len(self.shapes)
-        most = max(len(move[3]) for move in moves)
+        most = max([len(move[3]) for move in moves] + [0])
 
         def kernel(bits_ref, *refs):
-            bits = [bits_ref[i] for i in range(3)]
+            bits = [bits_ref[i] for i in range(4)]
             taken, given = refs[:n_in], refs[n_in : n_in + n_out]
             slots, sems = refs[n_in + n_out : -1], refs[-1]
             loads, stores = [], []
             for number, (source, source_at, _, goals) in enumerate(moves):
                 slot = slots[number]
                 loads.append(
-                    pltpu.make_async_copy(taken[source].at[source_at], slot, sems.at[0, number])
+                    pltpu.make_async_copy(
+                        taken[source].at[source_at(bits) if callable(source_at) else source_at],
+                        slot,
+                        sems.at[0, number],
+                    )
                 )
                 stores.append(
                     [
@@ -495,7 +488,7 @@
             [pl.BlockSpec(memory_space=pltpu.HBM)] * n_out,
             [jax.ShapeDtypeStruct(shape, BF16) for shape in self.shapes],
             [pltpu.VMEM(shape, BF16) for _, _, shape, _ in moves]
-            + [pltpu.SemaphoreType.DMA((1 + most, len(moves)))],
+            + [pltpu.SemaphoreType.DMA((1 + most, max(1, len(moves))))],
             None,
             self.aliases,
         )
@@ -529,31 +522,44 @@
     )
 
 
+FIRST = (swap_next, swap_mem)
+SECOND = (swap_mem, swap_next)
+
+
 class Wave:
-    def __init__(self, order, bits, shard, cut, direct):
-        self.order, self.bits, self.cut, self.direct = order, bits, cut, direct
+    def __init__(self, shard, windows, direct):
+        self.windows = [(pl.ds(start, size), kind) for start, size, kind in windows]
         self.rows, self.columns = shard.shape
-        self.stacked = outer_gather(shard, direct)
-        self.outer = self.stacked.shape[0]
-        self.windows = (pl.ds(0, cut), pl.ds(cut, self.columns - cut))
+        self.outer = lax.axis_size("dp") // 4
+        if direct:
+            self.shards = [shard] + [swap_outer(shard, far) for far in range(1, self.outer)]
+        else:
+            self.stacked = outer_gather(shard)
+        self.direct = direct
 
     def first(self, moves):
         def send(parts):
-            self.pairs = [(part, FIRST[half](part)) for half, part in enumerate(parts)]
-
-        if self.direct:
-            send((self.stacked[:, :, : self.cut], self.stacked[:, :, self.cut :]))
+            self.pairs = [(part, FIRST[kind](part)) for part, (_, kind) in zip(parts, self.windows)]
+
+        if not self.direct and len(self.windows) == 1:
+            target = moves.passed(self.stacked)
+            moves.then.append(lambda filled: send([filled[target]]))
             return
-        source = moves.source(self.stacked)
-        targets = [moves.target((self.outer, self.rows, w.size)) for w in self.windows]
-        for place in range(self.outer):
-            for target, window in zip(targets, self.windows):
+        targets = [moves.target((self.outer, self.rows, w.size)) for w, _ in self.windows]
+        sources = [moves.source(part) for part in (self.shards if self.direct else [self.stacked])]
+        for block in range(self.outer):
+            for target, (window, _) in zip(targets, self.windows):
                 shape = (self.rows, window.size)
-                moves.move(source, (place, slice(None), window), shape, (target, (place,)))
+                if self.direct:
+                    goal = (target, lambda bits, block=block: (bits[3] ^ block,))
+                    moves.move(sources[block], (slice(None), window), shape, goal)
+                else:
+                    goal = (target, (block,))
+                    moves.move(sources[0], (block, slice(None), window), shape, goal)
         moves.then.append(lambda filled: send([filled[target] for target in targets]))
 
-    def place(self, half, second, first, block, window):
-        near, mem = (first, second) if half == 0 else (second, first)
+    def place(self, kind, second, first, block, window):
+        near, mem = (first, second) if kind == 0 else (second, first)
         return lambda bits: (block, bits[0] ^ near, bits[2] ^ mem, slice(None), window)
 
     def second(self, moves):
@@ -561,26 +567,28 @@
         targets = [moves.target((2, *pair[0].shape)) for pair in self.pairs]
         own = moves.target((self.outer, 2, 2, self.rows, self.columns))
         for block in range(self.outer):
-            for half, window in enumerate(self.windows):
+            for number, (window, kind) in enumerate(self.windows):
                 for side in range(2):
-                    goal = (targets[half], (side, block))
-                    again = (own, self.place(half, 0, side, block, window))
+                    goal = (targets[number], (side, block))
+                    again = (own, self.place(kind, 0, side, block, window))
                     shape = (self.rows, window.size)
-                    moves.move(sources[half][side], (block,), shape, goal, again)
+                    moves.move(sources[number][side], (block,), shape, goal, again)
 
         def send(filled):
             self.own = filled[own]
-            self.far = [SECOND[half](filled[target]) for half, target in enumerate(targets)]
+            self.far = [
+                SECOND[kind](filled[target]) for target, (_, kind) in zip(targets, self.windows)
+            ]
 
         moves.then.append(send)
 
     def third(self, moves):
         own = moves.target(self.own.shape, self.own)
-        for half, window in enumerate(self.windows):
-            source = moves.source(self.far[half])
+        for number, (window, kind) in enumerate(self.windows):
+            source = moves.source(self.far[number])
             for block in range(self.outer):
                 for side in range(2):
-                    goal = (own, self.place(half, 1, side, block, window))
+                    goal = (own, self.place(kind, 1, side, block, window))
                     moves.move(source, (side, block), (self.rows, window.size), goal)
 
         def send(filled):
@@ -1083,20 +1091,20 @@
 
 
 class Spread:
-    def __init__(self, parts):
-        self.kept = (parts[1], parts[3])
-        self.once = [FIRST_BACK[half](parts[2 * half]) for half in range(2)]
+    def __init__(self, parts, kinds):
+        self.kinds, self.kept = kinds, parts[1::2]
+        self.once = [FIRST_BACK[kind](part) for part, kind in zip(parts[0::2], kinds)]
 
     def second(self):
-        return [[(self.kept[half], (1,)), (self.once[half], (1,))] for half in range(2)]
+        return [[(kept, (1,)), (once, (1,))] for kept, once in zip(self.kept, self.once)]
 
     def send(self, sent):
-        self.twice = [SECOND_BACK[half](part) for half, part in enumerate(sent)]
+        self.twice = [SECOND_BACK[kind](part) for part, kind in zip(sent, self.kinds)]
 
     def third(self):
         return [
-            [(self.kept[half], (0,)), (self.once[half], (0,)), (self.twice[half], ())]
-            for half in range(2)
+            [(kept, (0,)), (once, (0,)), (twice, ())]
+            for kept, once, twice in zip(self.kept, self.once, self.twice)
         ]
 
 
@@ -1119,8 +1127,10 @@
             sums.append((group, len(shapes) - 1, columns))
             shapes[-1] = (outer, rows, columns + block_shape(group)[2])
     filled = add_blocks(order, bits, sums, shapes)
-    for number, wave in enumerate(seconds):
-        wave.send(filled[2 * number : 2 * number + 2])
+    start = 0
+    for wave in seconds:
+        wave.send(filled[start : start + len(wave.kinds)])
+        start += len(wave.kinds)
     return filled[joined:]
 
 
@@ -1131,11 +1141,48 @@
     )
 
 
-def outer_sum_direct(joined):
+def outer_swaps(joined):
     place = lax.axis_index("dp") >> 2
     block = lambda far: lax.dynamic_index_in_dim(joined, place ^ far, 0, False)
-    parts = [block(0)] + [swap_outer(block(far), far) for far in range(1, joined.shape[0])]
-    return sum(part.astype(F32) for part in parts)
+    return [swap_outer(block(far), far) for far in range(1, joined.shape[0])]
+
+
+def last_shards(order, bits, joined, others, summed, spans):
+    outer, rows, columns = joined.shape
+    widths = [sum(size for _, _, size in span) for span in spans]
+
+    def kernel(bits_ref, joined_ref, *refs):
+        parts, refs = refs[: len(others)], refs[len(others) :]
+        summed_ref, refs = refs[0], refs[1:]
+        targets, (held, sem) = refs[:-2], refs[-2:]
+        load = pltpu.make_async_copy(joined_ref.at[bits_ref[3]], held, sem)
+        load.start()
+        load.wait()
+        total = held[...].astype(F32)
+        for ref in parts:
+            total += ref[...].astype(F32)
+        for target, span in zip(targets, spans):
+            at = 0
+            for wave, start, size in span:
+                if wave == 0:
+                    values = total[:, start : start + size]
+                else:
+                    values = summed_ref[:, start : start + size].astype(F32)
+                target[:, at : at + size] = values
+                at += size
+
+    return order.launch(
+        kernel,
+        "last_shards",
+        [bits, joined, *others, summed],
+        [pl.BlockSpec(memory_space=pltpu.HBM)]
+        + [pl.BlockSpec(memory_space=pltpu.VMEM)] * (len(others) + 1),
+        [pl.BlockSpec(memory_space=pltpu.VMEM)] * len(spans),
+        [jax.ShapeDtypeStruct((rows, width), F32) for width in widths],
+        [pltpu.VMEM((rows, columns), BF16), pltpu.SemaphoreType.DMA],
+        None,
+        {},
+    )
 
 
 FIRST_BACK = (swap_mem, swap_next)
@@ -1180,16 +1227,16 @@
         (ffn_out,),
     ]
     if staged:
-        shards = cast_shards(order, bits, groups[:1])
+        shards = list(cast_shards(order, bits, groups))
     else:
         shards = [jnp.concatenate([part.astype(BF16) for part in group], axis=1) for group in groups]
 
-    def gather(index, cut, direct=False):
+    def gather(index, windows, direct=False):
         shard = shards[index]
         widths = [part.shape[1] for part in groups[index]]
         starts = [sum(widths[:i]) for i in range(len(widths))]
         if staged:
-            wave = Wave(order, bits, shard, cut, direct)
+            wave = Wave(shard, windows, direct)
             return [Weight(wave, at, size) for at, size in zip(starts, widths)]
         full = lax.all_gather(shard, both, axis=0, tiled=True)
         rows = full.shape[0] // 16
@@ -1244,19 +1291,42 @@
 
     mem_rows = memory_in[0, :, 0]
     mem_live = memory_mask[0, :, 0]
-    near_rows = at_mem(mem_rows, own_index)
     near_live = at_mem(mem_live, own_index)
     far_live = swap_mem(at_mem(mem_live, 1 - own_index))
-    sent_rows = [at_mem(mem_rows[:, slot], 1 - own_index) for slot in range(slot_count)]
-
-    (w_qkv,) = gather(0, model_width, True)
+    piece_shape = (mem_piece, model_width)
+    if staged:
+        moves = Moves(order, bits)
+        source, near = moves.source(mem_rows), moves.target((slot_count, *piece_shape))
+        sent = [moves.target(piece_shape) for _ in range(slot_count)]
+        for slot in range(slot_count):
+            at_far = lambda bits, slot=slot: (1 - bits[2], slot)
+            at_near = lambda bits, slot=slot: (bits[2], slot)
+            moves.move(source, at_far, piece_shape, (sent[slot], (slice(None),)))
+            moves.move(source, at_near, piece_shape, (near, (slot,)))
+        given = {}
+        moves.then.append(lambda filled: given.update(near=filled[near], sent=[filled[t] for t in sent]))
+        moves.run()
+        near_rows, sent_rows = given["near"], given["sent"]
+    else:
+        near_rows = at_mem(mem_rows, own_index)
+        sent_rows = [at_mem(mem_rows[:, slot], 1 - own_index) for slot in range(slot_count)]
+
+    qkv_half = 3 * model_width // 2
+    (w_qkv,) = gather(0, [(0, qkv_half, 0), (qkv_half, qkv_half, 1)], True)
     far_parts = [swap_mem(sent_rows[0])]
     if staged:
-        order.before(w_qkv.wave.stacked)
-        shards += cast_shards(order, bits, groups[1:])
-    w_cq, w_co, w_norm, w_ckv, w_so = gather(1, 2 * model_width + LANES)
-    (w_in,) = gather(2, 3 * model_width // 2)
-    (w_out,) = gather(3, 3 * model_width // 8)
+        order.before(far_parts[0], far_live)
+        moves = Moves(order, bits)
+        w_qkv.wave.first(moves)
+        places = [moves.passed(shard) for shard in shards[1:]]
+        moves.then.append(lambda filled: shards.__setitem__(slice(1, None), [filled[i] for i in places]))
+        moves.run()
+    lead = 5 * model_width // 2
+    w_cq, w_co, w_norm, w_ckv, w_so = gather(
+        1, [(0, lead, 0), (lead, 5 * model_width + LANES - lead, 1)]
+    )
+    (w_in,) = gather(2, [(0, ffn_in.shape[1], 0)])
+    (w_out,) = gather(3, [(0, model_width, 1)])
 
     bucket = pick_entry(bucket_ids[0], own_index)
     lengths = target_lengths[0, 0]
@@ -1273,11 +1343,8 @@
             moves = Moves(order, bits)
             for weight, name in wanted:
                 getattr(weight.wave, name)(moves)
-            if moves.moves:
-                moves.run()
-
-    steps((w_qkv, "first"))
-    order.before(far_parts[0], far_live)
+            moves.run()
+
     steps((w_qkv, "second"))
     order.part()
     first_turned = Turned(target_in, near_flat)
@@ -1285,10 +1352,10 @@
     order.part()
     steps((w_qkv, "third"))
     first_turned.due()
+    order.part()
+    steps((w_ckv, "second"))
     (united,) = project(order, "self_project", bits, w_qkv, [target_in], 1024)
     far_parts += [swap_mem(part) for part in gate(order, bits, sent_rows[1:])]
-    order.part()
-    steps((w_ckv, "second"))
     steps((w_in, "first"))
     self_mixed, self_log = self_forward(order, self_meta, united)
     far_flat = jnp.concatenate(far_parts, axis=0)
@@ -1296,26 +1363,26 @@
     steps((w_ckv, "third"))
     order.before(*far_parts[1:])
     order.part()
-    steps((w_in, "second"))
     steps((w_out, "first"))
     table = norm_table(order, bits, w_norm)
     near_kv, far_kv = project(order, "cross_project", bits, w_ckv, [near_flat, far_flat], 1024)
     near_kv, far_kv = near_kv.reshape(slotted), far_kv.reshape(slotted)
+    order.part()
+    steps((w_in, "second"), (w_out, "second"))
     sum_one, first_out, first_low, cross_query = mix_norm(
         order, "self_mix", bits, w_so, self_mixed, target_in, table, 0, w_cq
     )
+    cross_mixed, cross_log = cross_forward(
+        order, cross_meta, cross_query, near_kv, far_kv, key_bias[:, None, :]
+    )
+    sum_two, second_out, second_low = mix_norm(
+        order, "cross_mix", bits, w_co, cross_mixed, first_out, table, 1
+    )
     order.part()
     steps((w_in, "third"))
+    later = Turned(self_mixed, first_low, cross_mixed, second_low, far_flat)
     order.part()
-    steps((w_out, "second"))
-    cross_mixed, cross_log = cross_forward(
-        order, cross_meta, cross_query, near_kv, far_kv, key_bias[:, None, :]
-    )
-    sum_two, second_out, second_low = mix_norm(
-        order, "cross_mix", bits, w_co, cross_mixed, first_out, table, 1
-    )
     steps((w_out, "third"))
-    later = Turned(self_mixed, first_low, cross_mixed, second_low, far_flat)
     activated, slope = feed_in(order, bits, w_in, second_low)
     later.due()
     hidden = Turned(activated)
@@ -1332,9 +1399,9 @@
 
     shards = {}
 
-    def spread(name, parts):
+    def spread(name, parts, kinds):
         if staged:
-            return Spread(parts)
+            return Spread(parts, kinds)
         shards[name] = whole_sum(parts)
         return None
 
@@ -1346,7 +1413,7 @@
                 shards[name] = outer_sum(part)
 
     out_grad.take(grad_ffn)
-    out_wave = spread("out", out_grad.make(model_width // 2))
+    out_wave = spread("out", out_grad.make(model_width // 2), (0, 1))
     grad_hidden = feed_back(order, bits, w_out, grad_ffn, slope)
     in_grad.take(grad_hidden)
     grad_two, grad_cross_out, grad_cross_mixed, stats_two = norm_back(
@@ -1355,7 +1422,7 @@
     co_grad.take(grad_cross_out)
     order.part()
     advance([out_wave])
-    in_wave = spread("in", in_grad.make(2 * model_width))
+    in_wave = spread("in", in_grad.make(2 * model_width), (0, 1))
     pair_width = 2 * model_width
     near_parts = co_grad.make(place=(0, 0, pair_width))
     grad_query_low, grad_near_kv, grad_far_kv = cross_backward(
@@ -1393,11 +1460,10 @@
         own = (own.astype(F32) + swap_core(other).astype(F32)).astype(BF16)
         norm_grads = (own[..., :LANES], own[..., LANES:])
         near_parts = cq_grad.make(place=(0, model_width, pair_width), held=near_parts)
-        mid_wave = spread("mid", [*near_parts, *ckv_grad.make(place=(1, 0, pair_width))])
+        mid_parts = [*near_parts, *ckv_grad.make(place=(1, 0, pair_width))]
     else:
-        parts = [near_parts, cq_grad.make(), ckv_grad.make()]
-        mid_wave = spread("mid", jnp.concatenate(parts, axis=1))
-    grad_far = swap_mem(memory_back(grad_far_kv))
+        mid_parts = jnp.concatenate([near_parts, cq_grad.make(), ckv_grad.make()], axis=1)
+    mid_wave = spread("mid", mid_parts, (0, 1))
     order.part()
     advance([], [("in", in_wave)])
     grad_united = self_backward(
@@ -1413,28 +1479,31 @@
     qkv_grad.take(grad_united)
     order.part()
     advance([mid_wave])
+    qkv_wave = spread("qkv", qkv_grad.make(qkv_half), (0, 1))
     if staged:
-        order.before(shards["out"])
-    qkv_wave = spread("qkv", qkv_grad.make(w_qkv.width // 2))
-    order.before(grad_far)
-    grad_near = memory_back(grad_near_kv)
+        order.before(shards["out"], shards["in"])
+        order.part()
+        advance([], [("mid", mid_wave)])
     half_width = model_width // 2
     if staged:
-        so_wave = spread("so", so_grad.make(half_width, extra=norm_grads))
+        so_wave = spread("so", so_grad.make(half_width, extra=norm_grads), (0, 1))
     else:
         part = so_grad.make()
         columns = [part[:, :half_width], norm_grads[:, :LANES], part[:, half_width:], norm_grads[:, LANES:]]
-        so_wave = spread("so", jnp.concatenate(columns, axis=1))
+        so_wave = spread("so", jnp.concatenate(columns, axis=1), (0, 1))
+    split = half_width + LANES
+    grad_far = memory_back(grad_far_kv)
     if staged:
-        order.before(shards["in"])
         order.part()
-        advance([qkv_wave], [("mid", mid_wave)])
+        advance([qkv_wave, so_wave])
+        (grad_far,) = gate(order, bits, [grad_far])
+    grad_far = swap_mem(grad_far)
+    grad_near = memory_back(grad_near_kv)
     if staged:
-        advance([so_wave])
+        order.before(shards["mid"])
+        order.part()
         (joined,) = spread_steps(order, bits, [], [so_wave, qkv_wave], True)
-        last = outer_sum_direct(joined)
-        split = 2 * (half_width + LANES)
-        shards["so"], shards["qkv"] = last[:, :split], last[:, split:]
+        others = outer_swaps(joined)
     target_grad = input_back(
         order,
         "target_back",
@@ -1444,7 +1513,13 @@
         grad_one,
         [(0, start, start, model_width) for start in range(0, w_qkv.width, model_width)],
     )
+    so_spans = [(0, 0, half_width), (0, split, half_width)]
+    norm_spans = [[(0, half_width, 3)], [(0, split + half_width, 3)]]
+    mid_spans = [[(1, i * model_width, model_width)] for i in range(2)]
+    mid_spans.append([(1, 2 * model_width, 2 * model_width)])
+    spans = [[(0, 2 * split, 2 * qkv_half)], so_spans, *norm_spans, *mid_spans]
     if staged:
+        last = last_shards(order, bits, joined, others, shards["mid"], spans)
         moves = Moves(order, bits)
         target = moves.target((2, *near_flat.shape))
         for number, part in enumerate((grad_near, grad_far)):
@@ -1456,24 +1531,26 @@
     else:
         grad_pair = jnp.stack((grad_near, grad_far))
         grad_pair = jnp.where(own_index == 0, grad_pair, grad_pair[::-1])
-    qkv_shard = shards["qkv"]
-    memory_grad = grad_pair.reshape(1, pieces, 1, *near_rows.shape)
-    so_shard, mid_shard = shards["so"], shards["mid"].astype(F32)
-    split = half_width + LANES
+        sources = (jnp.concatenate((shards["so"], shards["qkv"]), axis=1), shards["mid"])
+        last = [
+            jnp.concatenate([sources[w][:, at : at + size] for w, at, size in span], axis=1)
+            for span in spans
+        ]
+    qkv_shard, so_shard, gains, biases, co_shard, cq_shard, ckv_shard = last
 
     return (
         layer_out,
         target_grad,
-        memory_grad,
+        grad_pair.reshape(1, pieces, 1, *near_rows.shape),
         qkv_shard,
-        jnp.concatenate((so_shard[:, :half_width], so_shard[:, split : split + half_width]), axis=1),
-        mid_shard[:, model_width : 2 * model_width],
-        mid_shard[:, 2 * model_width :],
-        mid_shard[:, :model_width],
+        so_shard,
+        cq_shard,
+        ckv_shard,
+        co_shard,
         shards["in"].astype(F32),
         shards["out"].astype(F32),
-        so_shard[:, half_width : half_width + 3],
-        so_shard[:, split + half_width : split + half_width + 3],
+        gains,
+        biases,
     )
 
 

time: 589 us -> 554 us (0.941)
  local copies, waits for them, and re-layouts: 35.9 us -> 16.2 us
  waiting for transfers between devices: 101 us -> 90.6 us
    ppermute x22 -> x20, waiting for transfers between devices: 24.1 us -> 38 us  [swap_mem(): return lax.ppermute(values, 'mem', [(0, 1), (1, 0)])]
    ppermute x6, waiting for transfers between devices: 21 us -> 7.4 us  [swap_outer(): return lax.ppermute(values, 'dp', [(i, i ^ 4 * far) for i in range(size)])]
    slice x9 -> x0, local copies, waits for them, and re-layouts: 9.38 us -> none  [the longest x1 3.54 us: per_device(): mem_rows[:, slot]]
    ppermute x18 -> x16, waiting for transfers between devices: 35.4 us -> 26.3 us  [swap_next(): return lax.ppermute(values, 'dp', [(i, i ^ 2) for i in range(size)])]
    unnamed x93 -> x27, local copies, waits for them, and re-layouts: 13.9 us -> 6.09 us
    ppermute x18 -> x16, starting transfers between devices: 21.1 us -> 16.8 us  [swap_next(): return lax.ppermute(values, 'dp', [(i, i ^ 2) for i in range(size)])]
    pallas_call x49 -> x51, Pallas kernels: 355 us -> 357 us  [launch(): results = run(*operands, *ties)]
    ppermute x22 -> x20, starting transfers between devices: 24.3 us -> 24.1 us  [swap_mem(): return lax.ppermute(values, 'mem', [(0, 1), (1, 0)])]
  transfers between devices with their start and end apart: 68 -> 64, of which waited for: 20 -> 17; matrix products, arithmetic and copies ran while one was open for 5% -> 5% of each run, Pallas kernels for 58% -> 60%
where the time goes in v3:
time: 554 us; the launch traced here: 545 us
  Pallas kernels  357 us (64%)
  waiting for transfers between devices  90.6 us (16%)
  starting transfers between devices  53.9 us (10%)
  local copies, waits for them, and re-layouts  16.2 us (3%)
  between operations  15.7 us (3%)
  other arithmetic  11.7 us (2%)
    pallas_call x51, Pallas kernels, launch(): results = run(*operands, *ties)  357 us
    ppermute x20, waiting for transfers between devices, swap_mem(): return lax.ppermute(values, 'mem', [(0, 1), (1, 0)])  38 us
    ppermute x16, waiting for transfers between devices, swap_next(): return lax.ppermute(values, 'dp', [(i, i ^ 2) for i in range(size)])  26.3 us
    ppermute x20, starting transfers between devices, swap_mem(): return lax.ppermute(values, 'mem', [(0, 1), (1, 0)])  24.1 us
    ppermute x16, starting transfers between devices, swap_next(): return lax.ppermute(values, 'dp', [(i, i ^ 2) for i in range(size)])  16.8 us
    all_gather x3, waiting for transfers between devices, outer_gather(): lax.all_gather(shard, 'dp', axis_index_groups=outer_groups(), axis=0, til...  11.7 us
  transfers between devices with their start and end apart: 64, of which 17 were waited for; matrix products, arithmetic and copies ran while one was open for 5% of the time, Pallas kernels for 60%

profile of v3, /device:TPU:0, one launch (start us, length us, event | category | flops | bytes accessed | tf_op | source)
XLA Modules:
  0.0 545.0 jit_solution(11904858445561795858)
XLA Ops:
  11.8 3.7 move_blocks.13
  23.8 12.6 %collective-permute-done.4.refs_9_ = s32[2,384]{1,0:T(2,128)S(1)} collective-permute-done((s32[2,384]{1,0:T(2,128)S(1)}, s32[2,384]{1,0:T(2,128)S(1)}, u32[]{:S(2)}, u32[]{:S(2)}) %collective-permute-start.4) | collective-permute-done | bytes 3104 | tf_op jit(solution)/shard_map/ppermute | solution.py:386
  43.2 7.3 %collective-permute-done.5.refs_2_ = bf16[4,32,1536]{2,1,0:T(8,128)(2,1)} collective-permute-done((bf16[4,32,1536]{2,1,0:T(8,128)(2,1)}, bf16[4,32,1536]{2,1,0:T(8,128)(2,1)}, u32[]{:S(2)}, u32[]{:S(2)}) %collective-permute-start.5) | collective-permute-done | bytes 393248 | tf_op jit(solution)/shard_map/ppermute | solution.py:382
  51.6 3.6 move_blocks.15
  57.4 5.6 %turn_rows.3 = (bf16[512,1280]{1,0:T(8,128)(2,1)}, bf16[512,1280]{1,0:T(8,128)(2,1)}) custom-call(s32[4]{0:T(128)} %pad_add_fusion.refs_0_, bf16[512,1024]{1,0:T(8,128)(2,1)} %refs_2_.3, bf16[768,1024]{1,0:T(8,128)(2,1)} %bitcast.91, bf16[2,4,32,1536]{3,2,1,0:T(8,128)(2,1)} %get-tuple-element.121.refs_3_), custom_call_target="tpu_custom_call" | custom-call | flops 999999995904 | bytes 1 | tf_op jit(solution)/shard_map/turn_rows/pallas_call | solution.py:97
  62.9 11.7 %all-gather.4.cloned.1.call-done = bf16[128,5248]{1,0:T(8,128)(2,1)} async-done(((bf16[32,5248]{1,0:T(8,128)(2,1)}), bf16[128,5248]{1,0:T(8,128)(2,1)}) %all-gather.4.cloned.1.call-update) | async-done | bytes 1343504 | tf_op jit(solution)/shard_map/all_gather | solution.py:405
  83.7 11.2 %collective-permute-done.10.refs_2_ = bf16[4,32,2560]{2,1,0:T(8,128)(2,1)} collective-permute-done((bf16[4,32,2560]{2,1,0:T(8,128)(2,1)}, bf16[4,32,2560]{2,1,0:T(8,128)(2,1)}, u32[]{:S(2)}, u32[]{:S(2)}) %collective-permute-start.10) | collective-permute-done | bytes 655392 | tf_op jit(solution)/shard_map/ppermute | solution.py:382
  94.9 4.5 move_blocks.18
  105.9 8.6 %self_project.1.refs_2_.refs_1_.refs_3_ = bf16[512,3072]{1,0:T(8,128)(2,1)} custom-call(s32[4]{0:T(128)} %pad_add_fusion.refs_0_, bf16[512,1024]{1,0:T(8,128)(2,1)} %refs_2_.3, bf16[8,64,3072]{2,1,0:T(8,128)(2,1)} %bitcast.89, bf16[8,64,3072]{2,1,0:T(8,128)(2,1)} %collective-permute-done.9.refs_3_.refs_4_, bf16[2,4,32,2560]{3,2,1,0:T(8,128)(2,1)} %get-tuple-element.128.refs_4_), custom_call_target="tpu_custom_call" | custom-call | flops 1000000 | bytes 1 | tf_op jit(solution)/shard_map/self_project/pallas_call | solution.py:97
  117.5 14.2 %self_forward.1 = (bf16[512,1024]{1,0:T(8,128)(2,1)}, f32[512,1024]{1,0:T(8,128)}) custom-call(s32[3]{0:T(128)} %pad_add_fusion.1.refs_0_, bf16[512,3072]{1,0:T(8,128)(2,1)} %self_project.1.refs_2_.refs_1_.refs_3_, bf16[512,3072]{1,0:T(8,128)(2,1)} %self_project.1.refs_2_.refs_1_.refs_3_, bf16[512,3072]{1,0:T(8,128)(2,1)} %self_project.1.refs_2_.refs_1_.refs_3_, ...), custom_call_target="tpu_custom_call" | custom-call | flops 1000000 | bytes 1 | tf_op jit(solution)/shard_map/self_forward/pallas_call | solution.py:97
  133.1 3.5 move_blocks.20.refs_3_
  136.7 9.9 %collective-permute-done.16.refs_2_ = bf16[384,1024]{1,0:T(8,128)(2,1)} collective-permute-done((bf16[384,1024]{1,0:T(8,128)(2,1)}, bf16[384,1024]{1,0:T(8,128)(2,1)}, u32[]{:S(2)}, u32[]{:S(2)}) %collective-permute-start.16) | collective-permute-done | bytes 786464 | tf_op jit(solution)/shard_map/ppermute | solution.py:386
  155.1 11.9 %cross_project.1 = (bf16[768,2048]{1,0:T(8,128)(2,1)}, bf16[768,2048]{1,0:T(8,128)(2,1)}) custom-call(s32[4]{0:T(128)} %pad_add_fusion.refs_0_, bf16[768,1024]{1,0:T(8,128)(2,1)} %bitcast.92, bf16[768,1024]{1,0:T(8,128)(2,1)} %constant_dynamic-update-slice_fusion.refs_2_.refs_5_, bf16[8,64,5248]{2,1,0:T(8,128)(2,1)} %bitcast.67, ...), custom_call_target="tpu_custom_call" | custom-call | flops 1000000 | bytes 1 | tf_op jit(solution)/shard_map/cross_project/pallas_call | solution.py:97
  169.5 5.5 %move_blocks.22 = (bf16[2,4,32,4096]{3,2,1,0:T(8,128)(2,1)}, bf16[4,2,2,32,4096]{4,3,2,1,0:T(8,128)(2,1)}, bf16[2,4,128,1024]{3,2,1,0:T(8,128)(2,1)}, bf16[4,2,2,128,1024]{4,3,2,1,0:T(8,128)(2,1)}) custom-call(s32[4]{0:T(128)} %pad_add_fusion.refs_0_, bf16[4,32,4096]{2,1,0:T(8,128)(2,1)} %move_blocks.19.refs_4_.refs_1_, ...), custom_call_target="tpu_custom_call" | custom-call | flops 999999995904 | bytes 1 | tf_op jit(solution)/shard_map/move_blocks/pallas_call | solution.py:97
  177.7 8.2 %self_mix.1 = (f32[512,1024]{1,0:T(8,128)}, f32[512,1024]{1,0:T(8,128)}, bf16[512,1024]{1,0:T(8,128)(2,1)}, bf16[512,1024]{1,0:T(8,128)(2,1)}) custom-call(s32[4]{0:T(128)} %pad_add_fusion.refs_0_, bf16[512,1024]{1,0:T(8,128)(2,1)} %get-tuple-element.131.refs_4_.refs_1_, bf16[512,1024]{1,0:T(8,128)(2,1)} %refs_2_.3, ...), custom_call_target="tpu_custom_call" | custom-call | flops 1000000 | bytes 1 | tf_op jit(solution)/shard_map/self_mix/pallas_call | solution.py:97
  186.0 18.0 %cross_forward.1 = (bf16[512,1024]{1,0:T(8,128)(2,1)}, f32[512,1024]{1,0:T(8,128)}) custom-call(s32[1]{0:T(128)} %bitcast.5.refs_0_, bf16[512,1024]{1,0:T(8,128)(2,1)} %get-tuple-element.137.refs_1_, bf16[2,384,2048]{2,1,0:T(8,128)(2,1)} %bitcast.74, bf16[2,384,2048]{2,1,0:T(8,128)(2,1)} %bitcast.75, bf16[2,384,2048]{2,1,0:T(8,128)(2,1)} %bitcast.78, ...), custom_call_target="tpu_custom_call" | custom-call | flops 1000000 | bytes 1 | tf_op jit(solution)/shard_map/cross_forward/pallas_call | solution.py:97
  203.9 7.8 %cross_mix.1 = (f32[512,1024]{1,0:T(8,128)}, f32[512,1024]{1,0:T(8,128)}, bf16[512,1024]{1,0:T(8,128)(2,1)}) custom-call(s32[4]{0:T(128)} %pad_add_fusion.refs_0_, bf16[512,1024]{1,0:T(8,128)(2,1)} %get-tuple-element.140.refs_1_.refs_3_.refs_7_, f32[512,1024]{1,0:T(8,128)} %get-tuple-element.141.refs_2_, f32[8,1024]{1,0:T(8,128)} %norm_table.1.refs_5_.refs_3_.refs_4_, ...), custom_call_target="tpu_custom_call" | custom-call | flops 1000000 | bytes 1 | tf_op jit(solution)/shard_map/cross_mix/pallas_call | solution.py:97
  211.7 7.1 %collective-permute-done.19.refs_2_ = bf16[2,4,32,4096]{3,2,1,0:T(8,128)(2,1)} collective-permute-done((bf16[2,4,32,4096]{3,2,1,0:T(8,128)(2,1)}, bf16[2,4,32,4096]{3,2,1,0:T(8,128)(2,1)}, u32[]{:S(2)}, u32[]{:S(2)}) %collective-permute-start.19) | collective-permute-done | bytes 2097184 | tf_op jit(solution)/shard_map/ppermute | solution.py:386
  222.0 10.9 %turn_rows.4 = (bf16[512,2816]{1,0:T(8,128)(2,1)}, bf16[512,2816]{1,0:T(8,128)(2,1)}) custom-call(s32[4]{0:T(128)} %pad_add_fusion.refs_0_, bf16[512,1024]{1,0:T(8,128)(2,1)} %get-tuple-element.131.refs_4_.refs_1_, bf16[512,1024]{1,0:T(8,128)(2,1)} %get-tuple-element.147.refs_2_, bf16[512,1024]{1,0:T(8,128)(2,1)} %get-tuple-element.140.refs_1_.refs_3_.refs_7_, ...), custom_call_target="tpu_custom_call" | custom-call | flops 1000000 | bytes 1 | tf_op jit(solution)/shard_map/turn_rows/pallas_call | solution.py:97
  236.6 14.7 %feed_in.1 = (bf16[512,4096]{1,0:T(8,128)(2,1)}, bf16[512,4096]{1,0:T(8,128)(2,1)}) custom-call(s32[4]{0:T(128)} %pad_add_fusion.refs_0_, bf16[512,1024]{1,0:T(8,128)(2,1)} %get-tuple-element.142.refs_4_.refs_1_, bf16[8,64,4096]{2,1,0:T(8,128)(2,1)} %bitcast.86, bf16[8,64,4096]{2,1,0:T(8,128)(2,1)} %collective-permute-done.20.refs_3_.refs_6_, ...), custom_call_target="tpu_custom_call" | custom-call | flops 1000000 | bytes 1 | tf_op jit(solution)/shard_map/feed_in/pallas_call | solution.py:97
  251.3 7.4 %turn_rows.5 = (bf16[2048,512]{1,0:T(8,128)(2,1)}, bf16[2048,512]{1,0:T(8,128)(2,1)}) custom-call(s32[4]{0:T(128)} %pad_add_fusion.refs_0_, bf16[512,4096]{1,0:T(8,128)(2,1)} %get-tuple-element.149.refs_1_, bf16[512,2816]{1,0:T(8,128)(2,1)} %collective-permute-done.23.refs_2_.refs_10_.refs_11_.refs_12_), custom_call_target="tpu_custom_call" | custom-call | flops 1000000 | bytes 1 | tf_op jit(solution)/shard_map/turn_rows/pallas_call | solution.py:97
  259.0 14.1 %feed_out.1 = (bf16[512,1024]{1,0:T(8,128)(2,1)}, f32[512,1024]{1,0:T(8,128)}, bf16[512,1024]{1,0:T(8,128)(2,1)}, f32[16,1024]{1,0:T(8,128)}) custom-call(s32[4]{0:T(128)} %pad_add_fusion.refs_0_, bf16[512,4096]{1,0:T(8,128)(2,1)} %get-tuple-element.149.refs_1_, f32[512,1024]{1,0:T(8,128)} %get-tuple-element.150.refs_2_, ...), custom_call_target="tpu_custom_call" | custom-call | flops 1000000 | bytes 1 | tf_op jit(solution)/shard_map/feed_out/pallas_call | solution.py:97
  276.2 10.3 %weight_grad.7 = (bf16[2,4,128,512]{3,2,1,0:T(8,128)(2,1)}, bf16[2,4,128,512]{3,2,1,0:T(8,128)(2,1)}, bf16[2,4,128,512]{3,2,1,0:T(8,128)(2,1)}, bf16[2,4,128,512]{3,2,1,0:T(8,128)(2,1)}) custom-call(s32[4]{0:T(128)} %pad_add_fusion.refs_0_, bf16[2048,512]{1,0:T(8,128)(2,1)} %get-tuple-element.152.refs_7_.refs_1_, ...), custom_call_target="tpu_custom_call" | custom-call | flops 1000000 | bytes 1 | tf_op jit(solution)/shard_map/weight_grad/pallas_call | solution.py:97
  288.9 11.6 %feed_back.1.refs_1_.refs_3_ = bf16[512,4096]{1,0:T(8,128)(2,1)} custom-call(s32[4]{0:T(128)} %pad_add_fusion.refs_0_, bf16[512,1024]{1,0:T(8,128)(2,1)} %get-tuple-element.154.refs_3_.refs_1_, bf16[512,4096]{1,0:T(8,128)(2,1)} %get-tuple-element.155.refs_2_, bf16[8,256,1024]{2,1,0:T(8,128)(2,1)} %bitcast.84, ...), custom_call_target="tpu_custom_call" | custom-call | flops 1000000 | bytes 1 | tf_op jit(solution)/shard_map/feed_back/pallas_call | solution.py:97
  300.5 14.7 %cross_back.1 = (f32[512,1024]{1,0:T(8,128)}, bf16[512,1024]{1,0:T(8,128)(2,1)}, bf16[512,1024]{1,0:T(8,128)(2,1)}, f32[16,1024]{1,0:T(8,128)}) custom-call(s32[4]{0:T(128)} %pad_add_fusion.refs_0_, bf16[512,4096]{1,0:T(8,128)(2,1)} %feed_back.1.refs_1_.refs_3_, f32[512,1024]{1,0:T(8,128)} %get-tuple-element.158.refs_2_, ...), custom_call_target="tpu_custom_call" | custom-call | flops 1000000 | bytes 1 | tf_op jit(solution)/shard_map/cross_back/pallas_call | solution.py:97
  319.0 11.6 %weight_grad.8 = (bf16[2,4,32,2048]{3,2,1,0:T(8,128)(2,1)}, bf16[2,4,32,2048]{3,2,1,0:T(8,128)(2,1)}, bf16[2,4,32,2048]{3,2,1,0:T(8,128)(2,1)}, bf16[2,4,32,2048]{3,2,1,0:T(8,128)(2,1)}) custom-call(s32[4]{0:T(128)} %pad_add_fusion.refs_0_, bf16[512,2816]{1,0:T(8,128)(2,1)} %get-tuple-element.148.refs_3_.refs_1_.refs_4_.refs_5_.refs_6_, ...), custom_call_target="tpu_custom_call" | custom-call | flops 1000000 | bytes 1 | tf_op jit(solution)/shard_map/weight_grad/pallas_call | solution.py:97
  338.1 4.8 weight_grad.9
  344.0 24.2 %cross_backward.1 = (bf16[512,1024]{1,0:T(8,128)(2,1)}, bf16[768,2048]{1,0:T(8,128)(2,1)}, bf16[768,2048]{1,0:T(8,128)(2,1)}) custom-call(s32[1]{0:T(128)} %bitcast.5.refs_0_, bf16[512,1024]{1,0:T(8,128)(2,1)} %get-tuple-element.137.refs_1_, bf16[2,384,2048]{2,1,0:T(8,128)(2,1)} %bitcast.76, bf16[2,384,2048]{2,1,0:T(8,128)(2,1)} %bitcast.77, ...), custom_call_target="tpu_custom_call" | custom-call | flops 1000000 | bytes 1 | tf_op jit(solution)/shard_map/cross_backward/pallas_call | solution.py:97
  368.9 5.0 add_blocks.8
  375.8 9.4 %self_back.1 = (f32[512,1024]{1,0:T(8,128)}, bf16[512,1024]{1,0:T(8,128)(2,1)}, bf16[512,1024]{1,0:T(8,128)(2,1)}, f32[16,1024]{1,0:T(8,128)}) custom-call(s32[4]{0:T(128)} %pad_add_fusion.refs_0_, bf16[512,1024]{1,0:T(8,128)(2,1)} %get-tuple-element.169.refs_11_.refs_1_.refs_3_, f32[512,1024]{1,0:T(8,128)} %get-tuple-element.165.refs_5_.refs_2_, ...), custom_call_target="tpu_custom_call" | custom-call | flops 1000000 | bytes 1 | tf_op jit(solution)/shard_map/self_back/pallas_call | solution.py:97
  385.2 4.8 weight_grad.10
  395.1 12.5 %weight_grad.11 = (bf16[2,4,32,2048]{3,2,1,0:T(8,128)(2,1)}, bf16[2,4,32,2048]{3,2,1,0:T(8,128)(2,1)}) custom-call(s32[4]{0:T(128)} %pad_add_fusion.refs_0_, bf16[512,1280]{1,0:T(8,128)(2,1)} %get-tuple-element.124.refs_2_.refs_1_.refs_3_, bf16[512,1280]{1,0:T(8,128)(2,1)} %get-tuple-element.124.refs_2_.refs_1_.refs_3_, ...), custom_call_target="tpu_custom_call" | custom-call | flops 1000000 | bytes 1 | tf_op jit(solution)/shard_map/weight_grad/pallas_call | solution.py:97
  408.1 3.6 add_blocks.9.refs_7_
  411.7 15.5 %self_backward.1.refs_5_.refs_3_.refs_1_ = bf16[512,3072]{1,0:T(8,128)(2,1)} custom-call(s32[3]{0:T(128)} %pad_add_fusion.1.refs_0_, bf16[512,3072]{1,0:T(8,128)(2,1)} %self_project.1.refs_2_.refs_1_.refs_3_, bf16[512,3072]{1,0:T(8,128)(2,1)} %self_project.1.refs_2_.refs_1_.refs_3_, bf16[512,3072]{1,0:T(8,128)(2,1)} %self_project.1.refs_2_.refs_1_.refs_3_, ...), custom_call_target="tpu_custom_call" | custom-call | flops 1000000 | bytes 1 | tf_op jit(solution)/shard_map/self_backward/pallas_call | solution.py:97
  427.5 6.0 %collective-permute-done.42.refs_4_.refs_5_ = bf16[2,4,32,2048]{3,2,1,0:T(8,128)(2,1)} collective-permute-done((bf16[2,4,32,2048]{3,2,1,0:T(8,128)(2,1)}, bf16[2,4,32,2048]{3,2,1,0:T(8,128)(2,1)}, u32[]{:S(2)}, u32[]{:S(2)}) %collective-permute-start.42) | collective-permute-done | bytes 1048608 | tf_op jit(solution)/shard_map/ppermute | solution.py:382
  433.5 3.3 add_blocks.10
  439.6 9.4 %weight_grad.12 = (bf16[2,4,32,1536]{3,2,1,0:T(8,128)(2,1)}, bf16[2,4,32,1536]{3,2,1,0:T(8,128)(2,1)}, bf16[2,4,32,1536]{3,2,1,0:T(8,128)(2,1)}, bf16[2,4,32,1536]{3,2,1,0:T(8,128)(2,1)}) custom-call(s32[4]{0:T(128)} %pad_add_fusion.refs_0_, bf16[512,1280]{1,0:T(8,128)(2,1)} %get-tuple-element.124.refs_2_.refs_1_.refs_3_, ...), custom_call_target="tpu_custom_call" | custom-call | flops 1000000 | bytes 1 | tf_op jit(solution)/shard_map/weight_grad/pallas_call | solution.py:97
  452.2 4.2 reduce-scatter.6.cloned.1.call-done.refs_8_
  456.5 3.6 add_blocks.11.refs_7_
  460.1 5.1 weight_grad.13
  468.2 8.4 %memory_back.2.refs_9_.refs_1_ = bf16[768,1024]{1,0:T(8,128)(2,1)} custom-call(s32[4]{0:T(128)} %pad_add_fusion.refs_0_, bf16[768,2048]{1,0:T(8,128)(2,1)} %get-tuple-element.179.refs_14_.refs_1_, bf16[8,64,5248]{2,1,0:T(8,128)(2,1)} %bitcast.72, bf16[8,64,5248]{2,1,0:T(8,128)(2,1)} %collective-permute-done.15.refs_2_.refs_4_.refs_5_.refs_8_.refs_6_.refs_3_, ...), custom_call_target="tpu_custom_call" | custom-call | flops 1000000 | bytes 1 | tf_op jit(solution)/shard_map/memory_back/pallas_call | solution.py:97
  477.5 3.4 add_blocks.12
  486.2 8.2 %memory_back.3.refs_14_.refs_1_ = bf16[768,1024]{1,0:T(8,128)(2,1)} custom-call(s32[4]{0:T(128)} %pad_add_fusion.refs_0_, bf16[768,2048]{1,0:T(8,128)(2,1)} %get-tuple-element.178.refs_13_.refs_1_, bf16[8,64,5248]{2,1,0:T(8,128)(2,1)} %bitcast.73, bf16[8,64,5248]{2,1,0:T(8,128)(2,1)} %collective-permute-done.15.refs_2_.refs_4_.refs_5_.refs_8_.refs_6_.refs_3_, ...), custom_call_target="tpu_custom_call" | custom-call | flops 1000000 | bytes 1 | tf_op jit(solution)/shard_map/memory_back/pallas_call | solution.py:97
  495.2 3.4 collective-permute-done.51.refs_6_
  498.6 3.9 add_blocks.13.refs_5_.refs_1_
  512.8 9.1 %target_back.1.refs_6_ = bf16[512,1024]{1,0:T(8,128)(2,1)} custom-call(s32[4]{0:T(128)} %pad_add_fusion.refs_0_, bf16[512,3072]{1,0:T(8,128)(2,1)} %self_backward.1.refs_5_.refs_3_.refs_1_, f32[512,1024]{1,0:T(8,128)} %get-tuple-element.181.refs_7_.refs_2_, bf16[8,64,3072]{2,1,0:T(8,128)(2,1)} %bitcast.90, ...), custom_call_target="tpu_custom_call" | custom-call | flops 1000000 | bytes 1 | tf_op jit(solution)/shard_map/target_back/pallas_call | solution.py:97
  522.0 6.2 %collective-permute-done.56.refs_3_ = bf16[32,4352]{1,0:T(8,128)(2,1)} collective-permute-done((bf16[32,4352]{1,0:T(8,128)(2,1)}, bf16[32,4352]{1,0:T(8,128)(2,1)}, u32[]{:S(2)}, u32[]{:S(2)}) %collective-permute-start.56) | collective-permute-done | bytes 278560 | tf_op jit(solution)/shard_map/ppermute | solution.py:391
  534.1 3.8 move_blocks.25
  (198 shorter events, 121.5 us)
Async XLA Ops:
  7.2 67.4 %all-gather.4.cloned.1.call-start = ((), (), s32[]{:S(2)}) async-start(), calls=%async_computation.3 | async-start | bytes 1679360 | tf_op jit(solution)/shard_map/all_gather | solution.py:405
  15.5 22.1 %collective-permute-start.3 = (bf16[384,1024]{1,0:T(8,128)(2,1)}, bf16[384,1024]{1,0:T(8,128)(2,1)}, u32[]{:S(2)}, u32[]{:S(2)}) collective-permute-start(bf16[384,1024]{1,0:T(8,128)(2,1)} %get-tuple-element.116), channel_id=1, source_target_pairs={{0,1},{1,0},{2,3},{3,2},{4,5},{5,4},{6,7},{7,6},{8,9},{9,8},{10,11... | collective-permute-start | bytes 2359304 | tf_op jit(solution)/shard_map/ppermute | solution.py:386
  18.6 17.9 %collective-permute-start = (bf16[32,3072]{1,0:T(8,128)(2,1)}, bf16[32,3072]{1,0:T(8,128)(2,1)}, u32[]{:S(2)}, u32[]{:S(2)}) collective-permute-start(bf16[32,3072]{1,0:T(8,128)(2,1)} %get-tuple-element.112.refs_2_.refs_1_), channel_id=1, source_target_pairs={{0,8},{2,10},{4,12},{6,14},{8,0},{10,2},{12,4},{14,6},{16,24},{18,... | collective-permute-start | bytes 589832 | tf_op jit(solution)/shard_map/ppermute | solution.py:391
  20.1 17.5 %collective-permute-start.1 = (bf16[32,3072]{1,0:T(8,128)(2,1)}, bf16[32,3072]{1,0:T(8,128)(2,1)}, u32[]{:S(2)}, u32[]{:S(2)}) collective-permute-start(bf16[32,3072]{1,0:T(8,128)(2,1)} %get-tuple-element.112.refs_2_.refs_1_), channel_id=1, source_target_pairs={{0,16},{2,18},{4,20},{6,22},{8,24},{10,26},{12,28},{14,30},{16,0},... | collective-permute-start | bytes 589832 | tf_op jit(solution)/shard_map/ppermute | solution.py:391
  40.3 76.0 %all-gather.6.cloned.1.call-start = ((), (), s32[]{:S(2)}) async-start(), calls=%async_computation.4 | async-start | bytes 1310720 | tf_op jit(solution)/shard_map/all_gather | solution.py:405
  43.1 93.6 %all-gather.8.cloned.1.call-start = ((), (), s32[]{:S(2)}) async-start(), calls=%async_computation.5 | async-start | bytes 1310720 | tf_op jit(solution)/shard_map/all_gather | solution.py:405
  55.2 25.3 %collective-permute-start.7 = (bf16[2,4,32,1536]{3,2,1,0:T(8,128)(2,1)}, bf16[2,4,32,1536]{3,2,1,0:T(8,128)(2,1)}, u32[]{:S(2)}, u32[]{:S(2)}) collective-permute-start(bf16[2,4,32,1536]{3,2,1,0:T(8,128)(2,1)} %get-tuple-element.121.refs_3_), channel_id=1, source_target_pairs={{0,1},{1,0},{2,3},{3,2},{4,5},{5,4},{6,7},{7,6},{8,9},{9,8},{10,11... | collective-permute-start | bytes 2359304 | tf_op jit(solution)/shard_map/ppermute | solution.py:386
  56.8 23.7 %collective-permute-start.8 = (bf16[2,4,32,1536]{3,2,1,0:T(8,128)(2,1)}, bf16[2,4,32,1536]{3,2,1,0:T(8,128)(2,1)}, u32[]{:S(2)}, u32[]{:S(2)}) collective-permute-start(bf16[2,4,32,1536]{3,2,1,0:T(8,128)(2,1)} %get-tuple-element.122), channel_id=1, source_target_pairs={{0,4},{2,6},{4,0},{6,2},{8,12},{10,14},{12,8},{14,10},{16,20},{18,... | collective-permute-start | bytes 2359304 | tf_op jit(solution)/shard_map/ppermute | solution.py:382
  62.9 20.8 %collective-permute-start.12 = (bf16[512,1280]{1,0:T(8,128)(2,1)}, bf16[512,1280]{1,0:T(8,128)(2,1)}, u32[]{:S(2)}, u32[]{:S(2)}) collective-permute-start(bf16[512,1280]{1,0:T(8,128)(2,1)} %get-tuple-element.127), channel_id=1, source_target_pairs={{0,2},{2,0},{4,6},{6,4},{8,10},{10,8},{12,14},{14,12},{16,18},{18,... | collective-permute-start | bytes 3932168 | tf_op jit(solution)/shard_map/ppermute | solution.py:377
  77.5 17.4 %collective-permute-start.11 = (bf16[4,32,2688]{2,1,0:T(8,128)(2,1)}, bf16[4,32,2688]{2,1,0:T(8,128)(2,1)}, u32[]{:S(2)}, u32[]{:S(2)}) collective-permute-start(bf16[4,32,2688]{2,1,0:T(8,128)(2,1)} %get-tuple-element.126.refs_3_), channel_id=1, source_target_pairs={{0,1},{1,0},{2,3},{3,2},{4,5},{5,4},{6,7},{7,6},{8,9},{9,8},{10,11... | collective-permute-start | bytes 2064392 | tf_op jit(solution)/shard_map/ppermute | solution.py:386
  83.6 22.2 %collective-permute-start.9 = (bf16[8,64,3072]{2,1,0:T(8,128)(2,1)}, bf16[8,64,3072]{2,1,0:T(8,128)(2,1)}, u32[]{:S(2)}, u32[]{:S(2)}) collective-permute-start(bf16[8,64,3072]{2,1,0:T(8,128)(2,1)} %bitcast.88), channel_id=1, source_target_pairs={{0,2},{2,0},{4,6},{6,4},{8,10},{10,8},{12,14},{14,12},{16,18},{18,... | collective-permute-start | bytes 9437192 | tf_op jit(solution)/shard_map/ppermute | solution.py:377
  99.4 33.7 %collective-permute-start.14 = (bf16[2,4,32,2688]{3,2,1,0:T(8,128)(2,1)}, bf16[2,4,32,2688]{3,2,1,0:T(8,128)(2,1)}, u32[]{:S(2)}, u32[]{:S(2)}) collective-permute-start(bf16[2,4,32,2688]{3,2,1,0:T(8,128)(2,1)} %get-tuple-element.133), channel_id=1, source_target_pairs={{0,4},{2,6},{4,0},{6,2},{8,12},{10,14},{12,8},{14,10},{16,20},{18,... | collective-permute-start | bytes 4128776 | tf_op jit(solution)/shard_map/ppermute | solution.py:382
  101.1 32.0 %collective-permute-start.13 = (bf16[2,4,32,2560]{3,2,1,0:T(8,128)(2,1)}, bf16[2,4,32,2560]{3,2,1,0:T(8,128)(2,1)}, u32[]{:S(2)}, u32[]{:S(2)}) collective-permute-start(bf16[2,4,32,2560]{3,2,1,0:T(8,128)(2,1)} %get-tuple-element.128.refs_4_), channel_id=1, source_target_pairs={{0,1},{1,0},{2,3},{3,2},{4,5},{5,4},{6,7},{7,6},{8,9},{9,8},{10,11... | collective-permute-start | bytes 3932168 | tf_op jit(solution)/shard_map/ppermute | solution.py:386
  105.8 346.4 %reduce-scatter.4.cloned.1.call-start = ((), (), s32[]{:S(2)}) async-start(), calls=%async_computation.6 | async-start | bytes 1310720 | tf_op jit(solution)/shard_map/reduce_scatter | solution.py:1139
  115.1 31.5 %collective-permute-start.16 = (bf16[384,1024]{1,0:T(8,128)(2,1)}, bf16[384,1024]{1,0:T(8,128)(2,1)}, u32[]{:S(2)}, u32[]{:S(2)}) collective-permute-start(bf16[384,1024]{1,0:T(8,128)(2,1)} %gate.2.refs_2_), channel_id=1, source_target_pairs={{0,1},{1,0},{2,3},{3,2},{4,5},{5,4},{6,7},{7,6},{8,9},{9,8},{10,11... | collective-permute-start | bytes 2359304 | tf_op jit(solution)/shard_map/ppermute | solution.py:386
  117.0 50.0 %collective-permute-start.17 = (bf16[4,32,4096]{2,1,0:T(8,128)(2,1)}, bf16[4,32,4096]{2,1,0:T(8,128)(2,1)}, u32[]{:S(2)}, u32[]{:S(2)}) collective-permute-start(bf16[4,32,4096]{2,1,0:T(8,128)(2,1)} %move_blocks.19.refs_4_.refs_1_), channel_id=1, source_target_pairs={{0,4},{2,6},{4,0},{6,2},{8,12},{10,14},{12,8},{14,10},{16,20},{18,... | collective-permute-start | bytes 3145736 | tf_op jit(solution)/shard_map/ppermute | solution.py:382
  136.6 16.0 %collective-permute-start.15 = (bf16[8,64,5248]{2,1,0:T(8,128)(2,1)}, bf16[8,64,5248]{2,1,0:T(8,128)(2,1)}, u32[]{:S(2)}, u32[]{:S(2)}) collective-permute-start(bf16[8,64,5248]{2,1,0:T(8,128)(2,1)} %bitcast.65), channel_id=1, source_target_pairs={{0,2},{2,0},{4,6},{6,4},{8,10},{10,8},{12,14},{14,12},{16,18},{18,... | collective-permute-start | bytes 16121864 | tf_op jit(solution)/shard_map/ppermute | solution.py:377
  147.3 22.2 %collective-permute-start.18 = (bf16[4,128,1024]{2,1,0:T(8,128)(2,1)}, bf16[4,128,1024]{2,1,0:T(8,128)(2,1)}, u32[]{:S(2)}, u32[]{:S(2)}) collective-permute-start(bf16[4,128,1024]{2,1,0:T(8,128)(2,1)} %move_blocks.21.refs_3_), channel_id=1, source_target_pairs={{0,1},{1,0},{2,3},{3,2},{4,5},{5,4},{6,7},{7,6},{8,9},{9,8},{10,11... | collective-permute-start | bytes 3145736 | tf_op jit(solution)/shard_map/ppermute | solution.py:386
  175.1 43.7 %collective-permute-start.19 = (bf16[2,4,32,4096]{3,2,1,0:T(8,128)(2,1)}, bf16[2,4,32,4096]{3,2,1,0:T(8,128)(2,1)}, u32[]{:S(2)}, u32[]{:S(2)}) collective-permute-start(bf16[2,4,32,4096]{3,2,1,0:T(8,128)(2,1)} %get-tuple-element.136.refs_6_), channel_id=1, source_target_pairs={{0,1},{1,0},{2,3},{3,2},{4,5},{5,4},{6,7},{7,6},{8,9},{9,8},{10,11... | collective-permute-start | bytes 6291464 | tf_op jit(solution)/shard_map/ppermute | solution.py:386
  177.1 55.8 %collective-permute-start.21 = (bf16[2,4,128,1024]{3,2,1,0:T(8,128)(2,1)}, bf16[2,4,128,1024]{3,2,1,0:T(8,128)(2,1)}, u32[]{:S(2)}, u32[]{:S(2)}) collective-permute-start(bf16[2,4,128,1024]{3,2,1,0:T(8,128)(2,1)} %get-tuple-element.146), channel_id=1, source_target_pairs={{0,4},{2,6},{4,0},{6,2},{8,12},{10,14},{12,8},{14,10},{16,20},{18,... | collective-permute-start | bytes 6291464 | tf_op jit(solution)/shard_map/ppermute | solution.py:382
  236.0 23.0 %collective-permute-start.22 = (bf16[8,256,1024]{2,1,0:T(8,128)(2,1)}, bf16[8,256,1024]{2,1,0:T(8,128)(2,1)}, u32[]{:S(2)}, u32[]{:S(2)}) collective-permute-start(bf16[8,256,1024]{2,1,0:T(8,128)(2,1)} %bitcast.82), channel_id=1, source_target_pairs={{0,2},{2,0},{4,6},{6,4},{8,10},{10,8},{12,14},{14,12},{16,18},{18,... | collective-permute-start | bytes 12582920 | tf_op jit(solution)/shard_map/ppermute | solution.py:377
  258.7 17.5 %collective-permute-start.24 = (bf16[2048,512]{1,0:T(8,128)(2,1)}, bf16[2048,512]{1,0:T(8,128)(2,1)}, u32[]{:S(2)}, u32[]{:S(2)}) collective-permute-start(bf16[2048,512]{1,0:T(8,128)(2,1)} %get-tuple-element.156), channel_id=1, source_target_pairs={{0,2},{2,0},{4,6},{6,4},{8,10},{10,8},{12,14},{14,12},{16,18},{18,... | collective-permute-start | bytes 6291464 | tf_op jit(solution)/shard_map/ppermute | solution.py:377
  286.5 29.2 %collective-permute-start.28 = (bf16[2,4,128,512]{3,2,1,0:T(8,128)(2,1)}, bf16[2,4,128,512]{3,2,1,0:T(8,128)(2,1)}, u32[]{:S(2)}, u32[]{:S(2)}) collective-permute-start(bf16[2,4,128,512]{3,2,1,0:T(8,128)(2,1)} %get-tuple-element.157.refs_5_), channel_id=1, source_target_pairs={{0,1},{1,0},{2,3},{3,2},{4,5},{5,4},{6,7},{7,6},{8,9},{9,8},{10,11... | collective-permute-start | bytes 3145736 | tf_op jit(solution)/shard_map/ppermute | solution.py:386
  288.2 27.6 %collective-permute-start.29 = (bf16[2,4,128,512]{3,2,1,0:T(8,128)(2,1)}, bf16[2,4,128,512]{3,2,1,0:T(8,128)(2,1)}, u32[]{:S(2)}, u32[]{:S(2)}) collective-permute-start(bf16[2,4,128,512]{3,2,1,0:T(8,128)(2,1)} %get-tuple-element.164), channel_id=1, source_target_pairs={{0,4},{2,6},{4,0},{6,2},{8,12},{10,14},{12,8},{14,10},{16,20},{18,... | collective-permute-start | bytes 3145736 | tf_op jit(solution)/shard_map/ppermute | solution.py:382
  300.5 18.5 %collective-permute-start.27 = (bf16[512,4096]{1,0:T(8,128)(2,1)}, bf16[512,4096]{1,0:T(8,128)(2,1)}, u32[]{:S(2)}, u32[]{:S(2)}) collective-permute-start(bf16[512,4096]{1,0:T(8,128)(2,1)} %feed_back.1.refs_1_.refs_3_), channel_id=1, source_target_pairs={{0,2},{2,0},{4,6},{6,4},{8,10},{10,8},{12,14},{14,12},{16,18},{18,... | collective-permute-start | bytes 12582920 | tf_op jit(solution)/shard_map/ppermute | solution.py:377
  315.2 22.9 %collective-permute-start.26 = (bf16[512,1024]{1,0:T(8,128)(2,1)}, bf16[512,1024]{1,0:T(8,128)(2,1)}, u32[]{:S(2)}, u32[]{:S(2)}) collective-permute-start(bf16[512,1024]{1,0:T(8,128)(2,1)} %get-tuple-element.161.refs_3_), channel_id=1, source_target_pairs={{0,2},{2,0},{4,6},{6,4},{8,10},{10,8},{12,14},{14,12},{16,18},{18,... | collective-permute-start | bytes 3145736 | tf_op jit(solution)/shard_map/ppermute | solution.py:377
  330.5 38.4 %collective-permute-start.30 = (bf16[2,4,32,2048]{3,2,1,0:T(8,128)(2,1)}, bf16[2,4,32,2048]{3,2,1,0:T(8,128)(2,1)}, u32[]{:S(2)}, u32[]{:S(2)}) collective-permute-start(bf16[2,4,32,2048]{3,2,1,0:T(8,128)(2,1)} %get-tuple-element.167.refs_5_), channel_id=1, source_target_pairs={{0,1},{1,0},{2,3},{3,2},{4,5},{5,4},{6,7},{7,6},{8,9},{9,8},{10,11... | collective-permute-start | bytes 3145736 | tf_op jit(solution)/shard_map/ppermute | solution.py:386
  330.8 38.2 %collective-permute-start.31 = (bf16[2,4,32,2048]{3,2,1,0:T(8,128)(2,1)}, bf16[2,4,32,2048]{3,2,1,0:T(8,128)(2,1)}, u32[]{:S(2)}, u32[]{:S(2)}) collective-permute-start(bf16[2,4,32,2048]{3,2,1,0:T(8,128)(2,1)} %get-tuple-element.172), channel_id=1, source_target_pairs={{0,4},{2,6},{4,0},{6,2},{8,12},{10,14},{12,8},{14,10},{16,20},{18,... | collective-permute-start | bytes 3145736 | tf_op jit(solution)/shard_map/ppermute | solution.py:382
  333.6 34.7 %collective-permute-start.32 = (bf16[4,128,512]{2,1,0:T(8,128)(2,1)}, bf16[4,128,512]{2,1,0:T(8,128)(2,1)}, u32[]{:S(2)}, u32[]{:S(2)}) collective-permute-start(bf16[4,128,512]{2,1,0:T(8,128)(2,1)} %get-tuple-element.166.refs_5_), channel_id=1, source_target_pairs={{0,4},{2,6},{4,0},{6,2},{8,12},{10,14},{12,8},{14,10},{16,20},{18,... | collective-permute-start | bytes 1572872 | tf_op jit(solution)/shard_map/ppermute | solution.py:382
  334.2 34.6 %collective-permute-start.33 = (bf16[4,128,512]{2,1,0:T(8,128)(2,1)}, bf16[4,128,512]{2,1,0:T(8,128)(2,1)}, u32[]{:S(2)}, u32[]{:S(2)}) collective-permute-start(bf16[4,128,512]{2,1,0:T(8,128)(2,1)} %get-tuple-element.173), channel_id=1, source_target_pairs={{0,1},{1,0},{2,3},{3,2},{4,5},{5,4},{6,7},{7,6},{8,9},{9,8},{10,11... | collective-permute-start | bytes 1572872 | tf_op jit(solution)/shard_map/ppermute | solution.py:386
  368.2 17.0 %collective-permute-start.38 = (bf16[512,1024]{1,0:T(8,128)(2,1)}, bf16[512,1024]{1,0:T(8,128)(2,1)}, u32[]{:S(2)}, u32[]{:S(2)}) collective-permute-start(bf16[512,1024]{1,0:T(8,128)(2,1)} %get-tuple-element.169.refs_11_.refs_1_.refs_3_), channel_id=1, source_target_pairs={{0,2},{2,0},{4,6},{6,4},{8,10},{10,8},{12,14},{14,12},{16,18},{18,... | collective-permute-start | bytes 3145736 | tf_op jit(solution)/shard_map/ppermute | solution.py:377
  368.3 26.7 %collective-permute-start.36 = (bf16[768,2048]{1,0:T(8,128)(2,1)}, bf16[768,2048]{1,0:T(8,128)(2,1)}, u32[]{:S(2)}, u32[]{:S(2)}) collective-permute-start(bf16[768,2048]{1,0:T(8,128)(2,1)} %get-tuple-element.178.refs_13_.refs_1_), channel_id=1, source_target_pairs={{0,2},{2,0},{4,6},{6,4},{8,10},{10,8},{12,14},{14,12},{16,18},{18,... | collective-permute-start | bytes 9437192 | tf_op jit(solution)/shard_map/ppermute | solution.py:377
  368.8 26.2 %collective-permute-start.37 = (bf16[768,2048]{1,0:T(8,128)(2,1)}, bf16[768,2048]{1,0:T(8,128)(2,1)}, u32[]{:S(2)}, u32[]{:S(2)}) collective-permute-start(bf16[768,2048]{1,0:T(8,128)(2,1)} %get-tuple-element.179.refs_14_.refs_1_), channel_id=1, source_target_pairs={{0,2},{2,0},{4,6},{6,4},{8,10},{10,8},{12,14},{14,12},{16,18},{18,... | collective-permute-start | bytes 9437192 | tf_op jit(solution)/shard_map/ppermute | solution.py:377
  373.9 34.2 %collective-permute-start.34 = (bf16[4,32,2048]{2,1,0:T(8,128)(2,1)}, bf16[4,32,2048]{2,1,0:T(8,128)(2,1)}, u32[]{:S(2)}, u32[]{:S(2)}) collective-permute-start(bf16[4,32,2048]{2,1,0:T(8,128)(2,1)} %get-tuple-element.174.refs_7_), channel_id=1, source_target_pairs={{0,4},{2,6},{4,0},{6,2},{8,12},{10,14},{12,8},{14,10},{16,20},{18,... | collective-permute-start | bytes 1572872 | tf_op jit(solution)/shard_map/ppermute | solution.py:382
  375.3 32.8 %collective-permute-start.35 = (bf16[4,32,2048]{2,1,0:T(8,128)(2,1)}, bf16[4,32,2048]{2,1,0:T(8,128)(2,1)}, u32[]{:S(2)}, u32[]{:S(2)}) collective-permute-start(bf16[4,32,2048]{2,1,0:T(8,128)(2,1)} %get-tuple-element.177), channel_id=1, source_target_pairs={{0,1},{1,0},{2,3},{3,2},{4,5},{5,4},{6,7},{7,6},{8,9},{9,8},{10,11... | collective-permute-start | bytes 1572872 | tf_op jit(solution)/shard_map/ppermute | solution.py:386
  390.0 37.5 %collective-permute-start.41 = (bf16[2,4,32,2048]{3,2,1,0:T(8,128)(2,1)}, bf16[2,4,32,2048]{3,2,1,0:T(8,128)(2,1)}, u32[]{:S(2)}, u32[]{:S(2)}) collective-permute-start(bf16[2,4,32,2048]{3,2,1,0:T(8,128)(2,1)} %get-tuple-element.182.refs_17_), channel_id=1, source_target_pairs={{0,1},{1,0},{2,3},{3,2},{4,5},{5,4},{6,7},{7,6},{8,9},{9,8},{10,11... | collective-permute-start | bytes 3145736 | tf_op jit(solution)/shard_map/ppermute | solution.py:386
  391.5 64.9 %reduce-scatter.6.cloned.1.call-start = ((), (), s32[]{:S(2)}) async-start(), calls=%async_computation.7 | async-start | bytes 1310720 | tf_op jit(solution)/shard_map/reduce_scatter | solution.py:1139
  395.1 42.7 %collective-permute-start.40 = (bf16[2,2,4,32,256]{4,3,2,1,0:T(8,128)(2,1)}, bf16[2,2,4,32,256]{4,3,2,1,0:T(8,128)(2,1)}, u32[]{:S(2)}, u32[]{:S(2)}) collective-permute-start(bf16[2,2,4,32,256]{4,3,2,1,0:T(8,128)(2,1)} %slice_bitcast_fusion), channel_id=1, source_target_pairs={{0,2},{2,0},{4,6},{6,4},{8,10},{10,8},{12,14},{14,12},{16,18},{18,... | collective-permute-start | bytes 786440 | tf_op jit(solution)/shard_map/ppermute | solution.py:377
  407.6 26.0 %collective-permute-start.42 = (bf16[2,4,32,2048]{3,2,1,0:T(8,128)(2,1)}, bf16[2,4,32,2048]{3,2,1,0:T(8,128)(2,1)}, u32[]{:S(2)}, u32[]{:S(2)}) collective-permute-start(bf16[2,4,32,2048]{3,2,1,0:T(8,128)(2,1)} %get-tuple-element.183.refs_7_), channel_id=1, source_target_pairs={{0,4},{2,6},{4,0},{6,2},{8,12},{10,14},{12,8},{14,10},{16,20},{18,... | collective-permute-start | bytes 3145736 | tf_op jit(solution)/shard_map/ppermute | solution.py:382
  427.4 71.2 %reduce-scatter.8.cloned.1.call-start = ((), (), s32[]{:S(2)}) async-start(), calls=%async_computation.8 | async-start | bytes 1310720 | tf_op jit(solution)/shard_map/reduce_scatter | solution.py:1139
  437.7 22.3 %collective-permute-start.39 = (bf16[512,1024]{1,0:T(8,128)(2,1)}, bf16[512,1024]{1,0:T(8,128)(2,1)}, u32[]{:S(2)}, u32[]{:S(2)}) collective-permute-start(bf16[512,1024]{1,0:T(8,128)(2,1)} %get-tuple-element.184.refs_3_), channel_id=1, source_target_pairs={{0,2},{2,0},{4,6},{6,4},{8,10},{10,8},{12,14},{14,12},{16,18},{18,... | collective-permute-start | bytes 3145736 | tf_op jit(solution)/shard_map/ppermute | solution.py:377
  449.0 28.5 %collective-permute-start.47 = (bf16[2,4,32,1536]{3,2,1,0:T(8,128)(2,1)}, bf16[2,4,32,1536]{3,2,1,0:T(8,128)(2,1)}, u32[]{:S(2)}, u32[]{:S(2)}) collective-permute-start(bf16[2,4,32,1536]{3,2,1,0:T(8,128)(2,1)} %get-tuple-element.193.refs_9_), channel_id=1, source_target_pairs={{0,1},{1,0},{2,3},{3,2},{4,5},{5,4},{6,7},{7,6},{8,9},{9,8},{10,11... | collective-permute-start | bytes 2359304 | tf_op jit(solution)/shard_map/ppermute | solution.py:386
  450.5 27.0 %collective-permute-start.48 = (bf16[2,4,32,1536]{3,2,1,0:T(8,128)(2,1)}, bf16[2,4,32,1536]{3,2,1,0:T(8,128)(2,1)}, u32[]{:S(2)}, u32[]{:S(2)}) collective-permute-start(bf16[2,4,32,1536]{3,2,1,0:T(8,128)(2,1)} %get-tuple-element.198), channel_id=1, source_target_pairs={{0,4},{2,6},{4,0},{6,2},{8,12},{10,14},{12,8},{14,10},{16,20},{18,... | collective-permute-start | bytes 2359304 | tf_op jit(solution)/shard_map/ppermute | solution.py:382
  480.9 17.7 %collective-permute-start.52 = (bf16[4,32,1536]{2,1,0:T(8,128)(2,1)}, bf16[4,32,1536]{2,1,0:T(8,128)(2,1)}, u32[]{:S(2)}, u32[]{:S(2)}) collective-permute-start(bf16[4,32,1536]{2,1,0:T(8,128)(2,1)} %get-tuple-element.203.refs_2_), channel_id=1, source_target_pairs={{0,4},{2,6},{4,0},{6,2},{8,12},{10,14},{12,8},{14,10},{16,20},{18,... | collective-permute-start | bytes 1179656 | tf_op jit(solution)/shard_map/ppermute | solution.py:382
  485.7 48.5 %collective-permute-start.54 = (bf16[768,1024]{1,0:T(8,128)(2,1)}, bf16[768,1024]{1,0:T(8,128)(2,1)}, u32[]{:S(2)}, u32[]{:S(2)}) collective-permute-start(bf16[768,1024]{1,0:T(8,128)(2,1)} %gate.3.refs_4_), channel_id=1, source_target_pairs={{0,1},{1,0},{2,3},{3,2},{4,5},{5,4},{6,7},{7,6},{8,9},{9,8},{10,11... | collective-permute-start | bytes 4718600 | tf_op jit(solution)/shard_map/ppermute | solution.py:386
  504.7 17.3 %collective-permute-start.55 = (bf16[32,4352]{1,0:T(8,128)(2,1)}, bf16[32,4352]{1,0:T(8,128)(2,1)}, u32[]{:S(2)}, u32[]{:S(2)}) collective-permute-start(bf16[32,4352]{1,0:T(8,128)(2,1)} %get-tuple-element.250), channel_id=1, source_target_pairs={{0,8},{2,10},{4,12},{6,14},{8,0},{10,2},{12,4},{14,6},{16,24},{18,... | collective-permute-start | bytes 835592 | tf_op jit(solution)/shard_map/ppermute | solution.py:391
  507.2 21.0 %collective-permute-start.56 = (bf16[32,4352]{1,0:T(8,128)(2,1)}, bf16[32,4352]{1,0:T(8,128)(2,1)}, u32[]{:S(2)}, u32[]{:S(2)}) collective-permute-start(bf16[32,4352]{1,0:T(8,128)(2,1)} %get-tuple-element.249), channel_id=1, source_target_pairs={{0,16},{2,18},{4,20},{6,22},{8,24},{10,26},{12,28},{14,30},{16,0},... | collective-permute-start | bytes 835592 | tf_op jit(solution)/shard_map/ppermute | solution.py:391
  510.1 18.1 %collective-permute-start.57 = (bf16[32,4352]{1,0:T(8,128)(2,1)}, bf16[32,4352]{1,0:T(8,128)(2,1)}, u32[]{:S(2)}, u32[]{:S(2)}) collective-permute-start(bf16[32,4352]{1,0:T(8,128)(2,1)} %get-tuple-element.248), channel_id=1, source_target_pairs={{0,24},{2,26},{4,28},{6,30},{8,16},{10,18},{12,20},{14,22},{16,8},... | collective-permute-start | bytes 835592 | tf_op jit(solution)/shard_map/ppermute | solution.py:391
  (27 other events, 282.2 us)
Sparse Core Ops, SparseCore 0:
  40.4 34.1 all-gather.3
  76.8 26.8 all-gather.5
  105.9 26.7 all-gather.7
  391.7 27.9 reduce-scatter.3
  427.5 28.8 reduce-scatter.5
  468.3 23.9 reduce-scatter.7

commit v4 on v3

--- a/solution.py
+++ b/solution.py
@@ -9,6 +9,8 @@
 
 HD = 64
 LANES = 128
+PAIRS = 2
+WIDE = PAIRS * LANES
 ALPHA = 300.0**0.25
 NEG_LARGE = -1e30
 EPSILON = 1e-05
@@ -164,6 +166,10 @@
     return log_rows, delta_rows
 
 
+def pair_lanes(pair):
+    return slice(pair * LANES, (pair + 1) * LANES)
+
+
 def self_forward_kernel(meta, q_ref, k_ref, v_ref, mixed_ref, log_ref, bias):
     rows = q_ref.shape[0]
 
@@ -175,18 +181,23 @@
         bias[...] = jnp.where(seen, 0.0, NEG_LARGE)
 
     half = rows // 2
-    for start, stop in ((0, half), (half, rows)):
-        mixed, log_totals = pair_forward(
-            q_ref[start:stop, :], k_ref[:stop, :], v_ref[:stop, :], bias[start:stop, :stop]
-        )
-        mixed_ref[start:stop, :] = mixed.astype(BF16)
-        log_ref[start:stop, :] = log_totals
+    for pair in range(PAIRS):
+        lanes = pair_lanes(pair)
+        for start, stop in ((0, half), (half, rows)):
+            mixed, log_totals = pair_forward(
+                q_ref[start:stop, lanes],
+                k_ref[:stop, lanes],
+                v_ref[:stop, lanes],
+                bias[start:stop, :stop],
+            )
+            mixed_ref[start:stop, lanes] = mixed.astype(BF16)
+            log_ref[start:stop, lanes] = log_totals
 
 
 def self_forward(order, meta, united):
     rows, width = united.shape[0], united.shape[1] // 3
-    pairs = width // LANES
-    spec = lambda third: pl.BlockSpec((rows, LANES), lambda i, _: (0, third * pairs + i))
+    steps = width // WIDE
+    spec = lambda third: pl.BlockSpec((rows, WIDE), lambda i, _: (0, third * steps + i))
     return order.launch(
         self_forward_kernel,
         "self_forward",
@@ -195,7 +206,7 @@
         [spec(0), spec(0)],
         [jax.ShapeDtypeStruct((rows, width), kind) for kind in (BF16, F32)],
         [pltpu.VMEM((rows, rows), F32)],
-        (pairs,),
+        (steps,),
         {},
     )
 
@@ -205,44 +216,47 @@
 ):
     rows = q_ref.shape[0]
     width = grad_ref.shape[1] // 3
-    pair = pl.program_id(0)
-
-    @pl.when(pair == 0)
+    step = pl.program_id(0)
+
+    @pl.when(step == 0)
     def _():
         key_ids = lax.broadcasted_iota(jnp.int32, (rows, rows), 0)
         query_ids = lax.broadcasted_iota(jnp.int32, (rows, rows), 1)
         seen = visible(query_ids, key_ids, meta[0], meta[1], meta[2])
         bias[...] = jnp.where(seen, 0.0, NEG_LARGE)
 
-    log_rows, delta_rows = stat_rows(log_ref[...], mixed_ref[...], up_ref[...])
     half = rows // 2
-    parts = []
-    for start, stop in ((0, half), (half, rows)):
-        parts.append(
-            pair_backward(
-                q_ref[start:stop, :],
-                k_ref[:stop, :],
-                v_ref[:stop, :],
-                up_ref[start:stop, :],
-                bias[:stop, start:stop],
-                [row[:, start:stop] for row in log_rows],
-                [row[:, start:stop] for row in delta_rows],
+    for pair in range(PAIRS):
+        lanes = pair_lanes(pair)
+        log_rows, delta_rows = stat_rows(log_ref[:, lanes], mixed_ref[:, lanes], up_ref[:, lanes])
+        parts = []
+        for start, stop in ((0, half), (half, rows)):
+            parts.append(
+                pair_backward(
+                    q_ref[start:stop, lanes],
+                    k_ref[:stop, lanes],
+                    v_ref[:stop, lanes],
+                    up_ref[start:stop, lanes],
+                    bias[:stop, start:stop],
+                    [row[:, start:stop] for row in log_rows],
+                    [row[:, start:stop] for row in delta_rows],
+                )
             )
-        )
-    low, high = parts
-    columns = lambda third: pl.ds(pl.multiple_of(third * width + pair * LANES, LANES), LANES)
-    grad_ref[:half, columns(0)] = low[0].astype(BF16)
-    grad_ref[half:, columns(0)] = high[0].astype(BF16)
-    for third in (1, 2):
-        grad_ref[:half, columns(third)] = (low[third] + high[third][:half]).astype(BF16)
-        grad_ref[half:, columns(third)] = high[third][half:].astype(BF16)
-
-
-def self_backward(order, meta, united, mixed, upstream, log_totals, first, pairs):
+        low, high = parts
+        at = step * WIDE + pair * LANES
+        columns = lambda third: pl.ds(pl.multiple_of(third * width + at, LANES), LANES)
+        grad_ref[:half, columns(0)] = low[0].astype(BF16)
+        grad_ref[half:, columns(0)] = high[0].astype(BF16)
+        for third in (1, 2):
+            grad_ref[:half, columns(third)] = (low[third] + high[third][:half]).astype(BF16)
+            grad_ref[half:, columns(third)] = high[third][half:].astype(BF16)
+
+
+def self_backward(order, meta, united, mixed, upstream, log_totals):
     rows, width = mixed.shape
-    third = width // LANES
-    spec = lambda at: pl.BlockSpec((rows, LANES), lambda i, _: (0, at * third + first + i))
-    shape = (rows, 3 * pairs * LANES)
+    steps = width // WIDE
+    spec = lambda third: pl.BlockSpec((rows, WIDE), lambda i, _: (0, third * steps + i))
+    shape = (rows, 3 * width)
     return order.launch(
         self_backward_kernel,
         "self_backward",
@@ -251,7 +265,7 @@
         [whole_spec(shape)],
         [jax.ShapeDtypeStruct(shape, BF16)],
         [pltpu.VMEM((rows, rows), F32)],
-        (pairs,),
+        (steps,),
         {},
     )[0]
 
@@ -269,25 +283,29 @@
     half = q_ref.shape[0] // 2
     join_keys(kn_ref, kf_ref, keys)
     join_keys(vn_ref, vf_ref, values)
-    for part in range(2):
-        slot = part * meta[0]
-        rows = slice(part * half, (part + 1) * half)
-        mixed, log_totals = pair_forward(q_ref[rows, :], keys[slot], values[slot], bias_ref[slot])
-        mixed_ref[rows, :] = mixed.astype(BF16)
-        log_ref[rows, :] = log_totals
-
-
-def cross_specs(rows, slots, piece, pairs):
-    row_spec = pl.BlockSpec((rows, LANES), lambda i, _: (0, i))
-    half = lambda at: pl.BlockSpec((slots, piece, LANES), lambda i, _: (0, 0, at * pairs + i))
+    for pair in range(PAIRS):
+        lanes = pair_lanes(pair)
+        for part in range(2):
+            slot = part * meta[0]
+            rows = slice(part * half, (part + 1) * half)
+            mixed, log_totals = pair_forward(
+                q_ref[rows, lanes], keys[slot, :, lanes], values[slot, :, lanes], bias_ref[slot]
+            )
+            mixed_ref[rows, lanes] = mixed.astype(BF16)
+            log_ref[rows, lanes] = log_totals
+
+
+def cross_specs(rows, slots, piece, steps):
+    row_spec = pl.BlockSpec((rows, WIDE), lambda i, _: (0, i))
+    half = lambda at: pl.BlockSpec((slots, piece, WIDE), lambda i, _: (0, 0, at * steps + i))
     return row_spec, [row_spec, half(0), half(1), half(0), half(1)]
 
 
 def cross_forward(order, meta, query, near, far, bias):
     rows, width = query.shape
     slots, piece = near.shape[0], near.shape[1]
-    pairs = width // LANES
-    row_spec, specs = cross_specs(rows, slots, piece, pairs)
+    steps = width // WIDE
+    row_spec, specs = cross_specs(rows, slots, piece, steps)
     return order.launch(
         cross_forward_kernel,
         "cross_forward",
@@ -295,8 +313,8 @@
         specs + [whole_spec(bias.shape)],
         [row_spec, row_spec],
         [jax.ShapeDtypeStruct((rows, width), kind) for kind in (BF16, F32)],
-        [pltpu.VMEM((slots, 2 * piece, LANES), BF16)] * 2,
-        (pairs,),
+        [pltpu.VMEM((slots, 2 * piece, WIDE), BF16)] * 2,
+        (steps,),
         {},
     )
 
@@ -323,42 +341,44 @@
     width = grad_near_ref.shape[1] // 2
     join_keys(kn_ref, kf_ref, keys)
     join_keys(vn_ref, vf_ref, values)
-    log_rows, delta_rows = stat_rows(log_ref[...], mixed_ref[...], up_ref[...])
-    parts = []
-    for part in range(2):
-        slot = part * meta[0]
-        rows = slice(part * half, (part + 1) * half)
-        bias_column = bias_ref[slot]
-        grads = pair_backward(
-            q_ref[rows, :],
-            keys[slot],
-            values[slot],
-            up_ref[rows, :],
-            jnp.concatenate([bias_column] * (half // LANES), axis=1),
-            [row[:, rows] for row in log_rows],
-            [row[:, rows] for row in delta_rows],
-        )
-        grad_q_ref[rows, :] = grads[0].astype(BF16)
-        parts.append(grads)
     split = meta[0].astype(F32)
-    start = pl.program_id(0) * LANES
-    for which in range(2):
-        early, late = parts[0][1 + which], parts[1][1 + which]
-        columns = pl.ds(pl.multiple_of(which * width + start, LANES), LANES)
-        by_slot = (early + late * (1.0 - split), late * split)
-        for slot in range(slots):
-            for source, target in enumerate((grad_near_ref, grad_far_ref)):
-                target[slot * piece : (slot + 1) * piece, columns] = by_slot[slot][
-                    source * piece : (source + 1) * piece
-                ].astype(BF16)
+    for pair in range(PAIRS):
+        lanes = pair_lanes(pair)
+        log_rows, delta_rows = stat_rows(log_ref[:, lanes], mixed_ref[:, lanes], up_ref[:, lanes])
+        parts = []
+        for part in range(2):
+            slot = part * meta[0]
+            rows = slice(part * half, (part + 1) * half)
+            bias_column = bias_ref[slot]
+            grads = pair_backward(
+                q_ref[rows, lanes],
+                keys[slot, :, lanes],
+                values[slot, :, lanes],
+                up_ref[rows, lanes],
+                jnp.concatenate([bias_column] * (half // LANES), axis=1),
+                [row[:, rows] for row in log_rows],
+                [row[:, rows] for row in delta_rows],
+            )
+            grad_q_ref[rows, lanes] = grads[0].astype(BF16)
+            parts.append(grads)
+        start = pl.program_id(0) * WIDE + pair * LANES
+        for which in range(2):
+            early, late = parts[0][1 + which], parts[1][1 + which]
+            columns = pl.ds(pl.multiple_of(which * width + start, LANES), LANES)
+            by_slot = (early + late * (1.0 - split), late * split)
+            for slot in range(slots):
+                for source, target in enumerate((grad_near_ref, grad_far_ref)):
+                    target[slot * piece : (slot + 1) * piece, columns] = by_slot[slot][
+                        source * piece : (source + 1) * piece
+                    ].astype(BF16)
 
 
 def cross_backward(order, meta, query, near, far, bias, mixed, upstream, log_totals):
     rows, width = query.shape
     slots, piece = near.shape[0], near.shape[1]
-    pairs = width // LANES
+    steps = width // WIDE
     memory = (slots * piece, 2 * width)
-    row_spec, specs = cross_specs(rows, slots, piece, pairs)
+    row_spec, specs = cross_specs(rows, slots, piece, steps)
     return order.launch(
         cross_backward_kernel,
         "cross_backward",
@@ -366,8 +386,8 @@
         specs + [whole_spec(bias.shape)] + [row_spec] * 3,
         [row_spec, whole_spec(memory), whole_spec(memory)],
         [jax.ShapeDtypeStruct(shape, BF16) for shape in ((rows, width), memory, memory)],
-        [pltpu.VMEM((slots, 2 * piece, LANES), BF16)] * 2,
-        (pairs,),
+        [pltpu.VMEM((slots, 2 * piece, WIDE), BF16)] * 2,
+        (steps,),
         {},
     )
 
@@ -624,7 +644,8 @@
         ]
 
 
-def weight_call(order, name, bits, weights, plan, inputs, outs, scratch, body):
+def weight_call(order, name, bits, weights, plan, inputs, outs, scratch, body, streams=None, sends=0):
+    streams = streams or {}
     arrays = []
     for weight in weights:
         arrays += [a for a in weight.pieces() if not any(a is b for b in arrays)]
@@ -635,12 +656,17 @@
     else:
         chunk = (size, 2, lead.rows, lead.width)
     n_in, n_arrays, n_out = len(inputs), len(arrays), len(outs)
+    streamed = sorted(streams)
+    most = max([1] + [inputs[i].shape[1] // streams[i] for i in streamed])
 
     def kernel(bits_ref, *refs):
-        ins, refs = refs[:n_in], refs[n_in:]
+        ins, refs = list(refs[:n_in]), refs[n_in:]
         pieces, refs = refs[:n_arrays], refs[n_arrays:]
         out_refs, refs = refs[:n_out], refs[n_out:]
-        held, sems = refs[-2:]
+        held, sems, stream_sems, send_sems = refs[-4:]
+        staged = refs[: n_out if sends else 0]
+        stream_refs = refs[len(staged) : len(staged) + len(streamed)]
+        rest = refs[len(staged) + len(streamed) : -4]
         bits_now = [bits_ref[i] for i in range(3)]
 
         def find(array):
@@ -654,7 +680,7 @@
             ):
                 pltpu.make_async_copy(source, target, sems.at[slot]).start()
 
-        taken = [0]
+        taken, coming, sent = [0], {}, []
 
         def fetch():
             number = taken[0]
@@ -665,19 +691,52 @@
             pltpu.make_async_copy(held.at[slot], held.at[slot], sems.at[slot]).wait()
             return held[slot].reshape(-1, chunk[-1])
 
+        def need(which, part=0):
+            coming.pop((which, part)).wait()
+
+        def send(which, columns=None):
+            columns = slice(None) if columns is None else columns
+            copy = pltpu.make_async_copy(
+                staged[which].at[:, columns], out_refs[which].at[:, columns], send_sems.at[len(sent)]
+            )
+            copy.start()
+            sent.append(copy)
+
+        fetch.need, fetch.send = need, send
         issue(0)
-        body(fetch, ins, out_refs, refs[:-2])
-
+        for number, which in enumerate(streamed):
+            count = streams[which]
+            for part in range(inputs[which].shape[1] // count):
+                columns = pl.ds(part * count, count)
+                copy = pltpu.make_async_copy(
+                    ins[which].at[:, columns],
+                    stream_refs[number].at[:, columns],
+                    stream_sems.at[number, part],
+                )
+                copy.start()
+                coming[which, part] = copy
+            ins[which] = stream_refs[number]
+        body(fetch, ins, staged if sends else out_refs, rest)
+        for copy in sent + list(coming.values()):
+            copy.wait()
+
+    hbm, vmem = pl.BlockSpec(memory_space=pltpu.HBM), pl.BlockSpec(memory_space=pltpu.VMEM)
     return order.launch(
         kernel,
         name,
         [bits, *inputs, *arrays],
-        [pl.BlockSpec(memory_space=pltpu.VMEM)] * n_in
-        + [pl.BlockSpec(memory_space=pltpu.HBM)] * n_arrays,
-        [pl.BlockSpec(memory_space=pltpu.VMEM)] * n_out,
+        [hbm if i in streams else vmem for i in range(n_in)] + [hbm] * n_arrays,
+        [hbm if sends else vmem] * n_out,
         [jax.ShapeDtypeStruct(shape, kind) for shape, kind in outs],
-        [pltpu.VMEM(shape, kind) for shape, kind in scratch]
-        + [pltpu.VMEM((2, *chunk), BF16), pltpu.SemaphoreType.DMA((2,))],
+        ([pltpu.VMEM(shape, kind) for shape, kind in outs] if sends else [])
+        + [pltpu.VMEM(inputs[i].shape, inputs[i].dtype) for i in streamed]
+        + [pltpu.VMEM(shape, kind) for shape, kind in scratch]
+        + [
+            pltpu.VMEM((2, *chunk), BF16),
+            pltpu.SemaphoreType.DMA((2,)),
+            pltpu.SemaphoreType.DMA((max(1, len(streamed)), most)),
+            pltpu.SemaphoreType.DMA((max(1, sends),)),
+        ],
         None,
         {},
     )
@@ -727,16 +786,35 @@
     )[0]
 
 
-def project(order, name, bits, weight, sources, size):
+def project(order, name, bits, weight, sources, size, groups=None):
+    groups = groups or [1] * len(sources)
+    goals = []
+    for number, count in enumerate(groups):
+        row = 0
+        for _ in range(count):
+            goals.append((number, row))
+            row += sources[len(goals) - 1].shape[0]
+    rows = [
+        sum(source.shape[0] for source, (which, _) in zip(sources, goals) if which == number)
+        for number in range(len(groups))
+    ]
+
     def body(fetch, ins, outs, scratch):
         for start in range(0, weight.width, size):
-            chunk = fetch()
-            for source, target in zip(ins, outs):
-                target[:, start : start + size] = plain_dot(source[...], chunk).astype(BF16)
+            chunk, columns = fetch(), slice(start, start + size)
+            for number, (source, (which, row)) in enumerate(zip(ins, goals)):
+                if start == 0:
+                    fetch.need(number)
+                block = slice(row, row + source.shape[0])
+                outs[which][block, columns] = plain_dot(source[...], chunk).astype(BF16)
+            for which in range(len(groups)):
+                fetch.send(which, columns)
 
     return weight_call(
         order, name, bits, [weight], columns_plan(0, weight.width, size), sources,
-        [((source.shape[0], weight.width), BF16) for source in sources], [], body,
+        [((count, weight.width), BF16) for count in rows], [], body,
+        {i: source.shape[1] for i, source in enumerate(sources)},
+        weight.width // size * len(groups),
     )
 
 
@@ -747,10 +825,14 @@
     def body(fetch, ins, outs, scratch):
         mixed_ref, residual_ref, table_ref = ins
         summed, out, out_low = outs[:3]
+        fetch.need(0)
         for start in range(0, width, size):
             part = plain_dot(mixed_ref[...], fetch())
+            if start == 0:
+                fetch.need(1)
             columns = slice(start, start + size)
             summed[:, columns] = ALPHA * residual_ref[:, columns].astype(F32) + part
+        fetch.send(0)
         gain, shift = table_ref[index : index + 1, :], table_ref[3 + index : 4 + index, :]
 
         def step(block):
@@ -760,10 +842,13 @@
             out_low[block, :] = values.astype(BF16)
 
         row_blocks(rows, 128, step)
+        fetch.send(1)
+        fetch.send(2)
         if query_weight is not None:
             for start in range(0, width, size):
                 part = plain_dot(out_low[...], fetch())
                 outs[3][:, start : start + size] = part.astype(BF16)
+            fetch.send(3)
 
     weights = [weight] + ([query_weight] if query_weight is not None else [])
     plan = [entry for i in range(len(weights)) for entry in columns_plan(i, width, size)]
@@ -771,7 +856,8 @@
     if query_weight is not None:
         outs.append(((rows, width), BF16))
     return weight_call(
-        order, name, bits, weights, plan, [mixed, residual, table], outs, [], body
+        order, name, bits, weights, plan, [mixed, residual, table], outs, [], body,
+        {0: width, 1: width}, len(outs),
     )
 
 
@@ -780,6 +866,7 @@
 
     def body(fetch, ins, outs, scratch):
         held = scratch[0]
+        fetch.need(0)
         for start in range(0, weight.width, size):
             held[...] = plain_dot(ins[0][...], fetch())
 
@@ -791,11 +878,13 @@
                 outs[1][block, start : start + size] = (below + hidden * density).astype(BF16)
 
             row_blocks(rows, 256, step)
+            for which in range(2):
+                fetch.send(which, slice(start, start + size))
 
     out = ((rows, weight.width), BF16)
     return weight_call(
         order, "feed_in", bits, [weight], columns_plan(0, weight.width, size), [source], [out, out],
-        [((rows, size), F32)], body,
+        [((rows, size), F32)], body, {0: source.shape[1]}, 2 * weight.width // size,
     )
 
 
@@ -807,10 +896,14 @@
         act_ref, residual_ref, table_ref, up_ref = ins
         layer_out, grad, grad_low, stats = outs
         summed = scratch[0]
+        fetch.need(0)
         for start in range(0, width, size):
             columns = slice(start, start + size)
             part = plain_dot(act_ref[...], fetch())
+            if start == 0:
+                fetch.need(1)
             summed[:, columns] = ALPHA * residual_ref[:, columns] + part
+        fetch.need(3)
         gain, shift = table_ref[2:3, :], table_ref[5:6, :]
         stats[...] = jnp.zeros_like(stats)
 
@@ -829,6 +922,7 @@
     return weight_call(
         order, "feed_out", bits, [weight], columns_plan(0, width, size),
         [activated, residual, table, cotangent], outs, [((rows, width), F32)], body,
+        {0: activated.shape[1], 1: width, 3: width},
     )
 
 
@@ -838,15 +932,19 @@
     steps = features // size
 
     def body(fetch, ins, outs, scratch):
+        fetch.need(0)
         for number in range(steps):
             part = back_dot(ins[0][...], fetch())
+            fetch.need(1, number)
             columns = slice(number * size, (number + 1) * size)
             outs[0][:, columns] = (part * ins[1][:, columns].astype(F32)).astype(BF16)
+            fetch.send(0, columns)
 
     blocks = weight.blocks // steps
     return weight_call(
         order, "feed_back", bits, [weight], [(0, "rows", i * blocks, blocks) for i in range(steps)],
         [cotangent, slope], [((rows, features), BF16)], [], body,
+        {0: cotangent.shape[1], 1: size}, steps,
     )[0]
 
 
@@ -858,9 +956,13 @@
         up_ref, carried_ref, summed_ref, table_ref = ins
         grad, grad_low, grad_mixed, stats = outs
         total = scratch[0]
-        for start in range(0, weight.width, size):
+        for number, start in enumerate(range(0, weight.width, size)):
+            fetch.need(0, number)
             part = back_dot(up_ref[:, start : start + size], fetch())
+            if start == 0:
+                fetch.need(1)
             total[...] = part + (ALPHA * carried_ref[...] if start == 0 else total[...])
+        fetch.need(2)
         gain = table_ref[index : index + 1, :]
         stats[...] = jnp.zeros_like(stats)
 
@@ -873,13 +975,17 @@
             add_stats(stats, normed, upstream)
 
         row_blocks(rows, 128, step)
+        for which in (0, 1, 3):
+            fetch.send(which)
         grad_mixed[...] = back_dot(grad_low[...], fetch()).astype(BF16)
+        fetch.send(2)
 
     outs = [((rows, width), F32), ((rows, width), BF16), ((rows, width), BF16), ((16, width), F32)]
     return weight_call(
         order, name, bits, [weight, mix_weight],
         columns_plan(0, weight.width, size) + columns_plan(1, width, size),
         [cotangent, carried, summed, table], outs, [((rows, width), F32)], body,
+        {0: size, 1: width, 2: width}, len(outs),
     )
 
 
@@ -887,10 +993,16 @@
     rows, features = cotangents[0].shape[0], weight.features
     step = 512 if rows % 512 == 0 else rows // 2
     count = len(cotangents)
+    streams = {which: size for which, _, _, size in spans}
+    if carried is not None:
+        streams[count] = carried.shape[1]
 
     def body(fetch, ins, outs, scratch):
         for number, (which, first, _, size) in enumerate(spans):
             chunk = fetch()
+            fetch.need(which, first // size)
+            if number == 0 and carried is not None:
+                fetch.need(count)
             for row in range(0, rows, step):
                 block = slice(row, row + step)
                 part = back_dot(ins[which][block, first : first + size], chunk)
@@ -906,7 +1018,7 @@
     return weight_call(
         order, name, bits, [weight], [(0, "columns", start, size) for _, _, start, size in spans],
         [*cotangents] + ([carried] if carried is not None else []),
-        [((rows, features), BF16)], [((rows, features), F32)], body,
+        [((rows, features), BF16)], [((rows, features), F32)], body, streams,
     )[0]
 
 
@@ -962,7 +1074,8 @@
     n_grads = len(cotangents)
     total_rows = n_grads // 2 * each
     shard_rows = half_features // (4 * outer)
-    chunk = 512 if cut is None or cut % 512 == 0 else 256
+    parts = [width] + ([cut, width - cut] if place is None else [place[1], place[2]])
+    chunk = 1024 if all(part % 1024 == 0 for part in parts) else 512
     added = 0 if extra is None else LANES
     n_held = 2 if held is not None else 0
     if place is None:
@@ -1032,7 +1145,9 @@
     return blocks[0], blocks[1]
 
 
-def add_blocks(order, bits, sums, shapes):
+def add_blocks(order, bits, sums, shapes, apart=False):
+    if apart:
+        shapes = [shapes[0][1:]] * shapes[0][0]
     arrays = []
     for group, _, _ in sums:
         arrays += [a for a, _ in group if not any(a is b for b in arrays)]
@@ -1047,9 +1162,10 @@
         loads, stores = [], []
         for index, (number, place) in enumerate(chunks):
             loads.append([])
+            block = place ^ bits_ref[3] if apart else place
             for term, (array, at) in enumerate(sums[number][0]):
                 load = pltpu.make_async_copy(
-                    sources[find(array)].at[(*at, place)],
+                    sources[find(array)].at[(*at, block)],
                     held[number].at[term, place],
                     load_sems.at[index, term],
                 )
@@ -1061,11 +1177,9 @@
                 load.wait()
             values = [held[number][term, place].astype(F32) for term in range(len(group))]
             summed[number][place] = sum(values[1:], values[0]).astype(BF16)
-            store = pltpu.make_async_copy(
-                summed[number].at[place],
-                targets[which].at[place, :, pl.ds(column, blocks[number][2])],
-                store_sems.at[index],
-            )
+            columns = pl.ds(column, blocks[number][2])
+            goal = targets[place].at[:, columns] if apart else targets[which].at[place, :, columns]
+            store = pltpu.make_async_copy(summed[number].at[place], goal, store_sems.at[index])
             store.start()
             stores.append(store)
         for store in stores:
@@ -1126,7 +1240,7 @@
             outer, rows, columns = shapes[-1]
             sums.append((group, len(shapes) - 1, columns))
             shapes[-1] = (outer, rows, columns + block_shape(group)[2])
-    filled = add_blocks(order, bits, sums, shapes)
+    filled = add_blocks(order, bits, sums, shapes, together)
     start = 0
     for wave in seconds:
         wave.send(filled[start : start + len(wave.kinds)])
@@ -1141,25 +1255,14 @@
     )
 
 
-def outer_swaps(joined):
-    place = lax.axis_index("dp") >> 2
-    block = lambda far: lax.dynamic_index_in_dim(joined, place ^ far, 0, False)
-    return [swap_outer(block(far), far) for far in range(1, joined.shape[0])]
-
-
-def last_shards(order, bits, joined, others, summed, spans):
-    outer, rows, columns = joined.shape
+def last_shards(order, bits, parts, summed, spans):
+    rows, columns = parts[0].shape
     widths = [sum(size for _, _, size in span) for span in spans]
 
-    def kernel(bits_ref, joined_ref, *refs):
-        parts, refs = refs[: len(others)], refs[len(others) :]
-        summed_ref, refs = refs[0], refs[1:]
-        targets, (held, sem) = refs[:-2], refs[-2:]
-        load = pltpu.make_async_copy(joined_ref.at[bits_ref[3]], held, sem)
-        load.start()
-        load.wait()
-        total = held[...].astype(F32)
-        for ref in parts:
+    def kernel(bits_ref, *refs):
+        refs, summed_ref, targets = refs[: len(parts)], refs[len(parts)], refs[len(parts) + 1 :]
+        total = refs[0][...].astype(F32)
+        for ref in refs[1:]:
             total += ref[...].astype(F32)
         for target, span in zip(targets, spans):
             at = 0
@@ -1174,12 +1277,11 @@
     return order.launch(
         kernel,
         "last_shards",
-        [bits, joined, *others, summed],
-        [pl.BlockSpec(memory_space=pltpu.HBM)]
-        + [pl.BlockSpec(memory_space=pltpu.VMEM)] * (len(others) + 1),
+        [bits, *parts, summed],
+        [pl.BlockSpec(memory_space=pltpu.VMEM)] * (len(parts) + 1),
         [pl.BlockSpec(memory_space=pltpu.VMEM)] * len(spans),
         [jax.ShapeDtypeStruct((rows, width), F32) for width in widths],
-        [pltpu.VMEM((rows, columns), BF16), pltpu.SemaphoreType.DMA],
+        [],
         None,
         {},
     )
@@ -1259,16 +1361,16 @@
 
     class Grad:
         def __init__(self, *places):
-            self.sources = [source for _, source in places]
+            self.sources = [source for _, *sources in places for source in sources]
             self.turned = []
             for side in range(2 if staged else 0):
-                for turned, source in places:
+                for turned, *sources in places:
                     start = 0
                     for other in turned.sources:
-                        if other is source:
+                        if other is sources[0]:
                             break
                         start += other.shape[0]
-                    stop = start + source.shape[0]
+                    stop = start + sum(source.shape[0] for source in sources)
                     size = math.gcd(start, stop)
                     for at in range(start, stop, size):
                         self.turned.append((turned.both[side], at, size))
@@ -1321,7 +1423,7 @@
         places = [moves.passed(shard) for shard in shards[1:]]
         moves.then.append(lambda filled: shards.__setitem__(slice(1, None), [filled[i] for i in places]))
         moves.run()
-    lead = 5 * model_width // 2
+    lead = 2 * model_width + LANES
     w_cq, w_co, w_norm, w_ckv, w_so = gather(
         1, [(0, lead, 0), (lead, 5 * model_width + LANES - lead, 1)]
     )
@@ -1357,15 +1459,17 @@
     (united,) = project(order, "self_project", bits, w_qkv, [target_in], 1024)
     far_parts += [swap_mem(part) for part in gate(order, bits, sent_rows[1:])]
     steps((w_in, "first"))
+    order.before(key_columns)
     self_mixed, self_log = self_forward(order, self_meta, united)
-    far_flat = jnp.concatenate(far_parts, axis=0)
     order.part()
     steps((w_ckv, "third"))
     order.before(*far_parts[1:])
     order.part()
     steps((w_out, "first"))
     table = norm_table(order, bits, w_norm)
-    near_kv, far_kv = project(order, "cross_project", bits, w_ckv, [near_flat, far_flat], 1024)
+    near_kv, far_kv = project(
+        order, "cross_project", bits, w_ckv, [near_flat, *far_parts], 1024, [1, len(far_parts)]
+    )
     near_kv, far_kv = near_kv.reshape(slotted), far_kv.reshape(slotted)
     order.part()
     steps((w_in, "second"), (w_out, "second"))
@@ -1378,11 +1482,9 @@
     sum_two, second_out, second_low = mix_norm(
         order, "cross_mix", bits, w_co, cross_mixed, first_out, table, 1
     )
+    later = Turned(self_mixed, first_low, cross_mixed, second_low, *far_parts)
     order.part()
-    steps((w_in, "third"))
-    later = Turned(self_mixed, first_low, cross_mixed, second_low, far_flat)
-    order.part()
-    steps((w_out, "third"))
+    steps((w_in, "third"), (w_out, "third"))
     activated, slope = feed_in(order, bits, w_in, second_low)
     later.due()
     hidden = Turned(activated)
@@ -1391,7 +1493,7 @@
     )
     qkv_grad = Grad((first_turned, target_in))
     so_grad = Grad((later, self_mixed))
-    ckv_grad = Grad((first_turned, near_flat), (later, far_flat))
+    ckv_grad = Grad((first_turned, near_flat), (later, *far_parts))
     cq_grad = Grad((later, first_low))
     co_grad = Grad((later, cross_mixed))
     in_grad = Grad((later, second_low))
@@ -1459,8 +1561,9 @@
         own, other = relative_rows(bits, norm_grads, outer)
         own = (own.astype(F32) + swap_core(other).astype(F32)).astype(BF16)
         norm_grads = (own[..., :LANES], own[..., LANES:])
+        far_parts = ckv_grad.make(place=(1, 0, pair_width))
         near_parts = cq_grad.make(place=(0, model_width, pair_width), held=near_parts)
-        mid_parts = [*near_parts, *ckv_grad.make(place=(1, 0, pair_width))]
+        mid_parts = [*near_parts, *far_parts]
     else:
         mid_parts = jnp.concatenate([near_parts, cq_grad.make(), ckv_grad.make()], axis=1)
     mid_wave = spread("mid", mid_parts, (0, 1))
@@ -1473,10 +1576,15 @@
         self_mixed,
         grad_self_mixed,
         self_log,
-        0,
-        model_width // LANES,
     )
     qkv_grad.take(grad_united)
+    half_width = model_width // 2
+    if staged:
+        so_wave = spread("so", so_grad.make(half_width, extra=norm_grads), (0, 1))
+    else:
+        part = so_grad.make()
+        columns = [part[:, :half_width], norm_grads[:, :LANES], part[:, half_width:], norm_grads[:, LANES:]]
+        so_wave = spread("so", jnp.concatenate(columns, axis=1), (0, 1))
     order.part()
     advance([mid_wave])
     qkv_wave = spread("qkv", qkv_grad.make(qkv_half), (0, 1))
@@ -1484,13 +1592,6 @@
         order.before(shards["out"], shards["in"])
         order.part()
         advance([], [("mid", mid_wave)])
-    half_width = model_width // 2
-    if staged:
-        so_wave = spread("so", so_grad.make(half_width, extra=norm_grads), (0, 1))
-    else:
-        part = so_grad.make()
-        columns = [part[:, :half_width], norm_grads[:, :LANES], part[:, half_width:], norm_grads[:, LANES:]]
-        so_wave = spread("so", jnp.concatenate(columns, axis=1), (0, 1))
     split = half_width + LANES
     grad_far = memory_back(grad_far_kv)
     if staged:
@@ -1498,12 +1599,12 @@
         advance([qkv_wave, so_wave])
         (grad_far,) = gate(order, bits, [grad_far])
     grad_far = swap_mem(grad_far)
-    grad_near = memory_back(grad_near_kv)
     if staged:
         order.before(shards["mid"])
         order.part()
-        (joined,) = spread_steps(order, bits, [], [so_wave, qkv_wave], True)
-        others = outer_swaps(joined)
+        blocks = spread_steps(order, bits, [], [so_wave, qkv_wave], True)
+        blocks = [blocks[0]] + [swap_outer(blocks[far], far) for far in range(1, outer)]
+    grad_near = memory_back(grad_near_kv)
     target_grad = input_back(
         order,
         "target_back",
@@ -1519,7 +1620,7 @@
     mid_spans.append([(1, 2 * model_width, 2 * model_width)])
     spans = [[(0, 2 * split, 2 * qkv_half)], so_spans, *norm_spans, *mid_spans]
     if staged:
-        last = last_shards(order, bits, joined, others, shards["mid"], spans)
+        last = last_shards(order, bits, blocks, shards["mid"], spans)
         moves = Moves(order, bits)
         target = moves.target((2, *near_flat.shape))
         for number, part in enumerate((grad_near, grad_far)):

time: 554 us -> 540 us (0.975)
  Pallas kernels: 357 us -> 343 us
  waiting for transfers between devices: 90.6 us -> 102 us
  local copies, waits for them, and re-layouts: 16.2 us -> 8.39 us
    ppermute x16, waiting for transfers between devices: 26.3 us -> 41.7 us  [swap_next(): return lax.ppermute(values, 'dp', [(i, i ^ 2) for i in range(size)])]
    pallas_call x51 -> x50, Pallas kernels: 357 us -> 343 us  [launch(): results = run(*operands, *ties)]
    ppermute x16, waiting for transfers between devices: 2.87 us -> 16.6 us  [swap_core(): return lax.ppermute(values, 'dp', [(i, i ^ 1) for i in range(size)])]
    ppermute x20, waiting for transfers between devices: 38 us -> 29.9 us  [swap_mem(): return lax.ppermute(values, 'mem', [(0, 1), (1, 0)])]
  transfers between devices with their start and end apart: 64 -> 64, of which waited for: 17 -> 22; matrix products, arithmetic and copies ran while one was open for 5% -> 3% of each run, Pallas kernels for 60% -> 58%
where the time goes in v4:
time: 540 us; the launch traced here: 532 us
  Pallas kernels  343 us (64%)
  waiting for transfers between devices  102 us (19%)
  starting transfers between devices  51.4 us (10%)
  between operations  15.9 us (3%)
  other arithmetic  10.5 us (2%)
  local copies, waits for them, and re-layouts  8.39 us (2%)
    pallas_call x50, Pallas kernels, launch(): results = run(*operands, *ties)  343 us
    ppermute x16, waiting for transfers between devices, swap_next(): return lax.ppermute(values, 'dp', [(i, i ^ 2) for i in range(size)])  41.7 us
    ppermute x20, waiting for transfers between devices, swap_mem(): return lax.ppermute(values, 'mem', [(0, 1), (1, 0)])  29.9 us
    ppermute x20, starting transfers between devices, swap_mem(): return lax.ppermute(values, 'mem', [(0, 1), (1, 0)])  21.5 us
    ppermute x16, starting transfers between devices, swap_next(): return lax.ppermute(values, 'dp', [(i, i ^ 2) for i in range(size)])  18.1 us
    ppermute x16, waiting for transfers between devices, swap_core(): return lax.ppermute(values, 'dp', [(i, i ^ 1) for i in range(size)])  16.6 us
    all_gather x3, waiting for transfers between devices, outer_gather(): lax.all_gather(shard, 'dp', axis_index_groups=outer_groups(), axis=0, til...  11 us
  transfers between devices with their start and end apart: 64, of which 22 were waited for; matrix products, arithmetic and copies ran while one was open for 3% of the time, Pallas kernels for 58%

profile of v4, /device:TPU:0, one launch (start us, length us, event | category | flops | bytes accessed | tf_op | source)
XLA Modules:
  0.0 531.8 jit_solution(11917374972254361748)
XLA Ops:
  11.9 3.5 move_blocks.12
  18.5 3.6 collective-permute-start.2
  23.7 12.6 %collective-permute-done.4.refs_9_ = s32[2,384]{1,0:T(2,128)S(1)} collective-permute-done((s32[2,384]{1,0:T(2,128)S(1)}, s32[2,384]{1,0:T(2,128)S(1)}, u32[]{:S(2)}, u32[]{:S(2)}) %collective-permute-start.4) | collective-permute-done | bytes 3104 | tf_op jit(solution)/shard_map/ppermute | solution.py:406
  43.7 8.4 %collective-permute-done.5.refs_2_ = bf16[4,32,1536]{2,1,0:T(8,128)(2,1)} collective-permute-done((bf16[4,32,1536]{2,1,0:T(8,128)(2,1)}, bf16[4,32,1536]{2,1,0:T(8,128)(2,1)}, u32[]{:S(2)}, u32[]{:S(2)}) %collective-permute-start.5) | collective-permute-done | bytes 393248 | tf_op jit(solution)/shard_map/ppermute | solution.py:402
  53.3 3.6 move_blocks.14
  58.0 5.5 %turn_rows.3 = (bf16[512,1280]{1,0:T(8,128)(2,1)}, bf16[512,1280]{1,0:T(8,128)(2,1)}) custom-call(s32[4]{0:T(128)} %pad_add_fusion.refs_0_, bf16[512,1024]{1,0:T(8,128)(2,1)} %refs_2_.3, bf16[768,1024]{1,0:T(8,128)(2,1)} %bitcast.85, bf16[2,4,32,1536]{3,2,1,0:T(8,128)(2,1)} %get-tuple-element.127.refs_3_), custom_call_target="tpu_custom_call" | custom-call | flops 999999995904 | bytes 1 | tf_op jit(solution)/shard_map/turn_rows/pallas_call | solution.py:99
  63.6 11.0 %all-gather.4.cloned.1.call-done = bf16[128,5248]{1,0:T(8,128)(2,1)} async-done(((bf16[32,5248]{1,0:T(8,128)(2,1)}), bf16[128,5248]{1,0:T(8,128)(2,1)}) %all-gather.4.cloned.1.call-update) | async-done | bytes 1343504 | tf_op jit(solution)/shard_map/all_gather | solution.py:425
  83.7 7.9 %collective-permute-done.10.refs_2_ = bf16[4,32,2176]{2,1,0:T(8,128)(2,1)} collective-permute-done((bf16[4,32,2176]{2,1,0:T(8,128)(2,1)}, bf16[4,32,2176]{2,1,0:T(8,128)(2,1)}, u32[]{:S(2)}, u32[]{:S(2)}) %collective-permute-start.10) | collective-permute-done | bytes 557088 | tf_op jit(solution)/shard_map/ppermute | solution.py:402
  91.5 6.1 %collective-permute-done.11.refs_4_ = bf16[4,32,3072]{2,1,0:T(8,128)(2,1)} collective-permute-done((bf16[4,32,3072]{2,1,0:T(8,128)(2,1)}, bf16[4,32,3072]{2,1,0:T(8,128)(2,1)}, u32[]{:S(2)}, u32[]{:S(2)}) %collective-permute-start.11) | collective-permute-done | bytes 786464 | tf_op jit(solution)/shard_map/ppermute | solution.py:406
  97.6 4.5 move_blocks.17
  108.3 8.1 %self_project.1.refs_2_.refs_1_.refs_3_ = bf16[512,3072]{1,0:T(8,128)(2,1)} custom-call(s32[4]{0:T(128)} %pad_add_fusion.refs_0_, bf16[512,1024]{1,0:T(8,128)(2,1)} %refs_2_.3, bf16[8,64,3072]{2,1,0:T(8,128)(2,1)} %bitcast.83, bf16[8,64,3072]{2,1,0:T(8,128)(2,1)} %collective-permute-done.9.refs_3_.refs_4_, bf16[2,4,32,2176]{3,2,1,0:T(8,128)(2,1)} %get-tuple-element.134.refs_4_), custom_call_target="tpu_custom_call" | custom-call | flops 1000000 | bytes 1 | tf_op jit(solution)/shard_map/self_project/pallas_call | solution.py:99
  120.9 12.8 %self_forward.1 = (bf16[512,1024]{1,0:T(8,128)(2,1)}, f32[512,1024]{1,0:T(8,128)}) custom-call(s32[3]{0:T(128)} %pad_add_fusion.1.refs_0_, bf16[512,3072]{1,0:T(8,128)(2,1)} %self_project.1.refs_2_.refs_1_.refs_3_, bf16[512,3072]{1,0:T(8,128)(2,1)} %self_project.1.refs_2_.refs_1_.refs_3_, bf16[512,3072]{1,0:T(8,128)(2,1)} %self_project.1.refs_2_.refs_1_.refs_3_, ...), custom_call_target="tpu_custom_call" | custom-call | flops 1000000 | bytes 1 | tf_op jit(solution)/shard_map/self_forward/pallas_call | solution.py:99
  133.7 6.2 %collective-permute-done.14.refs_3_ = bf16[2,4,32,3072]{3,2,1,0:T(8,128)(2,1)} collective-permute-done((bf16[2,4,32,3072]{3,2,1,0:T(8,128)(2,1)}, bf16[2,4,32,3072]{3,2,1,0:T(8,128)(2,1)}, u32[]{:S(2)}, u32[]{:S(2)}) %collective-permute-start.14) | collective-permute-done | bytes 1572896 | tf_op jit(solution)/shard_map/ppermute | solution.py:402
  146.4 6.2 %collective-permute-done.15.refs_2_.refs_5_.refs_8_.refs_6_.refs_3_ = bf16[8,64,5248]{2,1,0:T(8,128)(2,1)} collective-permute-done((bf16[8,64,5248]{2,1,0:T(8,128)(2,1)}, bf16[8,64,5248]{2,1,0:T(8,128)(2,1)}, u32[]{:S(2)}, u32[]{:S(2)}) %collective-permute-start.15) | collective-permute-done | bytes 5373984 | tf_op jit(solution)/shard_map/ppermute | solution.py:397
  155.0 11.2 %cross_project.1 = (bf16[768,2048]{1,0:T(8,128)(2,1)}, bf16[768,2048]{1,0:T(8,128)(2,1)}) custom-call(s32[4]{0:T(128)} %pad_add_fusion.refs_0_, bf16[768,1024]{1,0:T(8,128)(2,1)} %bitcast.86, bf16[384,1024]{1,0:T(8,128)(2,1)} %collective-permute-done.3.refs_8_.refs_2_.refs_5_, bf16[384,1024]{1,0:T(8,128)(2,1)} %collective-permute-done.16.refs_2_.refs_3_.refs_6_, ...), custom_call_target="tpu_custom_call" | custom-call | flops 1000000 | bytes 1 | tf_op jit(solution)/shard_map/cross_project/pallas_call | solution.py:99
  166.2 3.9 collective-permute-done.18.refs_4_
  170.1 5.4 %move_blocks.21 = (bf16[2,4,32,4096]{3,2,1,0:T(8,128)(2,1)}, bf16[4,2,2,32,4096]{4,3,2,1,0:T(8,128)(2,1)}, bf16[2,4,128,1024]{3,2,1,0:T(8,128)(2,1)}, bf16[4,2,2,128,1024]{4,3,2,1,0:T(8,128)(2,1)}) custom-call(s32[4]{0:T(128)} %pad_add_fusion.refs_0_, bf16[4,32,4096]{2,1,0:T(8,128)(2,1)} %move_blocks.18.refs_5_.refs_1_, ...), custom_call_target="tpu_custom_call" | custom-call | flops 999999995904 | bytes 1 | tf_op jit(solution)/shard_map/move_blocks/pallas_call | solution.py:99
  178.4 7.6 %self_mix.1 = (f32[512,1024]{1,0:T(8,128)}, f32[512,1024]{1,0:T(8,128)}, bf16[512,1024]{1,0:T(8,128)(2,1)}, bf16[512,1024]{1,0:T(8,128)(2,1)}) custom-call(s32[4]{0:T(128)} %pad_add_fusion.refs_0_, bf16[512,1024]{1,0:T(8,128)(2,1)} %get-tuple-element.137.refs_4_.refs_1_, bf16[512,1024]{1,0:T(8,128)(2,1)} %refs_2_.3, ...), custom_call_target="tpu_custom_call" | custom-call | flops 1000000 | bytes 1 | tf_op jit(solution)/shard_map/self_mix/pallas_call | solution.py:99
  186.0 17.2 %cross_forward.1 = (bf16[512,1024]{1,0:T(8,128)(2,1)}, f32[512,1024]{1,0:T(8,128)}) custom-call(s32[1]{0:T(128)} %bitcast.5.refs_0_, bf16[512,1024]{1,0:T(8,128)(2,1)} %get-tuple-element.143.refs_1_, bf16[2,384,2048]{2,1,0:T(8,128)(2,1)} %bitcast.68, bf16[2,384,2048]{2,1,0:T(8,128)(2,1)} %bitcast.69, bf16[2,384,2048]{2,1,0:T(8,128)(2,1)} %bitcast.72, ...), custom_call_target="tpu_custom_call" | custom-call | flops 1000000 | bytes 1 | tf_op jit(solution)/shard_map/cross_forward/pallas_call | solution.py:99
  203.2 6.9 %cross_mix.1 = (f32[512,1024]{1,0:T(8,128)}, f32[512,1024]{1,0:T(8,128)}, bf16[512,1024]{1,0:T(8,128)(2,1)}) custom-call(s32[4]{0:T(128)} %pad_add_fusion.refs_0_, bf16[512,1024]{1,0:T(8,128)(2,1)} %get-tuple-element.146.refs_1_.refs_3_.refs_7_, f32[512,1024]{1,0:T(8,128)} %get-tuple-element.147.refs_2_, f32[8,1024]{1,0:T(8,128)} %norm_table.1.refs_6_.refs_3_.refs_4_, ...), custom_call_target="tpu_custom_call" | custom-call | flops 1000000 | bytes 1 | tf_op jit(solution)/shard_map/cross_mix/pallas_call | solution.py:99
  210.1 11.2 %turn_rows.4 = (bf16[512,2816]{1,0:T(8,128)(2,1)}, bf16[512,2816]{1,0:T(8,128)(2,1)}) custom-call(s32[4]{0:T(128)} %pad_add_fusion.refs_0_, bf16[512,1024]{1,0:T(8,128)(2,1)} %get-tuple-element.137.refs_4_.refs_1_, bf16[512,1024]{1,0:T(8,128)(2,1)} %get-tuple-element.152.refs_2_, bf16[512,1024]{1,0:T(8,128)(2,1)} %get-tuple-element.146.refs_1_.refs_3_.refs_7_, ...), custom_call_target="tpu_custom_call" | custom-call | flops 1000000 | bytes 1 | tf_op jit(solution)/shard_map/turn_rows/pallas_call | solution.py:99
  222.5 4.5 move_blocks.22
  227.7 6.9 %collective-permute-done.21.refs_3_.refs_6_ = bf16[8,64,4096]{2,1,0:T(8,128)(2,1)} collective-permute-done((bf16[8,64,4096]{2,1,0:T(8,128)(2,1)}, bf16[8,64,4096]{2,1,0:T(8,128)(2,1)}, u32[]{:S(2)}, u32[]{:S(2)}) %collective-permute-start.21) | collective-permute-done | bytes 4194336 | tf_op jit(solution)/shard_map/ppermute | solution.py:397
  234.6 13.0 %feed_in.1 = (bf16[512,4096]{1,0:T(8,128)(2,1)}, bf16[512,4096]{1,0:T(8,128)(2,1)}) custom-call(s32[4]{0:T(128)} %pad_add_fusion.refs_0_, bf16[512,1024]{1,0:T(8,128)(2,1)} %get-tuple-element.148.refs_4_.refs_1_, bf16[8,64,4096]{2,1,0:T(8,128)(2,1)} %bitcast.77, bf16[8,64,4096]{2,1,0:T(8,128)(2,1)} %collective-permute-done.21.refs_3_.refs_6_, ...), custom_call_target="tpu_custom_call" | custom-call | flops 1000000 | bytes 1 | tf_op jit(solution)/shard_map/feed_in/pallas_call | solution.py:99
  247.6 7.2 %turn_rows.5 = (bf16[2048,512]{1,0:T(8,128)(2,1)}, bf16[2048,512]{1,0:T(8,128)(2,1)}) custom-call(s32[4]{0:T(128)} %pad_add_fusion.refs_0_, bf16[512,4096]{1,0:T(8,128)(2,1)} %get-tuple-element.156.refs_1_, bf16[512,2816]{1,0:T(8,128)(2,1)} %collective-permute-done.23.refs_2_.refs_10_.refs_11_.refs_12_), custom_call_target="tpu_custom_call" | custom-call | flops 1000000 | bytes 1 | tf_op jit(solution)/shard_map/turn_rows/pallas_call | solution.py:99
  254.9 13.8 %feed_out.1 = (bf16[512,1024]{1,0:T(8,128)(2,1)}, f32[512,1024]{1,0:T(8,128)}, bf16[512,1024]{1,0:T(8,128)(2,1)}, f32[16,1024]{1,0:T(8,128)}) custom-call(s32[4]{0:T(128)} %pad_add_fusion.refs_0_, bf16[512,4096]{1,0:T(8,128)(2,1)} %get-tuple-element.156.refs_1_, f32[512,1024]{1,0:T(8,128)} %get-tuple-element.157.refs_2_, ...), custom_call_target="tpu_custom_call" | custom-call | flops 1000000 | bytes 1 | tf_op jit(solution)/shard_map/feed_out/pallas_call | solution.py:99
  271.8 10.4 %weight_grad.7 = (bf16[2,4,128,512]{3,2,1,0:T(8,128)(2,1)}, bf16[2,4,128,512]{3,2,1,0:T(8,128)(2,1)}, bf16[2,4,128,512]{3,2,1,0:T(8,128)(2,1)}, bf16[2,4,128,512]{3,2,1,0:T(8,128)(2,1)}) custom-call(s32[4]{0:T(128)} %pad_add_fusion.refs_0_, bf16[2048,512]{1,0:T(8,128)(2,1)} %get-tuple-element.160.refs_7_.refs_1_, ...), custom_call_target="tpu_custom_call" | custom-call | flops 1000000 | bytes 1 | tf_op jit(solution)/shard_map/weight_grad/pallas_call | solution.py:99
  285.2 11.0 %feed_back.1.refs_1_.refs_3_ = bf16[512,4096]{1,0:T(8,128)(2,1)} custom-call(s32[4]{0:T(128)} %pad_add_fusion.refs_0_, bf16[512,1024]{1,0:T(8,128)(2,1)} %get-tuple-element.162.refs_3_.refs_1_, bf16[512,4096]{1,0:T(8,128)(2,1)} %get-tuple-element.163.refs_2_, bf16[8,256,1024]{2,1,0:T(8,128)(2,1)} %bitcast.81, ...), custom_call_target="tpu_custom_call" | custom-call | flops 1000000 | bytes 1 | tf_op jit(solution)/shard_map/feed_back/pallas_call | solution.py:99
  296.3 14.2 %cross_back.1 = (f32[512,1024]{1,0:T(8,128)}, bf16[512,1024]{1,0:T(8,128)(2,1)}, bf16[512,1024]{1,0:T(8,128)(2,1)}, f32[16,1024]{1,0:T(8,128)}) custom-call(s32[4]{0:T(128)} %pad_add_fusion.refs_0_, bf16[512,4096]{1,0:T(8,128)(2,1)} %feed_back.1.refs_1_.refs_3_, f32[512,1024]{1,0:T(8,128)} %get-tuple-element.166.refs_2_, ...), custom_call_target="tpu_custom_call" | custom-call | flops 1000000 | bytes 1 | tf_op jit(solution)/shard_map/cross_back/pallas_call | solution.py:99
  314.2 10.1 %weight_grad.8 = (bf16[2,4,32,2048]{3,2,1,0:T(8,128)(2,1)}, bf16[2,4,32,2048]{3,2,1,0:T(8,128)(2,1)}, bf16[2,4,32,2048]{3,2,1,0:T(8,128)(2,1)}, bf16[2,4,32,2048]{3,2,1,0:T(8,128)(2,1)}) custom-call(s32[4]{0:T(128)} %pad_add_fusion.refs_0_, bf16[512,2816]{1,0:T(8,128)(2,1)} %get-tuple-element.154.refs_5_.refs_1_.refs_4_.refs_6_, ...), custom_call_target="tpu_custom_call" | custom-call | flops 1000000 | bytes 1 | tf_op jit(solution)/shard_map/weight_grad/pallas_call | solution.py:99
  330.6 4.7 weight_grad.9
  335.3 23.9 %cross_backward.1 = (bf16[512,1024]{1,0:T(8,128)(2,1)}, bf16[768,2048]{1,0:T(8,128)(2,1)}, bf16[768,2048]{1,0:T(8,128)(2,1)}) custom-call(s32[1]{0:T(128)} %bitcast.5.refs_0_, bf16[512,1024]{1,0:T(8,128)(2,1)} %get-tuple-element.143.refs_1_, bf16[2,384,2048]{2,1,0:T(8,128)(2,1)} %bitcast.70, bf16[2,384,2048]{2,1,0:T(8,128)(2,1)} %bitcast.71, ...), custom_call_target="tpu_custom_call" | custom-call | flops 1000000 | bytes 1 | tf_op jit(solution)/shard_map/cross_backward/pallas_call | solution.py:99
  361.6 5.0 add_blocks.8
  366.6 8.9 %self_back.1 = (f32[512,1024]{1,0:T(8,128)}, bf16[512,1024]{1,0:T(8,128)(2,1)}, bf16[512,1024]{1,0:T(8,128)(2,1)}, f32[16,1024]{1,0:T(8,128)}) custom-call(s32[4]{0:T(128)} %pad_add_fusion.refs_0_, bf16[512,1024]{1,0:T(8,128)(2,1)} %get-tuple-element.177.refs_11_.refs_1_.refs_3_, f32[512,1024]{1,0:T(8,128)} %get-tuple-element.173.refs_5_.refs_2_, ...), custom_call_target="tpu_custom_call" | custom-call | flops 1000000 | bytes 1 | tf_op jit(solution)/shard_map/self_back/pallas_call | solution.py:99
  381.8 13.2 %weight_grad.10 = (bf16[2,4,32,2048]{3,2,1,0:T(8,128)(2,1)}, bf16[2,4,32,2048]{3,2,1,0:T(8,128)(2,1)}) custom-call(s32[4]{0:T(128)} %pad_add_fusion.refs_0_, bf16[512,1280]{1,0:T(8,128)(2,1)} %get-tuple-element.130.refs_2_.refs_1_.refs_3_, bf16[512,1280]{1,0:T(8,128)(2,1)} %get-tuple-element.130.refs_2_.refs_1_.refs_3_, ...), custom_call_target="tpu_custom_call" | custom-call | flops 1000000 | bytes 1 | tf_op jit(solution)/shard_map/weight_grad/pallas_call | solution.py:99
  395.5 4.8 weight_grad.11
  400.7 3.6 add_blocks.9.refs_7_
  404.3 14.9 %self_backward.1.refs_7_.refs_3_.refs_1_ = bf16[512,3072]{1,0:T(8,128)(2,1)} custom-call(s32[3]{0:T(128)} %pad_add_fusion.1.refs_0_, bf16[512,3072]{1,0:T(8,128)(2,1)} %self_project.1.refs_2_.refs_1_.refs_3_, bf16[512,3072]{1,0:T(8,128)(2,1)} %self_project.1.refs_2_.refs_1_.refs_3_, bf16[512,3072]{1,0:T(8,128)(2,1)} %self_project.1.refs_2_.refs_1_.refs_3_, ...), custom_call_target="tpu_custom_call" | custom-call | flops 1000000 | bytes 1 | tf_op jit(solution)/shard_map/self_backward/pallas_call | solution.py:99
  419.3 4.9 weight_grad.12
  433.1 9.6 %weight_grad.13 = (bf16[2,4,32,1536]{3,2,1,0:T(8,128)(2,1)}, bf16[2,4,32,1536]{3,2,1,0:T(8,128)(2,1)}, bf16[2,4,32,1536]{3,2,1,0:T(8,128)(2,1)}, bf16[2,4,32,1536]{3,2,1,0:T(8,128)(2,1)}) custom-call(s32[4]{0:T(128)} %pad_add_fusion.refs_0_, bf16[512,1280]{1,0:T(8,128)(2,1)} %get-tuple-element.130.refs_2_.refs_1_.refs_3_, ...), custom_call_target="tpu_custom_call" | custom-call | flops 1000000 | bytes 1 | tf_op jit(solution)/shard_map/weight_grad/pallas_call | solution.py:99
  445.9 3.6 add_blocks.11.refs_4_
  449.5 7.7 %memory_back.2.refs_9_.refs_1_ = bf16[768,1024]{1,0:T(8,128)(2,1)} custom-call(s32[4]{0:T(128)} %pad_add_fusion.refs_0_, bf16[768,2048]{1,0:T(8,128)(2,1)} %get-tuple-element.188.refs_14_.refs_1_, bf16[8,64,5248]{2,1,0:T(8,128)(2,1)} %bitcast.66, bf16[8,64,5248]{2,1,0:T(8,128)(2,1)} %collective-permute-done.15.refs_2_.refs_5_.refs_8_.refs_6_.refs_3_, ...), custom_call_target="tpu_custom_call" | custom-call | flops 1000000 | bytes 1 | tf_op jit(solution)/shard_map/memory_back/pallas_call | solution.py:99
  457.2 10.1 %collective-permute-done.46.refs_4_.refs_11_ = bf16[2,4,32,1536]{3,2,1,0:T(8,128)(2,1)} collective-permute-done((bf16[2,4,32,1536]{3,2,1,0:T(8,128)(2,1)}, bf16[2,4,32,1536]{3,2,1,0:T(8,128)(2,1)}, u32[]{:S(2)}, u32[]{:S(2)}) %collective-permute-start.46) | collective-permute-done | bytes 786464 | tf_op jit(solution)/shard_map/ppermute | solution.py:402
  476.5 8.1 %collective-permute-done.50.refs_3_ = bf16[4,32,640]{2,1,0:T(8,128)(2,1)} collective-permute-done((bf16[4,32,640]{2,1,0:T(8,128)(2,1)}, bf16[4,32,640]{2,1,0:T(8,128)(2,1)}, u32[]{:S(2)}, u32[]{:S(2)}) %collective-permute-start.50) | collective-permute-done | bytes 163872 | tf_op jit(solution)/shard_map/ppermute | solution.py:402
  486.6 4.0 add_blocks.13
  498.7 7.7 %memory_back.3.refs_5_.refs_1_ = bf16[768,1024]{1,0:T(8,128)(2,1)} custom-call(s32[4]{0:T(128)} %pad_add_fusion.refs_0_, bf16[768,2048]{1,0:T(8,128)(2,1)} %get-tuple-element.187.refs_13_.refs_1_, bf16[8,64,5248]{2,1,0:T(8,128)(2,1)} %bitcast.67, bf16[8,64,5248]{2,1,0:T(8,128)(2,1)} %collective-permute-done.15.refs_2_.refs_5_.refs_8_.refs_6_.refs_3_, ...), custom_call_target="tpu_custom_call" | custom-call | flops 1000000 | bytes 1 | tf_op jit(solution)/shard_map/memory_back/pallas_call | solution.py:99
  506.3 9.3 %target_back.1.refs_6_ = bf16[512,1024]{1,0:T(8,128)(2,1)} custom-call(s32[4]{0:T(128)} %pad_add_fusion.refs_0_, bf16[512,3072]{1,0:T(8,128)(2,1)} %self_backward.1.refs_7_.refs_3_.refs_1_, f32[512,1024]{1,0:T(8,128)} %get-tuple-element.189.refs_17_.refs_2_, bf16[8,64,3072]{2,1,0:T(8,128)(2,1)} %bitcast.84, ...), custom_call_target="tpu_custom_call" | custom-call | flops 1000000 | bytes 1 | tf_op jit(solution)/shard_map/target_back/pallas_call | solution.py:99
  520.7 3.8 move_blocks.23
  (198 shorter events, 113.7 us)
Async XLA Ops:
  7.2 67.3 %all-gather.4.cloned.1.call-start = ((), (), s32[]{:S(2)}) async-start(), calls=%async_computation.3 | async-start | bytes 1679360 | tf_op jit(solution)/shard_map/all_gather | solution.py:425
  15.5 23.4 %collective-permute-start.3 = (bf16[384,1024]{1,0:T(8,128)(2,1)}, bf16[384,1024]{1,0:T(8,128)(2,1)}, u32[]{:S(2)}, u32[]{:S(2)}) collective-permute-start(bf16[384,1024]{1,0:T(8,128)(2,1)} %get-tuple-element.122), channel_id=1, source_target_pairs={{0,1},{1,0},{2,3},{3,2},{4,5},{5,4},{6,7},{7,6},{8,9},{9,8},{10,11... | collective-permute-start | bytes 2359304 | tf_op jit(solution)/shard_map/ppermute | solution.py:406
  18.5 17.9 %collective-permute-start.2 = (bf16[32,3072]{1,0:T(8,128)(2,1)}, bf16[32,3072]{1,0:T(8,128)(2,1)}, u32[]{:S(2)}, u32[]{:S(2)}) collective-permute-start(bf16[32,3072]{1,0:T(8,128)(2,1)} %get-tuple-element.118.refs_2_.refs_1_), channel_id=1, source_target_pairs={{0,24},{2,26},{4,28},{6,30},{8,16},{10,18},{12,20},{14,22},{16,8},... | collective-permute-start | bytes 589832 | tf_op jit(solution)/shard_map/ppermute | solution.py:411
  22.1 16.7 %collective-permute-start.1 = (bf16[32,3072]{1,0:T(8,128)(2,1)}, bf16[32,3072]{1,0:T(8,128)(2,1)}, u32[]{:S(2)}, u32[]{:S(2)}) collective-permute-start(bf16[32,3072]{1,0:T(8,128)(2,1)} %get-tuple-element.118.refs_2_.refs_1_), channel_id=1, source_target_pairs={{0,16},{2,18},{4,20},{6,22},{8,24},{10,26},{12,28},{14,30},{16,0},... | collective-permute-start | bytes 589832 | tf_op jit(solution)/shard_map/ppermute | solution.py:411
  41.5 76.0 %all-gather.6.cloned.1.call-start = ((), (), s32[]{:S(2)}) async-start(), calls=%async_computation.4 | async-start | bytes 1310720 | tf_op jit(solution)/shard_map/all_gather | solution.py:425
  43.7 99.8 %all-gather.8.cloned.1.call-start = ((), (), s32[]{:S(2)}) async-start(), calls=%async_computation.5 | async-start | bytes 1310720 | tf_op jit(solution)/shard_map/all_gather | solution.py:425
  56.9 23.6 %collective-permute-start.8 = (bf16[2,4,32,1536]{3,2,1,0:T(8,128)(2,1)}, bf16[2,4,32,1536]{3,2,1,0:T(8,128)(2,1)}, u32[]{:S(2)}, u32[]{:S(2)}) collective-permute-start(bf16[2,4,32,1536]{3,2,1,0:T(8,128)(2,1)} %get-tuple-element.128), channel_id=1, source_target_pairs={{0,4},{2,6},{4,0},{6,2},{8,12},{10,14},{12,8},{14,10},{16,20},{18,... | collective-permute-start | bytes 2359304 | tf_op jit(solution)/shard_map/ppermute | solution.py:402
  57.5 23.0 %collective-permute-start.7 = (bf16[2,4,32,1536]{3,2,1,0:T(8,128)(2,1)}, bf16[2,4,32,1536]{3,2,1,0:T(8,128)(2,1)}, u32[]{:S(2)}, u32[]{:S(2)}) collective-permute-start(bf16[2,4,32,1536]{3,2,1,0:T(8,128)(2,1)} %get-tuple-element.127.refs_3_), channel_id=1, source_target_pairs={{0,1},{1,0},{2,3},{3,2},{4,5},{5,4},{6,7},{7,6},{8,9},{9,8},{10,11... | collective-permute-start | bytes 2359304 | tf_op jit(solution)/shard_map/ppermute | solution.py:406
  63.6 20.1 %collective-permute-start.12 = (bf16[512,1280]{1,0:T(8,128)(2,1)}, bf16[512,1280]{1,0:T(8,128)(2,1)}, u32[]{:S(2)}, u32[]{:S(2)}) collective-permute-start(bf16[512,1280]{1,0:T(8,128)(2,1)} %get-tuple-element.133), channel_id=1, source_target_pairs={{0,2},{2,0},{4,6},{6,4},{8,10},{10,8},{12,14},{14,12},{16,18},{18,... | collective-permute-start | bytes 3932168 | tf_op jit(solution)/shard_map/ppermute | solution.py:397
  79.0 18.6 %collective-permute-start.11 = (bf16[4,32,3072]{2,1,0:T(8,128)(2,1)}, bf16[4,32,3072]{2,1,0:T(8,128)(2,1)}, u32[]{:S(2)}, u32[]{:S(2)}) collective-permute-start(bf16[4,32,3072]{2,1,0:T(8,128)(2,1)} %get-tuple-element.132.refs_3_), channel_id=1, source_target_pairs={{0,1},{1,0},{2,3},{3,2},{4,5},{5,4},{6,7},{7,6},{8,9},{9,8},{10,11... | collective-permute-start | bytes 2359304 | tf_op jit(solution)/shard_map/ppermute | solution.py:406
  83.6 24.7 %collective-permute-start.9 = (bf16[8,64,3072]{2,1,0:T(8,128)(2,1)}, bf16[8,64,3072]{2,1,0:T(8,128)(2,1)}, u32[]{:S(2)}, u32[]{:S(2)}) collective-permute-start(bf16[8,64,3072]{2,1,0:T(8,128)(2,1)} %bitcast.82), channel_id=1, source_target_pairs={{0,2},{2,0},{4,6},{6,4},{8,10},{10,8},{12,14},{14,12},{16,18},{18,... | collective-permute-start | bytes 9437192 | tf_op jit(solution)/shard_map/ppermute | solution.py:397
  102.1 37.7 %collective-permute-start.14 = (bf16[2,4,32,3072]{3,2,1,0:T(8,128)(2,1)}, bf16[2,4,32,3072]{3,2,1,0:T(8,128)(2,1)}, u32[]{:S(2)}, u32[]{:S(2)}) collective-permute-start(bf16[2,4,32,3072]{3,2,1,0:T(8,128)(2,1)} %get-tuple-element.139), channel_id=1, source_target_pairs={{0,4},{2,6},{4,0},{6,2},{8,12},{10,14},{12,8},{14,10},{16,20},{18,... | collective-permute-start | bytes 4718600 | tf_op jit(solution)/shard_map/ppermute | solution.py:402
  102.8 30.9 %collective-permute-start.13 = (bf16[2,4,32,2176]{3,2,1,0:T(8,128)(2,1)}, bf16[2,4,32,2176]{3,2,1,0:T(8,128)(2,1)}, u32[]{:S(2)}, u32[]{:S(2)}) collective-permute-start(bf16[2,4,32,2176]{3,2,1,0:T(8,128)(2,1)} %get-tuple-element.134.refs_4_), channel_id=1, source_target_pairs={{0,1},{1,0},{2,3},{3,2},{4,5},{5,4},{6,7},{7,6},{8,9},{9,8},{10,11... | collective-permute-start | bytes 3342344 | tf_op jit(solution)/shard_map/ppermute | solution.py:406
  108.3 336.8 %reduce-scatter.4.cloned.1.call-start = ((), (), s32[]{:S(2)}) async-start(), calls=%async_computation.6 | async-start | bytes 1310720 | tf_op jit(solution)/shard_map/reduce_scatter | solution.py:1253
  117.1 27.0 %collective-permute-start.16 = (bf16[384,1024]{1,0:T(8,128)(2,1)}, bf16[384,1024]{1,0:T(8,128)(2,1)}, u32[]{:S(2)}, u32[]{:S(2)}) collective-permute-start(bf16[384,1024]{1,0:T(8,128)(2,1)} %gate.2.refs_2_), channel_id=1, source_target_pairs={{0,1},{1,0},{2,3},{3,2},{4,5},{5,4},{6,7},{7,6},{8,9},{9,8},{10,11... | collective-permute-start | bytes 2359304 | tf_op jit(solution)/shard_map/ppermute | solution.py:406
  118.3 48.0 %collective-permute-start.17 = (bf16[4,32,4096]{2,1,0:T(8,128)(2,1)}, bf16[4,32,4096]{2,1,0:T(8,128)(2,1)}, u32[]{:S(2)}, u32[]{:S(2)}) collective-permute-start(bf16[4,32,4096]{2,1,0:T(8,128)(2,1)} %move_blocks.18.refs_5_.refs_1_), channel_id=1, source_target_pairs={{0,4},{2,6},{4,0},{6,2},{8,12},{10,14},{12,8},{14,10},{16,20},{18,... | collective-permute-start | bytes 3145736 | tf_op jit(solution)/shard_map/ppermute | solution.py:402
  144.8 25.3 %collective-permute-start.18 = (bf16[4,128,1024]{2,1,0:T(8,128)(2,1)}, bf16[4,128,1024]{2,1,0:T(8,128)(2,1)}, u32[]{:S(2)}, u32[]{:S(2)}) collective-permute-start(bf16[4,128,1024]{2,1,0:T(8,128)(2,1)} %move_blocks.20.refs_3_), channel_id=1, source_target_pairs={{0,1},{1,0},{2,3},{3,2},{4,5},{5,4},{6,7},{7,6},{8,9},{9,8},{10,11... | collective-permute-start | bytes 3145736 | tf_op jit(solution)/shard_map/ppermute | solution.py:406
  175.5 46.9 %collective-permute-start.20 = (bf16[2,4,128,1024]{3,2,1,0:T(8,128)(2,1)}, bf16[2,4,128,1024]{3,2,1,0:T(8,128)(2,1)}, u32[]{:S(2)}, u32[]{:S(2)}) collective-permute-start(bf16[2,4,128,1024]{3,2,1,0:T(8,128)(2,1)} %get-tuple-element.151), channel_id=1, source_target_pairs={{0,4},{2,6},{4,0},{6,2},{8,12},{10,14},{12,8},{14,10},{16,20},{18,... | collective-permute-start | bytes 6291464 | tf_op jit(solution)/shard_map/ppermute | solution.py:402
  176.2 46.3 %collective-permute-start.19 = (bf16[2,4,32,4096]{3,2,1,0:T(8,128)(2,1)}, bf16[2,4,32,4096]{3,2,1,0:T(8,128)(2,1)}, u32[]{:S(2)}, u32[]{:S(2)}) collective-permute-start(bf16[2,4,32,4096]{3,2,1,0:T(8,128)(2,1)} %get-tuple-element.142.refs_6_), channel_id=1, source_target_pairs={{0,1},{1,0},{2,3},{3,2},{4,5},{5,4},{6,7},{7,6},{8,9},{9,8},{10,11... | collective-permute-start | bytes 6291464 | tf_op jit(solution)/shard_map/ppermute | solution.py:406
  227.1 27.8 %collective-permute-start.22 = (bf16[8,256,1024]{2,1,0:T(8,128)(2,1)}, bf16[8,256,1024]{2,1,0:T(8,128)(2,1)}, u32[]{:S(2)}, u32[]{:S(2)}) collective-permute-start(bf16[8,256,1024]{2,1,0:T(8,128)(2,1)} %bitcast.79), channel_id=1, source_target_pairs={{0,2},{2,0},{4,6},{6,4},{8,10},{10,8},{12,14},{14,12},{16,18},{18,... | collective-permute-start | bytes 12582920 | tf_op jit(solution)/shard_map/ppermute | solution.py:397
  227.6 20.0 %collective-permute-start.23 = (bf16[512,2816]{1,0:T(8,128)(2,1)}, bf16[512,2816]{1,0:T(8,128)(2,1)}, u32[]{:S(2)}, u32[]{:S(2)}) collective-permute-start(bf16[512,2816]{1,0:T(8,128)(2,1)} %get-tuple-element.159), channel_id=1, source_target_pairs={{0,2},{2,0},{4,6},{6,4},{8,10},{10,8},{12,14},{14,12},{16,18},{18,... | collective-permute-start | bytes 8650760 | tf_op jit(solution)/shard_map/ppermute | solution.py:397
  254.8 17.0 %collective-permute-start.24 = (bf16[2048,512]{1,0:T(8,128)(2,1)}, bf16[2048,512]{1,0:T(8,128)(2,1)}, u32[]{:S(2)}, u32[]{:S(2)}) collective-permute-start(bf16[2048,512]{1,0:T(8,128)(2,1)} %get-tuple-element.164), channel_id=1, source_target_pairs={{0,2},{2,0},{4,6},{6,4},{8,10},{10,8},{12,14},{14,12},{16,18},{18,... | collective-permute-start | bytes 6291464 | tf_op jit(solution)/shard_map/ppermute | solution.py:397
  282.2 28.9 %collective-permute-start.29 = (bf16[2,4,128,512]{3,2,1,0:T(8,128)(2,1)}, bf16[2,4,128,512]{3,2,1,0:T(8,128)(2,1)}, u32[]{:S(2)}, u32[]{:S(2)}) collective-permute-start(bf16[2,4,128,512]{3,2,1,0:T(8,128)(2,1)} %get-tuple-element.172), channel_id=1, source_target_pairs={{0,4},{2,6},{4,0},{6,2},{8,12},{10,14},{12,8},{14,10},{16,20},{18,... | collective-permute-start | bytes 3145736 | tf_op jit(solution)/shard_map/ppermute | solution.py:402
  283.8 27.2 %collective-permute-start.28 = (bf16[2,4,128,512]{3,2,1,0:T(8,128)(2,1)}, bf16[2,4,128,512]{3,2,1,0:T(8,128)(2,1)}, u32[]{:S(2)}, u32[]{:S(2)}) collective-permute-start(bf16[2,4,128,512]{3,2,1,0:T(8,128)(2,1)} %get-tuple-element.165.refs_5_), channel_id=1, source_target_pairs={{0,1},{1,0},{2,3},{3,2},{4,5},{5,4},{6,7},{7,6},{8,9},{9,8},{10,11... | collective-permute-start | bytes 3145736 | tf_op jit(solution)/shard_map/ppermute | solution.py:406
  296.2 18.0 %collective-permute-start.27 = (bf16[512,4096]{1,0:T(8,128)(2,1)}, bf16[512,4096]{1,0:T(8,128)(2,1)}, u32[]{:S(2)}, u32[]{:S(2)}) collective-permute-start(bf16[512,4096]{1,0:T(8,128)(2,1)} %feed_back.1.refs_1_.refs_3_), channel_id=1, source_target_pairs={{0,2},{2,0},{4,6},{6,4},{8,10},{10,8},{12,14},{14,12},{16,18},{18,... | collective-permute-start | bytes 12582920 | tf_op jit(solution)/shard_map/ppermute | solution.py:397
  310.5 20.1 %collective-permute-start.26 = (bf16[512,1024]{1,0:T(8,128)(2,1)}, bf16[512,1024]{1,0:T(8,128)(2,1)}, u32[]{:S(2)}, u32[]{:S(2)}) collective-permute-start(bf16[512,1024]{1,0:T(8,128)(2,1)} %get-tuple-element.169.refs_3_), channel_id=1, source_target_pairs={{0,2},{2,0},{4,6},{6,4},{8,10},{10,8},{12,14},{14,12},{16,18},{18,... | collective-permute-start | bytes 3145736 | tf_op jit(solution)/shard_map/ppermute | solution.py:397
  324.4 37.2 %collective-permute-start.31 = (bf16[2,4,32,2048]{3,2,1,0:T(8,128)(2,1)}, bf16[2,4,32,2048]{3,2,1,0:T(8,128)(2,1)}, u32[]{:S(2)}, u32[]{:S(2)}) collective-permute-start(bf16[2,4,32,2048]{3,2,1,0:T(8,128)(2,1)} %get-tuple-element.180), channel_id=1, source_target_pairs={{0,4},{2,6},{4,0},{6,2},{8,12},{10,14},{12,8},{14,10},{16,20},{18,... | collective-permute-start | bytes 3145736 | tf_op jit(solution)/shard_map/ppermute | solution.py:402
  324.7 36.9 %collective-permute-start.30 = (bf16[2,4,32,2048]{3,2,1,0:T(8,128)(2,1)}, bf16[2,4,32,2048]{3,2,1,0:T(8,128)(2,1)}, u32[]{:S(2)}, u32[]{:S(2)}) collective-permute-start(bf16[2,4,32,2048]{3,2,1,0:T(8,128)(2,1)} %get-tuple-element.175.refs_5_), channel_id=1, source_target_pairs={{0,1},{1,0},{2,3},{3,2},{4,5},{5,4},{6,7},{7,6},{8,9},{9,8},{10,11... | collective-permute-start | bytes 3145736 | tf_op jit(solution)/shard_map/ppermute | solution.py:406
  325.4 35.7 %collective-permute-start.32 = (bf16[4,128,512]{2,1,0:T(8,128)(2,1)}, bf16[4,128,512]{2,1,0:T(8,128)(2,1)}, u32[]{:S(2)}, u32[]{:S(2)}) collective-permute-start(bf16[4,128,512]{2,1,0:T(8,128)(2,1)} %get-tuple-element.174.refs_5_), channel_id=1, source_target_pairs={{0,4},{2,6},{4,0},{6,2},{8,12},{10,14},{12,8},{14,10},{16,20},{18,... | collective-permute-start | bytes 1572872 | tf_op jit(solution)/shard_map/ppermute | solution.py:402
  327.1 34.0 %collective-permute-start.33 = (bf16[4,128,512]{2,1,0:T(8,128)(2,1)}, bf16[4,128,512]{2,1,0:T(8,128)(2,1)}, u32[]{:S(2)}, u32[]{:S(2)}) collective-permute-start(bf16[4,128,512]{2,1,0:T(8,128)(2,1)} %get-tuple-element.181), channel_id=1, source_target_pairs={{0,1},{1,0},{2,3},{3,2},{4,5},{5,4},{6,7},{7,6},{8,9},{9,8},{10,11... | collective-permute-start | bytes 1572872 | tf_op jit(solution)/shard_map/ppermute | solution.py:406
  359.3 36.2 %collective-permute-start.36 = (bf16[512,1024]{1,0:T(8,128)(2,1)}, bf16[512,1024]{1,0:T(8,128)(2,1)}, u32[]{:S(2)}, u32[]{:S(2)}) collective-permute-start(bf16[512,1024]{1,0:T(8,128)(2,1)} %get-tuple-element.177.refs_11_.refs_1_.refs_3_), channel_id=1, source_target_pairs={{0,2},{2,0},{4,6},{6,4},{8,10},{10,8},{12,14},{14,12},{16,18},{18,... | collective-permute-start | bytes 3145736 | tf_op jit(solution)/shard_map/ppermute | solution.py:397
  361.1 20.7 %collective-permute-start.37 = (bf16[768,2048]{1,0:T(8,128)(2,1)}, bf16[768,2048]{1,0:T(8,128)(2,1)}, u32[]{:S(2)}, u32[]{:S(2)}) collective-permute-start(bf16[768,2048]{1,0:T(8,128)(2,1)} %get-tuple-element.187.refs_13_.refs_1_), channel_id=1, source_target_pairs={{0,2},{2,0},{4,6},{6,4},{8,10},{10,8},{12,14},{14,12},{16,18},{18,... | collective-permute-start | bytes 9437192 | tf_op jit(solution)/shard_map/ppermute | solution.py:397
  361.1 20.7 %collective-permute-start.38 = (bf16[768,2048]{1,0:T(8,128)(2,1)}, bf16[768,2048]{1,0:T(8,128)(2,1)}, u32[]{:S(2)}, u32[]{:S(2)}) collective-permute-start(bf16[768,2048]{1,0:T(8,128)(2,1)} %get-tuple-element.188.refs_14_.refs_1_), channel_id=1, source_target_pairs={{0,2},{2,0},{4,6},{6,4},{8,10},{10,8},{12,14},{14,12},{16,18},{18,... | collective-permute-start | bytes 9437192 | tf_op jit(solution)/shard_map/ppermute | solution.py:397
  377.7 23.0 %collective-permute-start.35 = (bf16[4,32,2048]{2,1,0:T(8,128)(2,1)}, bf16[4,32,2048]{2,1,0:T(8,128)(2,1)}, u32[]{:S(2)}, u32[]{:S(2)}) collective-permute-start(bf16[4,32,2048]{2,1,0:T(8,128)(2,1)} %get-tuple-element.185), channel_id=1, source_target_pairs={{0,1},{1,0},{2,3},{3,2},{4,5},{5,4},{6,7},{7,6},{8,9},{9,8},{10,11... | collective-permute-start | bytes 1572872 | tf_op jit(solution)/shard_map/ppermute | solution.py:406
  379.2 21.5 %collective-permute-start.34 = (bf16[4,32,2048]{2,1,0:T(8,128)(2,1)}, bf16[4,32,2048]{2,1,0:T(8,128)(2,1)}, u32[]{:S(2)}, u32[]{:S(2)}) collective-permute-start(bf16[4,32,2048]{2,1,0:T(8,128)(2,1)} %get-tuple-element.182.refs_7_), channel_id=1, source_target_pairs={{0,4},{2,6},{4,0},{6,2},{8,12},{10,14},{12,8},{14,10},{16,20},{18,... | collective-permute-start | bytes 1572872 | tf_op jit(solution)/shard_map/ppermute | solution.py:402
  380.9 64.9 %reduce-scatter.6.cloned.1.call-start = ((), (), s32[]{:S(2)}) async-start(), calls=%async_computation.7 | async-start | bytes 1310720 | tf_op jit(solution)/shard_map/reduce_scatter | solution.py:1253
  381.8 37.5 %collective-permute-start.39 = (bf16[512,1024]{1,0:T(8,128)(2,1)}, bf16[512,1024]{1,0:T(8,128)(2,1)}, u32[]{:S(2)}, u32[]{:S(2)}) collective-permute-start(bf16[512,1024]{1,0:T(8,128)(2,1)} %get-tuple-element.192.refs_3_), channel_id=1, source_target_pairs={{0,2},{2,0},{4,6},{6,4},{8,10},{10,8},{12,14},{14,12},{16,18},{18,... | collective-permute-start | bytes 3145736 | tf_op jit(solution)/shard_map/ppermute | solution.py:397
  395.0 30.8 %collective-permute-start.44 = (bf16[2,4,32,2048]{3,2,1,0:T(8,128)(2,1)}, bf16[2,4,32,2048]{3,2,1,0:T(8,128)(2,1)}, u32[]{:S(2)}, u32[]{:S(2)}) collective-permute-start(bf16[2,4,32,2048]{3,2,1,0:T(8,128)(2,1)} %get-tuple-element.190.refs_7_), channel_id=1, source_target_pairs={{0,4},{2,6},{4,0},{6,2},{8,12},{10,14},{12,8},{14,10},{16,20},{18,... | collective-permute-start | bytes 3145736 | tf_op jit(solution)/shard_map/ppermute | solution.py:402
  400.2 25.6 %collective-permute-start.43 = (bf16[2,4,32,2048]{3,2,1,0:T(8,128)(2,1)}, bf16[2,4,32,2048]{3,2,1,0:T(8,128)(2,1)}, u32[]{:S(2)}, u32[]{:S(2)}) collective-permute-start(bf16[2,4,32,2048]{3,2,1,0:T(8,128)(2,1)} %get-tuple-element.191.refs_7_), channel_id=1, source_target_pairs={{0,1},{1,0},{2,3},{3,2},{4,5},{5,4},{6,7},{7,6},{8,9},{9,8},{10,11... | collective-permute-start | bytes 3145736 | tf_op jit(solution)/shard_map/ppermute | solution.py:406
  419.3 67.4 %reduce-scatter.8.cloned.1.call-start = ((), (), s32[]{:S(2)}) async-start(), calls=%async_computation.8 | async-start | bytes 1310720 | tf_op jit(solution)/shard_map/reduce_scatter | solution.py:1253
  431.3 25.8 %collective-permute-start.41 = (bf16[2,4,32,640]{3,2,1,0:T(8,128)(2,1)}, bf16[2,4,32,640]{3,2,1,0:T(8,128)(2,1)}, u32[]{:S(2)}, u32[]{:S(2)}) collective-permute-start(bf16[2,4,32,640]{3,2,1,0:T(8,128)(2,1)} %get-tuple-element.197.refs_5_), channel_id=1, source_target_pairs={{0,1},{1,0},{2,3},{3,2},{4,5},{5,4},{6,7},{7,6},{8,9},{9,8},{10,11... | collective-permute-start | bytes 983048 | tf_op jit(solution)/shard_map/ppermute | solution.py:406
  432.7 24.4 %collective-permute-start.47 = (bf16[2,4,32,640]{3,2,1,0:T(8,128)(2,1)}, bf16[2,4,32,640]{3,2,1,0:T(8,128)(2,1)}, u32[]{:S(2)}, u32[]{:S(2)}) collective-permute-start(bf16[2,4,32,640]{3,2,1,0:T(8,128)(2,1)} %get-tuple-element.206), channel_id=1, source_target_pairs={{0,4},{2,6},{4,0},{6,2},{8,12},{10,14},{12,8},{14,10},{16,20},{18,... | collective-permute-start | bytes 983048 | tf_op jit(solution)/shard_map/ppermute | solution.py:402
  442.7 24.5 %collective-permute-start.46 = (bf16[2,4,32,1536]{3,2,1,0:T(8,128)(2,1)}, bf16[2,4,32,1536]{3,2,1,0:T(8,128)(2,1)}, u32[]{:S(2)}, u32[]{:S(2)}) collective-permute-start(bf16[2,4,32,1536]{3,2,1,0:T(8,128)(2,1)} %get-tuple-element.204), channel_id=1, source_target_pairs={{0,4},{2,6},{4,0},{6,2},{8,12},{10,14},{12,8},{14,10},{16,20},{18,... | collective-permute-start | bytes 2359304 | tf_op jit(solution)/shard_map/ppermute | solution.py:402
  444.5 22.8 %collective-permute-start.45 = (bf16[2,4,32,1536]{3,2,1,0:T(8,128)(2,1)}, bf16[2,4,32,1536]{3,2,1,0:T(8,128)(2,1)}, u32[]{:S(2)}, u32[]{:S(2)}) collective-permute-start(bf16[2,4,32,1536]{3,2,1,0:T(8,128)(2,1)} %get-tuple-element.202.refs_9_), channel_id=1, source_target_pairs={{0,1},{1,0},{2,3},{3,2},{4,5},{5,4},{6,7},{7,6},{8,9},{9,8},{10,11... | collective-permute-start | bytes 2359304 | tf_op jit(solution)/shard_map/ppermute | solution.py:406
  475.5 45.3 %collective-permute-start.54 = (bf16[768,1024]{1,0:T(8,128)(2,1)}, bf16[768,1024]{1,0:T(8,128)(2,1)}, u32[]{:S(2)}, u32[]{:S(2)}) collective-permute-start(bf16[768,1024]{1,0:T(8,128)(2,1)} %gate.3.refs_14_), channel_id=1, source_target_pairs={{0,1},{1,0},{2,3},{3,2},{4,5},{5,4},{6,7},{7,6},{8,9},{9,8},{10,11... | collective-permute-start | bytes 4718600 | tf_op jit(solution)/shard_map/ppermute | solution.py:406
  490.6 25.0 %collective-permute-start.55 = (bf16[32,4352]{1,0:T(8,128)(2,1)}, bf16[32,4352]{1,0:T(8,128)(2,1)}, u32[]{:S(2)}, u32[]{:S(2)}) collective-permute-start(bf16[32,4352]{1,0:T(8,128)(2,1)} %get-tuple-element.214), channel_id=1, source_target_pairs={{0,8},{2,10},{4,12},{6,14},{8,0},{10,2},{12,4},{14,6},{16,24},{18,... | collective-permute-start | bytes 835592 | tf_op jit(solution)/shard_map/ppermute | solution.py:411
  491.3 24.3 %collective-permute-start.56 = (bf16[32,4352]{1,0:T(8,128)(2,1)}, bf16[32,4352]{1,0:T(8,128)(2,1)}, u32[]{:S(2)}, u32[]{:S(2)}) collective-permute-start(bf16[32,4352]{1,0:T(8,128)(2,1)} %get-tuple-element.215), channel_id=1, source_target_pairs={{0,16},{2,18},{4,20},{6,22},{8,24},{10,26},{12,28},{14,30},{16,0},... | collective-permute-start | bytes 835592 | tf_op jit(solution)/shard_map/ppermute | solution.py:411
  492.3 23.3 %collective-permute-start.57 = (bf16[32,4352]{1,0:T(8,128)(2,1)}, bf16[32,4352]{1,0:T(8,128)(2,1)}, u32[]{:S(2)}, u32[]{:S(2)}) collective-permute-start(bf16[32,4352]{1,0:T(8,128)(2,1)} %get-tuple-element.216), channel_id=1, source_target_pairs={{0,24},{2,26},{4,28},{6,30},{8,16},{10,18},{12,20},{14,22},{16,8},... | collective-permute-start | bytes 835592 | tf_op jit(solution)/shard_map/ppermute | solution.py:411
  (29 other events, 305.9 us)
Sparse Core Ops, SparseCore 0:
  41.6 32.8 all-gather.3
  76.7 26.8 all-gather.5
  108.4 26.6 all-gather.7
  381.1 24.3 reduce-scatter.3
  419.4 26.4 reduce-scatter.5
  449.6 25.7 reduce-scatter.7

commit v5 on v4

--- a/solution.py
+++ b/solution.py
@@ -702,7 +702,7 @@
             copy.start()
             sent.append(copy)
 
-        fetch.need, fetch.send = need, send
+        fetch.need, fetch.send, fetch.bits = need, send, bits_now
         issue(0)
         for number, which in enumerate(streamed):
             count = streams[which]
@@ -861,8 +861,26 @@
     )
 
 
-def feed_in(order, bits, weight, source):
+def feed_in(order, bits, weight, source, outer):
     rows, size = source.shape[0], 1024
+    shard_rows = weight.width // (8 * outer) if outer else 0
+    turning = shard_rows > 0 and LANES % shard_rows == 0
+
+    def turn_chunk(bits_now, values, start, targets):
+        for block in range(size // LANES):
+            turned = values[:, block * LANES : (block + 1) * LANES].T
+            for part in range(LANES // shard_rows):
+                device = (start + block * LANES) // shard_rows + part
+                mem, core, near = device & 1, (device >> 1) & 1, (device >> 2) & 1
+                place = (mem ^ bits_now[2]) * 2 + (near ^ bits_now[0])
+                place = (place * outer + (device >> 3)) * shard_rows
+                block_rows = pl.ds(pl.multiple_of(place, shard_rows), shard_rows)
+                piece = turned[part * shard_rows : (part + 1) * shard_rows]
+                for side, target in enumerate(targets):
+
+                    @pl.when((core ^ bits_now[1]) == side)
+                    def _():
+                        target[block_rows, :] = piece
 
     def body(fetch, ins, outs, scratch):
         held = scratch[0]
@@ -878,13 +896,19 @@
                 outs[1][block, start : start + size] = (below + hidden * density).astype(BF16)
 
             row_blocks(rows, 256, step)
+            columns = slice(start, start + size)
             for which in range(2):
-                fetch.send(which, slice(start, start + size))
-
-    out = ((rows, weight.width), BF16)
+                fetch.send(which, columns)
+            if turning:
+                turn_chunk(fetch.bits, outs[0][:, columns], start, outs[2:])
+        for which in range(2, len(outs)):
+            fetch.send(which)
+
+    out, turned = ((rows, weight.width), BF16), ((weight.width // 2, rows), BF16)
+    outs = [out, out] + ([turned, turned] if turning else [])
     return weight_call(
-        order, "feed_in", bits, [weight], columns_plan(0, weight.width, size), [source], [out, out],
-        [((rows, size), F32)], body, {0: source.shape[1]}, 2 * weight.width // size,
+        order, "feed_in", bits, [weight], columns_plan(0, weight.width, size), [source], outs,
+        [((rows, size), F32)], body, {0: source.shape[1]}, 2 * weight.width // size + len(outs) - 2,
     )
 
 
@@ -1351,9 +1375,9 @@
         return lax.psum_scatter(gradient, both, scatter_dimension=0, tiled=True).astype(F32)
 
     class Turned:
-        def __init__(self, *sources):
+        def __init__(self, *sources, turned=()):
             self.sources = sources
-            own, other = turn_rows(order, bits, sources, outer) if staged else (None, None)
+            own, other = turned or (turn_rows(order, bits, sources, outer) if staged else (None, None))
             self.both = (own, swap_core(other)) if staged else ()
 
         def due(self):
@@ -1466,13 +1490,17 @@
     order.before(*far_parts[1:])
     order.part()
     steps((w_out, "first"))
+    middle = Turned(self_mixed, *far_parts)
     table = norm_table(order, bits, w_norm)
     near_kv, far_kv = project(
         order, "cross_project", bits, w_ckv, [near_flat, *far_parts], 1024, [1, len(far_parts)]
     )
     near_kv, far_kv = near_kv.reshape(slotted), far_kv.reshape(slotted)
     order.part()
-    steps((w_in, "second"), (w_out, "second"))
+    steps((w_in, "second"))
+    order.part()
+    steps((w_out, "second"))
+    middle.due()
     sum_one, first_out, first_low, cross_query = mix_norm(
         order, "self_mix", bits, w_so, self_mixed, target_in, table, 0, w_cq
     )
@@ -1482,18 +1510,19 @@
     sum_two, second_out, second_low = mix_norm(
         order, "cross_mix", bits, w_co, cross_mixed, first_out, table, 1
     )
-    later = Turned(self_mixed, first_low, cross_mixed, second_low, *far_parts)
+    later = Turned(first_low, cross_mixed, second_low)
     order.part()
-    steps((w_in, "third"), (w_out, "third"))
-    activated, slope = feed_in(order, bits, w_in, second_low)
+    steps((w_in, "third"))
+    steps((w_out, "third"))
+    activated, slope, *turned = feed_in(order, bits, w_in, second_low, outer if staged else 0)
     later.due()
-    hidden = Turned(activated)
+    hidden = Turned(activated, turned=turned)
     layer_out, grad_three, grad_ffn, stats_three = feed_out(
         order, bits, w_out, activated, second_out, table, grad_out
     )
     qkv_grad = Grad((first_turned, target_in))
-    so_grad = Grad((later, self_mixed))
-    ckv_grad = Grad((first_turned, near_flat), (later, *far_parts))
+    so_grad = Grad((middle, self_mixed))
+    ckv_grad = Grad((first_turned, near_flat), (middle, *far_parts))
     cq_grad = Grad((later, first_low))
     co_grad = Grad((later, cross_mixed))
     in_grad = Grad((later, second_low))

time: 540 us -> 534 us (0.989)
  waiting for transfers between devices: 102 us -> 90.6 us
    ppermute x16 -> x17, waiting for transfers between devices: 16.6 us -> 5.57 us  [swap_core(): return lax.ppermute(values, 'dp', [(i, i ^ 1) for i in range(size)])]
    pallas_call x50 -> x52, Pallas kernels: 343 us -> 345 us  [launch(): results = run(*operands, *ties)]
  transfers between devices with their start and end apart: 64 -> 65, of which waited for: 22 -> 19; matrix products, arithmetic and copies ran while one was open for 3% -> 3% of each run, Pallas kernels for 58% -> 62%
where the time goes in v5:
time: 534 us; the launch traced here: 523 us
  Pallas kernels  345 us (65%)
  waiting for transfers between devices  90.6 us (17%)
  starting transfers between devices  52.5 us (10%)
  between operations  15.9 us (3%)
  other arithmetic  10.5 us (2%)
  local copies, waits for them, and re-layouts  8.35 us (2%)
    pallas_call x52, Pallas kernels, launch(): results = run(*operands, *ties)  345 us
    ppermute x16, waiting for transfers between devices, swap_next(): return lax.ppermute(values, 'dp', [(i, i ^ 2) for i in range(size)])  40.9 us
    ppermute x20, waiting for transfers between devices, swap_mem(): return lax.ppermute(values, 'mem', [(0, 1), (1, 0)])  28.9 us
    ppermute x20, starting transfers between devices, swap_mem(): return lax.ppermute(values, 'mem', [(0, 1), (1, 0)])  22.8 us
    ppermute x16, starting transfers between devices, swap_next(): return lax.ppermute(values, 'dp', [(i, i ^ 2) for i in range(size)])  18 us
    all_gather x3, waiting for transfers between devices, outer_gather(): lax.all_gather(shard, 'dp', axis_index_groups=outer_groups(), axis=0, til...  11 us
  transfers between devices with their start and end apart: 65, of which 19 were waited for; matrix products, arithmetic and copies ran while one was open for 3% of the time, Pallas kernels for 62%

profile of v5, /device:TPU:0, one launch (start us, length us, event | category | flops | bytes accessed | tf_op | source)
XLA Modules:
  0.0 523.1 jit_solution(17276248396421388295)
XLA Ops:
  11.9 3.7 move_blocks.14
  18.6 3.6 collective-permute-start.2
  23.9 12.6 %collective-permute-done.4.refs_9_ = s32[2,384]{1,0:T(2,128)S(1)} collective-permute-done((s32[2,384]{1,0:T(2,128)S(1)}, s32[2,384]{1,0:T(2,128)S(1)}, u32[]{:S(2)}, u32[]{:S(2)}) %collective-permute-start.4) | collective-permute-done | bytes 3104 | tf_op jit(solution)/shard_map/ppermute | solution.py:406
  43.8 8.4 %collective-permute-done.5.refs_2_ = bf16[4,32,1536]{2,1,0:T(8,128)(2,1)} collective-permute-done((bf16[4,32,1536]{2,1,0:T(8,128)(2,1)}, bf16[4,32,1536]{2,1,0:T(8,128)(2,1)}, u32[]{:S(2)}, u32[]{:S(2)}) %collective-permute-start.5) | collective-permute-done | bytes 393248 | tf_op jit(solution)/shard_map/ppermute | solution.py:402
  53.4 3.6 move_blocks.16
  58.2 5.5 %turn_rows.3 = (bf16[512,1280]{1,0:T(8,128)(2,1)}, bf16[512,1280]{1,0:T(8,128)(2,1)}) custom-call(s32[4]{0:T(128)} %pad_add_fusion.refs_0_, bf16[512,1024]{1,0:T(8,128)(2,1)} %refs_2_.3, bf16[768,1024]{1,0:T(8,128)(2,1)} %bitcast.85, bf16[2,4,32,1536]{3,2,1,0:T(8,128)(2,1)} %get-tuple-element.127.refs_3_), custom_call_target="tpu_custom_call" | custom-call | flops 999999995904 | bytes 1 | tf_op jit(solution)/shard_map/turn_rows/pallas_call | solution.py:99
  63.7 11.0 %all-gather.4.cloned.1.call-done = bf16[128,5248]{1,0:T(8,128)(2,1)} async-done(((bf16[32,5248]{1,0:T(8,128)(2,1)}), bf16[128,5248]{1,0:T(8,128)(2,1)}) %all-gather.4.cloned.1.call-update) | async-done | bytes 1343504 | tf_op jit(solution)/shard_map/all_gather | solution.py:425
  83.8 7.9 %collective-permute-done.10.refs_2_ = bf16[4,32,2176]{2,1,0:T(8,128)(2,1)} collective-permute-done((bf16[4,32,2176]{2,1,0:T(8,128)(2,1)}, bf16[4,32,2176]{2,1,0:T(8,128)(2,1)}, u32[]{:S(2)}, u32[]{:S(2)}) %collective-permute-start.10) | collective-permute-done | bytes 557088 | tf_op jit(solution)/shard_map/ppermute | solution.py:402
  91.7 6.1 %collective-permute-done.11.refs_4_ = bf16[4,32,3072]{2,1,0:T(8,128)(2,1)} collective-permute-done((bf16[4,32,3072]{2,1,0:T(8,128)(2,1)}, bf16[4,32,3072]{2,1,0:T(8,128)(2,1)}, u32[]{:S(2)}, u32[]{:S(2)}) %collective-permute-start.11) | collective-permute-done | bytes 786464 | tf_op jit(solution)/shard_map/ppermute | solution.py:406
  97.8 4.5 move_blocks.19
  109.0 8.1 %self_project.1.refs_2_.refs_1_.refs_3_ = bf16[512,3072]{1,0:T(8,128)(2,1)} custom-call(s32[4]{0:T(128)} %pad_add_fusion.refs_0_, bf16[512,1024]{1,0:T(8,128)(2,1)} %refs_2_.3, bf16[8,64,3072]{2,1,0:T(8,128)(2,1)} %bitcast.83, bf16[8,64,3072]{2,1,0:T(8,128)(2,1)} %collective-permute-done.9.refs_3_.refs_4_, bf16[2,4,32,2176]{3,2,1,0:T(8,128)(2,1)} %get-tuple-element.134.refs_4_), custom_call_target="tpu_custom_call" | custom-call | flops 1000000 | bytes 1 | tf_op jit(solution)/shard_map/self_project/pallas_call | solution.py:99
  121.6 12.3 %self_forward.1 = (bf16[512,1024]{1,0:T(8,128)(2,1)}, f32[512,1024]{1,0:T(8,128)}) custom-call(s32[3]{0:T(128)} %pad_add_fusion.1.refs_0_, bf16[512,3072]{1,0:T(8,128)(2,1)} %self_project.1.refs_2_.refs_1_.refs_3_, bf16[512,3072]{1,0:T(8,128)(2,1)} %self_project.1.refs_2_.refs_1_.refs_3_, bf16[512,3072]{1,0:T(8,128)(2,1)} %self_project.1.refs_2_.refs_1_.refs_3_, ...), custom_call_target="tpu_custom_call" | custom-call | flops 1000000 | bytes 1 | tf_op jit(solution)/shard_map/self_forward/pallas_call | solution.py:99
  133.9 6.1 %collective-permute-done.14.refs_3_ = bf16[2,4,32,3072]{3,2,1,0:T(8,128)(2,1)} collective-permute-done((bf16[2,4,32,3072]{3,2,1,0:T(8,128)(2,1)}, bf16[2,4,32,3072]{3,2,1,0:T(8,128)(2,1)}, u32[]{:S(2)}, u32[]{:S(2)}) %collective-permute-start.14) | collective-permute-done | bytes 1572896 | tf_op jit(solution)/shard_map/ppermute | solution.py:402
  140.0 3.5 move_blocks.21.refs_3_
  146.5 6.7 %turn_rows.4 = (bf16[512,1280]{1,0:T(8,128)(2,1)}, bf16[512,1280]{1,0:T(8,128)(2,1)}) custom-call(s32[4]{0:T(128)} %pad_add_fusion.refs_0_, bf16[512,1024]{1,0:T(8,128)(2,1)} %get-tuple-element.137.refs_4_.refs_1_, bf16[384,1024]{1,0:T(8,128)(2,1)} %collective-permute-done.3.refs_8_.refs_2_, bf16[384,1024]{1,0:T(8,128)(2,1)} %collective-permute-done.16.refs_2_.refs_3_, ...), custom_call_target="tpu_custom_call" | custom-call | flops 1000000 | bytes 1 | tf_op jit(solution)/shard_map/turn_rows/pallas_call | solution.py:99
  155.7 11.2 %cross_project.1 = (bf16[768,2048]{1,0:T(8,128)(2,1)}, bf16[768,2048]{1,0:T(8,128)(2,1)}) custom-call(s32[4]{0:T(128)} %pad_add_fusion.refs_0_, bf16[768,1024]{1,0:T(8,128)(2,1)} %bitcast.86, bf16[384,1024]{1,0:T(8,128)(2,1)} %collective-permute-done.3.refs_8_.refs_2_, bf16[384,1024]{1,0:T(8,128)(2,1)} %collective-permute-done.16.refs_2_.refs_3_, ...), custom_call_target="tpu_custom_call" | custom-call | flops 1000000 | bytes 1 | tf_op jit(solution)/shard_map/cross_project/pallas_call | solution.py:99
  166.9 3.8 move_blocks.23
  171.7 3.8 move_blocks.24
  176.6 7.8 %self_mix.1 = (f32[512,1024]{1,0:T(8,128)}, f32[512,1024]{1,0:T(8,128)}, bf16[512,1024]{1,0:T(8,128)(2,1)}, bf16[512,1024]{1,0:T(8,128)(2,1)}) custom-call(s32[4]{0:T(128)} %pad_add_fusion.refs_0_, bf16[512,1024]{1,0:T(8,128)(2,1)} %get-tuple-element.137.refs_4_.refs_1_, bf16[512,1024]{1,0:T(8,128)(2,1)} %refs_2_.3, ...), custom_call_target="tpu_custom_call" | custom-call | flops 1000000 | bytes 1 | tf_op jit(solution)/shard_map/self_mix/pallas_call | solution.py:99
  184.4 17.1 %cross_forward.1 = (bf16[512,1024]{1,0:T(8,128)(2,1)}, f32[512,1024]{1,0:T(8,128)}) custom-call(s32[1]{0:T(128)} %bitcast.5.refs_0_, bf16[512,1024]{1,0:T(8,128)(2,1)} %get-tuple-element.146.refs_1_, bf16[2,384,2048]{2,1,0:T(8,128)(2,1)} %bitcast.71, bf16[2,384,2048]{2,1,0:T(8,128)(2,1)} %bitcast.72, bf16[2,384,2048]{2,1,0:T(8,128)(2,1)} %bitcast.75, ...), custom_call_target="tpu_custom_call" | custom-call | flops 1000000 | bytes 1 | tf_op jit(solution)/shard_map/cross_forward/pallas_call | solution.py:99
  201.5 6.9 %cross_mix.1 = (f32[512,1024]{1,0:T(8,128)}, f32[512,1024]{1,0:T(8,128)}, bf16[512,1024]{1,0:T(8,128)(2,1)}) custom-call(s32[4]{0:T(128)} %pad_add_fusion.refs_0_, bf16[512,1024]{1,0:T(8,128)(2,1)} %get-tuple-element.149.refs_1_.refs_2_.refs_7_, f32[512,1024]{1,0:T(8,128)} %get-tuple-element.150.refs_2_, f32[8,1024]{1,0:T(8,128)} %norm_table.1.refs_6_.refs_3_.refs_4_, ...), custom_call_target="tpu_custom_call" | custom-call | flops 1000000 | bytes 1 | tf_op jit(solution)/shard_map/cross_mix/pallas_call | solution.py:99
  208.4 6.7 %turn_rows.5 = (bf16[512,1536]{1,0:T(8,128)(2,1)}, bf16[512,1536]{1,0:T(8,128)(2,1)}) custom-call(s32[4]{0:T(128)} %pad_add_fusion.refs_0_, bf16[512,1024]{1,0:T(8,128)(2,1)} %get-tuple-element.153.refs_1_, bf16[512,1024]{1,0:T(8,128)(2,1)} %get-tuple-element.149.refs_1_.refs_2_.refs_7_, bf16[512,1024]{1,0:T(8,128)(2,1)} %get-tuple-element.151.refs_3_.refs_1_, ...), custom_call_target="tpu_custom_call" | custom-call | flops 1000000 | bytes 1 | tf_op jit(solution)/shard_map/turn_rows/pallas_call | solution.py:99
  215.1 4.0 collective-permute-done.20.refs_2_
  229.8 16.8 %feed_in.1 = (bf16[512,4096]{1,0:T(8,128)(2,1)}, bf16[512,4096]{1,0:T(8,128)(2,1)}, bf16[2048,512]{1,0:T(8,128)(2,1)}, bf16[2048,512]{1,0:T(8,128)(2,1)}) custom-call(s32[4]{0:T(128)} %pad_add_fusion.refs_0_, bf16[512,1024]{1,0:T(8,128)(2,1)} %get-tuple-element.151.refs_3_.refs_1_, bf16[8,64,4096]{2,1,0:T(8,128)(2,1)} %bitcast.80, ...), custom_call_target="tpu_custom_call" | custom-call | flops 1000000 | bytes 1 | tf_op jit(solution)/shard_map/feed_in/pallas_call | solution.py:99
  246.8 13.9 %feed_out.1 = (bf16[512,1024]{1,0:T(8,128)(2,1)}, f32[512,1024]{1,0:T(8,128)}, bf16[512,1024]{1,0:T(8,128)(2,1)}, f32[16,1024]{1,0:T(8,128)}) custom-call(s32[4]{0:T(128)} %pad_add_fusion.refs_0_, bf16[512,4096]{1,0:T(8,128)(2,1)} %get-tuple-element.157.refs_1_, f32[512,1024]{1,0:T(8,128)} %get-tuple-element.158.refs_2_, ...), custom_call_target="tpu_custom_call" | custom-call | flops 1000000 | bytes 1 | tf_op jit(solution)/shard_map/feed_out/pallas_call | solution.py:99
  263.7 10.4 %weight_grad.7 = (bf16[2,4,128,512]{3,2,1,0:T(8,128)(2,1)}, bf16[2,4,128,512]{3,2,1,0:T(8,128)(2,1)}, bf16[2,4,128,512]{3,2,1,0:T(8,128)(2,1)}, bf16[2,4,128,512]{3,2,1,0:T(8,128)(2,1)}) custom-call(s32[4]{0:T(128)} %pad_add_fusion.refs_0_, bf16[2048,512]{1,0:T(8,128)(2,1)} %get-tuple-element.163.refs_1_, bf16[2048,512]{1,0:T(8,128)(2,1)} %collective-permute-done.25.refs_2_, ...), custom_call_target="tpu_custom_call" | custom-call | flops 1000000 | bytes 1 | tf_op jit(solution)/shard_map/weight_grad/pallas_call | solution.py:99
  276.0 10.9 %feed_back.1.refs_1_.refs_3_ = bf16[512,4096]{1,0:T(8,128)(2,1)} custom-call(s32[4]{0:T(128)} %pad_add_fusion.refs_0_, bf16[512,1024]{1,0:T(8,128)(2,1)} %get-tuple-element.161.refs_3_.refs_1_, bf16[512,4096]{1,0:T(8,128)(2,1)} %get-tuple-element.162.refs_2_, bf16[8,256,1024]{2,1,0:T(8,128)(2,1)} %bitcast.70, ...), custom_call_target="tpu_custom_call" | custom-call | flops 1000000 | bytes 1 | tf_op jit(solution)/shard_map/feed_back/pallas_call | solution.py:99
  287.1 14.2 %cross_back.1 = (f32[512,1024]{1,0:T(8,128)}, bf16[512,1024]{1,0:T(8,128)(2,1)}, bf16[512,1024]{1,0:T(8,128)(2,1)}, f32[16,1024]{1,0:T(8,128)}) custom-call(s32[4]{0:T(128)} %pad_add_fusion.refs_0_, bf16[512,4096]{1,0:T(8,128)(2,1)} %feed_back.1.refs_1_.refs_3_, f32[512,1024]{1,0:T(8,128)} %get-tuple-element.166.refs_2_, ...), custom_call_target="tpu_custom_call" | custom-call | flops 1000000 | bytes 1 | tf_op jit(solution)/shard_map/cross_back/pallas_call | solution.py:99
  305.0 10.1 %weight_grad.8 = (bf16[2,4,32,2048]{3,2,1,0:T(8,128)(2,1)}, bf16[2,4,32,2048]{3,2,1,0:T(8,128)(2,1)}, bf16[2,4,32,2048]{3,2,1,0:T(8,128)(2,1)}, bf16[2,4,32,2048]{3,2,1,0:T(8,128)(2,1)}) custom-call(s32[4]{0:T(128)} %pad_add_fusion.refs_0_, bf16[512,1536]{1,0:T(8,128)(2,1)} %get-tuple-element.155.refs_3_.refs_1_, ...), custom_call_target="tpu_custom_call" | custom-call | flops 1000000 | bytes 1 | tf_op jit(solution)/shard_map/weight_grad/pallas_call | solution.py:99
  321.4 4.8 weight_grad.9
  326.1 23.9 %cross_backward.1 = (bf16[512,1024]{1,0:T(8,128)(2,1)}, bf16[768,2048]{1,0:T(8,128)(2,1)}, bf16[768,2048]{1,0:T(8,128)(2,1)}) custom-call(s32[1]{0:T(128)} %bitcast.5.refs_0_, bf16[512,1024]{1,0:T(8,128)(2,1)} %get-tuple-element.146.refs_1_, bf16[2,384,2048]{2,1,0:T(8,128)(2,1)} %bitcast.73, bf16[2,384,2048]{2,1,0:T(8,128)(2,1)} %bitcast.74, ...), custom_call_target="tpu_custom_call" | custom-call | flops 1000000 | bytes 1 | tf_op jit(solution)/shard_map/cross_backward/pallas_call | solution.py:99
  352.7 5.0 add_blocks.8
  357.7 8.9 %self_back.1 = (f32[512,1024]{1,0:T(8,128)}, bf16[512,1024]{1,0:T(8,128)(2,1)}, bf16[512,1024]{1,0:T(8,128)(2,1)}, f32[16,1024]{1,0:T(8,128)}) custom-call(s32[4]{0:T(128)} %pad_add_fusion.refs_0_, bf16[512,1024]{1,0:T(8,128)(2,1)} %get-tuple-element.177.refs_11_.refs_1_.refs_3_, f32[512,1024]{1,0:T(8,128)} %get-tuple-element.173.refs_5_.refs_2_, ...), custom_call_target="tpu_custom_call" | custom-call | flops 1000000 | bytes 1 | tf_op jit(solution)/shard_map/self_back/pallas_call | solution.py:99
  372.7 13.0 %weight_grad.10 = (bf16[2,4,32,2048]{3,2,1,0:T(8,128)(2,1)}, bf16[2,4,32,2048]{3,2,1,0:T(8,128)(2,1)}) custom-call(s32[4]{0:T(128)} %pad_add_fusion.refs_0_, bf16[512,1280]{1,0:T(8,128)(2,1)} %get-tuple-element.130.refs_2_.refs_1_.refs_3_, bf16[512,1280]{1,0:T(8,128)(2,1)} %get-tuple-element.130.refs_2_.refs_1_.refs_3_, ...), custom_call_target="tpu_custom_call" | custom-call | flops 1000000 | bytes 1 | tf_op jit(solution)/shard_map/weight_grad/pallas_call | solution.py:99
  386.4 4.8 weight_grad.11
  392.6 3.6 add_blocks.9.refs_7_
  396.2 14.9 %self_backward.1.refs_7_.refs_3_.refs_1_ = bf16[512,3072]{1,0:T(8,128)(2,1)} custom-call(s32[3]{0:T(128)} %pad_add_fusion.1.refs_0_, bf16[512,3072]{1,0:T(8,128)(2,1)} %self_project.1.refs_2_.refs_1_.refs_3_, bf16[512,3072]{1,0:T(8,128)(2,1)} %self_project.1.refs_2_.refs_1_.refs_3_, bf16[512,3072]{1,0:T(8,128)(2,1)} %self_project.1.refs_2_.refs_1_.refs_3_, ...), custom_call_target="tpu_custom_call" | custom-call | flops 1000000 | bytes 1 | tf_op jit(solution)/shard_map/self_backward/pallas_call | solution.py:99
  411.2 4.9 weight_grad.12
  424.0 9.6 %weight_grad.13 = (bf16[2,4,32,1536]{3,2,1,0:T(8,128)(2,1)}, bf16[2,4,32,1536]{3,2,1,0:T(8,128)(2,1)}, bf16[2,4,32,1536]{3,2,1,0:T(8,128)(2,1)}, bf16[2,4,32,1536]{3,2,1,0:T(8,128)(2,1)}) custom-call(s32[4]{0:T(128)} %pad_add_fusion.refs_0_, bf16[512,1280]{1,0:T(8,128)(2,1)} %get-tuple-element.130.refs_2_.refs_1_.refs_3_, ...), custom_call_target="tpu_custom_call" | custom-call | flops 1000000 | bytes 1 | tf_op jit(solution)/shard_map/weight_grad/pallas_call | solution.py:99
  438.2 3.6 add_blocks.11.refs_4_
  441.8 7.7 %memory_back.2.refs_9_.refs_1_ = bf16[768,1024]{1,0:T(8,128)(2,1)} custom-call(s32[4]{0:T(128)} %pad_add_fusion.refs_0_, bf16[768,2048]{1,0:T(8,128)(2,1)} %get-tuple-element.188.refs_14_.refs_1_, bf16[8,64,5248]{2,1,0:T(8,128)(2,1)} %bitcast.66, bf16[8,64,5248]{2,1,0:T(8,128)(2,1)} %collective-permute-done.15.refs_2_.refs_5_.refs_8_.refs_6_.refs_3_, ...), custom_call_target="tpu_custom_call" | custom-call | flops 1000000 | bytes 1 | tf_op jit(solution)/shard_map/memory_back/pallas_call | solution.py:99
  449.6 9.1 %collective-permute-done.47.refs_4_.refs_11_ = bf16[2,4,32,1536]{3,2,1,0:T(8,128)(2,1)} collective-permute-done((bf16[2,4,32,1536]{3,2,1,0:T(8,128)(2,1)}, bf16[2,4,32,1536]{3,2,1,0:T(8,128)(2,1)}, u32[]{:S(2)}, u32[]{:S(2)}) %collective-permute-start.47) | collective-permute-done | bytes 786464 | tf_op jit(solution)/shard_map/ppermute | solution.py:402
  458.7 3.4 add_blocks.12
  467.9 8.5 %collective-permute-done.51.refs_3_ = bf16[4,32,640]{2,1,0:T(8,128)(2,1)} collective-permute-done((bf16[4,32,640]{2,1,0:T(8,128)(2,1)}, bf16[4,32,640]{2,1,0:T(8,128)(2,1)}, u32[]{:S(2)}, u32[]{:S(2)}) %collective-permute-start.51) | collective-permute-done | bytes 163872 | tf_op jit(solution)/shard_map/ppermute | solution.py:402
  478.0 3.9 add_blocks.13
  490.0 7.7 %memory_back.3.refs_5_.refs_1_ = bf16[768,1024]{1,0:T(8,128)(2,1)} custom-call(s32[4]{0:T(128)} %pad_add_fusion.refs_0_, bf16[768,2048]{1,0:T(8,128)(2,1)} %get-tuple-element.187.refs_13_.refs_1_, bf16[8,64,5248]{2,1,0:T(8,128)(2,1)} %bitcast.67, bf16[8,64,5248]{2,1,0:T(8,128)(2,1)} %collective-permute-done.15.refs_2_.refs_5_.refs_8_.refs_6_.refs_3_, ...), custom_call_target="tpu_custom_call" | custom-call | flops 1000000 | bytes 1 | tf_op jit(solution)/shard_map/memory_back/pallas_call | solution.py:99
  497.7 9.3 %target_back.1.refs_6_ = bf16[512,1024]{1,0:T(8,128)(2,1)} custom-call(s32[4]{0:T(128)} %pad_add_fusion.refs_0_, bf16[512,3072]{1,0:T(8,128)(2,1)} %self_backward.1.refs_7_.refs_3_.refs_1_, f32[512,1024]{1,0:T(8,128)} %get-tuple-element.189.refs_17_.refs_2_, bf16[8,64,3072]{2,1,0:T(8,128)(2,1)} %bitcast.84, ...), custom_call_target="tpu_custom_call" | custom-call | flops 1000000 | bytes 1 | tf_op jit(solution)/shard_map/target_back/pallas_call | solution.py:99
  512.1 3.8 move_blocks.27
  (198 shorter events, 115.8 us)
Async XLA Ops:
  7.2 67.5 %all-gather.4.cloned.1.call-start = ((), (), s32[]{:S(2)}) async-start(), calls=%async_computation.3 | async-start | bytes 1679360 | tf_op jit(solution)/shard_map/all_gather | solution.py:425
  15.6 23.4 %collective-permute-start.3 = (bf16[384,1024]{1,0:T(8,128)(2,1)}, bf16[384,1024]{1,0:T(8,128)(2,1)}, u32[]{:S(2)}, u32[]{:S(2)}) collective-permute-start(bf16[384,1024]{1,0:T(8,128)(2,1)} %get-tuple-element.122), channel_id=1, source_target_pairs={{0,1},{1,0},{2,3},{3,2},{4,5},{5,4},{6,7},{7,6},{8,9},{9,8},{10,11... | collective-permute-start | bytes 2359304 | tf_op jit(solution)/shard_map/ppermute | solution.py:406
  18.6 17.9 %collective-permute-start.2 = (bf16[32,3072]{1,0:T(8,128)(2,1)}, bf16[32,3072]{1,0:T(8,128)(2,1)}, u32[]{:S(2)}, u32[]{:S(2)}) collective-permute-start(bf16[32,3072]{1,0:T(8,128)(2,1)} %get-tuple-element.118.refs_2_.refs_1_), channel_id=1, source_target_pairs={{0,24},{2,26},{4,28},{6,30},{8,16},{10,18},{12,20},{14,22},{16,8},... | collective-permute-start | bytes 589832 | tf_op jit(solution)/shard_map/ppermute | solution.py:411
  41.6 76.6 %all-gather.6.cloned.1.call-start = ((), (), s32[]{:S(2)}) async-start(), calls=%async_computation.4 | async-start | bytes 1310720 | tf_op jit(solution)/shard_map/all_gather | solution.py:425
  43.8 99.8 %all-gather.8.cloned.1.call-start = ((), (), s32[]{:S(2)}) async-start(), calls=%async_computation.5 | async-start | bytes 1310720 | tf_op jit(solution)/shard_map/all_gather | solution.py:425
  57.0 23.6 %collective-permute-start.8 = (bf16[2,4,32,1536]{3,2,1,0:T(8,128)(2,1)}, bf16[2,4,32,1536]{3,2,1,0:T(8,128)(2,1)}, u32[]{:S(2)}, u32[]{:S(2)}) collective-permute-start(bf16[2,4,32,1536]{3,2,1,0:T(8,128)(2,1)} %get-tuple-element.128), channel_id=1, source_target_pairs={{0,4},{2,6},{4,0},{6,2},{8,12},{10,14},{12,8},{14,10},{16,20},{18,... | collective-permute-start | bytes 2359304 | tf_op jit(solution)/shard_map/ppermute | solution.py:402
  57.7 23.0 %collective-permute-start.7 = (bf16[2,4,32,1536]{3,2,1,0:T(8,128)(2,1)}, bf16[2,4,32,1536]{3,2,1,0:T(8,128)(2,1)}, u32[]{:S(2)}, u32[]{:S(2)}) collective-permute-start(bf16[2,4,32,1536]{3,2,1,0:T(8,128)(2,1)} %get-tuple-element.127.refs_3_), channel_id=1, source_target_pairs={{0,1},{1,0},{2,3},{3,2},{4,5},{5,4},{6,7},{7,6},{8,9},{9,8},{10,11... | collective-permute-start | bytes 2359304 | tf_op jit(solution)/shard_map/ppermute | solution.py:406
  63.7 20.1 %collective-permute-start.12 = (bf16[512,1280]{1,0:T(8,128)(2,1)}, bf16[512,1280]{1,0:T(8,128)(2,1)}, u32[]{:S(2)}, u32[]{:S(2)}) collective-permute-start(bf16[512,1280]{1,0:T(8,128)(2,1)} %get-tuple-element.133), channel_id=1, source_target_pairs={{0,2},{2,0},{4,6},{6,4},{8,10},{10,8},{12,14},{14,12},{16,18},{18,... | collective-permute-start | bytes 3932168 | tf_op jit(solution)/shard_map/ppermute | solution.py:397
  79.1 18.6 %collective-permute-start.11 = (bf16[4,32,3072]{2,1,0:T(8,128)(2,1)}, bf16[4,32,3072]{2,1,0:T(8,128)(2,1)}, u32[]{:S(2)}, u32[]{:S(2)}) collective-permute-start(bf16[4,32,3072]{2,1,0:T(8,128)(2,1)} %get-tuple-element.132.refs_3_), channel_id=1, source_target_pairs={{0,1},{1,0},{2,3},{3,2},{4,5},{5,4},{6,7},{7,6},{8,9},{9,8},{10,11... | collective-permute-start | bytes 2359304 | tf_op jit(solution)/shard_map/ppermute | solution.py:406
  83.7 25.3 %collective-permute-start.9 = (bf16[8,64,3072]{2,1,0:T(8,128)(2,1)}, bf16[8,64,3072]{2,1,0:T(8,128)(2,1)}, u32[]{:S(2)}, u32[]{:S(2)}) collective-permute-start(bf16[8,64,3072]{2,1,0:T(8,128)(2,1)} %bitcast.82), channel_id=1, source_target_pairs={{0,2},{2,0},{4,6},{6,4},{8,10},{10,8},{12,14},{14,12},{16,18},{18,... | collective-permute-start | bytes 9437192 | tf_op jit(solution)/shard_map/ppermute | solution.py:397
  102.3 37.7 %collective-permute-start.14 = (bf16[2,4,32,3072]{3,2,1,0:T(8,128)(2,1)}, bf16[2,4,32,3072]{3,2,1,0:T(8,128)(2,1)}, u32[]{:S(2)}, u32[]{:S(2)}) collective-permute-start(bf16[2,4,32,3072]{3,2,1,0:T(8,128)(2,1)} %get-tuple-element.139), channel_id=1, source_target_pairs={{0,4},{2,6},{4,0},{6,2},{8,12},{10,14},{12,8},{14,10},{16,20},{18,... | collective-permute-start | bytes 4718600 | tf_op jit(solution)/shard_map/ppermute | solution.py:402
  102.9 31.0 %collective-permute-start.13 = (bf16[2,4,32,2176]{3,2,1,0:T(8,128)(2,1)}, bf16[2,4,32,2176]{3,2,1,0:T(8,128)(2,1)}, u32[]{:S(2)}, u32[]{:S(2)}) collective-permute-start(bf16[2,4,32,2176]{3,2,1,0:T(8,128)(2,1)} %get-tuple-element.134.refs_4_), channel_id=1, source_target_pairs={{0,1},{1,0},{2,3},{3,2},{4,5},{5,4},{6,7},{7,6},{8,9},{9,8},{10,11... | collective-permute-start | bytes 3342344 | tf_op jit(solution)/shard_map/ppermute | solution.py:406
  109.0 327.6 %reduce-scatter.4.cloned.1.call-start = ((), (), s32[]{:S(2)}) async-start(), calls=%async_computation.6 | async-start | bytes 1310720 | tf_op jit(solution)/shard_map/reduce_scatter | solution.py:1277
  117.8 26.5 %collective-permute-start.16 = (bf16[384,1024]{1,0:T(8,128)(2,1)}, bf16[384,1024]{1,0:T(8,128)(2,1)}, u32[]{:S(2)}, u32[]{:S(2)}) collective-permute-start(bf16[384,1024]{1,0:T(8,128)(2,1)} %gate.2.refs_2_), channel_id=1, source_target_pairs={{0,1},{1,0},{2,3},{3,2},{4,5},{5,4},{6,7},{7,6},{8,9},{9,8},{10,11... | collective-permute-start | bytes 2359304 | tf_op jit(solution)/shard_map/ppermute | solution.py:406
  119.0 47.9 %collective-permute-start.19 = (bf16[4,32,4096]{2,1,0:T(8,128)(2,1)}, bf16[4,32,4096]{2,1,0:T(8,128)(2,1)}, u32[]{:S(2)}, u32[]{:S(2)}) collective-permute-start(bf16[4,32,4096]{2,1,0:T(8,128)(2,1)} %move_blocks.20.refs_5_.refs_1_), channel_id=1, source_target_pairs={{0,4},{2,6},{4,0},{6,2},{8,12},{10,14},{12,8},{14,10},{16,20},{18,... | collective-permute-start | bytes 3145736 | tf_op jit(solution)/shard_map/ppermute | solution.py:402
  144.9 26.8 %collective-permute-start.18 = (bf16[4,128,1024]{2,1,0:T(8,128)(2,1)}, bf16[4,128,1024]{2,1,0:T(8,128)(2,1)}, u32[]{:S(2)}, u32[]{:S(2)}) collective-permute-start(bf16[4,128,1024]{2,1,0:T(8,128)(2,1)} %move_blocks.22.refs_4_.refs_1_), channel_id=1, source_target_pairs={{0,1},{1,0},{2,3},{3,2},{4,5},{5,4},{6,7},{7,6},{8,9},{9,8},{10,11... | collective-permute-start | bytes 3145736 | tf_op jit(solution)/shard_map/ppermute | solution.py:406
  153.2 23.3 %collective-permute-start.17 = (bf16[512,1280]{1,0:T(8,128)(2,1)}, bf16[512,1280]{1,0:T(8,128)(2,1)}, u32[]{:S(2)}, u32[]{:S(2)}) collective-permute-start(bf16[512,1280]{1,0:T(8,128)(2,1)} %get-tuple-element.142), channel_id=1, source_target_pairs={{0,2},{2,0},{4,6},{6,4},{8,10},{10,8},{12,14},{14,12},{16,18},{18,... | collective-permute-start | bytes 3932168 | tf_op jit(solution)/shard_map/ppermute | solution.py:397
  170.7 48.4 %collective-permute-start.20 = (bf16[2,4,32,4096]{3,2,1,0:T(8,128)(2,1)}, bf16[2,4,32,4096]{3,2,1,0:T(8,128)(2,1)}, u32[]{:S(2)}, u32[]{:S(2)}) collective-permute-start(bf16[2,4,32,4096]{3,2,1,0:T(8,128)(2,1)} %get-tuple-element.144.refs_3_), channel_id=1, source_target_pairs={{0,1},{1,0},{2,3},{3,2},{4,5},{5,4},{6,7},{7,6},{8,9},{9,8},{10,11... | collective-permute-start | bytes 6291464 | tf_op jit(solution)/shard_map/ppermute | solution.py:406
  175.5 47.8 %collective-permute-start.22 = (bf16[2,4,128,1024]{3,2,1,0:T(8,128)(2,1)}, bf16[2,4,128,1024]{3,2,1,0:T(8,128)(2,1)}, u32[]{:S(2)}, u32[]{:S(2)}) collective-permute-start(bf16[2,4,128,1024]{3,2,1,0:T(8,128)(2,1)} %get-tuple-element.145.refs_7_), channel_id=1, source_target_pairs={{0,4},{2,6},{4,0},{6,2},{8,12},{10,14},{12,8},{14,10},{16,20},{18,... | collective-permute-start | bytes 6291464 | tf_op jit(solution)/shard_map/ppermute | solution.py:402
  226.3 20.5 %collective-permute-start.23 = (bf16[8,256,1024]{2,1,0:T(8,128)(2,1)}, bf16[8,256,1024]{2,1,0:T(8,128)(2,1)}, u32[]{:S(2)}, u32[]{:S(2)}) collective-permute-start(bf16[8,256,1024]{2,1,0:T(8,128)(2,1)} %bitcast.68), channel_id=1, source_target_pairs={{0,2},{2,0},{4,6},{6,4},{8,10},{10,8},{12,14},{14,12},{16,18},{18,... | collective-permute-start | bytes 12582920 | tf_op jit(solution)/shard_map/ppermute | solution.py:397
  226.4 20.4 %collective-permute-start.24 = (bf16[512,1536]{1,0:T(8,128)(2,1)}, bf16[512,1536]{1,0:T(8,128)(2,1)}, u32[]{:S(2)}, u32[]{:S(2)}) collective-permute-start(bf16[512,1536]{1,0:T(8,128)(2,1)} %get-tuple-element.159), channel_id=1, source_target_pairs={{0,2},{2,0},{4,6},{6,4},{8,10},{10,8},{12,14},{14,12},{16,18},{18,... | collective-permute-start | bytes 4718600 | tf_op jit(solution)/shard_map/ppermute | solution.py:397
  246.6 17.1 %collective-permute-start.25 = (bf16[2048,512]{1,0:T(8,128)(2,1)}, bf16[2048,512]{1,0:T(8,128)(2,1)}, u32[]{:S(2)}, u32[]{:S(2)}) collective-permute-start(bf16[2048,512]{1,0:T(8,128)(2,1)} %get-tuple-element.164), channel_id=1, source_target_pairs={{0,2},{2,0},{4,6},{6,4},{8,10},{10,8},{12,14},{14,12},{16,18},{18,... | collective-permute-start | bytes 6291464 | tf_op jit(solution)/shard_map/ppermute | solution.py:397
  274.1 27.7 %collective-permute-start.30 = (bf16[2,4,128,512]{3,2,1,0:T(8,128)(2,1)}, bf16[2,4,128,512]{3,2,1,0:T(8,128)(2,1)}, u32[]{:S(2)}, u32[]{:S(2)}) collective-permute-start(bf16[2,4,128,512]{3,2,1,0:T(8,128)(2,1)} %get-tuple-element.172), channel_id=1, source_target_pairs={{0,4},{2,6},{4,0},{6,2},{8,12},{10,14},{12,8},{14,10},{16,20},{18,... | collective-permute-start | bytes 3145736 | tf_op jit(solution)/shard_map/ppermute | solution.py:402
  275.5 26.3 %collective-permute-start.29 = (bf16[2,4,128,512]{3,2,1,0:T(8,128)(2,1)}, bf16[2,4,128,512]{3,2,1,0:T(8,128)(2,1)}, u32[]{:S(2)}, u32[]{:S(2)}) collective-permute-start(bf16[2,4,128,512]{3,2,1,0:T(8,128)(2,1)} %get-tuple-element.165.refs_5_), channel_id=1, source_target_pairs={{0,1},{1,0},{2,3},{3,2},{4,5},{5,4},{6,7},{7,6},{8,9},{9,8},{10,11... | collective-permute-start | bytes 3145736 | tf_op jit(solution)/shard_map/ppermute | solution.py:406
  287.0 18.0 %collective-permute-start.28 = (bf16[512,4096]{1,0:T(8,128)(2,1)}, bf16[512,4096]{1,0:T(8,128)(2,1)}, u32[]{:S(2)}, u32[]{:S(2)}) collective-permute-start(bf16[512,4096]{1,0:T(8,128)(2,1)} %feed_back.1.refs_1_.refs_3_), channel_id=1, source_target_pairs={{0,2},{2,0},{4,6},{6,4},{8,10},{10,8},{12,14},{14,12},{16,18},{18,... | collective-permute-start | bytes 12582920 | tf_op jit(solution)/shard_map/ppermute | solution.py:397
  301.3 20.1 %collective-permute-start.27 = (bf16[512,1024]{1,0:T(8,128)(2,1)}, bf16[512,1024]{1,0:T(8,128)(2,1)}, u32[]{:S(2)}, u32[]{:S(2)}) collective-permute-start(bf16[512,1024]{1,0:T(8,128)(2,1)} %get-tuple-element.169.refs_3_), channel_id=1, source_target_pairs={{0,2},{2,0},{4,6},{6,4},{8,10},{10,8},{12,14},{14,12},{16,18},{18,... | collective-permute-start | bytes 3145736 | tf_op jit(solution)/shard_map/ppermute | solution.py:397
  315.2 37.6 %collective-permute-start.32 = (bf16[2,4,32,2048]{3,2,1,0:T(8,128)(2,1)}, bf16[2,4,32,2048]{3,2,1,0:T(8,128)(2,1)}, u32[]{:S(2)}, u32[]{:S(2)}) collective-permute-start(bf16[2,4,32,2048]{3,2,1,0:T(8,128)(2,1)} %get-tuple-element.180), channel_id=1, source_target_pairs={{0,4},{2,6},{4,0},{6,2},{8,12},{10,14},{12,8},{14,10},{16,20},{18,... | collective-permute-start | bytes 3145736 | tf_op jit(solution)/shard_map/ppermute | solution.py:402
  315.8 36.9 %collective-permute-start.31 = (bf16[2,4,32,2048]{3,2,1,0:T(8,128)(2,1)}, bf16[2,4,32,2048]{3,2,1,0:T(8,128)(2,1)}, u32[]{:S(2)}, u32[]{:S(2)}) collective-permute-start(bf16[2,4,32,2048]{3,2,1,0:T(8,128)(2,1)} %get-tuple-element.175.refs_5_), channel_id=1, source_target_pairs={{0,1},{1,0},{2,3},{3,2},{4,5},{5,4},{6,7},{7,6},{8,9},{9,8},{10,11... | collective-permute-start | bytes 3145736 | tf_op jit(solution)/shard_map/ppermute | solution.py:406
  317.4 34.8 %collective-permute-start.33 = (bf16[4,128,512]{2,1,0:T(8,128)(2,1)}, bf16[4,128,512]{2,1,0:T(8,128)(2,1)}, u32[]{:S(2)}, u32[]{:S(2)}) collective-permute-start(bf16[4,128,512]{2,1,0:T(8,128)(2,1)} %get-tuple-element.174.refs_5_), channel_id=1, source_target_pairs={{0,4},{2,6},{4,0},{6,2},{8,12},{10,14},{12,8},{14,10},{16,20},{18,... | collective-permute-start | bytes 1572872 | tf_op jit(solution)/shard_map/ppermute | solution.py:402
  318.8 33.4 %collective-permute-start.34 = (bf16[4,128,512]{2,1,0:T(8,128)(2,1)}, bf16[4,128,512]{2,1,0:T(8,128)(2,1)}, u32[]{:S(2)}, u32[]{:S(2)}) collective-permute-start(bf16[4,128,512]{2,1,0:T(8,128)(2,1)} %get-tuple-element.181), channel_id=1, source_target_pairs={{0,1},{1,0},{2,3},{3,2},{4,5},{5,4},{6,7},{7,6},{8,9},{9,8},{10,11... | collective-permute-start | bytes 1572872 | tf_op jit(solution)/shard_map/ppermute | solution.py:406
  350.1 36.3 %collective-permute-start.37 = (bf16[512,1024]{1,0:T(8,128)(2,1)}, bf16[512,1024]{1,0:T(8,128)(2,1)}, u32[]{:S(2)}, u32[]{:S(2)}) collective-permute-start(bf16[512,1024]{1,0:T(8,128)(2,1)} %get-tuple-element.177.refs_11_.refs_1_.refs_3_), channel_id=1, source_target_pairs={{0,2},{2,0},{4,6},{6,4},{8,10},{10,8},{12,14},{14,12},{16,18},{18,... | collective-permute-start | bytes 3145736 | tf_op jit(solution)/shard_map/ppermute | solution.py:397
  352.2 20.5 %collective-permute-start.38 = (bf16[768,2048]{1,0:T(8,128)(2,1)}, bf16[768,2048]{1,0:T(8,128)(2,1)}, u32[]{:S(2)}, u32[]{:S(2)}) collective-permute-start(bf16[768,2048]{1,0:T(8,128)(2,1)} %get-tuple-element.187.refs_13_.refs_1_), channel_id=1, source_target_pairs={{0,2},{2,0},{4,6},{6,4},{8,10},{10,8},{12,14},{14,12},{16,18},{18,... | collective-permute-start | bytes 9437192 | tf_op jit(solution)/shard_map/ppermute | solution.py:397
  352.2 20.5 %collective-permute-start.39 = (bf16[768,2048]{1,0:T(8,128)(2,1)}, bf16[768,2048]{1,0:T(8,128)(2,1)}, u32[]{:S(2)}, u32[]{:S(2)}) collective-permute-start(bf16[768,2048]{1,0:T(8,128)(2,1)} %get-tuple-element.188.refs_14_.refs_1_), channel_id=1, source_target_pairs={{0,2},{2,0},{4,6},{6,4},{8,10},{10,8},{12,14},{14,12},{16,18},{18,... | collective-permute-start | bytes 9437192 | tf_op jit(solution)/shard_map/ppermute | solution.py:397
  368.8 23.8 %collective-permute-start.36 = (bf16[4,32,2048]{2,1,0:T(8,128)(2,1)}, bf16[4,32,2048]{2,1,0:T(8,128)(2,1)}, u32[]{:S(2)}, u32[]{:S(2)}) collective-permute-start(bf16[4,32,2048]{2,1,0:T(8,128)(2,1)} %get-tuple-element.185), channel_id=1, source_target_pairs={{0,1},{1,0},{2,3},{3,2},{4,5},{5,4},{6,7},{7,6},{8,9},{9,8},{10,11... | collective-permute-start | bytes 1572872 | tf_op jit(solution)/shard_map/ppermute | solution.py:406
  370.4 22.2 %collective-permute-start.35 = (bf16[4,32,2048]{2,1,0:T(8,128)(2,1)}, bf16[4,32,2048]{2,1,0:T(8,128)(2,1)}, u32[]{:S(2)}, u32[]{:S(2)}) collective-permute-start(bf16[4,32,2048]{2,1,0:T(8,128)(2,1)} %get-tuple-element.182.refs_7_), channel_id=1, source_target_pairs={{0,4},{2,6},{4,0},{6,2},{8,12},{10,14},{12,8},{14,10},{16,20},{18,... | collective-permute-start | bytes 1572872 | tf_op jit(solution)/shard_map/ppermute | solution.py:402
  371.8 66.5 %reduce-scatter.6.cloned.1.call-start = ((), (), s32[]{:S(2)}) async-start(), calls=%async_computation.7 | async-start | bytes 1310720 | tf_op jit(solution)/shard_map/reduce_scatter | solution.py:1277
  372.7 38.5 %collective-permute-start.40 = (bf16[512,1024]{1,0:T(8,128)(2,1)}, bf16[512,1024]{1,0:T(8,128)(2,1)}, u32[]{:S(2)}, u32[]{:S(2)}) collective-permute-start(bf16[512,1024]{1,0:T(8,128)(2,1)} %get-tuple-element.192.refs_3_), channel_id=1, source_target_pairs={{0,2},{2,0},{4,6},{6,4},{8,10},{10,8},{12,14},{14,12},{16,18},{18,... | collective-permute-start | bytes 3145736 | tf_op jit(solution)/shard_map/ppermute | solution.py:397
  385.6 31.1 %collective-permute-start.45 = (bf16[2,4,32,2048]{3,2,1,0:T(8,128)(2,1)}, bf16[2,4,32,2048]{3,2,1,0:T(8,128)(2,1)}, u32[]{:S(2)}, u32[]{:S(2)}) collective-permute-start(bf16[2,4,32,2048]{3,2,1,0:T(8,128)(2,1)} %get-tuple-element.190.refs_7_), channel_id=1, source_target_pairs={{0,4},{2,6},{4,0},{6,2},{8,12},{10,14},{12,8},{14,10},{16,20},{18,... | collective-permute-start | bytes 3145736 | tf_op jit(solution)/shard_map/ppermute | solution.py:402
  391.1 25.6 %collective-permute-start.44 = (bf16[2,4,32,2048]{3,2,1,0:T(8,128)(2,1)}, bf16[2,4,32,2048]{3,2,1,0:T(8,128)(2,1)}, u32[]{:S(2)}, u32[]{:S(2)}) collective-permute-start(bf16[2,4,32,2048]{3,2,1,0:T(8,128)(2,1)} %get-tuple-element.191.refs_7_), channel_id=1, source_target_pairs={{0,1},{1,0},{2,3},{3,2},{4,5},{5,4},{6,7},{7,6},{8,9},{9,8},{10,11... | collective-permute-start | bytes 3145736 | tf_op jit(solution)/shard_map/ppermute | solution.py:406
  411.1 66.9 %reduce-scatter.8.cloned.1.call-start = ((), (), s32[]{:S(2)}) async-start(), calls=%async_computation.8 | async-start | bytes 1310720 | tf_op jit(solution)/shard_map/reduce_scatter | solution.py:1277
  422.8 26.8 %collective-permute-start.42 = (bf16[2,4,32,640]{3,2,1,0:T(8,128)(2,1)}, bf16[2,4,32,640]{3,2,1,0:T(8,128)(2,1)}, u32[]{:S(2)}, u32[]{:S(2)}) collective-permute-start(bf16[2,4,32,640]{3,2,1,0:T(8,128)(2,1)} %get-tuple-element.197.refs_5_), channel_id=1, source_target_pairs={{0,1},{1,0},{2,3},{3,2},{4,5},{5,4},{6,7},{7,6},{8,9},{9,8},{10,11... | collective-permute-start | bytes 983048 | tf_op jit(solution)/shard_map/ppermute | solution.py:406
  423.4 26.2 %collective-permute-start.48 = (bf16[2,4,32,640]{3,2,1,0:T(8,128)(2,1)}, bf16[2,4,32,640]{3,2,1,0:T(8,128)(2,1)}, u32[]{:S(2)}, u32[]{:S(2)}) collective-permute-start(bf16[2,4,32,640]{3,2,1,0:T(8,128)(2,1)} %get-tuple-element.206), channel_id=1, source_target_pairs={{0,4},{2,6},{4,0},{6,2},{8,12},{10,14},{12,8},{14,10},{16,20},{18,... | collective-permute-start | bytes 983048 | tf_op jit(solution)/shard_map/ppermute | solution.py:402
  433.6 25.1 %collective-permute-start.47 = (bf16[2,4,32,1536]{3,2,1,0:T(8,128)(2,1)}, bf16[2,4,32,1536]{3,2,1,0:T(8,128)(2,1)}, u32[]{:S(2)}, u32[]{:S(2)}) collective-permute-start(bf16[2,4,32,1536]{3,2,1,0:T(8,128)(2,1)} %get-tuple-element.204), channel_id=1, source_target_pairs={{0,4},{2,6},{4,0},{6,2},{8,12},{10,14},{12,8},{14,10},{16,20},{18,... | collective-permute-start | bytes 2359304 | tf_op jit(solution)/shard_map/ppermute | solution.py:402
  435.1 23.6 %collective-permute-start.46 = (bf16[2,4,32,1536]{3,2,1,0:T(8,128)(2,1)}, bf16[2,4,32,1536]{3,2,1,0:T(8,128)(2,1)}, u32[]{:S(2)}, u32[]{:S(2)}) collective-permute-start(bf16[2,4,32,1536]{3,2,1,0:T(8,128)(2,1)} %get-tuple-element.202.refs_9_), channel_id=1, source_target_pairs={{0,1},{1,0},{2,3},{3,2},{4,5},{5,4},{6,7},{7,6},{8,9},{9,8},{10,11... | collective-permute-start | bytes 2359304 | tf_op jit(solution)/shard_map/ppermute | solution.py:406
  466.9 45.2 %collective-permute-start.55 = (bf16[768,1024]{1,0:T(8,128)(2,1)}, bf16[768,1024]{1,0:T(8,128)(2,1)}, u32[]{:S(2)}, u32[]{:S(2)}) collective-permute-start(bf16[768,1024]{1,0:T(8,128)(2,1)} %gate.3.refs_14_), channel_id=1, source_target_pairs={{0,1},{1,0},{2,3},{3,2},{4,5},{5,4},{6,7},{7,6},{8,9},{9,8},{10,11... | collective-permute-start | bytes 4718600 | tf_op jit(solution)/shard_map/ppermute | solution.py:406
  482.0 25.0 %collective-permute-start.56 = (bf16[32,4352]{1,0:T(8,128)(2,1)}, bf16[32,4352]{1,0:T(8,128)(2,1)}, u32[]{:S(2)}, u32[]{:S(2)}) collective-permute-start(bf16[32,4352]{1,0:T(8,128)(2,1)} %get-tuple-element.214), channel_id=1, source_target_pairs={{0,8},{2,10},{4,12},{6,14},{8,0},{10,2},{12,4},{14,6},{16,24},{18,... | collective-permute-start | bytes 835592 | tf_op jit(solution)/shard_map/ppermute | solution.py:411
  483.7 23.3 %collective-permute-start.57 = (bf16[32,4352]{1,0:T(8,128)(2,1)}, bf16[32,4352]{1,0:T(8,128)(2,1)}, u32[]{:S(2)}, u32[]{:S(2)}) collective-permute-start(bf16[32,4352]{1,0:T(8,128)(2,1)} %get-tuple-element.215), channel_id=1, source_target_pairs={{0,16},{2,18},{4,20},{6,22},{8,24},{10,26},{12,28},{14,30},{16,0},... | collective-permute-start | bytes 835592 | tf_op jit(solution)/shard_map/ppermute | solution.py:411
  485.7 21.3 %collective-permute-start.58 = (bf16[32,4352]{1,0:T(8,128)(2,1)}, bf16[32,4352]{1,0:T(8,128)(2,1)}, u32[]{:S(2)}, u32[]{:S(2)}) collective-permute-start(bf16[32,4352]{1,0:T(8,128)(2,1)} %get-tuple-element.216), channel_id=1, source_target_pairs={{0,24},{2,26},{4,28},{6,30},{8,16},{10,18},{12,20},{14,22},{16,8},... | collective-permute-start | bytes 835592 | tf_op jit(solution)/shard_map/ppermute | solution.py:411
  (28 other events, 299.4 us)
Sparse Core Ops, SparseCore 0:
  41.8 32.8 all-gather.3
  76.8 26.8 all-gather.5
  109.1 26.7 all-gather.7
  371.9 26.9 reduce-scatter.3
  411.3 26.9 reduce-scatter.5
  442.0 25.8 reduce-scatter.7

commit v6 on v5

--- a/solution.py
+++ b/solution.py
@@ -656,6 +656,7 @@
     else:
         chunk = (size, 2, lead.rows, lead.width)
     n_in, n_arrays, n_out = len(inputs), len(arrays), len(outs)
+    depth = min(3, len(plan))
     streamed = sorted(streams)
     most = max([1] + [inputs[i].shape[1] // streams[i] for i in streamed])
 
@@ -674,7 +675,7 @@
 
         def issue(number):
             which, kind, start, size = plan[number]
-            slot = number % 2
+            slot = number % depth
             for source, target in weights[which].copies(
                 kind, start, size, bits_now, find, held.at[slot]
             ):
@@ -685,9 +686,9 @@
         def fetch():
             number = taken[0]
             taken[0] += 1
-            if number + 1 < len(plan):
-                issue(number + 1)
-            slot = number % 2
+            if depth > 1 and number + depth - 1 < len(plan):
+                issue(number + depth - 1)
+            slot = number % depth
             pltpu.make_async_copy(held.at[slot], held.at[slot], sems.at[slot]).wait()
             return held[slot].reshape(-1, chunk[-1])
 
@@ -703,7 +704,8 @@
             sent.append(copy)
 
         fetch.need, fetch.send, fetch.bits = need, send, bits_now
-        issue(0)
+        for number in range(max(1, depth - 1)):
+            issue(number)
         for number, which in enumerate(streamed):
             count = streams[which]
             for part in range(inputs[which].shape[1] // count):
@@ -732,8 +734,8 @@
         + [pltpu.VMEM(inputs[i].shape, inputs[i].dtype) for i in streamed]
         + [pltpu.VMEM(shape, kind) for shape, kind in scratch]
         + [
-            pltpu.VMEM((2, *chunk), BF16),
-            pltpu.SemaphoreType.DMA((2,)),
+            pltpu.VMEM((depth, *chunk), BF16),
+            pltpu.SemaphoreType.DMA((depth,)),
             pltpu.SemaphoreType.DMA((max(1, len(streamed)), most)),
             pltpu.SemaphoreType.DMA((max(1, sends),)),
         ],

time: 534 us -> 534 us (level)
  no operation moved by 1% of the time
where the time goes in v6:
time: 534 us; the launch traced here: 524 us
  Pallas kernels  346 us (65%)
  waiting for transfers between devices  90.6 us (17%)
  starting transfers between devices  52.6 us (10%)
  between operations  15.9 us (3%)
  other arithmetic  10.5 us (2%)
  local copies, waits for them, and re-layouts  8.35 us (2%)
    pallas_call x52, Pallas kernels, launch(): results = run(*operands, *ties)  346 us
    ppermute x16, waiting for transfers between devices, swap_next(): return lax.ppermute(values, 'dp', [(i, i ^ 2) for i in range(size)])  40.9 us
    ppermute x20, waiting for transfers between devices, swap_mem(): return lax.ppermute(values, 'mem', [(0, 1), (1, 0)])  28.9 us
    ppermute x20, starting transfers between devices, swap_mem(): return lax.ppermute(values, 'mem', [(0, 1), (1, 0)])  22.8 us
    ppermute x16, starting transfers between devices, swap_next(): return lax.ppermute(values, 'dp', [(i, i ^ 2) for i in range(size)])  18 us
    all_gather x3, waiting for transfers between devices, outer_gather(): lax.all_gather(shard, 'dp', axis_index_groups=outer_groups(), axis=0, til...  11 us
  transfers between devices with their start and end apart: 65, of which 19 were waited for; matrix products, arithmetic and copies ran while one was open for 3% of the time, Pallas kernels for 62%

profile of v6, /device:TPU:0, one launch (start us, length us, event | category | flops | bytes accessed | tf_op | source)
XLA Modules:
  0.0 523.6 jit_solution(15540129722670822108)
XLA Ops:
  11.9 3.7 move_blocks.14
  18.6 3.6 collective-permute-start.2
  23.9 12.6 %collective-permute-done.4.refs_9_ = s32[2,384]{1,0:T(2,128)S(1)} collective-permute-done((s32[2,384]{1,0:T(2,128)S(1)}, s32[2,384]{1,0:T(2,128)S(1)}, u32[]{:S(2)}, u32[]{:S(2)}) %collective-permute-start.4) | collective-permute-done | bytes 3104 | tf_op jit(solution)/shard_map/ppermute | solution.py:406
  43.8 8.4 %collective-permute-done.5.refs_2_ = bf16[4,32,1536]{2,1,0:T(8,128)(2,1)} collective-permute-done((bf16[4,32,1536]{2,1,0:T(8,128)(2,1)}, bf16[4,32,1536]{2,1,0:T(8,128)(2,1)}, u32[]{:S(2)}, u32[]{:S(2)}) %collective-permute-start.5) | collective-permute-done | bytes 393248 | tf_op jit(solution)/shard_map/ppermute | solution.py:402
  53.4 3.6 move_blocks.16
  58.2 5.5 %turn_rows.3 = (bf16[512,1280]{1,0:T(8,128)(2,1)}, bf16[512,1280]{1,0:T(8,128)(2,1)}) custom-call(s32[4]{0:T(128)} %pad_add_fusion.refs_0_, bf16[512,1024]{1,0:T(8,128)(2,1)} %refs_2_.3, bf16[768,1024]{1,0:T(8,128)(2,1)} %bitcast.85, bf16[2,4,32,1536]{3,2,1,0:T(8,128)(2,1)} %get-tuple-element.127.refs_3_), custom_call_target="tpu_custom_call" | custom-call | flops 999999995904 | bytes 1 | tf_op jit(solution)/shard_map/turn_rows/pallas_call | solution.py:99
  63.7 11.0 %all-gather.4.cloned.1.call-done = bf16[128,5248]{1,0:T(8,128)(2,1)} async-done(((bf16[32,5248]{1,0:T(8,128)(2,1)}), bf16[128,5248]{1,0:T(8,128)(2,1)}) %all-gather.4.cloned.1.call-update) | async-done | bytes 1343504 | tf_op jit(solution)/shard_map/all_gather | solution.py:425
  83.8 7.9 %collective-permute-done.10.refs_2_ = bf16[4,32,2176]{2,1,0:T(8,128)(2,1)} collective-permute-done((bf16[4,32,2176]{2,1,0:T(8,128)(2,1)}, bf16[4,32,2176]{2,1,0:T(8,128)(2,1)}, u32[]{:S(2)}, u32[]{:S(2)}) %collective-permute-start.10) | collective-permute-done | bytes 557088 | tf_op jit(solution)/shard_map/ppermute | solution.py:402
  91.7 6.1 %collective-permute-done.11.refs_4_ = bf16[4,32,3072]{2,1,0:T(8,128)(2,1)} collective-permute-done((bf16[4,32,3072]{2,1,0:T(8,128)(2,1)}, bf16[4,32,3072]{2,1,0:T(8,128)(2,1)}, u32[]{:S(2)}, u32[]{:S(2)}) %collective-permute-start.11) | collective-permute-done | bytes 786464 | tf_op jit(solution)/shard_map/ppermute | solution.py:406
  97.8 4.5 move_blocks.19
  109.0 8.0 %self_project.1.refs_2_.refs_1_.refs_3_ = bf16[512,3072]{1,0:T(8,128)(2,1)} custom-call(s32[4]{0:T(128)} %pad_add_fusion.refs_0_, bf16[512,1024]{1,0:T(8,128)(2,1)} %refs_2_.3, bf16[8,64,3072]{2,1,0:T(8,128)(2,1)} %bitcast.83, bf16[8,64,3072]{2,1,0:T(8,128)(2,1)} %collective-permute-done.9.refs_3_.refs_4_, bf16[2,4,32,2176]{3,2,1,0:T(8,128)(2,1)} %get-tuple-element.134.refs_4_), custom_call_target="tpu_custom_call" | custom-call | flops 1000000 | bytes 1 | tf_op jit(solution)/shard_map/self_project/pallas_call | solution.py:99
  121.6 12.3 %self_forward.1 = (bf16[512,1024]{1,0:T(8,128)(2,1)}, f32[512,1024]{1,0:T(8,128)}) custom-call(s32[3]{0:T(128)} %pad_add_fusion.1.refs_0_, bf16[512,3072]{1,0:T(8,128)(2,1)} %self_project.1.refs_2_.refs_1_.refs_3_, bf16[512,3072]{1,0:T(8,128)(2,1)} %self_project.1.refs_2_.refs_1_.refs_3_, bf16[512,3072]{1,0:T(8,128)(2,1)} %self_project.1.refs_2_.refs_1_.refs_3_, ...), custom_call_target="tpu_custom_call" | custom-call | flops 1000000 | bytes 1 | tf_op jit(solution)/shard_map/self_forward/pallas_call | solution.py:99
  133.9 6.1 %collective-permute-done.14.refs_3_ = bf16[2,4,32,3072]{3,2,1,0:T(8,128)(2,1)} collective-permute-done((bf16[2,4,32,3072]{3,2,1,0:T(8,128)(2,1)}, bf16[2,4,32,3072]{3,2,1,0:T(8,128)(2,1)}, u32[]{:S(2)}, u32[]{:S(2)}) %collective-permute-start.14) | collective-permute-done | bytes 1572896 | tf_op jit(solution)/shard_map/ppermute | solution.py:402
  140.0 3.5 move_blocks.21.refs_3_
  146.5 6.7 %turn_rows.4 = (bf16[512,1280]{1,0:T(8,128)(2,1)}, bf16[512,1280]{1,0:T(8,128)(2,1)}) custom-call(s32[4]{0:T(128)} %pad_add_fusion.refs_0_, bf16[512,1024]{1,0:T(8,128)(2,1)} %get-tuple-element.137.refs_4_.refs_1_, bf16[384,1024]{1,0:T(8,128)(2,1)} %collective-permute-done.3.refs_8_.refs_2_, bf16[384,1024]{1,0:T(8,128)(2,1)} %collective-permute-done.16.refs_2_.refs_3_, ...), custom_call_target="tpu_custom_call" | custom-call | flops 1000000 | bytes 1 | tf_op jit(solution)/shard_map/turn_rows/pallas_call | solution.py:99
  155.7 11.2 %cross_project.1 = (bf16[768,2048]{1,0:T(8,128)(2,1)}, bf16[768,2048]{1,0:T(8,128)(2,1)}) custom-call(s32[4]{0:T(128)} %pad_add_fusion.refs_0_, bf16[768,1024]{1,0:T(8,128)(2,1)} %bitcast.86, bf16[384,1024]{1,0:T(8,128)(2,1)} %collective-permute-done.3.refs_8_.refs_2_, bf16[384,1024]{1,0:T(8,128)(2,1)} %collective-permute-done.16.refs_2_.refs_3_, ...), custom_call_target="tpu_custom_call" | custom-call | flops 1000000 | bytes 1 | tf_op jit(solution)/shard_map/cross_project/pallas_call | solution.py:99
  166.9 3.8 move_blocks.23
  171.7 3.8 move_blocks.24
  176.6 7.8 %self_mix.1 = (f32[512,1024]{1,0:T(8,128)}, f32[512,1024]{1,0:T(8,128)}, bf16[512,1024]{1,0:T(8,128)(2,1)}, bf16[512,1024]{1,0:T(8,128)(2,1)}) custom-call(s32[4]{0:T(128)} %pad_add_fusion.refs_0_, bf16[512,1024]{1,0:T(8,128)(2,1)} %get-tuple-element.137.refs_4_.refs_1_, bf16[512,1024]{1,0:T(8,128)(2,1)} %refs_2_.3, ...), custom_call_target="tpu_custom_call" | custom-call | flops 1000000 | bytes 1 | tf_op jit(solution)/shard_map/self_mix/pallas_call | solution.py:99
  184.4 17.1 %cross_forward.1 = (bf16[512,1024]{1,0:T(8,128)(2,1)}, f32[512,1024]{1,0:T(8,128)}) custom-call(s32[1]{0:T(128)} %bitcast.5.refs_0_, bf16[512,1024]{1,0:T(8,128)(2,1)} %get-tuple-element.146.refs_1_, bf16[2,384,2048]{2,1,0:T(8,128)(2,1)} %bitcast.71, bf16[2,384,2048]{2,1,0:T(8,128)(2,1)} %bitcast.72, bf16[2,384,2048]{2,1,0:T(8,128)(2,1)} %bitcast.75, ...), custom_call_target="tpu_custom_call" | custom-call | flops 1000000 | bytes 1 | tf_op jit(solution)/shard_map/cross_forward/pallas_call | solution.py:99
  201.5 6.9 %cross_mix.1 = (f32[512,1024]{1,0:T(8,128)}, f32[512,1024]{1,0:T(8,128)}, bf16[512,1024]{1,0:T(8,128)(2,1)}) custom-call(s32[4]{0:T(128)} %pad_add_fusion.refs_0_, bf16[512,1024]{1,0:T(8,128)(2,1)} %get-tuple-element.149.refs_1_.refs_2_.refs_7_, f32[512,1024]{1,0:T(8,128)} %get-tuple-element.150.refs_2_, f32[8,1024]{1,0:T(8,128)} %norm_table.1.refs_6_.refs_3_.refs_4_, ...), custom_call_target="tpu_custom_call" | custom-call | flops 1000000 | bytes 1 | tf_op jit(solution)/shard_map/cross_mix/pallas_call | solution.py:99
  208.4 6.7 %turn_rows.5 = (bf16[512,1536]{1,0:T(8,128)(2,1)}, bf16[512,1536]{1,0:T(8,128)(2,1)}) custom-call(s32[4]{0:T(128)} %pad_add_fusion.refs_0_, bf16[512,1024]{1,0:T(8,128)(2,1)} %get-tuple-element.153.refs_1_, bf16[512,1024]{1,0:T(8,128)(2,1)} %get-tuple-element.149.refs_1_.refs_2_.refs_7_, bf16[512,1024]{1,0:T(8,128)(2,1)} %get-tuple-element.151.refs_3_.refs_1_, ...), custom_call_target="tpu_custom_call" | custom-call | flops 1000000 | bytes 1 | tf_op jit(solution)/shard_map/turn_rows/pallas_call | solution.py:99
  215.1 4.0 collective-permute-done.20.refs_2_
  229.8 17.4 %feed_in.1 = (bf16[512,4096]{1,0:T(8,128)(2,1)}, bf16[512,4096]{1,0:T(8,128)(2,1)}, bf16[2048,512]{1,0:T(8,128)(2,1)}, bf16[2048,512]{1,0:T(8,128)(2,1)}) custom-call(s32[4]{0:T(128)} %pad_add_fusion.refs_0_, bf16[512,1024]{1,0:T(8,128)(2,1)} %get-tuple-element.151.refs_3_.refs_1_, bf16[8,64,4096]{2,1,0:T(8,128)(2,1)} %bitcast.80, ...), custom_call_target="tpu_custom_call" | custom-call | flops 1000000 | bytes 1 | tf_op jit(solution)/shard_map/feed_in/pallas_call | solution.py:99
  247.4 13.9 %feed_out.1 = (bf16[512,1024]{1,0:T(8,128)(2,1)}, f32[512,1024]{1,0:T(8,128)}, bf16[512,1024]{1,0:T(8,128)(2,1)}, f32[16,1024]{1,0:T(8,128)}) custom-call(s32[4]{0:T(128)} %pad_add_fusion.refs_0_, bf16[512,4096]{1,0:T(8,128)(2,1)} %get-tuple-element.157.refs_1_, f32[512,1024]{1,0:T(8,128)} %get-tuple-element.158.refs_2_, ...), custom_call_target="tpu_custom_call" | custom-call | flops 1000000 | bytes 1 | tf_op jit(solution)/shard_map/feed_out/pallas_call | solution.py:99
  264.4 10.4 %weight_grad.7 = (bf16[2,4,128,512]{3,2,1,0:T(8,128)(2,1)}, bf16[2,4,128,512]{3,2,1,0:T(8,128)(2,1)}, bf16[2,4,128,512]{3,2,1,0:T(8,128)(2,1)}, bf16[2,4,128,512]{3,2,1,0:T(8,128)(2,1)}) custom-call(s32[4]{0:T(128)} %pad_add_fusion.refs_0_, bf16[2048,512]{1,0:T(8,128)(2,1)} %get-tuple-element.163.refs_1_, bf16[2048,512]{1,0:T(8,128)(2,1)} %collective-permute-done.25.refs_2_, ...), custom_call_target="tpu_custom_call" | custom-call | flops 1000000 | bytes 1 | tf_op jit(solution)/shard_map/weight_grad/pallas_call | solution.py:99
  276.7 10.1 %feed_back.1.refs_1_.refs_3_ = bf16[512,4096]{1,0:T(8,128)(2,1)} custom-call(s32[4]{0:T(128)} %pad_add_fusion.refs_0_, bf16[512,1024]{1,0:T(8,128)(2,1)} %get-tuple-element.161.refs_3_.refs_1_, bf16[512,4096]{1,0:T(8,128)(2,1)} %get-tuple-element.162.refs_2_, bf16[8,256,1024]{2,1,0:T(8,128)(2,1)} %bitcast.70, ...), custom_call_target="tpu_custom_call" | custom-call | flops 1000000 | bytes 1 | tf_op jit(solution)/shard_map/feed_back/pallas_call | solution.py:99
  286.9 14.4 %cross_back.1 = (f32[512,1024]{1,0:T(8,128)}, bf16[512,1024]{1,0:T(8,128)(2,1)}, bf16[512,1024]{1,0:T(8,128)(2,1)}, f32[16,1024]{1,0:T(8,128)}) custom-call(s32[4]{0:T(128)} %pad_add_fusion.refs_0_, bf16[512,4096]{1,0:T(8,128)(2,1)} %feed_back.1.refs_1_.refs_3_, f32[512,1024]{1,0:T(8,128)} %get-tuple-element.166.refs_2_, ...), custom_call_target="tpu_custom_call" | custom-call | flops 1000000 | bytes 1 | tf_op jit(solution)/shard_map/cross_back/pallas_call | solution.py:99
  305.1 10.1 %weight_grad.8 = (bf16[2,4,32,2048]{3,2,1,0:T(8,128)(2,1)}, bf16[2,4,32,2048]{3,2,1,0:T(8,128)(2,1)}, bf16[2,4,32,2048]{3,2,1,0:T(8,128)(2,1)}, bf16[2,4,32,2048]{3,2,1,0:T(8,128)(2,1)}) custom-call(s32[4]{0:T(128)} %pad_add_fusion.refs_0_, bf16[512,1536]{1,0:T(8,128)(2,1)} %get-tuple-element.155.refs_3_.refs_1_, ...), custom_call_target="tpu_custom_call" | custom-call | flops 1000000 | bytes 1 | tf_op jit(solution)/shard_map/weight_grad/pallas_call | solution.py:99
  321.5 4.8 weight_grad.9
  326.2 23.9 %cross_backward.1 = (bf16[512,1024]{1,0:T(8,128)(2,1)}, bf16[768,2048]{1,0:T(8,128)(2,1)}, bf16[768,2048]{1,0:T(8,128)(2,1)}) custom-call(s32[1]{0:T(128)} %bitcast.5.refs_0_, bf16[512,1024]{1,0:T(8,128)(2,1)} %get-tuple-element.146.refs_1_, bf16[2,384,2048]{2,1,0:T(8,128)(2,1)} %bitcast.73, bf16[2,384,2048]{2,1,0:T(8,128)(2,1)} %bitcast.74, ...), custom_call_target="tpu_custom_call" | custom-call | flops 1000000 | bytes 1 | tf_op jit(solution)/shard_map/cross_backward/pallas_call | solution.py:99
  352.8 5.0 add_blocks.8
  357.8 8.9 %self_back.1 = (f32[512,1024]{1,0:T(8,128)}, bf16[512,1024]{1,0:T(8,128)(2,1)}, bf16[512,1024]{1,0:T(8,128)(2,1)}, f32[16,1024]{1,0:T(8,128)}) custom-call(s32[4]{0:T(128)} %pad_add_fusion.refs_0_, bf16[512,1024]{1,0:T(8,128)(2,1)} %get-tuple-element.177.refs_11_.refs_1_.refs_3_, f32[512,1024]{1,0:T(8,128)} %get-tuple-element.173.refs_5_.refs_2_, ...), custom_call_target="tpu_custom_call" | custom-call | flops 1000000 | bytes 1 | tf_op jit(solution)/shard_map/self_back/pallas_call | solution.py:99
  372.8 13.0 %weight_grad.10 = (bf16[2,4,32,2048]{3,2,1,0:T(8,128)(2,1)}, bf16[2,4,32,2048]{3,2,1,0:T(8,128)(2,1)}) custom-call(s32[4]{0:T(128)} %pad_add_fusion.refs_0_, bf16[512,1280]{1,0:T(8,128)(2,1)} %get-tuple-element.130.refs_2_.refs_1_.refs_3_, bf16[512,1280]{1,0:T(8,128)(2,1)} %get-tuple-element.130.refs_2_.refs_1_.refs_3_, ...), custom_call_target="tpu_custom_call" | custom-call | flops 1000000 | bytes 1 | tf_op jit(solution)/shard_map/weight_grad/pallas_call | solution.py:99
  386.5 4.8 weight_grad.11
  392.7 3.6 add_blocks.9.refs_7_
  396.3 14.9 %self_backward.1.refs_7_.refs_3_.refs_1_ = bf16[512,3072]{1,0:T(8,128)(2,1)} custom-call(s32[3]{0:T(128)} %pad_add_fusion.1.refs_0_, bf16[512,3072]{1,0:T(8,128)(2,1)} %self_project.1.refs_2_.refs_1_.refs_3_, bf16[512,3072]{1,0:T(8,128)(2,1)} %self_project.1.refs_2_.refs_1_.refs_3_, bf16[512,3072]{1,0:T(8,128)(2,1)} %self_project.1.refs_2_.refs_1_.refs_3_, ...), custom_call_target="tpu_custom_call" | custom-call | flops 1000000 | bytes 1 | tf_op jit(solution)/shard_map/self_backward/pallas_call | solution.py:99
  411.3 4.9 weight_grad.12
  424.1 9.6 %weight_grad.13 = (bf16[2,4,32,1536]{3,2,1,0:T(8,128)(2,1)}, bf16[2,4,32,1536]{3,2,1,0:T(8,128)(2,1)}, bf16[2,4,32,1536]{3,2,1,0:T(8,128)(2,1)}, bf16[2,4,32,1536]{3,2,1,0:T(8,128)(2,1)}) custom-call(s32[4]{0:T(128)} %pad_add_fusion.refs_0_, bf16[512,1280]{1,0:T(8,128)(2,1)} %get-tuple-element.130.refs_2_.refs_1_.refs_3_, ...), custom_call_target="tpu_custom_call" | custom-call | flops 1000000 | bytes 1 | tf_op jit(solution)/shard_map/weight_grad/pallas_call | solution.py:99
  438.3 3.6 add_blocks.11.refs_4_
  441.9 7.7 %memory_back.2.refs_9_.refs_1_ = bf16[768,1024]{1,0:T(8,128)(2,1)} custom-call(s32[4]{0:T(128)} %pad_add_fusion.refs_0_, bf16[768,2048]{1,0:T(8,128)(2,1)} %get-tuple-element.188.refs_14_.refs_1_, bf16[8,64,5248]{2,1,0:T(8,128)(2,1)} %bitcast.66, bf16[8,64,5248]{2,1,0:T(8,128)(2,1)} %collective-permute-done.15.refs_2_.refs_5_.refs_8_.refs_6_.refs_3_, ...), custom_call_target="tpu_custom_call" | custom-call | flops 1000000 | bytes 1 | tf_op jit(solution)/shard_map/memory_back/pallas_call | solution.py:99
  449.7 9.1 %collective-permute-done.47.refs_4_.refs_11_ = bf16[2,4,32,1536]{3,2,1,0:T(8,128)(2,1)} collective-permute-done((bf16[2,4,32,1536]{3,2,1,0:T(8,128)(2,1)}, bf16[2,4,32,1536]{3,2,1,0:T(8,128)(2,1)}, u32[]{:S(2)}, u32[]{:S(2)}) %collective-permute-start.47) | collective-permute-done | bytes 786464 | tf_op jit(solution)/shard_map/ppermute | solution.py:402
  458.8 3.4 add_blocks.12
  468.0 8.5 %collective-permute-done.51.refs_3_ = bf16[4,32,640]{2,1,0:T(8,128)(2,1)} collective-permute-done((bf16[4,32,640]{2,1,0:T(8,128)(2,1)}, bf16[4,32,640]{2,1,0:T(8,128)(2,1)}, u32[]{:S(2)}, u32[]{:S(2)}) %collective-permute-start.51) | collective-permute-done | bytes 163872 | tf_op jit(solution)/shard_map/ppermute | solution.py:402
  478.1 3.9 add_blocks.13
  490.1 7.7 %memory_back.3.refs_5_.refs_1_ = bf16[768,1024]{1,0:T(8,128)(2,1)} custom-call(s32[4]{0:T(128)} %pad_add_fusion.refs_0_, bf16[768,2048]{1,0:T(8,128)(2,1)} %get-tuple-element.187.refs_13_.refs_1_, bf16[8,64,5248]{2,1,0:T(8,128)(2,1)} %bitcast.67, bf16[8,64,5248]{2,1,0:T(8,128)(2,1)} %collective-permute-done.15.refs_2_.refs_5_.refs_8_.refs_6_.refs_3_, ...), custom_call_target="tpu_custom_call" | custom-call | flops 1000000 | bytes 1 | tf_op jit(solution)/shard_map/memory_back/pallas_call | solution.py:99
  497.8 9.6 %target_back.1.refs_6_ = bf16[512,1024]{1,0:T(8,128)(2,1)} custom-call(s32[4]{0:T(128)} %pad_add_fusion.refs_0_, bf16[512,3072]{1,0:T(8,128)(2,1)} %self_backward.1.refs_7_.refs_3_.refs_1_, f32[512,1024]{1,0:T(8,128)} %get-tuple-element.189.refs_17_.refs_2_, bf16[8,64,3072]{2,1,0:T(8,128)(2,1)} %bitcast.84, ...), custom_call_target="tpu_custom_call" | custom-call | flops 1000000 | bytes 1 | tf_op jit(solution)/shard_map/target_back/pallas_call | solution.py:99
  512.5 3.8 move_blocks.27
  (198 shorter events, 115.9 us)
Async XLA Ops:
  7.2 67.5 %all-gather.4.cloned.1.call-start = ((), (), s32[]{:S(2)}) async-start(), calls=%async_computation.3 | async-start | bytes 1679360 | tf_op jit(solution)/shard_map/all_gather | solution.py:425
  15.6 23.4 %collective-permute-start.3 = (bf16[384,1024]{1,0:T(8,128)(2,1)}, bf16[384,1024]{1,0:T(8,128)(2,1)}, u32[]{:S(2)}, u32[]{:S(2)}) collective-permute-start(bf16[384,1024]{1,0:T(8,128)(2,1)} %get-tuple-element.122), channel_id=1, source_target_pairs={{0,1},{1,0},{2,3},{3,2},{4,5},{5,4},{6,7},{7,6},{8,9},{9,8},{10,11... | collective-permute-start | bytes 2359304 | tf_op jit(solution)/shard_map/ppermute | solution.py:406
  18.6 17.9 %collective-permute-start.2 = (bf16[32,3072]{1,0:T(8,128)(2,1)}, bf16[32,3072]{1,0:T(8,128)(2,1)}, u32[]{:S(2)}, u32[]{:S(2)}) collective-permute-start(bf16[32,3072]{1,0:T(8,128)(2,1)} %get-tuple-element.118.refs_2_.refs_1_), channel_id=1, source_target_pairs={{0,24},{2,26},{4,28},{6,30},{8,16},{10,18},{12,20},{14,22},{16,8},... | collective-permute-start | bytes 589832 | tf_op jit(solution)/shard_map/ppermute | solution.py:411
  41.6 76.6 %all-gather.6.cloned.1.call-start = ((), (), s32[]{:S(2)}) async-start(), calls=%async_computation.4 | async-start | bytes 1310720 | tf_op jit(solution)/shard_map/all_gather | solution.py:425
  43.8 99.8 %all-gather.8.cloned.1.call-start = ((), (), s32[]{:S(2)}) async-start(), calls=%async_computation.5 | async-start | bytes 1310720 | tf_op jit(solution)/shard_map/all_gather | solution.py:425
  57.0 23.6 %collective-permute-start.8 = (bf16[2,4,32,1536]{3,2,1,0:T(8,128)(2,1)}, bf16[2,4,32,1536]{3,2,1,0:T(8,128)(2,1)}, u32[]{:S(2)}, u32[]{:S(2)}) collective-permute-start(bf16[2,4,32,1536]{3,2,1,0:T(8,128)(2,1)} %get-tuple-element.128), channel_id=1, source_target_pairs={{0,4},{2,6},{4,0},{6,2},{8,12},{10,14},{12,8},{14,10},{16,20},{18,... | collective-permute-start | bytes 2359304 | tf_op jit(solution)/shard_map/ppermute | solution.py:402
  57.7 23.0 %collective-permute-start.7 = (bf16[2,4,32,1536]{3,2,1,0:T(8,128)(2,1)}, bf16[2,4,32,1536]{3,2,1,0:T(8,128)(2,1)}, u32[]{:S(2)}, u32[]{:S(2)}) collective-permute-start(bf16[2,4,32,1536]{3,2,1,0:T(8,128)(2,1)} %get-tuple-element.127.refs_3_), channel_id=1, source_target_pairs={{0,1},{1,0},{2,3},{3,2},{4,5},{5,4},{6,7},{7,6},{8,9},{9,8},{10,11... | collective-permute-start | bytes 2359304 | tf_op jit(solution)/shard_map/ppermute | solution.py:406
  63.7 20.1 %collective-permute-start.12 = (bf16[512,1280]{1,0:T(8,128)(2,1)}, bf16[512,1280]{1,0:T(8,128)(2,1)}, u32[]{:S(2)}, u32[]{:S(2)}) collective-permute-start(bf16[512,1280]{1,0:T(8,128)(2,1)} %get-tuple-element.133), channel_id=1, source_target_pairs={{0,2},{2,0},{4,6},{6,4},{8,10},{10,8},{12,14},{14,12},{16,18},{18,... | collective-permute-start | bytes 3932168 | tf_op jit(solution)/shard_map/ppermute | solution.py:397
  79.1 18.6 %collective-permute-start.11 = (bf16[4,32,3072]{2,1,0:T(8,128)(2,1)}, bf16[4,32,3072]{2,1,0:T(8,128)(2,1)}, u32[]{:S(2)}, u32[]{:S(2)}) collective-permute-start(bf16[4,32,3072]{2,1,0:T(8,128)(2,1)} %get-tuple-element.132.refs_3_), channel_id=1, source_target_pairs={{0,1},{1,0},{2,3},{3,2},{4,5},{5,4},{6,7},{7,6},{8,9},{9,8},{10,11... | collective-permute-start | bytes 2359304 | tf_op jit(solution)/shard_map/ppermute | solution.py:406
  83.7 25.3 %collective-permute-start.9 = (bf16[8,64,3072]{2,1,0:T(8,128)(2,1)}, bf16[8,64,3072]{2,1,0:T(8,128)(2,1)}, u32[]{:S(2)}, u32[]{:S(2)}) collective-permute-start(bf16[8,64,3072]{2,1,0:T(8,128)(2,1)} %bitcast.82), channel_id=1, source_target_pairs={{0,2},{2,0},{4,6},{6,4},{8,10},{10,8},{12,14},{14,12},{16,18},{18,... | collective-permute-start | bytes 9437192 | tf_op jit(solution)/shard_map/ppermute | solution.py:397
  102.3 37.7 %collective-permute-start.14 = (bf16[2,4,32,3072]{3,2,1,0:T(8,128)(2,1)}, bf16[2,4,32,3072]{3,2,1,0:T(8,128)(2,1)}, u32[]{:S(2)}, u32[]{:S(2)}) collective-permute-start(bf16[2,4,32,3072]{3,2,1,0:T(8,128)(2,1)} %get-tuple-element.139), channel_id=1, source_target_pairs={{0,4},{2,6},{4,0},{6,2},{8,12},{10,14},{12,8},{14,10},{16,20},{18,... | collective-permute-start | bytes 4718600 | tf_op jit(solution)/shard_map/ppermute | solution.py:402
  102.9 30.9 %collective-permute-start.13 = (bf16[2,4,32,2176]{3,2,1,0:T(8,128)(2,1)}, bf16[2,4,32,2176]{3,2,1,0:T(8,128)(2,1)}, u32[]{:S(2)}, u32[]{:S(2)}) collective-permute-start(bf16[2,4,32,2176]{3,2,1,0:T(8,128)(2,1)} %get-tuple-element.134.refs_4_), channel_id=1, source_target_pairs={{0,1},{1,0},{2,3},{3,2},{4,5},{5,4},{6,7},{7,6},{8,9},{9,8},{10,11... | collective-permute-start | bytes 3342344 | tf_op jit(solution)/shard_map/ppermute | solution.py:406
  109.0 327.7 %reduce-scatter.4.cloned.1.call-start = ((), (), s32[]{:S(2)}) async-start(), calls=%async_computation.6 | async-start | bytes 1310720 | tf_op jit(solution)/shard_map/reduce_scatter | solution.py:1279
  117.7 26.6 %collective-permute-start.16 = (bf16[384,1024]{1,0:T(8,128)(2,1)}, bf16[384,1024]{1,0:T(8,128)(2,1)}, u32[]{:S(2)}, u32[]{:S(2)}) collective-permute-start(bf16[384,1024]{1,0:T(8,128)(2,1)} %gate.2.refs_2_), channel_id=1, source_target_pairs={{0,1},{1,0},{2,3},{3,2},{4,5},{5,4},{6,7},{7,6},{8,9},{9,8},{10,11... | collective-permute-start | bytes 2359304 | tf_op jit(solution)/shard_map/ppermute | solution.py:406
  118.9 47.9 %collective-permute-start.19 = (bf16[4,32,4096]{2,1,0:T(8,128)(2,1)}, bf16[4,32,4096]{2,1,0:T(8,128)(2,1)}, u32[]{:S(2)}, u32[]{:S(2)}) collective-permute-start(bf16[4,32,4096]{2,1,0:T(8,128)(2,1)} %move_blocks.20.refs_5_.refs_1_), channel_id=1, source_target_pairs={{0,4},{2,6},{4,0},{6,2},{8,12},{10,14},{12,8},{14,10},{16,20},{18,... | collective-permute-start | bytes 3145736 | tf_op jit(solution)/shard_map/ppermute | solution.py:402
  144.9 26.8 %collective-permute-start.18 = (bf16[4,128,1024]{2,1,0:T(8,128)(2,1)}, bf16[4,128,1024]{2,1,0:T(8,128)(2,1)}, u32[]{:S(2)}, u32[]{:S(2)}) collective-permute-start(bf16[4,128,1024]{2,1,0:T(8,128)(2,1)} %move_blocks.22.refs_4_.refs_1_), channel_id=1, source_target_pairs={{0,1},{1,0},{2,3},{3,2},{4,5},{5,4},{6,7},{7,6},{8,9},{9,8},{10,11... | collective-permute-start | bytes 3145736 | tf_op jit(solution)/shard_map/ppermute | solution.py:406
  153.2 23.3 %collective-permute-start.17 = (bf16[512,1280]{1,0:T(8,128)(2,1)}, bf16[512,1280]{1,0:T(8,128)(2,1)}, u32[]{:S(2)}, u32[]{:S(2)}) collective-permute-start(bf16[512,1280]{1,0:T(8,128)(2,1)} %get-tuple-element.142), channel_id=1, source_target_pairs={{0,2},{2,0},{4,6},{6,4},{8,10},{10,8},{12,14},{14,12},{16,18},{18,... | collective-permute-start | bytes 3932168 | tf_op jit(solution)/shard_map/ppermute | solution.py:397
  170.7 48.4 %collective-permute-start.20 = (bf16[2,4,32,4096]{3,2,1,0:T(8,128)(2,1)}, bf16[2,4,32,4096]{3,2,1,0:T(8,128)(2,1)}, u32[]{:S(2)}, u32[]{:S(2)}) collective-permute-start(bf16[2,4,32,4096]{3,2,1,0:T(8,128)(2,1)} %get-tuple-element.144.refs_3_), channel_id=1, source_target_pairs={{0,1},{1,0},{2,3},{3,2},{4,5},{5,4},{6,7},{7,6},{8,9},{9,8},{10,11... | collective-permute-start | bytes 6291464 | tf_op jit(solution)/shard_map/ppermute | solution.py:406
  175.5 47.8 %collective-permute-start.22 = (bf16[2,4,128,1024]{3,2,1,0:T(8,128)(2,1)}, bf16[2,4,128,1024]{3,2,1,0:T(8,128)(2,1)}, u32[]{:S(2)}, u32[]{:S(2)}) collective-permute-start(bf16[2,4,128,1024]{3,2,1,0:T(8,128)(2,1)} %get-tuple-element.145.refs_7_), channel_id=1, source_target_pairs={{0,4},{2,6},{4,0},{6,2},{8,12},{10,14},{12,8},{14,10},{16,20},{18,... | collective-permute-start | bytes 6291464 | tf_op jit(solution)/shard_map/ppermute | solution.py:402
  226.3 21.1 %collective-permute-start.23 = (bf16[8,256,1024]{2,1,0:T(8,128)(2,1)}, bf16[8,256,1024]{2,1,0:T(8,128)(2,1)}, u32[]{:S(2)}, u32[]{:S(2)}) collective-permute-start(bf16[8,256,1024]{2,1,0:T(8,128)(2,1)} %bitcast.68), channel_id=1, source_target_pairs={{0,2},{2,0},{4,6},{6,4},{8,10},{10,8},{12,14},{14,12},{16,18},{18,... | collective-permute-start | bytes 12582920 | tf_op jit(solution)/shard_map/ppermute | solution.py:397
  226.4 21.0 %collective-permute-start.24 = (bf16[512,1536]{1,0:T(8,128)(2,1)}, bf16[512,1536]{1,0:T(8,128)(2,1)}, u32[]{:S(2)}, u32[]{:S(2)}) collective-permute-start(bf16[512,1536]{1,0:T(8,128)(2,1)} %get-tuple-element.159), channel_id=1, source_target_pairs={{0,2},{2,0},{4,6},{6,4},{8,10},{10,8},{12,14},{14,12},{16,18},{18,... | collective-permute-start | bytes 4718600 | tf_op jit(solution)/shard_map/ppermute | solution.py:397
  247.2 17.1 %collective-permute-start.25 = (bf16[2048,512]{1,0:T(8,128)(2,1)}, bf16[2048,512]{1,0:T(8,128)(2,1)}, u32[]{:S(2)}, u32[]{:S(2)}) collective-permute-start(bf16[2048,512]{1,0:T(8,128)(2,1)} %get-tuple-element.164), channel_id=1, source_target_pairs={{0,2},{2,0},{4,6},{6,4},{8,10},{10,8},{12,14},{14,12},{16,18},{18,... | collective-permute-start | bytes 6291464 | tf_op jit(solution)/shard_map/ppermute | solution.py:397
  274.8 27.1 %collective-permute-start.30 = (bf16[2,4,128,512]{3,2,1,0:T(8,128)(2,1)}, bf16[2,4,128,512]{3,2,1,0:T(8,128)(2,1)}, u32[]{:S(2)}, u32[]{:S(2)}) collective-permute-start(bf16[2,4,128,512]{3,2,1,0:T(8,128)(2,1)} %get-tuple-element.172), channel_id=1, source_target_pairs={{0,4},{2,6},{4,0},{6,2},{8,12},{10,14},{12,8},{14,10},{16,20},{18,... | collective-permute-start | bytes 3145736 | tf_op jit(solution)/shard_map/ppermute | solution.py:402
  276.2 25.8 %collective-permute-start.29 = (bf16[2,4,128,512]{3,2,1,0:T(8,128)(2,1)}, bf16[2,4,128,512]{3,2,1,0:T(8,128)(2,1)}, u32[]{:S(2)}, u32[]{:S(2)}) collective-permute-start(bf16[2,4,128,512]{3,2,1,0:T(8,128)(2,1)} %get-tuple-element.165.refs_5_), channel_id=1, source_target_pairs={{0,1},{1,0},{2,3},{3,2},{4,5},{5,4},{6,7},{7,6},{8,9},{9,8},{10,11... | collective-permute-start | bytes 3145736 | tf_op jit(solution)/shard_map/ppermute | solution.py:406
  286.8 18.3 %collective-permute-start.28 = (bf16[512,4096]{1,0:T(8,128)(2,1)}, bf16[512,4096]{1,0:T(8,128)(2,1)}, u32[]{:S(2)}, u32[]{:S(2)}) collective-permute-start(bf16[512,4096]{1,0:T(8,128)(2,1)} %feed_back.1.refs_1_.refs_3_), channel_id=1, source_target_pairs={{0,2},{2,0},{4,6},{6,4},{8,10},{10,8},{12,14},{14,12},{16,18},{18,... | collective-permute-start | bytes 12582920 | tf_op jit(solution)/shard_map/ppermute | solution.py:397
  301.4 20.1 %collective-permute-start.27 = (bf16[512,1024]{1,0:T(8,128)(2,1)}, bf16[512,1024]{1,0:T(8,128)(2,1)}, u32[]{:S(2)}, u32[]{:S(2)}) collective-permute-start(bf16[512,1024]{1,0:T(8,128)(2,1)} %get-tuple-element.169.refs_3_), channel_id=1, source_target_pairs={{0,2},{2,0},{4,6},{6,4},{8,10},{10,8},{12,14},{14,12},{16,18},{18,... | collective-permute-start | bytes 3145736 | tf_op jit(solution)/shard_map/ppermute | solution.py:397
  315.2 37.5 %collective-permute-start.32 = (bf16[2,4,32,2048]{3,2,1,0:T(8,128)(2,1)}, bf16[2,4,32,2048]{3,2,1,0:T(8,128)(2,1)}, u32[]{:S(2)}, u32[]{:S(2)}) collective-permute-start(bf16[2,4,32,2048]{3,2,1,0:T(8,128)(2,1)} %get-tuple-element.180), channel_id=1, source_target_pairs={{0,4},{2,6},{4,0},{6,2},{8,12},{10,14},{12,8},{14,10},{16,20},{18,... | collective-permute-start | bytes 3145736 | tf_op jit(solution)/shard_map/ppermute | solution.py:402
  315.9 36.9 %collective-permute-start.31 = (bf16[2,4,32,2048]{3,2,1,0:T(8,128)(2,1)}, bf16[2,4,32,2048]{3,2,1,0:T(8,128)(2,1)}, u32[]{:S(2)}, u32[]{:S(2)}) collective-permute-start(bf16[2,4,32,2048]{3,2,1,0:T(8,128)(2,1)} %get-tuple-element.175.refs_5_), channel_id=1, source_target_pairs={{0,1},{1,0},{2,3},{3,2},{4,5},{5,4},{6,7},{7,6},{8,9},{9,8},{10,11... | collective-permute-start | bytes 3145736 | tf_op jit(solution)/shard_map/ppermute | solution.py:406
  317.5 34.8 %collective-permute-start.33 = (bf16[4,128,512]{2,1,0:T(8,128)(2,1)}, bf16[4,128,512]{2,1,0:T(8,128)(2,1)}, u32[]{:S(2)}, u32[]{:S(2)}) collective-permute-start(bf16[4,128,512]{2,1,0:T(8,128)(2,1)} %get-tuple-element.174.refs_5_), channel_id=1, source_target_pairs={{0,4},{2,6},{4,0},{6,2},{8,12},{10,14},{12,8},{14,10},{16,20},{18,... | collective-permute-start | bytes 1572872 | tf_op jit(solution)/shard_map/ppermute | solution.py:402
  318.9 33.4 %collective-permute-start.34 = (bf16[4,128,512]{2,1,0:T(8,128)(2,1)}, bf16[4,128,512]{2,1,0:T(8,128)(2,1)}, u32[]{:S(2)}, u32[]{:S(2)}) collective-permute-start(bf16[4,128,512]{2,1,0:T(8,128)(2,1)} %get-tuple-element.181), channel_id=1, source_target_pairs={{0,1},{1,0},{2,3},{3,2},{4,5},{5,4},{6,7},{7,6},{8,9},{9,8},{10,11... | collective-permute-start | bytes 1572872 | tf_op jit(solution)/shard_map/ppermute | solution.py:406
  350.2 36.3 %collective-permute-start.37 = (bf16[512,1024]{1,0:T(8,128)(2,1)}, bf16[512,1024]{1,0:T(8,128)(2,1)}, u32[]{:S(2)}, u32[]{:S(2)}) collective-permute-start(bf16[512,1024]{1,0:T(8,128)(2,1)} %get-tuple-element.177.refs_11_.refs_1_.refs_3_), channel_id=1, source_target_pairs={{0,2},{2,0},{4,6},{6,4},{8,10},{10,8},{12,14},{14,12},{16,18},{18,... | collective-permute-start | bytes 3145736 | tf_op jit(solution)/shard_map/ppermute | solution.py:397
  352.3 20.5 %collective-permute-start.38 = (bf16[768,2048]{1,0:T(8,128)(2,1)}, bf16[768,2048]{1,0:T(8,128)(2,1)}, u32[]{:S(2)}, u32[]{:S(2)}) collective-permute-start(bf16[768,2048]{1,0:T(8,128)(2,1)} %get-tuple-element.187.refs_13_.refs_1_), channel_id=1, source_target_pairs={{0,2},{2,0},{4,6},{6,4},{8,10},{10,8},{12,14},{14,12},{16,18},{18,... | collective-permute-start | bytes 9437192 | tf_op jit(solution)/shard_map/ppermute | solution.py:397
  352.3 20.5 %collective-permute-start.39 = (bf16[768,2048]{1,0:T(8,128)(2,1)}, bf16[768,2048]{1,0:T(8,128)(2,1)}, u32[]{:S(2)}, u32[]{:S(2)}) collective-permute-start(bf16[768,2048]{1,0:T(8,128)(2,1)} %get-tuple-element.188.refs_14_.refs_1_), channel_id=1, source_target_pairs={{0,2},{2,0},{4,6},{6,4},{8,10},{10,8},{12,14},{14,12},{16,18},{18,... | collective-permute-start | bytes 9437192 | tf_op jit(solution)/shard_map/ppermute | solution.py:397
  368.9 23.8 %collective-permute-start.36 = (bf16[4,32,2048]{2,1,0:T(8,128)(2,1)}, bf16[4,32,2048]{2,1,0:T(8,128)(2,1)}, u32[]{:S(2)}, u32[]{:S(2)}) collective-permute-start(bf16[4,32,2048]{2,1,0:T(8,128)(2,1)} %get-tuple-element.185), channel_id=1, source_target_pairs={{0,1},{1,0},{2,3},{3,2},{4,5},{5,4},{6,7},{7,6},{8,9},{9,8},{10,11... | collective-permute-start | bytes 1572872 | tf_op jit(solution)/shard_map/ppermute | solution.py:406
  370.5 22.2 %collective-permute-start.35 = (bf16[4,32,2048]{2,1,0:T(8,128)(2,1)}, bf16[4,32,2048]{2,1,0:T(8,128)(2,1)}, u32[]{:S(2)}, u32[]{:S(2)}) collective-permute-start(bf16[4,32,2048]{2,1,0:T(8,128)(2,1)} %get-tuple-element.182.refs_7_), channel_id=1, source_target_pairs={{0,4},{2,6},{4,0},{6,2},{8,12},{10,14},{12,8},{14,10},{16,20},{18,... | collective-permute-start | bytes 1572872 | tf_op jit(solution)/shard_map/ppermute | solution.py:402
  371.9 66.5 %reduce-scatter.6.cloned.1.call-start = ((), (), s32[]{:S(2)}) async-start(), calls=%async_computation.7 | async-start | bytes 1310720 | tf_op jit(solution)/shard_map/reduce_scatter | solution.py:1279
  372.8 38.5 %collective-permute-start.40 = (bf16[512,1024]{1,0:T(8,128)(2,1)}, bf16[512,1024]{1,0:T(8,128)(2,1)}, u32[]{:S(2)}, u32[]{:S(2)}) collective-permute-start(bf16[512,1024]{1,0:T(8,128)(2,1)} %get-tuple-element.192.refs_3_), channel_id=1, source_target_pairs={{0,2},{2,0},{4,6},{6,4},{8,10},{10,8},{12,14},{14,12},{16,18},{18,... | collective-permute-start | bytes 3145736 | tf_op jit(solution)/shard_map/ppermute | solution.py:397
  385.7 31.1 %collective-permute-start.45 = (bf16[2,4,32,2048]{3,2,1,0:T(8,128)(2,1)}, bf16[2,4,32,2048]{3,2,1,0:T(8,128)(2,1)}, u32[]{:S(2)}, u32[]{:S(2)}) collective-permute-start(bf16[2,4,32,2048]{3,2,1,0:T(8,128)(2,1)} %get-tuple-element.190.refs_7_), channel_id=1, source_target_pairs={{0,4},{2,6},{4,0},{6,2},{8,12},{10,14},{12,8},{14,10},{16,20},{18,... | collective-permute-start | bytes 3145736 | tf_op jit(solution)/shard_map/ppermute | solution.py:402
  391.2 25.6 %collective-permute-start.44 = (bf16[2,4,32,2048]{3,2,1,0:T(8,128)(2,1)}, bf16[2,4,32,2048]{3,2,1,0:T(8,128)(2,1)}, u32[]{:S(2)}, u32[]{:S(2)}) collective-permute-start(bf16[2,4,32,2048]{3,2,1,0:T(8,128)(2,1)} %get-tuple-element.191.refs_7_), channel_id=1, source_target_pairs={{0,1},{1,0},{2,3},{3,2},{4,5},{5,4},{6,7},{7,6},{8,9},{9,8},{10,11... | collective-permute-start | bytes 3145736 | tf_op jit(solution)/shard_map/ppermute | solution.py:406
  411.2 66.9 %reduce-scatter.8.cloned.1.call-start = ((), (), s32[]{:S(2)}) async-start(), calls=%async_computation.8 | async-start | bytes 1310720 | tf_op jit(solution)/shard_map/reduce_scatter | solution.py:1279
  422.9 26.8 %collective-permute-start.42 = (bf16[2,4,32,640]{3,2,1,0:T(8,128)(2,1)}, bf16[2,4,32,640]{3,2,1,0:T(8,128)(2,1)}, u32[]{:S(2)}, u32[]{:S(2)}) collective-permute-start(bf16[2,4,32,640]{3,2,1,0:T(8,128)(2,1)} %get-tuple-element.197.refs_5_), channel_id=1, source_target_pairs={{0,1},{1,0},{2,3},{3,2},{4,5},{5,4},{6,7},{7,6},{8,9},{9,8},{10,11... | collective-permute-start | bytes 983048 | tf_op jit(solution)/shard_map/ppermute | solution.py:406
  423.5 26.2 %collective-permute-start.48 = (bf16[2,4,32,640]{3,2,1,0:T(8,128)(2,1)}, bf16[2,4,32,640]{3,2,1,0:T(8,128)(2,1)}, u32[]{:S(2)}, u32[]{:S(2)}) collective-permute-start(bf16[2,4,32,640]{3,2,1,0:T(8,128)(2,1)} %get-tuple-element.206), channel_id=1, source_target_pairs={{0,4},{2,6},{4,0},{6,2},{8,12},{10,14},{12,8},{14,10},{16,20},{18,... | collective-permute-start | bytes 983048 | tf_op jit(solution)/shard_map/ppermute | solution.py:402
  433.7 25.1 %collective-permute-start.47 = (bf16[2,4,32,1536]{3,2,1,0:T(8,128)(2,1)}, bf16[2,4,32,1536]{3,2,1,0:T(8,128)(2,1)}, u32[]{:S(2)}, u32[]{:S(2)}) collective-permute-start(bf16[2,4,32,1536]{3,2,1,0:T(8,128)(2,1)} %get-tuple-element.204), channel_id=1, source_target_pairs={{0,4},{2,6},{4,0},{6,2},{8,12},{10,14},{12,8},{14,10},{16,20},{18,... | collective-permute-start | bytes 2359304 | tf_op jit(solution)/shard_map/ppermute | solution.py:402
  435.2 23.6 %collective-permute-start.46 = (bf16[2,4,32,1536]{3,2,1,0:T(8,128)(2,1)}, bf16[2,4,32,1536]{3,2,1,0:T(8,128)(2,1)}, u32[]{:S(2)}, u32[]{:S(2)}) collective-permute-start(bf16[2,4,32,1536]{3,2,1,0:T(8,128)(2,1)} %get-tuple-element.202.refs_9_), channel_id=1, source_target_pairs={{0,1},{1,0},{2,3},{3,2},{4,5},{5,4},{6,7},{7,6},{8,9},{9,8},{10,11... | collective-permute-start | bytes 2359304 | tf_op jit(solution)/shard_map/ppermute | solution.py:406
  466.9 45.6 %collective-permute-start.55 = (bf16[768,1024]{1,0:T(8,128)(2,1)}, bf16[768,1024]{1,0:T(8,128)(2,1)}, u32[]{:S(2)}, u32[]{:S(2)}) collective-permute-start(bf16[768,1024]{1,0:T(8,128)(2,1)} %gate.3.refs_14_), channel_id=1, source_target_pairs={{0,1},{1,0},{2,3},{3,2},{4,5},{5,4},{6,7},{7,6},{8,9},{9,8},{10,11... | collective-permute-start | bytes 4718600 | tf_op jit(solution)/shard_map/ppermute | solution.py:406
  482.1 25.3 %collective-permute-start.56 = (bf16[32,4352]{1,0:T(8,128)(2,1)}, bf16[32,4352]{1,0:T(8,128)(2,1)}, u32[]{:S(2)}, u32[]{:S(2)}) collective-permute-start(bf16[32,4352]{1,0:T(8,128)(2,1)} %get-tuple-element.214), channel_id=1, source_target_pairs={{0,8},{2,10},{4,12},{6,14},{8,0},{10,2},{12,4},{14,6},{16,24},{18,... | collective-permute-start | bytes 835592 | tf_op jit(solution)/shard_map/ppermute | solution.py:411
  483.8 23.7 %collective-permute-start.57 = (bf16[32,4352]{1,0:T(8,128)(2,1)}, bf16[32,4352]{1,0:T(8,128)(2,1)}, u32[]{:S(2)}, u32[]{:S(2)}) collective-permute-start(bf16[32,4352]{1,0:T(8,128)(2,1)} %get-tuple-element.215), channel_id=1, source_target_pairs={{0,16},{2,18},{4,20},{6,22},{8,24},{10,26},{12,28},{14,30},{16,0},... | collective-permute-start | bytes 835592 | tf_op jit(solution)/shard_map/ppermute | solution.py:411
  485.8 21.6 %collective-permute-start.58 = (bf16[32,4352]{1,0:T(8,128)(2,1)}, bf16[32,4352]{1,0:T(8,128)(2,1)}, u32[]{:S(2)}, u32[]{:S(2)}) collective-permute-start(bf16[32,4352]{1,0:T(8,128)(2,1)} %get-tuple-element.216), channel_id=1, source_target_pairs={{0,24},{2,26},{4,28},{6,30},{8,16},{10,18},{12,20},{14,22},{16,8},... | collective-permute-start | bytes 835592 | tf_op jit(solution)/shard_map/ppermute | solution.py:411
  (28 other events, 299.4 us)
Sparse Core Ops, SparseCore 0:
  41.8 32.8 all-gather.3
  76.8 26.8 all-gather.5
  109.1 26.7 all-gather.7
  372.0 26.9 reduce-scatter.3
  411.3 26.9 reduce-scatter.5
  442.0 25.7 reduce-scatter.7
